TPU v7x, 32 devices: a whole 2x2x4 slice. The times are simulated.
32 devices in a mesh: dp: 4 (over z), expert: 8 (over y, x, core).
Axes of the slice: x: 2, y: 2, z: 4, core: 2. Of those that a mesh axis runs over, the one named last changes fastest.
Arguments:
- hidden_in: bfloat16 [128, 5120], P(('dp', 'expert')), may hold values from -6 to 6
- query: bfloat16 [128, 36864], P(('dp', 'expert')), may hold values from -6 to 24
- prefix_pool: bfloat16 [64, 36864], P('dp'), may hold values from -6 to 6
- suffix_cache: bfloat16 [128, 73728], P(('dp', 'expert')), may hold values from -6 to 6
- block_list: int32 [128, 16], P(('dp', 'expert')), may hold values from 0 to 63, as said below
- prefix_count: int32 [128], P(('dp', 'expert')), may hold values from 1 to 16
- suffix_count: int32 [128], P(('dp', 'expert')), may hold values from 1 to 128
- value_up: bfloat16 [64, 512, 128], P('expert'), may hold values from -0.25 to 0.25
- out_proj: bfloat16 [8192, 5120], P('expert'), may hold values from -0.5 to 0.5
- norm_gain: bfloat16 [5120], replicated, may hold values from 0.5 to 1.5
- expert_ids: int32 [128, 6], P(('dp', 'expert')), may hold values from 0 to 7, all different within a row; in each aligned block of 4 rows (0 to 3, 4 to 7, ...) at most 3 rows name the same one
- gate_weights: bfloat16 [128, 6], P(('dp', 'expert')), may hold values from 0.049804688 to 1
- gate_proj: bfloat16 [8, 5120, 1536], P('expert', None, 'dp'), may hold values from -0.078125 to 0.078125
- up_proj: bfloat16 [8, 5120, 1536], P('expert', None, 'dp'), may hold values from -0.078125 to 0.078125
- down_proj: bfloat16 [8, 1536, 5120], P('expert', 'dp'), may hold values from -0.15625 to 0.15625
Outputs:
- residual_out: float32 [128, 5120], P(('dp', 'expert'))
- moe_out: float32 [128, 5120], P(('dp', 'expert'))
Inputs may be any that keep to these rules, and one draw needn't show every extreme that they name: `block_list`: each list names 16 distinct blocks; the lists form a prefix tree: two requests with the same block at a position have the same blocks at all earlier positions. `expert_ids`: each row names 6 different experts; among the rows of one device no expert is named more than 3 times.
All inputs are finite; a program needn't handle non-finite values.
Results may differ from a plain program's by a relative error of at most 0.025.
Values may be sent and summed in bfloat16 or wider, within the bound.
No kernel may reach another device: no remote copies, remote signals or barrier semaphores. Data moves between devices by JAX's collectives and lax.ppermute only.
A program may use at most 128 MiB of HBM per device.

v0:
```python
import jax
import jax.numpy as jnp
from jax import lax
from jax.sharding import PartitionSpec as P

HEADS = 64
LAT = 512
TOPK = 6
BLOCK = 64
SUFFIX = 128
KDIM = 576


NEG_FILL = -1e30
SCORE_SCALE = 192.0 ** (-0.5)
NORM_EPS = 1e-06


def slot_table(expert_rows, expert_total):
    matches = (expert_rows[..., None] == jnp.arange(expert_total, dtype=jnp.int32)).astype(
        jnp.int32
    )
    row_load = jnp.sum(matches, axis=-2)
    earlier = jnp.cumsum(row_load, axis=-2) - row_load
    return jnp.sum(matches * earlier[..., None, :], axis=-1)


def dispatch_matrix(expert_rows, slot_rows, expert_total, capacity):
    expert_match = expert_rows[..., None] == jnp.arange(expert_total, dtype=jnp.int32)
    slot_match = slot_rows[..., None] == jnp.arange(capacity, dtype=jnp.int32)
    joined = expert_match[..., :, None] & slot_match[..., None, :]
    return jnp.any(joined, axis=-3).astype(jnp.bfloat16)


def merge_keys(state, queries, key_rows, live_mask):
    running_max, running_sum, numerator = state
    scores = (
        jnp.einsum("rhk,nk->rhn", queries, key_rows, preferred_element_type=jnp.float32)
        * SCORE_SCALE
    )
    live_keys = live_mask[:, None, :]
    scores = jnp.where(live_keys, scores, NEG_FILL)
    new_max = jnp.maximum(running_max, jnp.max(scores, axis=-1))
    weights = jnp.where(live_keys, jnp.exp(scores - new_max[..., None]), 0.0)
    rescale = jnp.exp(running_max - new_max)
    running_sum = running_sum * rescale + jnp.sum(weights, axis=-1)
    numerator = numerator * rescale[..., None] + jnp.einsum(
        "rhn,nl->rhl",
        weights.astype(jnp.bfloat16),
        key_rows[:, :LAT],
        preferred_element_type=jnp.float32,
    )
    return (new_max, running_sum, numerator)


def prefix_partial(state, pool_piece, queries, block_rows, counts):
    piece_blocks = pool_piece.shape[0]
    key_rows = pool_piece.reshape(piece_blocks * BLOCK, KDIM)
    block_ids = jnp.arange(piece_blocks, dtype=jnp.int32)
    in_prefix = jnp.arange(block_rows.shape[1], dtype=jnp.int32)[None, :] < counts[:, None]
    member = jnp.any(
        (block_rows[:, :, None] == block_ids[None, None, :]) & in_prefix[:, :, None], axis=1
    )
    live_mask = jnp.repeat(member, BLOCK, axis=1)
    return merge_keys(state, queries, key_rows, live_mask)


def own_partial(queries, own_keys, own_live):
    scores = (
        jnp.einsum("rhk,rnk->rhn", queries, own_keys, preferred_element_type=jnp.float32)
        * SCORE_SCALE
    )
    live_keys = own_live[:, None, :]
    scores = jnp.where(live_keys, scores, NEG_FILL)
    row_max = jnp.max(scores, axis=-1)
    weights = jnp.where(live_keys, jnp.exp(scores - row_max[..., None]), 0.0)
    numerator = jnp.einsum(
        "rhn,rnl->rhl",
        weights.astype(jnp.bfloat16),
        own_keys[:, :, :LAT],
        preferred_element_type=jnp.float32,
    )
    return (row_max, jnp.sum(weights, axis=-1), numerator)


def run_experts(arrived, expert_axis, gate_proj, up_proj, down_proj):
    local_count = gate_proj.shape[0]
    arrived_shape = arrived.shape
    grouped = arrived.reshape(
        arrived_shape[:expert_axis]
        + (arrived_shape[expert_axis] // local_count, local_count)
        + arrived_shape[expert_axis + 1 :]
    )
    selected = lax.index_in_dim(grouped, 0, expert_axis + 1, keepdims=False)
    flat_rows = selected.reshape(-1, arrived_shape[-1])
    gate_part = jnp.dot(flat_rows, gate_proj[0], preferred_element_type=jnp.float32)
    up_part = jnp.dot(flat_rows, up_proj[0], preferred_element_type=jnp.float32)
    hidden = (jax.nn.silu(gate_part) * up_part).astype(jnp.bfloat16)
    result = jnp.dot(hidden, down_proj[0], preferred_element_type=jnp.float32).astype(jnp.bfloat16)
    outputs = [result.reshape(selected.shape)]
    return jnp.stack(outputs, axis=expert_axis + 1).reshape(arrived_shape)


def per_device(
    hidden_in,
    query,
    prefix_pool,
    suffix_cache,
    block_list,
    prefix_count,
    suffix_count,
    value_up,
    out_proj,
    norm_gain,
    expert_ids,
    gate_weights,
    gate_proj,
    up_proj,
    down_proj,
):
    row_count = hidden_in.shape[0]
    queries = query.reshape(row_count, HEADS, KDIM)
    own_keys = suffix_cache.reshape(row_count, SUFFIX, KDIM)
    own_live = jnp.arange(SUFFIX, dtype=jnp.int32)[None, :] < suffix_count[:, None]
    own_state = own_partial(queries, own_keys, own_live)
    running_max, running_sum, numerator = prefix_partial(
        own_state,
        lax.all_gather(prefix_pool, "dp", axis=0, tiled=True),
        queries,
        block_list,
        prefix_count,
    )
    context = (numerator / running_sum[..., None]).astype(jnp.bfloat16)
    head_context = lax.all_to_all(context, "expert", split_axis=1, concat_axis=0, tiled=True)
    head_values = jnp.einsum(
        "thl,hlv->thv", head_context, value_up, preferred_element_type=jnp.float32
    ).astype(jnp.bfloat16)
    value_rows = head_values.reshape(head_values.shape[0], -1)
    attended = lax.psum_scatter(
        jnp.dot(value_rows, out_proj, preferred_element_type=jnp.float32),
        "expert",
        scatter_dimension=0,
        tiled=True,
    )
    residual_out = hidden_in.astype(jnp.float32) + attended
    scale_rows = lax.rsqrt(jnp.mean(residual_out * residual_out, axis=-1, keepdims=True) + NORM_EPS)
    normed = (residual_out * scale_rows * norm_gain.astype(jnp.float32)).astype(jnp.bfloat16)
    expert_total = gate_proj.shape[0] * lax.axis_size("expert")
    capacity = max(2, (row_count * TOPK + expert_total - 1) // expert_total)
    group_tokens, group_ids, group_gates = (
        lax.all_gather(normed, "dp", axis=0, tiled=True),
        lax.all_gather(expert_ids, "dp", axis=0, tiled=True),
        lax.all_gather(gate_weights, "dp", axis=0, tiled=True),
    )
    holders = lax.axis_size("dp")
    group_tokens = group_tokens.reshape(holders, row_count, -1)
    group_ids = group_ids.reshape(holders, row_count, TOPK)
    group_gates = group_gates.reshape(holders, row_count, TOPK).astype(jnp.float32)
    group_slots = slot_table(group_ids, expert_total)
    dispatch_table = dispatch_matrix(group_ids, group_slots, expert_total, capacity)
    outgoing = jnp.einsum(
        "nrec,nrd->encd", dispatch_table, group_tokens, preferred_element_type=jnp.float32
    ).astype(jnp.bfloat16)
    finished = run_experts(
        lax.all_to_all(outgoing, "expert", split_axis=0, concat_axis=0, tiled=True),
        0,
        gate_proj,
        up_proj,
        down_proj,
    )
    returned = lax.all_to_all(finished, "expert", split_axis=0, concat_axis=0, tiled=True)
    source_rows = jnp.arange(holders, dtype=jnp.int32)[:, None, None]
    picked = returned[group_ids, source_rows, group_slots]
    weighted = jnp.sum(picked.astype(jnp.float32) * group_gates[..., None], axis=2)
    moe_sum = lax.psum_scatter(weighted, "dp", scatter_dimension=0, tiled=True).reshape(
        row_count, -1
    )
    return (residual_out, moe_sum)


def solution(mesh):
    in_specs = (
        P(("dp", "expert"), None),
        P(("dp", "expert"), None),
        P("dp", None),
        P(("dp", "expert"), None),
        P(("dp", "expert"), None),
        P(("dp", "expert")),
        P(("dp", "expert")),
        P("expert", None, None),
        P("expert", None),
        P(),
        P(("dp", "expert"), None),
        P(("dp", "expert"), None),
        P("expert", None, "dp"),
        P("expert", None, "dp"),
        P("expert", "dp", None),
    )
    out_specs = (P(("dp", "expert"), None), P(("dp", "expert"), None))
    return jax.shard_map(
        per_device, mesh=mesh, in_specs=in_specs, out_specs=out_specs, check_vma=False
    )
```

profile of v0, /device:TPU:0, one launch (start us, length us, event | category | flops | bytes accessed | tf_op | source)
XLA Modules:
  0.0 306.6 jit_solution(17505986570849867368)
XLA Ops:
  7.2 0.0 copy-start
  7.2 0.0 all-gather.5.cloned.1.call-start
  7.2 0.7 all-gather.5.cloned.1.call-update
  7.9 1.3 reshape.165
  9.2 0.7 iota_compare_fusion.3
  10.0 0.8 fusion.47
  10.7 0.1 broadcast_in_dim.74
  10.9 0.1 broadcast_in_dim.75
  11.0 1.7 reshape.166
  12.7 13.8 %all-gather.1 = s32[4,4,6]{2,1,0:T(4,128)S(1)} all-gather(s32[1,4,6]{2,1,0:T(4,128)} %bitcast.67), channel_id=1, replica_groups=mesh['dp'=4,'expert'=8] {'dp'}, dimensions={0}, use_global_device_ids=true | all-gather | bytes 480 | tf_op jit(solution)/shard_map/all_gather | solution.py:152
  26.5 0.1 copy.47
  26.6 0.7 iota_compare_fusion.4
  27.3 0.5 fusion.57
  27.8 0.2 fusion.35
  28.0 73.8 %all-gather.5.cloned.1.call-done = bf16[64,36864]{1,0:T(8,128)(2,1)} async-done(((bf16[16,36864]{1,0:T(8,128)(2,1)}), bf16[64,36864]{1,0:T(8,128)(2,1)}) %all-gather.5.cloned.1.call-update) | async-done | bytes 4718608 | tf_op jit(solution)/shard_map/all_gather | solution.py:128
  101.8 9.9 %reshape.167 = bf16[4096,576]{1,0:T(8,128)(2,1)} reshape(bf16[64,36864]{1,0:T(8,128)(2,1)} %all-gather.5.cloned.1.call-done) | data formatting | bytes 9437184 | tf_op jit(solution)/shard_map/reshape | solution.py:58
  111.7 4.7 %fusion.58 = (f32[4,64]{1,0:T(4,128)S(1)}, f32[4,64,4096]{2,1,0:T(8,128)S(1)}) fusion(bf16[4,64,576]{2,1,0:T(8,128)(2,1)S(1)} %reshape.165, bf16[4096,576]{1,0:T(8,128)(2,1)} %reshape.167, pred[4,4096]{1,0:T(4,128)(4,1)S(1)} %broadcast_in_dim.75), kind=kOutput, calls=%fused_computation.79 | convolution fusion | flops 1211105024 | bytes 9225216 | tf_op jit(solution)/shard_map/rhk,nk->rhn/dot_general | solution.py:38
  116.4 1.3 fusion.3
  117.7 0.0 copy-start.4
  117.7 0.0 copy-start.7
  117.7 1.0 fusion.9
  118.8 0.3 fusion.17
  119.1 0.9 copy.44
  120.0 3.7 %all-to-all-start = ((bf16[4,64,512]{2,0,1:T(4,128)(2,1)}), bf16[4,64,512]{2,0,1:T(4,128)(2,1)S(1)}, u32[]{:S(2)}, u32[]{:S(2)}) async-start(bf16[4,64,512]{2,0,1:T(4,128)(2,1)} %copy.44), calls=%async_computation | async-start | bytes 524288 | tf_op jit(solution)/shard_map/all_to_all | solution.py:134
  123.6 0.0 all-reduce.5.cloned.1.call-start
  123.7 0.1 convert_reduce_fusion
  123.9 0.6 dynamic-slice
  125.1 0.5 select_reduce_fusion
  125.6 5.0 %all-to-all-done = bf16[4,64,512]{2,0,1:T(4,128)(2,1)S(1)} async-done(((bf16[4,64,512]{2,0,1:T(4,128)(2,1)}), bf16[4,64,512]{2,0,1:T(4,128)(2,1)S(1)}, u32[]{:S(2)}, u32[]{:S(2)}) %all-to-all-start) | async-done | bytes 262176 | tf_op jit(solution)/shard_map/all_to_all | solution.py:134
  130.6 0.1 copy.62
  130.7 0.1 all_to_all.22
  130.8 0.3 fusion.25
  131.0 0.0 copy-start.3
  131.0 6.8 %fusion.39 = f32[32,5120]{1,0:T(8,128)} fusion(bf16[1024,5120]{1,0:T(8,128)(2,1)} %param.23, bf16[8,4,8,128]{3,2,1,0:T(8,128)(2,1)S(1)} %fusion.25), kind=kOutput, calls=%fused_computation.48 | convolution fusion | flops 335544320 | bytes 11206656 | tf_op jit(solution)/shard_map/dot_general | solution.py:140
  137.8 0.0 all-reduce.5.cloned.1.call-update
  137.9 0.2 and_reduce_fusion
  138.0 51.6 %all-reduce.5.cloned.1.call-done = f32[32,5120]{1,0:T(8,128)} async-done(((f32[32,5120]{1,0:T(8,128)}), f32[32,5120]{1,0:T(8,128)}) %all-reduce.5.cloned.1.call-update) | async-done | bytes 655376
  189.7 1.1 multiply_reduce_fusion.1
  190.8 0.1 fusion.45
  190.9 13.6 %all-gather = bf16[4,4,5120]{2,1,0:T(4,128)(2,1)S(1)} all-gather(bf16[1,4,5120]{2,1,0:T(4,128)(2,1)S(1)} %fusion.45), channel_id=1, replica_groups=mesh['dp'=4,'expert'=8] {'dp'}, dimensions={0}, use_global_device_ids=true | all-gather | bytes 204800 | tf_op jit(solution)/shard_map/all_gather | solution.py:151
  204.4 0.5 fusion
  204.9 0.8 copy.48
  205.7 17.1 %all_to_all.28 = bf16[8,4,3,5120]{3,1,2,0:T(4,128)(2,1)S(1)} all-to-all(bf16[8,4,3,5120]{3,1,2,0:T(4,128)(2,1)S(1)} %copy.48), channel_id=1, replica_groups=mesh['dp'=4,'expert'=8] {'expert'}, dimensions={0} | all-to-all | bytes 1966080 | tf_op jit(solution)/shard_map/all_to_all | solution.py:165
  222.7 0.7 copy.49
  223.4 0.9 reshape_squeeze_reshape.3
  224.3 2.9 fusion.7
  227.2 5.0 %convolution_convert_fusion = bf16[96,5120]{1,0:T(8,128)(2,1)S(1)} fusion(bf16[1,384,5120]{2,1,0:T(8,128)(2,1)} %param.29, bf16[96,5120]{1,0:T(8,128)(2,1)S(1)} %reshape_squeeze_reshape.3, bf16[1,5120,384]{2,1,0:T(8,128)(2,1)} %param.28, f32[96,384]{1,0:T(8,128)S(1)} %fusion.7), kind=kOutput, calls=%fused_computation.1 | convolution fusion | flops 755687424 | bytes 9977856 | tf_op jit(solution)/shard_map/dot_general | solution.py:99
  232.2 0.0 copy-start.5
  232.2 0.6 reshape_stack_reshape.3
  232.8 1.5 copy.50
  234.4 3.6 %all-to-all-start.2 = ((bf16[8,4,3,5120]{3,1,2,0:T(4,128)(2,1)}), bf16[8,4,3,5120]{3,1,2,0:T(4,128)(2,1)S(1)}, u32[]{:S(2)}, u32[]{:S(2)}) async-start(bf16[8,4,3,5120]{3,1,2,0:T(4,128)(2,1)} %copy.50), calls=%async_computation.2 | async-start | bytes 1966080 | tf_op jit(solution)/shard_map/all_to_all | solution.py:171
  237.9 0.0 all-reduce.7.cloned.1.call-start
  238.0 0.1 copy.51
  238.1 0.1 reshape.173
  238.2 10.7 %all-gather.2 = bf16[4,4,6]{2,1,0:T(4,128)(2,1)S(1)} all-gather(bf16[1,4,6]{2,1,0:T(4,128)(2,1)S(1)} %bitcast.68), channel_id=1, replica_groups=mesh['dp'=4,'expert'=8] {'dp'}, dimensions={0}, use_global_device_ids=true | all-gather | bytes 240 | tf_op jit(solution)/shard_map/all_gather | solution.py:153
  249.0 3.6 %all-to-all-done.2 = bf16[8,4,3,5120]{3,1,2,0:T(4,128)(2,1)S(1)} async-done(((bf16[8,4,3,5120]{3,1,2,0:T(4,128)(2,1)}), bf16[8,4,3,5120]{3,1,2,0:T(4,128)(2,1)S(1)}, u32[]{:S(2)}, u32[]{:S(2)}) %all-to-all-start.2) | async-done | bytes 983072 | tf_op jit(solution)/shard_map/all_to_all | solution.py:171
  252.6 4.8 %gather_fusion = bf16[96,5120]{1,0:T(8,128)(2,1)S(1)} fusion(bf16[8,4,3,5120]{3,1,2,0:T(4,128)(2,1)S(1)} %all-to-all-done.2, s32[96]{0:T(128)S(1)} %reshape.173), kind=kCustom, calls=%fused_computation | custom fusion | bytes 1967232 | tf_op jit(solution)/shard_map/gather | solution.py:173
  257.4 0.0 copy-start.6
  257.4 1.7 reshape.179
  259.1 3.4 %multiply_reduce_fusion = f32[4,4,5120]{2,1,0:T(4,128)} fusion(f32[4,4,6,5120]{3,2,1,0:T(8,128)} %reshape.179, f32[4,4,6]{2,1,0:T(4,128)S(1)} %convert_element_type.71), kind=kLoop, calls=%fused_computation.17 | loop fusion | flops 901120 | bytes 2294144 | tf_op jit(solution)/shard_map/reduce_sum | solution.py:174
  262.5 0.0 all-reduce.7.cloned.1.call-update
  262.5 0.7 dynamic-slice.2
  263.2 34.7 %all-reduce.7.cloned.1.call-done = f32[4,4,5120]{2,1,0:T(4,128)} async-done(((f32[4,4,5120]{2,1,0:T(4,128)}), f32[4,4,5120]{2,1,0:T(4,128)}) %all-reduce.7.cloned.1.call-update) | async-done | bytes 327696
  297.9 2.2 dynamic-slice_bitcast_fusion
  (19 shorter events, 0.1 us)
Async XLA Ops:
  7.2 123.6 %copy-start = (bf16[8,512,128]{2,1,0:T(8,128)(2,1)S(1)}, bf16[8,512,128]{2,1,0:T(8,128)(2,1)}, u32[]{:S(2)}) copy-start(bf16[8,512,128]{2,1,0:T(8,128)(2,1)} %param.22) | copy-start | bytes 3145732
  7.2 94.6 %all-gather.5.cloned.1.call-start = ((), (), s32[]{:S(2)}) async-start(), calls=%async_computation.3 | async-start | bytes 5898240 | tf_op jit(solution)/shard_map/all_gather | solution.py:128
  111.7 4.7 %copy-start.1 = (bf16[4096,576]{1,0:T(8,128)(2,1)S(1)}, bf16[4096,576]{1,0:T(8,128)(2,1)}, u32[]{:S(2)}) copy-start(bf16[4096,576]{1,0:T(8,128)(2,1)} %reshape.167) | copy-start | bytes 14155780
  117.7 6.2 %copy-start.4 = (bf16[5120]{0:T(1024)(128)(2,1)S(1)}, bf16[5120]{0:T(1024)(128)(2,1)}, u32[]{:S(2)}) copy-start(bf16[5120]{0:T(1024)(128)(2,1)} %param.24) | copy-start | bytes 30724
  117.7 6.2 %copy-start.7 = (u32[32]{0:T(128)S(1)}, u32[32]{0:T(128)}, u32[]{:S(2)}) copy-start(u32[32]{0:T(128)} %constant.65) | copy-start | bytes 388
  120.0 10.6 %all-to-all-start = ((bf16[4,64,512]{2,0,1:T(4,128)(2,1)}), bf16[4,64,512]{2,0,1:T(4,128)(2,1)S(1)}, u32[]{:S(2)}, u32[]{:S(2)}) async-start(bf16[4,64,512]{2,0,1:T(4,128)(2,1)} %copy.44), calls=%async_computation | async-start | bytes 524288 | tf_op jit(solution)/shard_map/all_to_all | solution.py:134
  123.6 66.0 %all-reduce.5.cloned.1.call-start = ((), (), s32[]{:S(2)}) async-start(), calls=%async_computation.4 | async-start | bytes 1310720
  131.0 58.7 %copy-start.3 = (bf16[4,5120]{1,0:T(4,128)(2,1)S(1)}, bf16[4,5120]{1,0:T(4,128)(2,1)}, u32[]{:S(2)}) copy-start(bf16[4,5120]{1,0:T(4,128)(2,1)} %param.15) | copy-start | bytes 122884
  190.8 33.5 %copy-start.2 = (f32[4,5120]{1,0:T(4,128)}, f32[4,5120]{1,0:T(4,128)S(1)}, u32[]{:S(2)}) copy-start(f32[4,5120]{1,0:T(4,128)S(1)} %get-tuple-element.3) | copy-start | bytes 245764
  232.2 6.0 %copy-start.5 = (bf16[4,6]{1,0:T(4,128)(2,1)S(1)}, bf16[4,6]{1,0:T(4,128)(2,1)}, u32[]{:S(2)}) copy-start(bf16[4,6]{1,0:T(4,128)(2,1)} %param.26) | copy-start | bytes 148
  234.4 18.2 %all-to-all-start.2 = ((bf16[8,4,3,5120]{3,1,2,0:T(4,128)(2,1)}), bf16[8,4,3,5120]{3,1,2,0:T(4,128)(2,1)S(1)}, u32[]{:S(2)}, u32[]{:S(2)}) async-start(bf16[8,4,3,5120]{3,1,2,0:T(4,128)(2,1)} %copy.50), calls=%async_computation.2 | async-start | bytes 1966080 | tf_op jit(solution)/shard_map/all_to_all | solution.py:171
  237.9 60.0 %all-reduce.7.cloned.1.call-start = ((), (), s32[]{:S(2)}) async-start(), calls=%async_computation.5 | async-start | bytes 655360
  257.4 5.1 %copy-start.6 = (u32[32]{0:T(128)S(1)}, u32[32]{0:T(128)}, u32[]{:S(2)}) copy-start(u32[32]{0:T(128)} %constant.69) | copy-start | bytes 388
Sparse Core Ops, SparseCore 0:
  9.6 92.1 all-gather.4
  138.0 51.6 all-reduce.4
  262.6 35.2 all-reduce.6
where the time goes:
time: 307 us
  waiting for transfers between devices  169 us (55%)
  blocking collectives  55.1 us (18%)
  local copies, waits for them, and re-layouts  29 us (9%)
  matrix products  22.1 us (7%)
  between operations  14.7 us (5%)
  other arithmetic  8.92 us (3%)
  starting transfers between devices  7.37 us (2%)
    unnamed x5, waiting for transfers between devices  87 us
    all_gather x1, waiting for transfers between devices, per_device(): lax.all_gather(prefix_pool, 'dp', axis=0, tiled=True)  73.8 us
    all_to_all x1, blocking collectives, per_device(): lax.all_to_all(outgoing, 'expert', split_axis=0, concat_axis=0, tiled=True)  17.1 us
    all_gather x1, blocking collectives, per_device(): lax.all_gather(expert_ids, 'dp', axis=0, tiled=True)  13.8 us
    all_gather x1, blocking collectives, per_device(): lax.all_gather(normed, 'dp', axis=0, tiled=True)  13.6 us
    all_gather x1, blocking collectives, per_device(): lax.all_gather(gate_weights, 'dp', axis=0, tiled=True)  10.7 us
    reshape x1, local copies, waits for them, and re-layouts, prefix_partial(): key_rows = pool_piece.reshape(piece_blocks * BLOCK, KDIM)  9.91 us
    dot_general x1, matrix products, per_device(): jnp.dot(value_rows, out_proj, preferred_element_type=jnp.float32)  6.79 us
  transfers between devices with their start and end apart: 5, of which 5 were waited for; matrix products, arithmetic and copies ran while one was open for 3% of the time, Pallas kernels for 0%

commit v1 on v0

v1 whole, which is shorter than its diff:
```python
import jax
import jax.numpy as jnp
from jax import lax
from jax.sharding import PartitionSpec as P

HEADS = 64
LAT = 512
TOPK = 6
BLOCK = 64
SUFFIX = 128
KDIM = 576


NEG_FILL = -1e30
SCORE_SCALE = 192.0 ** (-0.5)
NORM_EPS = 1e-06
LANES = 128


def swap(value, axis, mask):
    size = lax.axis_size(axis)
    return lax.ppermute(value, axis, [(i, i ^ mask) for i in range(size)])


def rounded(value):
    return lax.reduce_precision(value, 8, 7)


def dot(a, b, dims):
    return lax.dot_general(a, b, (dims, ((), ())), preferred_element_type=jnp.float32)


def own_partial(queries, own_keys, own_live):
    scores = (
        jnp.einsum("rhk,rnk->rhn", queries, own_keys, preferred_element_type=jnp.float32)
        * SCORE_SCALE
    )
    live_keys = own_live[:, None, :]
    scores = jnp.where(live_keys, scores, NEG_FILL)
    row_max = rounded(jnp.max(scores, axis=-1))
    weights = jnp.where(live_keys, jnp.exp(scores - row_max[..., None]), 0.0)
    numerator = jnp.einsum(
        "rhn,rnl->rhl",
        weights.astype(jnp.bfloat16),
        own_keys[:, :, :LAT],
        preferred_element_type=jnp.float32,
    )
    return (row_max, jnp.sum(weights, axis=-1), numerator)


def split_heads(value, members, place):
    rows, heads, width = value.shape
    groups = value.reshape(rows, members, heads // members, width)
    return [
        lax.dynamic_index_in_dim(groups, place ^ j, 1, keepdims=False) for j in range(members)
    ]


def to_head_owners(value, members, place):
    groups = split_heads(value, members, place)
    chips = members // 2
    mine = jnp.stack(groups[0::2])
    other = swap(jnp.stack(groups[1::2]), "expert", 1)
    both = jnp.stack([mine, other], axis=1)
    return jnp.concatenate(
        [both[:1]] + [swap(both[k], "expert", 2 * k)[None] for k in range(1, chips)]
    )


def sum_over_heads(partial, members):
    chips = members // 2
    away = swap(partial[:, 1].astype(jnp.bfloat16), "expert", 1)
    held = partial[:, 0] + away.astype(jnp.float32)
    total = held[0]
    sent = held.astype(jnp.bfloat16)
    for k in range(1, chips):
        total = total + swap(sent[k], "expert", 2 * k).astype(jnp.float32)
    return total


def spread(rows, members, holders):
    by_z = jnp.stack([rows] + [swap(rows, "dp", q) for q in range(1, holders)])
    by_chip = jnp.stack([by_z] + [swap(by_z, "expert", 2 * k) for k in range(1, members // 2)])
    return jnp.stack([by_chip, swap(by_chip, "expert", 1)])


def gather_sums(partial, members, holders):
    held = partial[0].astype(jnp.float32) + swap(partial[1], "expert", 1).astype(jnp.float32)
    sent = held.astype(jnp.bfloat16)
    total = held[0]
    for k in range(1, members // 2):
        total = total + swap(sent[k], "expert", 2 * k).astype(jnp.float32)
    sent = total.astype(jnp.bfloat16)
    result = total[0]
    for q in range(1, holders):
        result = result + swap(sent[q], "dp", q).astype(jnp.float32)
    return result


def per_device(
    hidden_in,
    query,
    prefix_pool,
    suffix_cache,
    block_list,
    prefix_count,
    suffix_count,
    value_up,
    out_proj,
    norm_gain,
    expert_ids,
    gate_weights,
    gate_proj,
    up_proj,
    down_proj,
):
    bf16 = jnp.bfloat16
    row_count, width = hidden_in.shape
    members = lax.axis_size("expert")
    holders = lax.axis_size("dp")
    chips = members // 2
    place = lax.axis_index("expert")
    shard = lax.axis_index("dp")
    shard_blocks = prefix_pool.shape[0]
    total_blocks = shard_blocks * holders

    shard_rows = shard_blocks * BLOCK
    row_block = shard * shard_blocks + jnp.arange(shard_rows, dtype=jnp.int32) // BLOCK
    one_hot = (row_block[:, None] == jnp.arange(total_blocks, dtype=jnp.int32)).astype(bf16)
    own_pool = jnp.concatenate([prefix_pool.reshape(shard_rows, KDIM), one_hot], axis=1)
    slice_rows = shard_rows // members
    piece = lax.dynamic_slice_in_dim(own_pool, place * slice_rows, slice_rows, 0)
    arrived = [swap(piece, "dp", q) for q in range(1, holders)]

    queries = query.reshape(row_count, HEADS, KDIM)
    own_keys = suffix_cache.reshape(row_count, SUFFIX, KDIM)
    own_live = jnp.arange(SUFFIX, dtype=jnp.int32)[None, :] < suffix_count[:, None]
    own_max, own_sum, own_num = own_partial(queries, own_keys, own_live)
    sum_high = rounded(own_sum)
    stats = jnp.stack([own_max, sum_high, own_sum - sum_high], axis=-1).astype(bf16)
    in_prefix = jnp.arange(block_list.shape[1], dtype=jnp.int32)[None, :] < prefix_count[:, None]
    member = jnp.any(
        (block_list[:, :, None] == jnp.arange(total_blocks, dtype=jnp.int32))
        & in_prefix[:, :, None],
        axis=1,
    )
    bias = jnp.where(member, 0.0, NEG_FILL).astype(bf16)
    bias = jnp.broadcast_to(bias[:, None, :], (row_count, HEADS, total_blocks))
    payload = jnp.concatenate(
        [
            queries,
            bias,
            own_num.astype(bf16),
            jnp.pad(stats, ((0, 0), (0, 0), (0, LANES - stats.shape[-1]))),
        ],
        axis=-1,
    )
    held = to_head_owners(payload, members, place)
    key_width = KDIM + total_blocks
    flat = held.reshape(-1, held.shape[-1])
    head_queries = flat[:, :key_width]
    own_num = flat[:, key_width : key_width + LAT].astype(jnp.float32)
    stats = flat[:, key_width + LAT :].astype(jnp.float32)
    own_max = stats[:, 0:1]
    own_sum = stats[:, 1:2] + stats[:, 2:3]

    chunks = [own_pool]
    for block in arrived:
        mine = jnp.concatenate([block] + [swap(block, "expert", 2 * k) for k in range(1, chips)])
        chunks.append(mine)
        chunks.append(swap(mine, "expert", 1))
    scores = [dot(head_queries, keys, ((1,), (1,))) * SCORE_SCALE for keys in chunks]
    new_max = own_max
    for part in scores:
        new_max = jnp.maximum(new_max, jnp.max(part, axis=-1, keepdims=True))
    rescale = jnp.exp(own_max - new_max)
    numerator = own_num * rescale
    denominator = own_sum * rescale
    for part, keys in zip(scores, chunks):
        weights = jnp.exp(part - new_max)
        denominator = denominator + jnp.sum(weights, axis=-1, keepdims=True)
        numerator = numerator + dot(weights.astype(bf16), keys[:, :LAT], ((1,), (0,)))
    context = (numerator / denominator).astype(bf16)

    group_heads = HEADS // members
    context = context.reshape(-1, group_heads, LAT)
    head_values = jnp.einsum(
        "thl,hlv->thv", context, value_up, preferred_element_type=jnp.float32
    ).astype(bf16)
    value_rows = head_values.reshape(head_values.shape[0], -1)
    partial = jnp.dot(value_rows, out_proj, preferred_element_type=jnp.float32)
    attended = sum_over_heads(partial.reshape(chips, 2, row_count, width), members)
    residual_out = hidden_in.astype(jnp.float32) + attended
    scale_rows = lax.rsqrt(jnp.mean(residual_out * residual_out, axis=-1, keepdims=True) + NORM_EPS)
    normed = (residual_out * scale_rows * norm_gain.astype(jnp.float32)).astype(bf16)

    expert_total = gate_proj.shape[0] * members
    chosen = expert_ids[:, :, None] == jnp.arange(LANES, dtype=jnp.int32)
    gates = jnp.sum(jnp.where(chosen, gate_weights[:, :, None], 0.0), axis=1).astype(bf16)
    rows = spread(jnp.concatenate([normed, gates], axis=1), members, holders)
    flat = rows.reshape(-1, width + LANES)
    tokens = flat[:, :width]
    gate = lax.dynamic_slice_in_dim(flat[:, width:], place, 1, 1).astype(jnp.float32)
    gate_part = jnp.dot(tokens, gate_proj[0], preferred_element_type=jnp.float32)
    up_part = jnp.dot(tokens, up_proj[0], preferred_element_type=jnp.float32)
    hidden = (jax.nn.silu(gate_part) * up_part).astype(bf16)
    result = jnp.dot(hidden, down_proj[0], preferred_element_type=jnp.float32) * gate
    result = result.astype(bf16).reshape(2, chips, holders, row_count, width)
    moe_sum = gather_sums(result, members, holders)
    return (residual_out, moe_sum)


def solution(mesh):
    in_specs = (
        P(("dp", "expert"), None),
        P(("dp", "expert"), None),
        P("dp", None),
        P(("dp", "expert"), None),
        P(("dp", "expert"), None),
        P(("dp", "expert")),
        P(("dp", "expert")),
        P("expert", None, None),
        P("expert", None),
        P(),
        P(("dp", "expert"), None),
        P(("dp", "expert"), None),
        P("expert", None, "dp"),
        P("expert", None, "dp"),
        P("expert", "dp", None),
    )
    out_specs = (P(("dp", "expert"), None), P(("dp", "expert"), None))
    return jax.shard_map(
        per_device, mesh=mesh, in_specs=in_specs, out_specs=out_specs, check_vma=False
    )
```

time: 307 us -> 153 us (0.50)
  waiting for transfers between devices: 169 us -> 33.7 us
  blocking collectives: 55.1 us -> 0 us
  starting transfers between devices: 7.37 us -> 41.9 us
  between operations: 14.7 us -> 1.33 us
  matrix products: 22.1 us -> 35.1 us
    unnamed x5 -> x0, waiting for transfers between devices: 87 us -> none
    all_gather x1 -> x0, waiting for transfers between devices: 73.8 us -> none  [per_device(): lax.all_gather(prefix_pool, 'dp', axis=0, tiled=True)]
    ppermute x0 -> x37, starting transfers between devices: none -> 41.9 us  [swap(): return lax.ppermute(value, axis, [(i, i ^ mask) for i in range(size)])]
    all_gather x3 -> x0, blocking collectives: 38.1 us -> none  [the longest x1 13.8 us: per_device(): lax.all_gather(expert_ids, 'dp', axis=0, tiled=True)]
    ppermute x0 -> x37, waiting for transfers between devices: none -> 33.7 us  [swap(): return lax.ppermute(value, axis, [(i, i ^ mask) for i in range(size)])]
    all_to_all x1 -> x0, blocking collectives: 17.1 us -> none  [per_device(): lax.all_to_all(outgoing, 'expert', split_axis=0, concat_axis=0, tiled=True)]
    dot_general x7 -> x18, matrix products: 21.4 us -> 34.3 us  [the longest x14 19.1 us: dot(): lax.dot_general(a, b, (dims, ((), ())), preferred_element_type=jnp.float32)]
    unnamed x18 -> x36, local copies, waits for them, and re-layouts: 1.3 us -> 10.9 us
  transfers between devices with their start and end apart: 5 -> 37, of which waited for: 5 -> 19; matrix products, arithmetic and copies ran while one was open for 3% -> 22% of each run, Pallas kernels for 0% -> 0%
where the time goes in v1:
time: 153 us; the launch traced here: 152 us
  starting transfers between devices  41.9 us (27%)
  matrix products  35.1 us (23%)
  waiting for transfers between devices  33.7 us (22%)
  local copies, waits for them, and re-layouts  28.4 us (19%)
  other arithmetic  11.8 us (8%)
    ppermute x37, starting transfers between devices, swap(): return lax.ppermute(value, axis, [(i, i ^ mask) for i in range(size)])  41.9 us
    ppermute x37, waiting for transfers between devices, swap(): return lax.ppermute(value, axis, [(i, i ^ mask) for i in range(size)])  33.7 us
    dot_general x14, matrix products, dot(): lax.dot_general(a, b, (dims, ((), ())), preferred_element_type=jnp.float32)  19.1 us
    unnamed x36, local copies, waits for them, and re-layouts  10.9 us
    dot_general x1, matrix products, per_device(): jnp.dot(hidden, down_proj[0], preferred_element_type=jnp.float32) * gate  6.12 us
    dot_general x1, matrix products, per_device(): partial = jnp.dot(value_rows, out_proj, preferred_element_type=jnp.float32)  5.83 us
    concatenate x6, local copies, waits for them, and re-layouts, per_device(): jnp.concatenate([queries, bias, own_num.astype(bf16), jnp.pad(stats, ((0,...  3.41 us
  transfers between devices with their start and end apart: 37, of which 19 were waited for; matrix products, arithmetic and copies ran while one was open for 22% of the time, Pallas kernels for 0%

profile of v1, /device:TPU:0, one launch (start us, length us, event | category | flops | bytes accessed | tf_op | source)
XLA Modules:
  0.0 152.2 jit_solution(15275789991629523563)
XLA Ops:
  0.7 2.7 %reshape.142 = bf16[1024,576]{1,0:T(8,128)(2,1)S(1)} reshape(bf16[16,36864]{1,0:T(8,128)(2,1)} %param.17) | data formatting | bytes 2359296 | tf_op jit(solution)/shard_map/reshape | solution.py:130
  4.4 3.0 %collective-permute-start.4 = (bf16[128,640]{1,0:T(8,128)(2,1)}, bf16[128,640]{1,0:T(8,128)(2,1)}, u32[]{:S(2)}, u32[]{:S(2)}) collective-permute-start(bf16[128,640]{1,0:T(8,128)(2,1)} %fusion.65), channel_id=1, source_target_pairs={{0,8},{8,0},{16,24},{24,16},{1,9},{9,1},{17,25},{25,17},{2,10},{10... | collective-permute-start | bytes 491528 | tf_op jit(solution)/shard_map/ppermute | solution.py:22
  7.4 2.6 %collective-permute-start.9 = (bf16[128,640]{1,0:T(8,128)(2,1)}, bf16[128,640]{1,0:T(8,128)(2,1)}, u32[]{:S(2)}, u32[]{:S(2)}) collective-permute-start(bf16[128,640]{1,0:T(8,128)(2,1)} %fusion.65), channel_id=1, source_target_pairs={{0,16},{8,24},{16,0},{24,8},{1,17},{9,25},{17,1},{25,9},{2,18},{10... | collective-permute-start | bytes 491528 | tf_op jit(solution)/shard_map/ppermute | solution.py:22
  10.1 1.7 %reshape.140 = bf16[4,128,576]{2,1,0:T(8,128)(2,1)S(1)} reshape(bf16[4,73728]{1,0:T(4,128)(2,1)} %param.18) | data formatting | bytes 1179648 | tf_op jit(solution)/shard_map/reshape | solution.py:136
  11.8 1.3 reshape.139
  14.1 1.3 concatenate.28
  16.7 1.3 concatenate.31
  18.3 1.6 %constant_dynamic-update-slice_fusion.3 = bf16[512,640]{1,0:T(8,128)(2,1)} fusion(bf16[128,640]{1,0:T(8,128)(2,1)} %collective-permute-done.4), kind=kLoop, calls=%fused_computation.161 | loop fusion | bytes 327680
  19.9 1.7 %collective-permute-start.5 = (bf16[128,640]{1,0:T(8,128)(2,1)}, bf16[128,640]{1,0:T(8,128)(2,1)S(1)}, u32[]{:S(2)}, u32[]{:S(2)}) collective-permute-start(bf16[128,640]{1,0:T(8,128)(2,1)} %collective-permute-done.4), channel_id=1, source_target_pairs={{0,2},{1,3},{2,0},{3,1},{4,6},{5,7},{6,4},{7,5},{8,10},{9,11},{10,... | collective-permute-start | bytes 491528 | tf_op jit(solution)/shard_map/ppermute | solution.py:22
  21.6 1.5 collective-permute-start.6
  23.1 2.1 %collective-permute-start.7 = (bf16[128,640]{1,0:T(8,128)(2,1)}, bf16[128,640]{1,0:T(8,128)(2,1)S(1)}, u32[]{:S(2)}, u32[]{:S(2)}) collective-permute-start(bf16[128,640]{1,0:T(8,128)(2,1)} %collective-permute-done.4), channel_id=1, source_target_pairs={{0,6},{1,7},{2,4},{3,5},{4,2},{5,3},{6,0},{7,1},{8,14},{9,15},{10,... | collective-permute-start | bytes 491528 | tf_op jit(solution)/shard_map/ppermute | solution.py:22
  25.2 1.6 %constant_dynamic-update-slice_fusion.7 = bf16[512,640]{1,0:T(8,128)(2,1)} fusion(bf16[128,640]{1,0:T(8,128)(2,1)} %collective-permute-done.9), kind=kLoop, calls=%fused_computation.165 | loop fusion | bytes 327680
  27.4 1.6 %constant_dynamic-update-slice_fusion.11 = bf16[512,640]{1,0:T(8,128)(2,1)} fusion(bf16[128,640]{1,0:T(8,128)(2,1)} %collective-permute-done.14), kind=kLoop, calls=%fused_computation.169 | loop fusion | bytes 327680
  29.9 2.2 %collective-permute-start.12 = (bf16[128,640]{1,0:T(8,128)(2,1)}, bf16[128,640]{1,0:T(8,128)(2,1)S(1)}, u32[]{:S(2)}, u32[]{:S(2)}) collective-permute-start(bf16[128,640]{1,0:T(8,128)(2,1)} %collective-permute-done.9), channel_id=1, source_target_pairs={{0,6},{1,7},{2,4},{3,5},{4,2},{5,3},{6,0},{7,1},{8,14},{9,15},{10,... | collective-permute-start | bytes 491528 | tf_op jit(solution)/shard_map/ppermute | solution.py:22
  35.5 2.1 %collective-permute-start.17 = (bf16[128,640]{1,0:T(8,128)(2,1)}, bf16[128,640]{1,0:T(8,128)(2,1)S(1)}, u32[]{:S(2)}, u32[]{:S(2)}) collective-permute-start(bf16[128,640]{1,0:T(8,128)(2,1)} %collective-permute-done.14), channel_id=1, source_target_pairs={{0,6},{1,7},{2,4},{3,5},{4,2},{5,3},{6,0},{7,1},{8,14},{9,15},{10,... | collective-permute-start | bytes 491528 | tf_op jit(solution)/shard_map/ppermute | solution.py:22
  38.3 0.9 collective-permute-done.11
  39.2 1.2 collective-permute-start.1
  42.3 1.8 %collective-permute-start.3 = (bf16[2,4,8,1280]{3,2,1,0:T(8,128)(2,1)S(1)}, bf16[2,4,8,1280]{3,2,1,0:T(8,128)(2,1)S(1)}, u32[]{:S(2)}, u32[]{:S(2)}) collective-permute-start(bf16[2,4,8,1280]{3,2,1,0:T(8,128)(2,1)S(1)} %get-tuple-element.25), channel_id=1, source_target_pairs={{0,6},{1,7},{2,4},{3,5},{4,2},{5,3},{6,0},{7,1},{8,14},{9,15},{10,... | collective-permute-start | bytes 491528 | tf_op jit(solution)/shard_map/ppermute | solution.py:22
  44.7 1.5 collective-permute-done.16
  48.8 3.9 %collective-permute-done.2 = bf16[2,4,8,1280]{3,2,1,0:T(8,128)(2,1)S(1)} collective-permute-done((bf16[2,4,8,1280]{3,2,1,0:T(8,128)(2,1)S(1)}, bf16[2,4,8,1280]{3,2,1,0:T(8,128)(2,1)S(1)}, u32[]{:S(2)}, u32[]{:S(2)}) %collective-permute-start.2) | collective-permute-done | bytes 163872 | tf_op jit(solution)/shard_map/ppermute | solution.py:22
  52.8 1.6 %fusion.130 = (f32[256]{0:T(256)S(1)}, f32[256,512]{1,0:T(8,128)S(1)}) fusion(bf16[512,640]{1,0:T(8,128)(2,1)} %constant_dynamic-update-slice_fusion, bf16[256,1280]{1,0:T(8,128)(2,1)S(1)} %bitcast.158), kind=kOutput, calls=%fused_computation.212 | convolution fusion | flops 168034048 | bytes 1508352 | tf_op jit(solution)/shard_map/dot_general | solution.py:30
  55.0 1.6 %copy.123 = bf16[256,128]{0,1:T(8,128)(2,1)} copy(bf16[256,128]{1,0:T(8,128)(2,1)} %slice.155) | data formatting | bytes 131072
  57.5 1.6 %fusion.128 = (f32[256]{0:T(256)S(1)}, f32[256,512]{1,0:T(8,128)S(1)}) fusion(bf16[512,640]{1,0:T(8,128)(2,1)} %constant_dynamic-update-slice_fusion.4, bf16[256,1280]{1,0:T(8,128)(2,1)S(1)} %bitcast.160), kind=kOutput, calls=%fused_computation.210 | convolution fusion | flops 168034048 | bytes 1508352 | tf_op jit(solution)/shard_map/dot_general | solution.py:30
  59.1 1.6 %fusion.126 = (f32[256]{0:T(256)S(1)}, f32[256,512]{1,0:T(8,128)S(1)}) fusion(bf16[512,640]{1,0:T(8,128)(2,1)} %constant_dynamic-update-slice_fusion.8, bf16[256,1280]{1,0:T(8,128)(2,1)S(1)} %bitcast.161), kind=kOutput, calls=%fused_computation.208 | convolution fusion | flops 168034048 | bytes 1508352 | tf_op jit(solution)/shard_map/dot_general | solution.py:30
  61.4 1.6 %fusion.129 = (f32[256]{0:T(256)S(1)}, f32[256,512]{1,0:T(8,128)S(1)}) fusion(bf16[512,640]{1,0:T(8,128)(2,1)} %collective-permute-done.8, bf16[256,1280]{1,0:T(8,128)(2,1)S(1)} %bitcast.163), kind=kOutput, calls=%fused_computation.211 | convolution fusion | flops 168034048 | bytes 1508352 | tf_op jit(solution)/shard_map/dot_general | solution.py:30
  62.9 1.6 %fusion.127 = (f32[256]{0:T(256)S(1)}, f32[256,512]{1,0:T(8,128)S(1)}) fusion(bf16[512,640]{1,0:T(8,128)(2,1)} %collective-permute-done.13, bf16[256,1280]{1,0:T(8,128)(2,1)S(1)} %bitcast.164), kind=kOutput, calls=%fused_computation.209 | convolution fusion | flops 168034048 | bytes 1508352 | tf_op jit(solution)/shard_map/dot_general | solution.py:30
  64.5 1.6 %fusion.125 = (f32[256]{0:T(256)S(1)}, f32[256,512]{1,0:T(8,128)S(1)}) fusion(bf16[512,640]{1,0:T(8,128)(2,1)} %collective-permute-done.18, bf16[256,1280]{1,0:T(8,128)(2,1)S(1)} %bitcast.165), kind=kOutput, calls=%fused_computation.207 | convolution fusion | flops 168034048 | bytes 1508352 | tf_op jit(solution)/shard_map/dot_general | solution.py:30
  67.6 1.4 fusion.30
  68.9 1.4 fusion.11
  70.4 1.4 fusion.27
  71.8 1.4 fusion.10
  73.2 1.4 fusion.24
  74.6 1.4 fusion.14
  76.4 5.8 %fusion = f32[4,2,4,5120]{3,2,1,0:T(4,128)S(1)} fusion(bf16[4,2,4,1024]{3,2,1,0:T(4,128)(2,1)S(1)} %dot_general.82, bf16[1024,5120]{1,0:T(8,128)(2,1)} %param.23), kind=kOutput, calls=%fused_computation | convolution fusion | flops 335544320 | bytes 11206656 | tf_op jit(solution)/shard_map/dot_general | solution.py:191
  82.6 1.2 collective-permute-done.19
  84.0 1.4 collective-permute-start.20
  86.1 1.4 collective-permute-start.22
  88.0 1.8 %collective-permute-done.21 = bf16[4,5120]{1,0:T(4,128)(2,1)S(1)} collective-permute-done((bf16[4,5120]{1,0:T(4,128)(2,1)S(1)}, bf16[4,5120]{1,0:T(4,128)(2,1)S(1)}, u32[]{:S(2)}, u32[]{:S(2)}) %collective-permute-start.21) | collective-permute-done | bytes 40992 | tf_op jit(solution)/shard_map/ppermute | solution.py:22
  89.8 1.2 collective-permute-done.22
  92.1 3.5 %collective-permute-start.24 = (bf16[4,5248]{1,0:T(4,128)(2,1)S(1)}, bf16[4,5248]{1,0:T(4,128)(2,1)S(1)}, u32[]{:S(2)}, u32[]{:S(2)}) collective-permute-start(bf16[4,5248]{1,0:T(4,128)(2,1)S(1)} %get-tuple-element.42), channel_id=1, source_target_pairs={{0,16},{8,24},{16,0},{24,8},{1,17},{9,25},{17,1},{25,9},{2,18},{10... | collective-permute-start | bytes 125960 | tf_op jit(solution)/shard_map/ppermute | solution.py:22
  95.8 2.7 %collective-permute-done.24 = bf16[4,5248]{1,0:T(4,128)(2,1)S(1)} collective-permute-done((bf16[4,5248]{1,0:T(4,128)(2,1)S(1)}, bf16[4,5248]{1,0:T(4,128)(2,1)S(1)}, u32[]{:S(2)}, u32[]{:S(2)}) %collective-permute-start.24) | collective-permute-done | bytes 42016 | tf_op jit(solution)/shard_map/ppermute | solution.py:22
  98.4 2.9 %collective-permute-done.25 = bf16[4,5248]{1,0:T(4,128)(2,1)S(1)} collective-permute-done((bf16[4,5248]{1,0:T(4,128)(2,1)S(1)}, bf16[4,5248]{1,0:T(4,128)(2,1)S(1)}, u32[]{:S(2)}, u32[]{:S(2)}) %collective-permute-start.25) | collective-permute-done | bytes 42016 | tf_op jit(solution)/shard_map/ppermute | solution.py:22
  101.5 1.6 %collective-permute-start.26 = (bf16[4,4,5248]{2,1,0:T(4,128)(2,1)S(1)}, bf16[4,4,5248]{2,1,0:T(4,128)(2,1)S(1)}, u32[]{:S(2)}, u32[]{:S(2)}) collective-permute-start(bf16[4,4,5248]{2,1,0:T(4,128)(2,1)S(1)} %pad_maximum_fusion.6), channel_id=1, source_target_pairs={{0,2},{1,3},{2,0},{3,1},{4,6},{5,7},{6,4},{7,5},{8,10},{9,11},{10,... | collective-permute-start | bytes 503816 | tf_op jit(solution)/shard_map/ppermute | solution.py:22
  103.6 1.5 collective-permute-start.28
  105.2 1.7 %collective-permute-done.26 = bf16[4,4,5248]{2,1,0:T(4,128)(2,1)S(1)} collective-permute-done((bf16[4,4,5248]{2,1,0:T(4,128)(2,1)S(1)}, bf16[4,4,5248]{2,1,0:T(4,128)(2,1)S(1)}, u32[]{:S(2)}, u32[]{:S(2)}) %collective-permute-start.26) | collective-permute-done | bytes 167968 | tf_op jit(solution)/shard_map/ppermute | solution.py:22
  106.9 3.3 %collective-permute-done.27 = bf16[4,4,5248]{2,1,0:T(4,128)(2,1)S(1)} collective-permute-done((bf16[4,4,5248]{2,1,0:T(4,128)(2,1)S(1)}, bf16[4,4,5248]{2,1,0:T(4,128)(2,1)S(1)}, u32[]{:S(2)}, u32[]{:S(2)}) %collective-permute-start.27) | collective-permute-done | bytes 167968 | tf_op jit(solution)/shard_map/ppermute | solution.py:22
  111.6 1.5 collective-permute-done.29
  113.0 2.3 %pad_maximum_fusion.1 = bf16[2,4,4,4,5248]{4,3,2,1,0:T(4,128)(2,1)} fusion(bf16[1,4,4,4,5248]{4,3,2,1,0:T(4,128)(2,1)S(1)} %bitcast.167, bf16[1,4,4,4,5248]{4,3,2,1,0:T(4,128)(2,1)S(1)} %fusion.142), kind=kLoop, calls=%fused_computation.12 | loop fusion | flops 671744 | bytes 2686976 | tf_op jit(solution)/shard_map/stack | solution.py:84
  115.3 2.5 %reshape.144 = bf16[128,5248]{1,0:T(8,128)(2,1)S(1)} reshape(bf16[2,4,4,4,5248]{4,3,2,1,0:T(4,128)(2,1)} %pad_maximum_fusion.1) | data formatting | bytes 2686976 | tf_op jit(solution)/shard_map/reshape | solution.py:201
  117.8 3.0 %fusion.4 = f32[128,384]{1,0:T(8,128)S(1)} fusion(bf16[1,5120,384]{2,1,0:T(8,128)(2,1)} %param.28, bf16[128,5248]{1,0:T(8,128)(2,1)S(1)} %reshape.144), kind=kOutput, calls=%fused_computation.5 | convolution fusion | flops 503316480 | bytes 5439488 | tf_op jit(solution)/shard_map/dot_general | solution.py:205
  121.0 6.1 %fusion.2 = bf16[128,5120]{1,0:T(8,128)(2,1)} fusion(bf16[1,384,5120]{2,1,0:T(8,128)(2,1)} %param.29, f32[128]{0:T(128)S(1)} %bitcast_convert_fusion, f32[128,384]{1,0:T(8,128)S(1)} %fusion.4, bf16[1,5120,384]{2,1,0:T(8,128)(2,1)} %param.27, bf16[128,5248]{1,0:T(8,128)(2,1)S(1)} %reshape.144), kind=kOutput, calls=%fused_computation.3 | convolution fusion | flops 1008238592 | bytes 10682880 | tf_op jit(solution)/shard_map/dot_general | solution.py:207
  127.1 1.4 fusion.123
  128.5 1.1 squeeze.82
  129.8 1.5 reshape.146
  131.9 1.8 %fusion.119 = (bf16[4,4,4,5120]{3,2,1,0:T(4,128)(2,1)S(1)}, f32[4,4,4,5120]{3,2,1,0:T(4,128)S(1)}) fusion(f32[4,4,4,5120]{3,2,1,0:T(4,128)} %reshape.146, bf16[4,4,4,5120]{3,2,1,0:T(4,128)(2,1)S(1)} %collective-permute-done.30), kind=kLoop, calls=%fused_computation.203 | loop fusion | flops 983040 | bytes 3932160 | tf_op jit(solution)/shard_map/convert_element_type | solution.py:89
  133.9 1.0 collective-permute-start.31
  134.9 0.9 collective-permute-start.32
  135.8 1.7 %collective-permute-start.33 = (bf16[4,4,5120]{2,1,0:T(4,128)(2,1)S(1)}, bf16[4,4,5120]{2,1,0:T(4,128)(2,1)S(1)}, u32[]{:S(2)}, u32[]{:S(2)}) collective-permute-start(bf16[4,4,5120]{2,1,0:T(4,128)(2,1)S(1)} %get-tuple-element.21), channel_id=1, source_target_pairs={{0,6},{1,7},{2,4},{3,5},{4,2},{5,3},{6,0},{7,1},{8,14},{9,15},{10,... | collective-permute-start | bytes 491528 | tf_op jit(solution)/shard_map/ppermute | solution.py:22
  137.5 3.6 %collective-permute-done.31 = bf16[4,4,5120]{2,1,0:T(4,128)(2,1)S(1)} collective-permute-done((bf16[4,4,5120]{2,1,0:T(4,128)(2,1)S(1)}, bf16[4,4,5120]{2,1,0:T(4,128)(2,1)S(1)}, u32[]{:S(2)}, u32[]{:S(2)}) %collective-permute-start.31) | collective-permute-done | bytes 163872 | tf_op jit(solution)/shard_map/ppermute | solution.py:22
  141.7 2.7 %collective-permute-done.33 = bf16[4,4,5120]{2,1,0:T(4,128)(2,1)S(1)} collective-permute-done((bf16[4,4,5120]{2,1,0:T(4,128)(2,1)S(1)}, bf16[4,4,5120]{2,1,0:T(4,128)(2,1)S(1)}, u32[]{:S(2)}, u32[]{:S(2)}) %collective-permute-start.33) | collective-permute-done | bytes 163872 | tf_op jit(solution)/shard_map/ppermute | solution.py:22
  144.7 1.0 collective-permute-start.35
  145.7 3.4 %collective-permute-start.36 = (bf16[4,5120]{1,0:T(4,128)(2,1)S(1)}, bf16[4,5120]{1,0:T(4,128)(2,1)S(1)}, u32[]{:S(2)}, u32[]{:S(2)}) collective-permute-start(bf16[4,5120]{1,0:T(4,128)(2,1)S(1)} %get-tuple-element.36), channel_id=1, source_target_pairs={{0,24},{8,16},{16,8},{24,0},{1,25},{9,17},{17,9},{25,1},{2,26},{10... | collective-permute-start | bytes 122888 | tf_op jit(solution)/shard_map/ppermute | solution.py:22
  149.1 0.9 collective-permute-done.35
  149.9 1.6 %collective-permute-done.36 = bf16[4,5120]{1,0:T(4,128)(2,1)S(1)} collective-permute-done((bf16[4,5120]{1,0:T(4,128)(2,1)S(1)}, bf16[4,5120]{1,0:T(4,128)(2,1)S(1)}, u32[]{:S(2)}, u32[]{:S(2)}) %collective-permute-start.36) | collective-permute-done | bytes 40992 | tf_op jit(solution)/shard_map/ppermute | solution.py:22
  (129 shorter events, 26.1 us)
Async XLA Ops:
  0.6 75.4 %copy-start = (bf16[8,512,128]{2,1,0:T(8,128)(2,1)S(1)}, bf16[8,512,128]{2,1,0:T(8,128)(2,1)}, u32[]{:S(2)}) copy-start(bf16[8,512,128]{2,1,0:T(8,128)(2,1)} %param.22) | copy-start | bytes 3145732
  3.4 6.6 %copy-start.9 = (s32[4]{0:T(128)S(1)}, s32[4]{0:T(128)}, u32[]{:S(2)}) copy-start(s32[4]{0:T(128)} %param.21) | copy-start | bytes 52
  3.6 6.4 %copy-start.1 = (bf16[1024,64]{1,0:T(8,128)(2,1)}, bf16[1024,64]{1,0:T(8,128)(2,1)S(1)}, u32[]{:S(2)}) copy-start(bf16[1024,64]{1,0:T(8,128)(2,1)S(1)} %fusion.35) | copy-start | bytes 393220
  4.4 13.9 %collective-permute-start.4 = (bf16[128,640]{1,0:T(8,128)(2,1)}, bf16[128,640]{1,0:T(8,128)(2,1)}, u32[]{:S(2)}, u32[]{:S(2)}) collective-permute-start(bf16[128,640]{1,0:T(8,128)(2,1)} %fusion.65), channel_id=1, source_target_pairs={{0,8},{8,0},{16,24},{24,16},{1,9},{9,1},{17,25},{25,17},{2,10},{10... | collective-permute-start | bytes 491528 | tf_op jit(solution)/shard_map/ppermute | solution.py:22
  7.4 15.7 %collective-permute-start.9 = (bf16[128,640]{1,0:T(8,128)(2,1)}, bf16[128,640]{1,0:T(8,128)(2,1)}, u32[]{:S(2)}, u32[]{:S(2)}) collective-permute-start(bf16[128,640]{1,0:T(8,128)(2,1)} %fusion.65), channel_id=1, source_target_pairs={{0,16},{8,24},{16,0},{24,8},{1,17},{9,25},{17,1},{25,9},{2,18},{10... | collective-permute-start | bytes 491528 | tf_op jit(solution)/shard_map/ppermute | solution.py:22
  10.0 16.8 %collective-permute-start.14 = (bf16[128,640]{1,0:T(8,128)(2,1)}, bf16[128,640]{1,0:T(8,128)(2,1)}, u32[]{:S(2)}, u32[]{:S(2)}) collective-permute-start(bf16[128,640]{1,0:T(8,128)(2,1)} %fusion.65), channel_id=1, source_target_pairs={{0,24},{8,16},{16,8},{24,0},{1,25},{9,17},{17,9},{25,1},{2,26},{10... | collective-permute-start | bytes 491528 | tf_op jit(solution)/shard_map/ppermute | solution.py:22
  13.8 2.6 %copy-start.10 = (s32[4]{0:T(128)S(1)}, s32[4]{0:T(128)}, u32[]{:S(2)}) copy-start(s32[4]{0:T(128)} %param.20) | copy-start | bytes 52
  13.8 2.7 %copy-start.7 = (s32[4,16]{1,0:T(4,128)S(1)}, s32[4,16]{1,0:T(4,128)}, u32[]{:S(2)}) copy-start(s32[4,16]{1,0:T(4,128)} %param.19) | copy-start | bytes 772
  18.2 10.8 %collective-permute-start = (bf16[4,4,8,1280]{3,2,1,0:T(8,128)(2,1)S(1)}, bf16[4,4,8,1280]{3,2,1,0:T(8,128)(2,1)S(1)}, u32[]{:S(2)}, u32[]{:S(2)}) collective-permute-start(bf16[4,4,8,1280]{3,2,1,0:T(8,128)(2,1)S(1)} %pad_maximum_fusion.5), channel_id=1, source_target_pairs={{0,1},{1,0},{2,3},{3,2},{4,5},{5,4},{6,7},{7,6},{8,9},{9,8},{10,11... | collective-permute-start | bytes 983048 | tf_op jit(solution)/shard_map/ppermute | solution.py:22
  19.9 10.0 %collective-permute-start.5 = (bf16[128,640]{1,0:T(8,128)(2,1)}, bf16[128,640]{1,0:T(8,128)(2,1)S(1)}, u32[]{:S(2)}, u32[]{:S(2)}) collective-permute-start(bf16[128,640]{1,0:T(8,128)(2,1)} %collective-permute-done.4), channel_id=1, source_target_pairs={{0,2},{1,3},{2,0},{3,1},{4,6},{5,7},{6,4},{7,5},{8,10},{9,11},{10,... | collective-permute-start | bytes 491528 | tf_op jit(solution)/shard_map/ppermute | solution.py:22
  21.6 11.1 %collective-permute-start.6 = (bf16[128,640]{1,0:T(8,128)(2,1)}, bf16[128,640]{1,0:T(8,128)(2,1)S(1)}, u32[]{:S(2)}, u32[]{:S(2)}) collective-permute-start(bf16[128,640]{1,0:T(8,128)(2,1)} %collective-permute-done.4), channel_id=1, source_target_pairs={{0,4},{1,5},{2,6},{3,7},{4,0},{5,1},{6,2},{7,3},{8,12},{9,13},{10,... | collective-permute-start | bytes 491528 | tf_op jit(solution)/shard_map/ppermute | solution.py:22
  23.1 10.8 %collective-permute-start.7 = (bf16[128,640]{1,0:T(8,128)(2,1)}, bf16[128,640]{1,0:T(8,128)(2,1)S(1)}, u32[]{:S(2)}, u32[]{:S(2)}) collective-permute-start(bf16[128,640]{1,0:T(8,128)(2,1)} %collective-permute-done.4), channel_id=1, source_target_pairs={{0,6},{1,7},{2,4},{3,5},{4,2},{5,3},{6,0},{7,1},{8,14},{9,15},{10,... | collective-permute-start | bytes 491528 | tf_op jit(solution)/shard_map/ppermute | solution.py:22
  26.8 8.7 %collective-permute-start.10 = (bf16[128,640]{1,0:T(8,128)(2,1)}, bf16[128,640]{1,0:T(8,128)(2,1)S(1)}, u32[]{:S(2)}, u32[]{:S(2)}) collective-permute-start(bf16[128,640]{1,0:T(8,128)(2,1)} %collective-permute-done.9), channel_id=1, source_target_pairs={{0,2},{1,3},{2,0},{3,1},{4,6},{5,7},{6,4},{7,5},{8,10},{9,11},{10,... | collective-permute-start | bytes 491528 | tf_op jit(solution)/shard_map/ppermute | solution.py:22
  29.0 10.2 %collective-permute-start.11 = (bf16[128,640]{1,0:T(8,128)(2,1)}, bf16[128,640]{1,0:T(8,128)(2,1)S(1)}, u32[]{:S(2)}, u32[]{:S(2)}) collective-permute-start(bf16[128,640]{1,0:T(8,128)(2,1)} %collective-permute-done.9), channel_id=1, source_target_pairs={{0,4},{1,5},{2,6},{3,7},{4,0},{5,1},{6,2},{7,3},{8,12},{9,13},{10,... | collective-permute-start | bytes 491528 | tf_op jit(solution)/shard_map/ppermute | solution.py:22
  29.9 11.2 %collective-permute-start.12 = (bf16[128,640]{1,0:T(8,128)(2,1)}, bf16[128,640]{1,0:T(8,128)(2,1)S(1)}, u32[]{:S(2)}, u32[]{:S(2)}) collective-permute-start(bf16[128,640]{1,0:T(8,128)(2,1)} %collective-permute-done.9), channel_id=1, source_target_pairs={{0,6},{1,7},{2,4},{3,5},{4,2},{5,3},{6,0},{7,1},{8,14},{9,15},{10,... | collective-permute-start | bytes 491528 | tf_op jit(solution)/shard_map/ppermute | solution.py:22
  32.8 9.5 %collective-permute-start.15 = (bf16[128,640]{1,0:T(8,128)(2,1)}, bf16[128,640]{1,0:T(8,128)(2,1)S(1)}, u32[]{:S(2)}, u32[]{:S(2)}) collective-permute-start(bf16[128,640]{1,0:T(8,128)(2,1)} %collective-permute-done.14), channel_id=1, source_target_pairs={{0,2},{1,3},{2,0},{3,1},{4,6},{5,7},{6,4},{7,5},{8,10},{9,11},{10,... | collective-permute-start | bytes 491528 | tf_op jit(solution)/shard_map/ppermute | solution.py:22
  34.0 12.2 %collective-permute-start.16 = (bf16[128,640]{1,0:T(8,128)(2,1)}, bf16[128,640]{1,0:T(8,128)(2,1)S(1)}, u32[]{:S(2)}, u32[]{:S(2)}) collective-permute-start(bf16[128,640]{1,0:T(8,128)(2,1)} %collective-permute-done.14), channel_id=1, source_target_pairs={{0,4},{1,5},{2,6},{3,7},{4,0},{5,1},{6,2},{7,3},{8,12},{9,13},{10,... | collective-permute-start | bytes 491528 | tf_op jit(solution)/shard_map/ppermute | solution.py:22
  35.5 11.4 %collective-permute-start.17 = (bf16[128,640]{1,0:T(8,128)(2,1)}, bf16[128,640]{1,0:T(8,128)(2,1)S(1)}, u32[]{:S(2)}, u32[]{:S(2)}) collective-permute-start(bf16[128,640]{1,0:T(8,128)(2,1)} %collective-permute-done.14), channel_id=1, source_target_pairs={{0,6},{1,7},{2,4},{3,5},{4,2},{5,3},{6,0},{7,1},{8,14},{9,15},{10,... | collective-permute-start | bytes 491528 | tf_op jit(solution)/shard_map/ppermute | solution.py:22
  39.2 9.6 %collective-permute-start.1 = (bf16[2,4,8,1280]{3,2,1,0:T(8,128)(2,1)S(1)}, bf16[2,4,8,1280]{3,2,1,0:T(8,128)(2,1)S(1)}, u32[]{:S(2)}, u32[]{:S(2)}) collective-permute-start(bf16[2,4,8,1280]{3,2,1,0:T(8,128)(2,1)S(1)} %get-tuple-element.24), channel_id=1, source_target_pairs={{0,2},{1,3},{2,0},{3,1},{4,6},{5,7},{6,4},{7,5},{8,10},{9,11},{10,... | collective-permute-start | bytes 491528 | tf_op jit(solution)/shard_map/ppermute | solution.py:22
  41.1 11.7 %collective-permute-start.2 = (bf16[2,4,8,1280]{3,2,1,0:T(8,128)(2,1)S(1)}, bf16[2,4,8,1280]{3,2,1,0:T(8,128)(2,1)S(1)}, u32[]{:S(2)}, u32[]{:S(2)}) collective-permute-start(bf16[2,4,8,1280]{3,2,1,0:T(8,128)(2,1)S(1)} %get-tuple-element.26), channel_id=1, source_target_pairs={{0,4},{1,5},{2,6},{3,7},{4,0},{5,1},{6,2},{7,3},{8,12},{9,13},{10,... | collective-permute-start | bytes 491528 | tf_op jit(solution)/shard_map/ppermute | solution.py:22
  42.3 10.4 %collective-permute-start.3 = (bf16[2,4,8,1280]{3,2,1,0:T(8,128)(2,1)S(1)}, bf16[2,4,8,1280]{3,2,1,0:T(8,128)(2,1)S(1)}, u32[]{:S(2)}, u32[]{:S(2)}) collective-permute-start(bf16[2,4,8,1280]{3,2,1,0:T(8,128)(2,1)S(1)} %get-tuple-element.25), channel_id=1, source_target_pairs={{0,6},{1,7},{2,4},{3,5},{4,2},{5,3},{6,0},{7,1},{8,14},{9,15},{10,... | collective-permute-start | bytes 491528 | tf_op jit(solution)/shard_map/ppermute | solution.py:22
  46.2 15.2 %collective-permute-start.8 = (bf16[512,640]{1,0:T(8,128)(2,1)}, bf16[512,640]{1,0:T(8,128)(2,1)}, u32[]{:S(2)}, u32[]{:S(2)}) collective-permute-start(bf16[512,640]{1,0:T(8,128)(2,1)} %constant_dynamic-update-slice_fusion), channel_id=1, source_target_pairs={{0,1},{1,0},{2,3},{3,2},{4,5},{5,4},{6,7},{7,6},{8,9},{9,8},{10,11... | collective-permute-start | bytes 1966088 | tf_op jit(solution)/shard_map/ppermute | solution.py:22
  46.9 16.1 %collective-permute-start.13 = (bf16[512,640]{1,0:T(8,128)(2,1)}, bf16[512,640]{1,0:T(8,128)(2,1)}, u32[]{:S(2)}, u32[]{:S(2)}) collective-permute-start(bf16[512,640]{1,0:T(8,128)(2,1)} %constant_dynamic-update-slice_fusion.4), channel_id=1, source_target_pairs={{0,1},{1,0},{2,3},{3,2},{4,5},{5,4},{6,7},{7,6},{8,9},{9,8},{10,11... | collective-permute-start | bytes 1966088 | tf_op jit(solution)/shard_map/ppermute | solution.py:22
  48.8 15.7 %collective-permute-start.18 = (bf16[512,640]{1,0:T(8,128)(2,1)}, bf16[512,640]{1,0:T(8,128)(2,1)}, u32[]{:S(2)}, u32[]{:S(2)}) collective-permute-start(bf16[512,640]{1,0:T(8,128)(2,1)} %constant_dynamic-update-slice_fusion.8), channel_id=1, source_target_pairs={{0,1},{1,0},{2,3},{3,2},{4,5},{5,4},{6,7},{7,6},{8,9},{9,8},{10,11... | collective-permute-start | bytes 1966088 | tf_op jit(solution)/shard_map/ppermute | solution.py:22
  57.4 3.2 %copy-start.2 = (bf16[1024,64]{1,0:T(8,128)(2,1)S(1)}, bf16[1024,64]{1,0:T(8,128)(2,1)}, u32[]{:S(2)}) copy-start(bf16[1024,64]{1,0:T(8,128)(2,1)} %copy-done.1) | copy-start | bytes 393220
  76.4 6.0 %copy-start.6 = (s32[4,6]{1,0:T(4,128)S(1)}, s32[4,6]{1,0:T(4,128)}, u32[]{:S(2)}) copy-start(s32[4,6]{1,0:T(4,128)} %param.25) | copy-start | bytes 292
  76.4 6.1 %copy-start.8 = (bf16[4,6]{1,0:T(4,128)(2,1)S(1)}, bf16[4,6]{1,0:T(4,128)(2,1)}, u32[]{:S(2)}) copy-start(bf16[4,6]{1,0:T(4,128)(2,1)} %param.26) | copy-start | bytes 148
  82.2 5.4 %copy-start.5 = (bf16[5120]{0:T(1024)(128)(2,1)S(1)}, bf16[5120]{0:T(1024)(128)(2,1)}, u32[]{:S(2)}) copy-start(bf16[5120]{0:T(1024)(128)(2,1)} %param.24) | copy-start | bytes 30724
  82.3 8.7 %copy-start.4 = (bf16[4,5120]{1,0:T(4,128)(2,1)S(1)}, bf16[4,5120]{1,0:T(4,128)(2,1)}, u32[]{:S(2)}) copy-start(bf16[4,5120]{1,0:T(4,128)(2,1)} %param.15) | copy-start | bytes 122884
  82.3 1.5 collective-permute-start.19
  84.0 4.1 %collective-permute-start.20 = (bf16[4,5120]{1,0:T(4,128)(2,1)S(1)}, bf16[4,5120]{1,0:T(4,128)(2,1)S(1)}, u32[]{:S(2)}, u32[]{:S(2)}) collective-permute-start(bf16[4,5120]{1,0:T(4,128)(2,1)S(1)} %get-tuple-element.38), channel_id=1, source_target_pairs={{0,2},{1,3},{2,0},{3,1},{4,6},{5,7},{6,4},{7,5},{8,10},{9,11},{10,... | collective-permute-start | bytes 122888 | tf_op jit(solution)/shard_map/ppermute | solution.py:22
  85.4 4.4 %collective-permute-start.21 = (bf16[4,5120]{1,0:T(4,128)(2,1)S(1)}, bf16[4,5120]{1,0:T(4,128)(2,1)S(1)}, u32[]{:S(2)}, u32[]{:S(2)}) collective-permute-start(bf16[4,5120]{1,0:T(4,128)(2,1)S(1)} %get-tuple-element.40), channel_id=1, source_target_pairs={{0,4},{1,5},{2,6},{3,7},{4,0},{5,1},{6,2},{7,3},{8,12},{9,13},{10,... | collective-permute-start | bytes 122888 | tf_op jit(solution)/shard_map/ppermute | solution.py:22
  86.1 4.9 %collective-permute-start.22 = (bf16[4,5120]{1,0:T(4,128)(2,1)S(1)}, bf16[4,5120]{1,0:T(4,128)(2,1)S(1)}, u32[]{:S(2)}, u32[]{:S(2)}) collective-permute-start(bf16[4,5120]{1,0:T(4,128)(2,1)S(1)} %get-tuple-element.39), channel_id=1, source_target_pairs={{0,6},{1,7},{2,4},{3,5},{4,2},{5,3},{6,0},{7,1},{8,14},{9,15},{10,... | collective-permute-start | bytes 122888 | tf_op jit(solution)/shard_map/ppermute | solution.py:22
  91.2 20.4 %copy-start.3 = (f32[4,5120]{1,0:T(4,128)}, f32[4,5120]{1,0:T(4,128)S(1)}, u32[]{:S(2)}) copy-start(f32[4,5120]{1,0:T(4,128)S(1)} %get-tuple-element.13) | copy-start | bytes 245764
  91.3 4.5 %collective-permute-start.23 = (bf16[4,5248]{1,0:T(4,128)(2,1)S(1)}, bf16[4,5248]{1,0:T(4,128)(2,1)S(1)}, u32[]{:S(2)}, u32[]{:S(2)}) collective-permute-start(bf16[4,5248]{1,0:T(4,128)(2,1)S(1)} %get-tuple-element.42), channel_id=1, source_target_pairs={{0,8},{8,0},{16,24},{24,16},{1,9},{9,1},{17,25},{25,17},{2,10},{10... | collective-permute-start | bytes 125960 | tf_op jit(solution)/shard_map/ppermute | solution.py:22
  92.1 6.4 %collective-permute-start.24 = (bf16[4,5248]{1,0:T(4,128)(2,1)S(1)}, bf16[4,5248]{1,0:T(4,128)(2,1)S(1)}, u32[]{:S(2)}, u32[]{:S(2)}) collective-permute-start(bf16[4,5248]{1,0:T(4,128)(2,1)S(1)} %get-tuple-element.42), channel_id=1, source_target_pairs={{0,16},{8,24},{16,0},{24,8},{1,17},{9,25},{17,1},{25,9},{2,18},{10... | collective-permute-start | bytes 125960 | tf_op jit(solution)/shard_map/ppermute | solution.py:22
  95.6 5.8 %collective-permute-start.25 = (bf16[4,5248]{1,0:T(4,128)(2,1)S(1)}, bf16[4,5248]{1,0:T(4,128)(2,1)S(1)}, u32[]{:S(2)}, u32[]{:S(2)}) collective-permute-start(bf16[4,5248]{1,0:T(4,128)(2,1)S(1)} %get-tuple-element.42), channel_id=1, source_target_pairs={{0,24},{8,16},{16,8},{24,0},{1,25},{9,17},{17,9},{25,1},{2,26},{10... | collective-permute-start | bytes 125960 | tf_op jit(solution)/shard_map/ppermute | solution.py:22
  101.5 5.4 %collective-permute-start.26 = (bf16[4,4,5248]{2,1,0:T(4,128)(2,1)S(1)}, bf16[4,4,5248]{2,1,0:T(4,128)(2,1)S(1)}, u32[]{:S(2)}, u32[]{:S(2)}) collective-permute-start(bf16[4,4,5248]{2,1,0:T(4,128)(2,1)S(1)} %pad_maximum_fusion.6), channel_id=1, source_target_pairs={{0,2},{1,3},{2,0},{3,1},{4,6},{5,7},{6,4},{7,5},{8,10},{9,11},{10,... | collective-permute-start | bytes 503816 | tf_op jit(solution)/shard_map/ppermute | solution.py:22
  103.1 7.2 %collective-permute-start.27 = (bf16[4,4,5248]{2,1,0:T(4,128)(2,1)S(1)}, bf16[4,4,5248]{2,1,0:T(4,128)(2,1)S(1)}, u32[]{:S(2)}, u32[]{:S(2)}) collective-permute-start(bf16[4,4,5248]{2,1,0:T(4,128)(2,1)S(1)} %pad_maximum_fusion.6), channel_id=1, source_target_pairs={{0,4},{1,5},{2,6},{3,7},{4,0},{5,1},{6,2},{7,3},{8,12},{9,13},{10,... | collective-permute-start | bytes 503816 | tf_op jit(solution)/shard_map/ppermute | solution.py:22
  103.6 6.7 %collective-permute-start.28 = (bf16[4,4,5248]{2,1,0:T(4,128)(2,1)S(1)}, bf16[4,4,5248]{2,1,0:T(4,128)(2,1)S(1)}, u32[]{:S(2)}, u32[]{:S(2)}) collective-permute-start(bf16[4,4,5248]{2,1,0:T(4,128)(2,1)S(1)} %pad_maximum_fusion.6), channel_id=1, source_target_pairs={{0,6},{1,7},{2,4},{3,5},{4,2},{5,3},{6,0},{7,1},{8,14},{9,15},{10,... | collective-permute-start | bytes 503816 | tf_op jit(solution)/shard_map/ppermute | solution.py:22
  110.9 2.2 %collective-permute-start.29 = (bf16[4,4,4,5248]{3,2,1,0:T(4,128)(2,1)S(1)}, bf16[4,4,4,5248]{3,2,1,0:T(4,128)(2,1)S(1)}, u32[]{:S(2)}, u32[]{:S(2)}) collective-permute-start(bf16[4,4,4,5248]{3,2,1,0:T(4,128)(2,1)S(1)} %pad_maximum_fusion.3), channel_id=1, source_target_pairs={{0,1},{1,0},{2,3},{3,2},{4,5},{5,4},{6,7},{7,6},{8,9},{9,8},{10,11... | collective-permute-start | bytes 2015240 | tf_op jit(solution)/shard_map/ppermute | solution.py:22
  129.6 2.3 %collective-permute-start.30 = (bf16[4,4,4,5120]{3,2,1,0:T(4,128)(2,1)}, bf16[4,4,4,5120]{3,2,1,0:T(4,128)(2,1)S(1)}, u32[]{:S(2)}, u32[]{:S(2)}) collective-permute-start(bf16[4,4,4,5120]{3,2,1,0:T(4,128)(2,1)} %squeeze.82), channel_id=1, source_target_pairs={{0,1},{1,0},{2,3},{3,2},{4,5},{5,4},{6,7},{7,6},{8,9},{9,8},{10,11... | collective-permute-start | bytes 1966088 | tf_op jit(solution)/shard_map/ppermute | solution.py:22
  133.9 7.1 %collective-permute-start.31 = (bf16[4,4,5120]{2,1,0:T(4,128)(2,1)S(1)}, bf16[4,4,5120]{2,1,0:T(4,128)(2,1)S(1)}, u32[]{:S(2)}, u32[]{:S(2)}) collective-permute-start(bf16[4,4,5120]{2,1,0:T(4,128)(2,1)S(1)} %get-tuple-element.20), channel_id=1, source_target_pairs={{0,2},{1,3},{2,0},{3,1},{4,6},{5,7},{6,4},{7,5},{8,10},{9,11},{10,... | collective-permute-start | bytes 491528 | tf_op jit(solution)/shard_map/ppermute | solution.py:22
  134.9 6.8 %collective-permute-start.32 = (bf16[4,4,5120]{2,1,0:T(4,128)(2,1)S(1)}, bf16[4,4,5120]{2,1,0:T(4,128)(2,1)S(1)}, u32[]{:S(2)}, u32[]{:S(2)}) collective-permute-start(bf16[4,4,5120]{2,1,0:T(4,128)(2,1)S(1)} %get-tuple-element.22), channel_id=1, source_target_pairs={{0,4},{1,5},{2,6},{3,7},{4,0},{5,1},{6,2},{7,3},{8,12},{9,13},{10,... | collective-permute-start | bytes 491528 | tf_op jit(solution)/shard_map/ppermute | solution.py:22
  135.8 8.6 %collective-permute-start.33 = (bf16[4,4,5120]{2,1,0:T(4,128)(2,1)S(1)}, bf16[4,4,5120]{2,1,0:T(4,128)(2,1)S(1)}, u32[]{:S(2)}, u32[]{:S(2)}) collective-permute-start(bf16[4,4,5120]{2,1,0:T(4,128)(2,1)S(1)} %get-tuple-element.21), channel_id=1, source_target_pairs={{0,6},{1,7},{2,4},{3,5},{4,2},{5,3},{6,0},{7,1},{8,14},{9,15},{10,... | collective-permute-start | bytes 491528 | tf_op jit(solution)/shard_map/ppermute | solution.py:22
  144.6 4.5 %collective-permute-start.34 = (bf16[4,5120]{1,0:T(4,128)(2,1)S(1)}, bf16[4,5120]{1,0:T(4,128)(2,1)S(1)}, u32[]{:S(2)}, u32[]{:S(2)}) collective-permute-start(bf16[4,5120]{1,0:T(4,128)(2,1)S(1)} %get-tuple-element.35), channel_id=1, source_target_pairs={{0,8},{8,0},{16,24},{24,16},{1,9},{9,1},{17,25},{25,17},{2,10},{10... | collective-permute-start | bytes 122888 | tf_op jit(solution)/shard_map/ppermute | solution.py:22
  144.7 5.2 %collective-permute-start.35 = (bf16[4,5120]{1,0:T(4,128)(2,1)S(1)}, bf16[4,5120]{1,0:T(4,128)(2,1)S(1)}, u32[]{:S(2)}, u32[]{:S(2)}) collective-permute-start(bf16[4,5120]{1,0:T(4,128)(2,1)S(1)} %get-tuple-element.37), channel_id=1, source_target_pairs={{0,16},{8,24},{16,0},{24,8},{1,17},{9,25},{17,1},{25,9},{2,18},{10... | collective-permute-start | bytes 122888 | tf_op jit(solution)/shard_map/ppermute | solution.py:22
  145.7 5.8 %collective-permute-start.36 = (bf16[4,5120]{1,0:T(4,128)(2,1)S(1)}, bf16[4,5120]{1,0:T(4,128)(2,1)S(1)}, u32[]{:S(2)}, u32[]{:S(2)}) collective-permute-start(bf16[4,5120]{1,0:T(4,128)(2,1)S(1)} %get-tuple-element.36), channel_id=1, source_target_pairs={{0,24},{8,16},{16,8},{24,0},{1,25},{9,17},{17,9},{25,1},{2,26},{10... | collective-permute-start | bytes 122888 | tf_op jit(solution)/shard_map/ppermute | solution.py:22

commit v2 on v1

v2 whole, which is shorter than its diff:
```python
import functools

import jax
import jax.numpy as jnp
from jax import lax
from jax.experimental import pallas as pl
from jax.experimental.pallas import tpu as pltpu
from jax.sharding import PartitionSpec as P

HEADS = 64
LAT = 512
TOPK = 6
BLOCK = 64
SUFFIX = 128
KDIM = 576


NEG_FILL = -1e30
SCORE_SCALE = 192.0 ** (-0.5)
NORM_EPS = 1e-06
LANES = 128


def swap(value, axis, mask):
    size = lax.axis_size(axis)
    return lax.ppermute(value, axis, [(i, i ^ mask) for i in range(size)])


def rounded(value):
    return lax.reduce_precision(value, 8, 7)


def dot(a, b, dims):
    return lax.dot_general(a, b, (dims, ((), ())), preferred_element_type=jnp.float32)


def vmem_call(kernel, out_shape, operands, flops, scalars=0):
    specs = [pl.BlockSpec(memory_space=pltpu.SMEM)] * scalars
    specs += [pl.BlockSpec(memory_space=pltpu.VMEM)] * (len(operands) - scalars)
    size = sum(o.size * o.dtype.itemsize for o in operands)
    return pl.pallas_call(
        kernel,
        out_shape=out_shape,
        in_specs=specs,
        out_specs=jax.tree.map(lambda _: pl.BlockSpec(memory_space=pltpu.VMEM), out_shape),
        cost_estimate=pl.CostEstimate(flops=flops, bytes_accessed=size, transcendentals=0),
        compiler_params=pltpu.CompilerParams(vmem_limit_bytes=48 * 1024 * 1024),
    )(*operands)


def suffix_kernel(count_ref, query_ref, keys_ref, out_ref):
    for r in range(query_ref.shape[0]):
        keys = keys_ref[r]
        scores = dot(query_ref[r], keys, ((1,), (1,))) * SCORE_SCALE
        live = lax.broadcasted_iota(jnp.int32, scores.shape, 1) < count_ref[r]
        scores = jnp.where(live, scores, NEG_FILL)
        top = jnp.max(scores, axis=-1, keepdims=True).astype(jnp.bfloat16).astype(jnp.float32)
        weights = jnp.where(live, jnp.exp(scores - top), 0.0)
        total = jnp.sum(weights, axis=-1, keepdims=True)
        high = total.astype(jnp.bfloat16).astype(jnp.float32)
        numerator = dot(weights.astype(jnp.bfloat16), keys[:, :LAT], ((1,), (0,)))
        lane = lax.broadcasted_iota(jnp.int32, (scores.shape[0], LANES), 1)
        stats = jnp.where(lane == 0, top, jnp.where(lane == 1, high, total - high))
        out_ref[r, :, :LAT] = numerator.astype(jnp.bfloat16)
        out_ref[r, :, LAT:] = stats.astype(jnp.bfloat16)


PAIR = 2 * KDIM
WIDE = KDIM + 64


def pair_keys(chunks, spot):
    blocks = chunks[0].shape[0]
    lane = lax.broadcasted_iota(jnp.int32, (blocks, LANES), 1)
    block = lax.broadcasted_iota(jnp.int32, (blocks, LANES), 0)
    first = (lane < 64).astype(jnp.float32).astype(jnp.bfloat16)
    last = (lane >= 64).astype(jnp.float32).astype(jnp.bfloat16)
    hot_even = (lane == 64 + spot + block).astype(jnp.float32).astype(jnp.bfloat16)
    hot_odd = (lane == spot + block).astype(jnp.float32).astype(jnp.bfloat16)
    even, odd = [], []
    for ref in chunks:
        for at in range(0, ref.shape[1], PAIR):
            middle = ref[:, at + LAT : at + LAT + LANES]
            even.append(
                jnp.concatenate([ref[:, at : at + LAT], middle * first + hot_even], axis=1)
            )
            odd.append(
                jnp.concatenate(
                    [middle * last + hot_odd, ref[:, at + LAT + LANES : at + PAIR]], axis=1
                )
            )
    return jnp.concatenate(even, axis=0), jnp.concatenate(odd, axis=0)


def advance(query_even, query_odd, even, odd, state):
    score_even = dot(query_even, even, ((1,), (1,))) * SCORE_SCALE
    score_odd = dot(query_odd, odd, ((1,), (1,))) * SCORE_SCALE
    top = jnp.maximum(
        jnp.max(score_even, axis=-1, keepdims=True), jnp.max(score_odd, axis=-1, keepdims=True)
    )
    if state is not None:
        top = jnp.maximum(top, state[0])
    weight_even = jnp.exp(score_even - top)
    weight_odd = jnp.exp(score_odd - top)
    total = jnp.sum(weight_even, axis=-1, keepdims=True)
    total = total + jnp.sum(weight_odd, axis=-1, keepdims=True)
    sum_even = dot(weight_even.astype(jnp.bfloat16), even[:, :LAT], ((1,), (0,)))
    sum_odd = dot(weight_odd.astype(jnp.bfloat16), odd, ((1,), (0,)))
    if state is not None:
        keep = jnp.exp(state[0] - top)
        total = total + state[1] * keep
        sum_even = sum_even + state[2] * keep
        sum_odd = sum_odd + state[3] * keep
    return top, total, sum_even, sum_odd


def prefix_kernel(count, spots, has_state, *refs):
    query_even, query_odd = refs[0][...], refs[1][...]
    refs = refs[2:]
    state = None
    if has_state:
        state = (refs[0][:, :1], refs[1][:, :1], refs[2][...], refs[3][...])
        refs = refs[4:]
    for spot in spots:
        even, odd = pair_keys(refs[:count], spot)
        refs = refs[count:]
        state = advance(query_even, query_odd, even, odd, state)
    top_ref, total_ref, even_ref, odd_ref = refs
    top_ref[...] = jnp.broadcast_to(state[0], top_ref.shape)
    total_ref[...] = jnp.broadcast_to(state[1], total_ref.shape)
    even_ref[...] = state[2]
    odd_ref[...] = state[3]


def prefix_step(queries, sources, spots, state):
    rows = queries[0].shape[0]
    count = len(sources[0])
    chunks = [c for source in sources for c in source]
    operands = list(queries) + list(state or ()) + chunks
    f32 = jnp.float32
    out_shape = (
        jax.ShapeDtypeStruct((rows, LANES), f32),
        jax.ShapeDtypeStruct((rows, LANES), f32),
        jax.ShapeDtypeStruct((rows, LAT), f32),
        jax.ShapeDtypeStruct((rows, WIDE), f32),
    )
    flops = sum(c.size for c in chunks) * rows * 4
    kernel = functools.partial(prefix_kernel, count, tuple(spots), state is not None)
    return vmem_call(kernel, out_shape, operands, flops)


def finish_kernel(top_ref, total_ref, even_ref, odd_ref, own_ref, value_ref, out_ref):
    heads = value_ref.shape[0]
    rows = top_ref.shape[0] // heads
    for h in range(heads):
        at = pl.ds(h * rows, rows)
        stats = own_ref[at, LAT:].astype(jnp.float32)
        own_top = stats[:, 0:1]
        own_total = stats[:, 1:2] + stats[:, 2:3]
        top = jnp.maximum(top_ref[at, :1], own_top)
        keep = jnp.exp(top_ref[at, :1] - top)
        own_keep = jnp.exp(own_top - top)
        numerator = (even_ref[at, :] + odd_ref[at, 64 : 64 + LAT]) * keep
        numerator = numerator + own_ref[at, :LAT].astype(jnp.float32) * own_keep
        total = total_ref[at, :1] * keep + own_total * own_keep
        context = (numerator / total).astype(jnp.bfloat16)
        out_ref[:, h * value_ref.shape[2] : (h + 1) * value_ref.shape[2]] = dot(
            context, value_ref[h], ((1,), (0,))
        ).astype(jnp.bfloat16)


def to_head_owners(groups, members):
    chips = members // 2
    mine = jnp.stack(groups[0::2])
    other = swap(jnp.stack(groups[1::2]), "expert", 1)
    both = jnp.stack([mine, other], axis=1)
    return jnp.stack([both[0]] + [swap(both[k], "expert", 2 * k) for k in range(1, chips)])


def sum_over_heads(partial, members):
    chips = members // 2
    away = swap(partial[:, 1].astype(jnp.bfloat16), "expert", 1)
    held = partial[:, 0] + away.astype(jnp.float32)
    total = held[0]
    sent = held.astype(jnp.bfloat16)
    for k in range(1, chips):
        total = total + swap(sent[k], "expert", 2 * k).astype(jnp.float32)
    return total


def spread(rows, members, holders):
    by_z = jnp.stack([rows] + [swap(rows, "dp", q) for q in range(1, holders)])
    by_chip = jnp.stack([by_z] + [swap(by_z, "expert", 2 * k) for k in range(1, members // 2)])
    return jnp.stack([by_chip, swap(by_chip, "expert", 1)])


def gather_sums(partial, members, holders):
    held = partial[0].astype(jnp.float32) + swap(partial[1], "expert", 1).astype(jnp.float32)
    sent = held.astype(jnp.bfloat16)
    total = held[0]
    for k in range(1, members // 2):
        total = total + swap(sent[k], "expert", 2 * k).astype(jnp.float32)
    sent = total.astype(jnp.bfloat16)
    result = total[0]
    for q in range(1, holders):
        result = result + swap(sent[q], "dp", q).astype(jnp.float32)
    return result


def per_device(
    hidden_in,
    query,
    prefix_pool,
    suffix_cache,
    block_list,
    prefix_count,
    suffix_count,
    value_up,
    out_proj,
    norm_gain,
    expert_ids,
    gate_weights,
    gate_proj,
    up_proj,
    down_proj,
):
    bf16 = jnp.bfloat16
    row_count, width = hidden_in.shape
    members = lax.axis_size("expert")
    holders = lax.axis_size("dp")
    chips = members // 2
    place = lax.axis_index("expert")
    shard = lax.axis_index("dp")
    shard_blocks = prefix_pool.shape[0]
    total_blocks = shard_blocks * holders

    piece_width = prefix_pool.shape[1] // members
    piece = lax.dynamic_slice_in_dim(prefix_pool, place * piece_width, piece_width, 1)
    arrived = [swap(piece, "dp", q) for q in range(1, holders)]

    in_prefix = jnp.arange(block_list.shape[1], dtype=jnp.int32)[None, :] < prefix_count[:, None]
    slots = jnp.arange(total_blocks, dtype=jnp.int32)
    ids = (shard ^ (slots // shard_blocks)) * shard_blocks + slots % shard_blocks
    member = jnp.any((block_list[:, :, None] == ids) & in_prefix[:, :, None], axis=1)
    bias = jnp.where(member, 0.0, NEG_FILL).astype(bf16)
    bias = jnp.pad(bias, ((0, 0), (0, LANES - total_blocks)))
    group_heads = HEADS // members
    group_width = group_heads * KDIM
    groups = [
        jnp.concatenate(
            [
                lax.dynamic_slice_in_dim(query, (place ^ j) * group_width, group_width, 1),
                bias,
            ],
            axis=1,
        )
        for j in range(members)
    ]
    held = to_head_owners(groups, members).reshape(-1, group_width + LANES)
    head_queries = held[:, :group_width].reshape(-1, group_heads, KDIM)
    head_queries = head_queries.transpose(1, 0, 2).reshape(-1, KDIM)
    head_bias = jnp.tile(held[:, group_width:], (group_heads, 1))
    variants = []
    for at in range(0, total_blocks, 64):
        part = head_bias[:, at : at + 64]
        variants.append(
            (
                jnp.concatenate([head_queries, part], axis=1),
                jnp.concatenate([part, head_queries], axis=1),
            )
        )

    queries = query.reshape(row_count, HEADS, KDIM)
    own_keys = suffix_cache.reshape(row_count, SUFFIX, KDIM)
    own = vmem_call(
        suffix_kernel,
        jax.ShapeDtypeStruct((row_count, HEADS, LAT + LANES), bf16),
        [suffix_count, queries, own_keys],
        4 * row_count * HEADS * SUFFIX * KDIM,
        scalars=1,
    )
    own_groups = own.reshape(row_count, members, group_heads, LAT + LANES)
    own = to_head_owners(
        [
            lax.dynamic_index_in_dim(own_groups, place ^ j, 1, keepdims=False)
            for j in range(members)
        ],
        members,
    )
    own = own.reshape(-1, group_heads, LAT + LANES).transpose(1, 0, 2)
    own = own.reshape(-1, LAT + LANES)

    state = prefix_step(variants[0], [[prefix_pool]], [0], None)
    for q in range(1, holders):
        mine = [arrived[q - 1]]
        mine += [swap(mine[0], "expert", 2 * k) for k in range(1, chips)]
        chunks = mine + [swap(block, "expert", 1) for block in mine]
        spot = q * shard_blocks
        state = prefix_step(variants[spot // 64], [chunks], [spot % 64], state)
    value_rows = vmem_call(
        finish_kernel,
        jax.ShapeDtypeStruct((state[0].shape[0] // group_heads, group_heads * 128), bf16),
        list(state) + [own, value_up],
        2 * state[2].size * 128,
    )
    partial = jnp.dot(value_rows, out_proj, preferred_element_type=jnp.float32)
    attended = sum_over_heads(partial.reshape(chips, 2, row_count, width), members)
    residual_out = hidden_in.astype(jnp.float32) + attended
    scale_rows = lax.rsqrt(jnp.mean(residual_out * residual_out, axis=-1, keepdims=True) + NORM_EPS)
    normed = (residual_out * scale_rows * norm_gain.astype(jnp.float32)).astype(bf16)

    expert_total = gate_proj.shape[0] * members
    chosen = expert_ids[:, :, None] == jnp.arange(LANES, dtype=jnp.int32)
    gates = jnp.sum(jnp.where(chosen, gate_weights[:, :, None], 0.0), axis=1).astype(bf16)
    rows = spread(jnp.concatenate([normed, gates], axis=1), members, holders)
    flat = rows.reshape(-1, width + LANES)
    tokens = flat[:, :width]
    gate = lax.dynamic_slice_in_dim(flat[:, width:], place, 1, 1).astype(jnp.float32)
    gate_part = jnp.dot(tokens, gate_proj[0], preferred_element_type=jnp.float32)
    up_part = jnp.dot(tokens, up_proj[0], preferred_element_type=jnp.float32)
    hidden = (jax.nn.silu(gate_part) * up_part).astype(bf16)
    result = jnp.dot(hidden, down_proj[0], preferred_element_type=jnp.float32) * gate
    result = result.astype(bf16).reshape(2, chips, holders, row_count, width)
    moe_sum = gather_sums(result, members, holders)
    return (residual_out, moe_sum)


def solution(mesh):
    in_specs = (
        P(("dp", "expert"), None),
        P(("dp", "expert"), None),
        P("dp", None),
        P(("dp", "expert"), None),
        P(("dp", "expert"), None),
        P(("dp", "expert")),
        P(("dp", "expert")),
        P("expert", None, None),
        P("expert", None),
        P(),
        P(("dp", "expert"), None),
        P(("dp", "expert"), None),
        P("expert", None, "dp"),
        P("expert", None, "dp"),
        P("expert", "dp", None),
    )
    out_specs = (P(("dp", "expert"), None), P(("dp", "expert"), None))
    return jax.shard_map(
        per_device, mesh=mesh, in_specs=in_specs, out_specs=out_specs, check_vma=False
    )
```

time: 153 us -> 131 us (0.86)
  matrix products: 35.1 us -> 14.1 us
  local copies, waits for them, and re-layouts: 28.4 us -> 11.9 us
  starting transfers between devices: 41.9 us -> 52.1 us
  Pallas kernels: 0 us -> 7.75 us
    dot_general x17 -> x0, matrix products: 20.1 us -> none  [the longest x14 19.1 us: dot(): lax.dot_general(a, b, (dims, ((), ())), preferred_element_type=jnp.float32)]
    ppermute x37 -> x50, starting transfers between devices: 41.9 us -> 52.1 us  [swap(): return lax.ppermute(value, axis, [(i, i ^ mask) for i in range(size)])]
    unnamed x36 -> x33, local copies, waits for them, and re-layouts: 10.9 us -> 1.22 us
    pallas_call x0 -> x6, Pallas kernels: none -> 7.75 us  [vmem_call(): pl.pallas_call(kernel, out_shape=out_shape, in_specs=specs, out_specs=jax...]
    concatenate x9 -> x0, local copies, waits for them, and re-layouts: 5.49 us -> none  [the longest x6 3.41 us: per_device(): jnp.concatenate([queries, bias, own_num.astype(bf16), jnp.pad(stats, ((0,...]
    reshape x1, local copies, waits for them, and re-layouts: 2.47 us -> 0.35 us  [per_device(): flat = rows.reshape(-1, width + LANES)]
    dynamic_slice x0 -> x2, local copies, waits for them, and re-layouts: none -> 2.02 us  [the longest x1 1.02 us: per_device(): lax.dynamic_slice_in_dim(query, (place ^ j) * group_width, group_width, 1)]
    ppermute x37 -> x50, waiting for transfers between devices: 33.7 us -> 32.4 us  [swap(): return lax.ppermute(value, axis, [(i, i ^ mask) for i in range(size)])]
  transfers between devices with their start and end apart: 37 -> 50, of which waited for: 19 -> 20; matrix products, arithmetic and copies ran while one was open for 22% -> 9% of each run, Pallas kernels for 0% -> 4%
where the time goes in v2:
time: 131 us; the launch traced here: 130 us
  starting transfers between devices  52.1 us (40%)
  waiting for transfers between devices  32.4 us (25%)
  matrix products  14.1 us (11%)
  local copies, waits for them, and re-layouts  11.9 us (9%)
  other arithmetic  10.7 us (8%)
  Pallas kernels  7.75 us (6%)
  between operations  1.31 us (1%)
    ppermute x50, starting transfers between devices, swap(): return lax.ppermute(value, axis, [(i, i ^ mask) for i in range(size)])  52.1 us
    ppermute x50, waiting for transfers between devices, swap(): return lax.ppermute(value, axis, [(i, i ^ mask) for i in range(size)])  32.4 us
    pallas_call x6, Pallas kernels, vmem_call(): pl.pallas_call(kernel, out_shape=out_shape, in_specs=specs, out_specs=jax...  7.75 us
    dot_general x1, matrix products, per_device(): partial = jnp.dot(value_rows, out_proj, preferred_element_type=jnp.float32)  6.06 us
    dot_general x1, matrix products, per_device(): jnp.dot(hidden, down_proj[0], preferred_element_type=jnp.float32) * gate  5.02 us
    dot_general x1, matrix products, per_device(): up_part = jnp.dot(tokens, up_proj[0], preferred_element_type=jnp.float32)  3.01 us
  transfers between devices with their start and end apart: 50, of which 20 were waited for; matrix products, arithmetic and copies ran while one was open for 9% of the time, Pallas kernels for 4%

profile of v2, /device:TPU:0, one launch (start us, length us, event | category | flops | bytes accessed | tf_op | source)
XLA Modules:
  0.0 130.2 jit_solution(12905436146681780299)
XLA Ops:
  0.7 1.0 constant_dynamic-slice_fusion.1
  1.7 3.1 %collective-permute-start.4 = (bf16[16,4608]{1,0:T(8,128)(2,1)S(1)}, bf16[16,4608]{1,0:T(8,128)(2,1)S(1)}, u32[]{:S(2)}, u32[]{:S(2)}) collective-permute-start(bf16[16,4608]{1,0:T(8,128)(2,1)S(1)} %constant_dynamic-slice_fusion.1), channel_id=1, source_target_pairs={{0,8},{8,0},{16,24},{24,16},{1,9},{9,1},{17,25},{25,17},{2,10},{10... | collective-permute-start | bytes 442376 | tf_op jit(solution)/shard_map/ppermute | solution.py:26
  4.7 2.6 %collective-permute-start.12 = (bf16[16,4608]{1,0:T(8,128)(2,1)S(1)}, bf16[16,4608]{1,0:T(8,128)(2,1)S(1)}, u32[]{:S(2)}, u32[]{:S(2)}) collective-permute-start(bf16[16,4608]{1,0:T(8,128)(2,1)S(1)} %constant_dynamic-slice_fusion.1), channel_id=1, source_target_pairs={{0,16},{8,24},{16,0},{24,8},{1,17},{9,25},{17,1},{25,9},{2,18},{10... | collective-permute-start | bytes 442376 | tf_op jit(solution)/shard_map/ppermute | solution.py:26
  7.3 0.7 iota_compare_fusion.2
  8.1 0.8 and_reduce_fusion
  8.9 1.0 constant_dynamic-slice_fusion.9
  11.5 1.7 %shard_map.162 = bf16[4,64,640]{2,1,0:T(8,128)(2,1)S(1)} custom-call(s32[4]{0:T(128)S(1)} %copy-done.2, bf16[4,64,576]{2,1,0:T(8,128)(2,1)S(1)} %reshape.113.query_ref, bf16[4,128,576]{2,1,0:T(8,128)(2,1)S(1)} %reshape.114.keys_ref), custom_call_target="tpu_custom_call" | custom-call | flops 75497472 | bytes 884752 | tf_op jit(solution)/shard_map/pallas_call | solution.py:41
  14.1 1.8 %collective-permute-start.5 = (bf16[16,4608]{1,0:T(8,128)(2,1)S(1)}, bf16[16,4608]{1,0:T(8,128)(2,1)S(1)}, u32[]{:S(2)}, u32[]{:S(2)}) collective-permute-start(bf16[16,4608]{1,0:T(8,128)(2,1)S(1)} %collective-permute-done.4.refs_6_), channel_id=1, source_target_pairs={{0,2},{1,3},{2,0},{3,1},{4,6},{5,7},{6,4},{7,5},{8,10},{9,11},{10,... | collective-permute-start | bytes 442376 | tf_op jit(solution)/shard_map/ppermute | solution.py:26
  16.1 1.6 %collective-permute-start.3 = (bf16[2,4,4736]{2,1,0:T(4,128)(2,1)S(1)}, bf16[2,4,4736]{2,1,0:T(4,128)(2,1)S(1)}, u32[]{:S(2)}, u32[]{:S(2)}) collective-permute-start(bf16[2,4,4736]{2,1,0:T(4,128)(2,1)S(1)} %get-tuple-element.63), channel_id=1, source_target_pairs={{0,6},{1,7},{2,4},{3,5},{4,2},{5,3},{6,0},{7,1},{8,14},{9,15},{10,... | collective-permute-start | bytes 227336 | tf_op jit(solution)/shard_map/ppermute | solution.py:26
  18.7 2.5 %collective-permute-start.31 = (bf16[2,4,8,640]{3,2,1,0:T(8,128)(2,1)S(1)}, bf16[2,4,8,640]{3,2,1,0:T(8,128)(2,1)S(1)}, u32[]{:S(2)}, u32[]{:S(2)}) collective-permute-start(bf16[2,4,8,640]{3,2,1,0:T(8,128)(2,1)S(1)} %get-tuple-element.51), channel_id=1, source_target_pairs={{0,6},{1,7},{2,4},{3,5},{4,2},{5,3},{6,0},{7,1},{8,14},{9,15},{10,... | collective-permute-start | bytes 245768 | tf_op jit(solution)/shard_map/ppermute | solution.py:26
  21.8 1.9 %collective-permute-done.3 = bf16[2,4,4736]{2,1,0:T(4,128)(2,1)S(1)} collective-permute-done((bf16[2,4,4736]{2,1,0:T(4,128)(2,1)S(1)}, bf16[2,4,4736]{2,1,0:T(4,128)(2,1)S(1)}, u32[]{:S(2)}, u32[]{:S(2)}) %collective-permute-start.3) | collective-permute-done | bytes 75808 | tf_op jit(solution)/shard_map/ppermute | solution.py:26
  23.7 1.5 %collective-permute-start.29 = (bf16[2,4,8,640]{3,2,1,0:T(8,128)(2,1)S(1)}, bf16[2,4,8,640]{3,2,1,0:T(8,128)(2,1)}, u32[]{:S(2)}, u32[]{:S(2)}) collective-permute-start(bf16[2,4,8,640]{3,2,1,0:T(8,128)(2,1)S(1)} %get-tuple-element.50), channel_id=1, source_target_pairs={{0,2},{1,3},{2,0},{3,1},{4,6},{5,7},{6,4},{7,5},{8,10},{9,11},{10,... | collective-permute-start | bytes 245768 | tf_op jit(solution)/shard_map/ppermute | solution.py:26
  25.2 1.7 %collective-permute-start.1 = (bf16[2,4,4736]{2,1,0:T(4,128)(2,1)S(1)}, bf16[2,4,4736]{2,1,0:T(4,128)(2,1)S(1)}, u32[]{:S(2)}, u32[]{:S(2)}) collective-permute-start(bf16[2,4,4736]{2,1,0:T(4,128)(2,1)S(1)} %get-tuple-element.62), channel_id=1, source_target_pairs={{0,2},{1,3},{2,0},{3,1},{4,6},{5,7},{6,4},{7,5},{8,10},{9,11},{10,... | collective-permute-start | bytes 227336 | tf_op jit(solution)/shard_map/ppermute | solution.py:26
  26.8 2.7 %collective-permute-done.1 = bf16[2,4,4736]{2,1,0:T(4,128)(2,1)S(1)} collective-permute-done((bf16[2,4,4736]{2,1,0:T(4,128)(2,1)S(1)}, bf16[2,4,4736]{2,1,0:T(4,128)(2,1)S(1)}, u32[]{:S(2)}, u32[]{:S(2)}) %collective-permute-start.1) | collective-permute-done | bytes 75808 | tf_op jit(solution)/shard_map/ppermute | solution.py:26
  29.5 0.8 collective-permute-start.6
  30.3 2.3 %collective-permute-start.7 = (bf16[16,4608]{1,0:T(8,128)(2,1)S(1)}, bf16[16,4608]{1,0:T(8,128)(2,1)S(1)}, u32[]{:S(2)}, u32[]{:S(2)}) collective-permute-start(bf16[16,4608]{1,0:T(8,128)(2,1)S(1)} %collective-permute-done.4.refs_6_), channel_id=1, source_target_pairs={{0,6},{1,7},{2,4},{3,5},{4,2},{5,3},{6,0},{7,1},{8,14},{9,15},{10,... | collective-permute-start | bytes 442376 | tf_op jit(solution)/shard_map/ppermute | solution.py:26
  33.7 0.8 collective-permute-start.14
  34.7 2.1 %collective-permute-start.15 = (bf16[16,4608]{1,0:T(8,128)(2,1)S(1)}, bf16[16,4608]{1,0:T(8,128)(2,1)S(1)}, u32[]{:S(2)}, u32[]{:S(2)}) collective-permute-start(bf16[16,4608]{1,0:T(8,128)(2,1)S(1)} %collective-permute-done.12.refs_6_), channel_id=1, source_target_pairs={{0,6},{1,7},{2,4},{3,5},{4,2},{5,3},{6,0},{7,1},{8,14},{9,15},{10,... | collective-permute-start | bytes 442376 | tf_op jit(solution)/shard_map/ppermute | solution.py:26
  37.0 2.4 %collective-permute-start.21 = (bf16[16,4608]{1,0:T(8,128)(2,1)S(1)}, bf16[16,4608]{1,0:T(8,128)(2,1)S(1)}, u32[]{:S(2)}, u32[]{:S(2)}) collective-permute-start(bf16[16,4608]{1,0:T(8,128)(2,1)S(1)} %collective-permute-done.20.refs_6_), channel_id=1, source_target_pairs={{0,2},{1,3},{2,0},{3,1},{4,6},{5,7},{6,4},{7,5},{8,10},{9,11},{10,... | collective-permute-start | bytes 442376 | tf_op jit(solution)/shard_map/ppermute | solution.py:26
  39.3 0.7 collective-permute-done.13.refs_7_
  40.1 1.0 collective-permute-start.22
  41.1 3.1 %collective-permute-start.23 = (bf16[16,4608]{1,0:T(8,128)(2,1)S(1)}, bf16[16,4608]{1,0:T(8,128)(2,1)S(1)}, u32[]{:S(2)}, u32[]{:S(2)}) collective-permute-start(bf16[16,4608]{1,0:T(8,128)(2,1)S(1)} %collective-permute-done.20.refs_6_), channel_id=1, source_target_pairs={{0,6},{1,7},{2,4},{3,5},{4,2},{5,3},{6,0},{7,1},{8,14},{9,15},{10,... | collective-permute-start | bytes 442376 | tf_op jit(solution)/shard_map/ppermute | solution.py:26
  44.5 0.7 slice.125
  45.3 2.1 %reshape.111 = bf16[32,8,576]{2,1,0:T(8,128)(2,1)} reshape(bf16[32,4608]{1,0:T(8,128)(2,1)} %slice.125) | data formatting | bytes 589824 | tf_op jit(solution)/shard_map/reshape | solution.py:260
  47.3 1.0 copy.48
  49.8 1.2 shard_map.158
  52.6 0.9 pad_maximum_fusion.4
  53.5 1.3 %shard_map.159 = (f32[256,128]{1,0:T(8,128)S(1)}, f32[256,128]{1,0:T(8,128)S(1)}, f32[256,512]{1,0:T(8,128)S(1)}, f32[256,640]{1,0:T(8,128)S(1)}) custom-call(bf16[256,640]{1,0:T(8,128)(2,1)S(1)} %get-tuple-element.48.refs_0_, bf16[256,640]{1,0:T(8,128)(2,1)S(1)} %get-tuple-element.47.refs_1_, f32[256,128]{1,0:T(8,128)S(1)} %get-tuple-element.18.refs_2_, ...), custom_call_target="tpu_custom_call" | custom-call | flops 603979776 | bytes 3276800 | tf_op jit(solution)/shard_map/pallas_call | solution.py:41
  54.9 1.3 %shard_map.160 = (f32[256,128]{1,0:T(8,128)S(1)}, f32[256,128]{1,0:T(8,128)S(1)}, f32[256,512]{1,0:T(8,128)S(1)}, f32[256,640]{1,0:T(8,128)S(1)}) custom-call(bf16[256,640]{1,0:T(8,128)(2,1)S(1)} %get-tuple-element.48.refs_0_, bf16[256,640]{1,0:T(8,128)(2,1)S(1)} %get-tuple-element.47.refs_1_, f32[256,128]{1,0:T(8,128)S(1)} %get-tuple-element.22.refs_2_, ...), custom_call_target="tpu_custom_call" | custom-call | flops 603979776 | bytes 3276800 | tf_op jit(solution)/shard_map/pallas_call | solution.py:41
  56.3 1.3 %shard_map.161 = (f32[256,128]{1,0:T(8,128)S(1)}, f32[256,128]{1,0:T(8,128)S(1)}, f32[256,512]{1,0:T(8,128)S(1)}, f32[256,640]{1,0:T(8,128)S(1)}) custom-call(bf16[256,640]{1,0:T(8,128)(2,1)S(1)} %get-tuple-element.48.refs_0_, bf16[256,640]{1,0:T(8,128)(2,1)S(1)} %get-tuple-element.47.refs_1_, f32[256,128]{1,0:T(8,128)S(1)} %get-tuple-element.26.refs_2_, ...), custom_call_target="tpu_custom_call" | custom-call | flops 603979776 | bytes 3276800 | tf_op jit(solution)/shard_map/pallas_call | solution.py:41
  57.6 0.8 shard_map.163
  58.4 6.1 %fusion.58 = f32[32,5120]{1,0:T(8,128)S(1)} fusion(bf16[32,1024]{1,0:T(8,128)(2,1)S(1)} %shard_map.163, bf16[1024,5120]{1,0:T(8,128)(2,1)} %param.23), kind=kOutput, calls=%fused_computation.131 | convolution fusion | flops 335544320 | bytes 11206656 | tf_op jit(solution)/shard_map/dot_general | solution.py:306
  65.4 0.9 collective-permute-done.32
  66.4 2.3 %collective-permute-start.35 = (bf16[4,5120]{1,0:T(4,128)(2,1)S(1)}, bf16[4,5120]{1,0:T(4,128)(2,1)S(1)}, u32[]{:S(2)}, u32[]{:S(2)}) collective-permute-start(bf16[4,5120]{1,0:T(4,128)(2,1)S(1)} %get-tuple-element.77), channel_id=1, source_target_pairs={{0,6},{1,7},{2,4},{3,5},{4,2},{5,3},{6,0},{7,1},{8,14},{9,15},{10,... | collective-permute-start | bytes 122888 | tf_op jit(solution)/shard_map/ppermute | solution.py:26
  68.8 1.0 collective-permute-start.34
  69.8 0.7 collective-permute-start.33
  70.6 0.8 collective-permute-done.35
  71.4 1.4 %collective-permute-done.34 = bf16[4,5120]{1,0:T(4,128)(2,1)S(1)} collective-permute-done((bf16[4,5120]{1,0:T(4,128)(2,1)S(1)}, bf16[4,5120]{1,0:T(4,128)(2,1)S(1)}, u32[]{:S(2)}, u32[]{:S(2)}) %collective-permute-start.34) | collective-permute-done | bytes 40992 | tf_op jit(solution)/shard_map/ppermute | solution.py:26
  72.8 1.0 collective-permute-done.33
  74.1 3.7 %collective-permute-start.38 = (bf16[4,5248]{1,0:T(4,128)(2,1)S(1)}, bf16[4,5248]{1,0:T(4,128)(2,1)S(1)}, u32[]{:S(2)}, u32[]{:S(2)}) collective-permute-start(bf16[4,5248]{1,0:T(4,128)(2,1)S(1)} %get-tuple-element.80), channel_id=1, source_target_pairs={{0,24},{8,16},{16,8},{24,0},{1,25},{9,17},{17,9},{25,1},{2,26},{10... | collective-permute-start | bytes 125960 | tf_op jit(solution)/shard_map/ppermute | solution.py:26
  77.8 0.8 collective-permute-start.36
  78.6 1.5 %collective-permute-done.38 = bf16[4,5248]{1,0:T(4,128)(2,1)S(1)} collective-permute-done((bf16[4,5248]{1,0:T(4,128)(2,1)S(1)}, bf16[4,5248]{1,0:T(4,128)(2,1)S(1)}, u32[]{:S(2)}, u32[]{:S(2)}) %collective-permute-start.38) | collective-permute-done | bytes 42016 | tf_op jit(solution)/shard_map/ppermute | solution.py:26
  80.1 2.6 %collective-permute-done.37 = bf16[4,5248]{1,0:T(4,128)(2,1)S(1)} collective-permute-done((bf16[4,5248]{1,0:T(4,128)(2,1)S(1)}, bf16[4,5248]{1,0:T(4,128)(2,1)S(1)}, u32[]{:S(2)}, u32[]{:S(2)}) %collective-permute-start.37) | collective-permute-done | bytes 42016 | tf_op jit(solution)/shard_map/ppermute | solution.py:26
  82.9 2.2 %collective-permute-start.41 = (bf16[4,4,5248]{2,1,0:T(4,128)(2,1)S(1)}, bf16[4,4,5248]{2,1,0:T(4,128)(2,1)S(1)}, u32[]{:S(2)}, u32[]{:S(2)}) collective-permute-start(bf16[4,4,5248]{2,1,0:T(4,128)(2,1)S(1)} %pad_maximum_fusion.6), channel_id=1, source_target_pairs={{0,6},{1,7},{2,4},{3,5},{4,2},{5,3},{6,0},{7,1},{8,14},{9,15},{10,... | collective-permute-start | bytes 503816 | tf_op jit(solution)/shard_map/ppermute | solution.py:26
  85.1 1.3 %collective-permute-start.39 = (bf16[4,4,5248]{2,1,0:T(4,128)(2,1)S(1)}, bf16[4,4,5248]{2,1,0:T(4,128)(2,1)S(1)}, u32[]{:S(2)}, u32[]{:S(2)}) collective-permute-start(bf16[4,4,5248]{2,1,0:T(4,128)(2,1)S(1)} %pad_maximum_fusion.6), channel_id=1, source_target_pairs={{0,2},{1,3},{2,0},{3,1},{4,6},{5,7},{6,4},{7,5},{8,10},{9,11},{10,... | collective-permute-start | bytes 503816 | tf_op jit(solution)/shard_map/ppermute | solution.py:26
  86.6 3.6 %collective-permute-done.41 = bf16[4,4,5248]{2,1,0:T(4,128)(2,1)S(1)} collective-permute-done((bf16[4,4,5248]{2,1,0:T(4,128)(2,1)S(1)}, bf16[4,4,5248]{2,1,0:T(4,128)(2,1)S(1)}, u32[]{:S(2)}, u32[]{:S(2)}) %collective-permute-start.41) | collective-permute-done | bytes 167968 | tf_op jit(solution)/shard_map/ppermute | solution.py:26
  90.2 1.4 %collective-permute-done.40 = bf16[4,4,5248]{2,1,0:T(4,128)(2,1)S(1)} collective-permute-done((bf16[4,4,5248]{2,1,0:T(4,128)(2,1)S(1)}, bf16[4,4,5248]{2,1,0:T(4,128)(2,1)S(1)}, u32[]{:S(2)}, u32[]{:S(2)}) %collective-permute-start.40) | collective-permute-done | bytes 167968 | tf_op jit(solution)/shard_map/ppermute | solution.py:26
  93.0 1.5 %collective-permute-done.42 = bf16[4,4,4,5248]{3,2,1,0:T(4,128)(2,1)S(1)} collective-permute-done((bf16[4,4,4,5248]{3,2,1,0:T(4,128)(2,1)S(1)}, bf16[4,4,4,5248]{3,2,1,0:T(4,128)(2,1)S(1)}, u32[]{:S(2)}, u32[]{:S(2)}) %collective-permute-start.42) | collective-permute-done | bytes 671776 | tf_op jit(solution)/shard_map/ppermute | solution.py:26
  94.4 0.9 pad_maximum_fusion
  95.9 3.0 %fusion.2 = f32[128,384]{1,0:T(8,128)S(1)} fusion(bf16[1,5120,384]{2,1,0:T(8,128)(2,1)} %param.28, bf16[128,5248]{1,0:T(8,128)(2,1)S(1)} %reshape.119), kind=kOutput, calls=%fused_computation.3 | convolution fusion | flops 503316480 | bytes 5439488 | tf_op jit(solution)/shard_map/dot_general | solution.py:320
  98.9 5.0 %fusion = bf16[128,5120]{1,0:T(8,128)(2,1)S(1)} fusion(bf16[1,384,5120]{2,1,0:T(8,128)(2,1)} %param.29, f32[128]{0:T(128)S(1)} %bitcast_convert_fusion, f32[128,384]{1,0:T(8,128)S(1)} %fusion.2, bf16[1,5120,384]{2,1,0:T(8,128)(2,1)} %param.27, bf16[128,5248]{1,0:T(8,128)(2,1)S(1)} %reshape.119), kind=kOutput, calls=%fused_computation.1 | convolution fusion | flops 1008238592 | bytes 10682880 | tf_op jit(solution)/shard_map/dot_general | solution.py:322
  104.0 1.0 fusion.57
  104.9 2.4 %squeeze.94 = bf16[4,4,4,5120]{3,2,1,0:T(4,128)(2,1)} reshape(bf16[64,5120]{1,0:T(8,128)(2,1)} %get-tuple-element.42) | data formatting | bytes 1310720 | tf_op jit(solution)/shard_map/squeeze | solution.py:198
  107.8 1.9 %collective-permute-done.43 = bf16[4,4,4,5120]{3,2,1,0:T(4,128)(2,1)} collective-permute-done((bf16[4,4,4,5120]{3,2,1,0:T(4,128)(2,1)}, bf16[4,4,4,5120]{3,2,1,0:T(4,128)(2,1)}, u32[]{:S(2)}, u32[]{:S(2)}) %collective-permute-start.43) | collective-permute-done | bytes 655392 | tf_op jit(solution)/shard_map/ppermute | solution.py:26
  109.7 1.6 %fusion.53 = (bf16[4,4,4,5120]{3,2,1,0:T(4,128)(2,1)S(1)}, f32[4,4,4,5120]{3,2,1,0:T(4,128)S(1)}) fusion(f32[4,4,4,5120]{3,2,1,0:T(4,128)S(1)} %reshape.121, bf16[4,4,4,5120]{3,2,1,0:T(4,128)(2,1)} %collective-permute-done.43), kind=kLoop, calls=%fused_computation.128 | loop fusion | flops 983040 | bytes 3932160 | tf_op jit(solution)/shard_map/convert_element_type | solution.py:199
  111.5 1.8 %collective-permute-start.46 = (bf16[4,4,5120]{2,1,0:T(4,128)(2,1)S(1)}, bf16[4,4,5120]{2,1,0:T(4,128)(2,1)S(1)}, u32[]{:S(2)}, u32[]{:S(2)}) collective-permute-start(bf16[4,4,5120]{2,1,0:T(4,128)(2,1)S(1)} %get-tuple-element.45), channel_id=1, source_target_pairs={{0,6},{1,7},{2,4},{3,5},{4,2},{5,3},{6,0},{7,1},{8,14},{9,15},{10,... | collective-permute-start | bytes 491528 | tf_op jit(solution)/shard_map/ppermute | solution.py:26
  113.3 1.0 collective-permute-start.45
  114.3 0.7 collective-permute-start.44
  115.0 4.5 %collective-permute-done.46 = bf16[4,4,5120]{2,1,0:T(4,128)(2,1)S(1)} collective-permute-done((bf16[4,4,5120]{2,1,0:T(4,128)(2,1)S(1)}, bf16[4,4,5120]{2,1,0:T(4,128)(2,1)S(1)}, u32[]{:S(2)}, u32[]{:S(2)}) %collective-permute-start.46) | collective-permute-done | bytes 163872 | tf_op jit(solution)/shard_map/ppermute | solution.py:26
  119.5 2.7 %collective-permute-done.45 = bf16[4,4,5120]{2,1,0:T(4,128)(2,1)S(1)} collective-permute-done((bf16[4,4,5120]{2,1,0:T(4,128)(2,1)S(1)}, bf16[4,4,5120]{2,1,0:T(4,128)(2,1)S(1)}, u32[]{:S(2)}, u32[]{:S(2)}) %collective-permute-start.45) | collective-permute-done | bytes 163872 | tf_op jit(solution)/shard_map/ppermute | solution.py:26
  122.5 1.3 collective-permute-start.49
  124.2 2.7 %collective-permute-start.47 = (bf16[4,5120]{1,0:T(4,128)(2,1)S(1)}, bf16[4,5120]{1,0:T(4,128)(2,1)S(1)}, u32[]{:S(2)}, u32[]{:S(2)}) collective-permute-start(bf16[4,5120]{1,0:T(4,128)(2,1)S(1)} %get-tuple-element.73), channel_id=1, source_target_pairs={{0,8},{8,0},{16,24},{24,16},{1,9},{9,1},{17,25},{25,17},{2,10},{10... | collective-permute-start | bytes 122888 | tf_op jit(solution)/shard_map/ppermute | solution.py:26
  126.9 1.6 %collective-permute-done.49 = bf16[4,5120]{1,0:T(4,128)(2,1)S(1)} collective-permute-done((bf16[4,5120]{1,0:T(4,128)(2,1)S(1)}, bf16[4,5120]{1,0:T(4,128)(2,1)S(1)}, u32[]{:S(2)}, u32[]{:S(2)}) %collective-permute-start.49) | collective-permute-done | bytes 40992 | tf_op jit(solution)/shard_map/ppermute | solution.py:26
  128.5 1.1 collective-permute-done.48
  (131 shorter events, 14.3 us)
Async XLA Ops:
  0.6 9.7 %copy-start.3 = (bf16[4,36864]{1,0:T(4,128)(2,1)S(1)}, bf16[4,36864]{1,0:T(4,128)(2,1)}, u32[]{:S(2)}) copy-start(bf16[4,36864]{1,0:T(4,128)(2,1)} %param.16) | copy-start | bytes 884740
  0.6 10.1 %copy-start.4 = (bf16[4,73728]{1,0:T(4,128)(2,1)S(1)}, bf16[4,73728]{1,0:T(4,128)(2,1)}, u32[]{:S(2)}) copy-start(bf16[4,73728]{1,0:T(4,128)(2,1)} %param.18) | copy-start | bytes 1769476
  1.7 12.4 %collective-permute-start.4 = (bf16[16,4608]{1,0:T(8,128)(2,1)S(1)}, bf16[16,4608]{1,0:T(8,128)(2,1)S(1)}, u32[]{:S(2)}, u32[]{:S(2)}) collective-permute-start(bf16[16,4608]{1,0:T(8,128)(2,1)S(1)} %constant_dynamic-slice_fusion.1), channel_id=1, source_target_pairs={{0,8},{8,0},{16,24},{24,16},{1,9},{9,1},{17,25},{25,17},{2,10},{10... | collective-permute-start | bytes 442376 | tf_op jit(solution)/shard_map/ppermute | solution.py:26
  4.7 14.0 %collective-permute-start.12 = (bf16[16,4608]{1,0:T(8,128)(2,1)S(1)}, bf16[16,4608]{1,0:T(8,128)(2,1)S(1)}, u32[]{:S(2)}, u32[]{:S(2)}) collective-permute-start(bf16[16,4608]{1,0:T(8,128)(2,1)S(1)} %constant_dynamic-slice_fusion.1), channel_id=1, source_target_pairs={{0,16},{8,24},{16,0},{24,8},{1,17},{9,25},{17,1},{25,9},{2,18},{10... | collective-permute-start | bytes 442376 | tf_op jit(solution)/shard_map/ppermute | solution.py:26
  7.3 13.9 %collective-permute-start.20 = (bf16[16,4608]{1,0:T(8,128)(2,1)S(1)}, bf16[16,4608]{1,0:T(8,128)(2,1)S(1)}, u32[]{:S(2)}, u32[]{:S(2)}) collective-permute-start(bf16[16,4608]{1,0:T(8,128)(2,1)S(1)} %constant_dynamic-slice_fusion.1), channel_id=1, source_target_pairs={{0,24},{8,16},{16,8},{24,0},{1,25},{9,17},{17,9},{25,1},{2,26},{10... | collective-permute-start | bytes 442376 | tf_op jit(solution)/shard_map/ppermute | solution.py:26
  9.9 1.5 %copy-start.2 = (s32[4]{0:T(128)S(1)}, s32[4]{0:T(128)}, u32[]{:S(2)}) copy-start(s32[4]{0:T(128)} %count_ref.1) | copy-start | bytes 52
  10.2 5.6 %collective-permute-start = (bf16[4,4,4736]{2,1,0:T(4,128)(2,1)S(1)}, bf16[4,4,4736]{2,1,0:T(4,128)(2,1)S(1)}, u32[]{:S(2)}, u32[]{:S(2)}) collective-permute-start(bf16[4,4,4736]{2,1,0:T(4,128)(2,1)S(1)} %pad_maximum_fusion.8), channel_id=1, source_target_pairs={{0,1},{1,0},{2,3},{3,2},{4,5},{5,4},{6,7},{7,6},{8,9},{9,8},{10,11... | collective-permute-start | bytes 454664 | tf_op jit(solution)/shard_map/ppermute | solution.py:26
  13.3 4.3 %collective-permute-start.28 = (bf16[4,4,8,640]{3,2,1,0:T(8,128)(2,1)S(1)}, bf16[4,4,8,640]{3,2,1,0:T(8,128)(2,1)S(1)}, u32[]{:S(2)}, u32[]{:S(2)}) collective-permute-start(bf16[4,4,8,640]{3,2,1,0:T(8,128)(2,1)S(1)} %pad_maximum_fusion.7), channel_id=1, source_target_pairs={{0,1},{1,0},{2,3},{3,2},{4,5},{5,4},{6,7},{7,6},{8,9},{9,8},{10,11... | collective-permute-start | bytes 491528 | tf_op jit(solution)/shard_map/ppermute | solution.py:26
  14.1 19.6 %collective-permute-start.5 = (bf16[16,4608]{1,0:T(8,128)(2,1)S(1)}, bf16[16,4608]{1,0:T(8,128)(2,1)S(1)}, u32[]{:S(2)}, u32[]{:S(2)}) collective-permute-start(bf16[16,4608]{1,0:T(8,128)(2,1)S(1)} %collective-permute-done.4.refs_6_), channel_id=1, source_target_pairs={{0,2},{1,3},{2,0},{3,1},{4,6},{5,7},{6,4},{7,5},{8,10},{9,11},{10,... | collective-permute-start | bytes 442376 | tf_op jit(solution)/shard_map/ppermute | solution.py:26
  16.1 7.6 %collective-permute-start.3 = (bf16[2,4,4736]{2,1,0:T(4,128)(2,1)S(1)}, bf16[2,4,4736]{2,1,0:T(4,128)(2,1)S(1)}, u32[]{:S(2)}, u32[]{:S(2)}) collective-permute-start(bf16[2,4,4736]{2,1,0:T(4,128)(2,1)S(1)} %get-tuple-element.63), channel_id=1, source_target_pairs={{0,6},{1,7},{2,4},{3,5},{4,2},{5,3},{6,0},{7,1},{8,14},{9,15},{10,... | collective-permute-start | bytes 227336 | tf_op jit(solution)/shard_map/ppermute | solution.py:26
  17.6 7.5 %collective-permute-start.2 = (bf16[2,4,4736]{2,1,0:T(4,128)(2,1)S(1)}, bf16[2,4,4736]{2,1,0:T(4,128)(2,1)S(1)}, u32[]{:S(2)}, u32[]{:S(2)}) collective-permute-start(bf16[2,4,4736]{2,1,0:T(4,128)(2,1)S(1)} %get-tuple-element.64), channel_id=1, source_target_pairs={{0,4},{1,5},{2,6},{3,7},{4,0},{5,1},{6,2},{7,3},{8,12},{9,13},{10,... | collective-permute-start | bytes 227336 | tf_op jit(solution)/shard_map/ppermute | solution.py:26
  18.7 11.6 %collective-permute-start.31 = (bf16[2,4,8,640]{3,2,1,0:T(8,128)(2,1)S(1)}, bf16[2,4,8,640]{3,2,1,0:T(8,128)(2,1)S(1)}, u32[]{:S(2)}, u32[]{:S(2)}) collective-permute-start(bf16[2,4,8,640]{3,2,1,0:T(8,128)(2,1)S(1)} %get-tuple-element.51), channel_id=1, source_target_pairs={{0,6},{1,7},{2,4},{3,5},{4,2},{5,3},{6,0},{7,1},{8,14},{9,15},{10,... | collective-permute-start | bytes 245768 | tf_op jit(solution)/shard_map/ppermute | solution.py:26
  21.3 11.4 %collective-permute-start.30 = (bf16[2,4,8,640]{3,2,1,0:T(8,128)(2,1)S(1)}, bf16[2,4,8,640]{3,2,1,0:T(8,128)(2,1)S(1)}, u32[]{:S(2)}, u32[]{:S(2)}) collective-permute-start(bf16[2,4,8,640]{3,2,1,0:T(8,128)(2,1)S(1)} %get-tuple-element.52), channel_id=1, source_target_pairs={{0,4},{1,5},{2,6},{3,7},{4,0},{5,1},{6,2},{7,3},{8,12},{9,13},{10,... | collective-permute-start | bytes 245768 | tf_op jit(solution)/shard_map/ppermute | solution.py:26
  23.7 9.7 %collective-permute-start.29 = (bf16[2,4,8,640]{3,2,1,0:T(8,128)(2,1)S(1)}, bf16[2,4,8,640]{3,2,1,0:T(8,128)(2,1)}, u32[]{:S(2)}, u32[]{:S(2)}) collective-permute-start(bf16[2,4,8,640]{3,2,1,0:T(8,128)(2,1)S(1)} %get-tuple-element.50), channel_id=1, source_target_pairs={{0,2},{1,3},{2,0},{3,1},{4,6},{5,7},{6,4},{7,5},{8,10},{9,11},{10,... | collective-permute-start | bytes 245768 | tf_op jit(solution)/shard_map/ppermute | solution.py:26
  25.2 4.4 %collective-permute-start.1 = (bf16[2,4,4736]{2,1,0:T(4,128)(2,1)S(1)}, bf16[2,4,4736]{2,1,0:T(4,128)(2,1)S(1)}, u32[]{:S(2)}, u32[]{:S(2)}) collective-permute-start(bf16[2,4,4736]{2,1,0:T(4,128)(2,1)S(1)} %get-tuple-element.62), channel_id=1, source_target_pairs={{0,2},{1,3},{2,0},{3,1},{4,6},{5,7},{6,4},{7,5},{8,10},{9,11},{10,... | collective-permute-start | bytes 227336 | tf_op jit(solution)/shard_map/ppermute | solution.py:26
  29.5 5.1 %collective-permute-start.6 = (bf16[16,4608]{1,0:T(8,128)(2,1)S(1)}, bf16[16,4608]{1,0:T(8,128)(2,1)S(1)}, u32[]{:S(2)}, u32[]{:S(2)}) collective-permute-start(bf16[16,4608]{1,0:T(8,128)(2,1)S(1)} %collective-permute-done.4.refs_6_), channel_id=1, source_target_pairs={{0,4},{1,5},{2,6},{3,7},{4,0},{5,1},{6,2},{7,3},{8,12},{9,13},{10,... | collective-permute-start | bytes 442376 | tf_op jit(solution)/shard_map/ppermute | solution.py:26
  30.3 6.6 %copy-start.7 = (bf16[2,4,8,640]{3,2,1,0:T(8,128)(2,1)}, bf16[2,4,8,640]{3,2,1,0:T(8,128)(2,1)S(1)}, u32[]{:S(2)}) copy-start(bf16[2,4,8,640]{3,2,1,0:T(8,128)(2,1)S(1)} %collective-permute-done.31) | copy-start | bytes 245764
  30.3 6.6 %collective-permute-start.7 = (bf16[16,4608]{1,0:T(8,128)(2,1)S(1)}, bf16[16,4608]{1,0:T(8,128)(2,1)S(1)}, u32[]{:S(2)}, u32[]{:S(2)}) collective-permute-start(bf16[16,4608]{1,0:T(8,128)(2,1)S(1)} %collective-permute-done.4.refs_6_), channel_id=1, source_target_pairs={{0,6},{1,7},{2,4},{3,5},{4,2},{5,3},{6,0},{7,1},{8,14},{9,15},{10,... | collective-permute-start | bytes 442376 | tf_op jit(solution)/shard_map/ppermute | solution.py:26
  32.7 4.3 %collective-permute-start.8 = (bf16[16,4608]{1,0:T(8,128)(2,1)S(1)}, bf16[16,4608]{1,0:T(8,128)(2,1)S(1)}, u32[]{:S(2)}, u32[]{:S(2)}) collective-permute-start(bf16[16,4608]{1,0:T(8,128)(2,1)S(1)} %collective-permute-done.4.refs_6_), channel_id=1, source_target_pairs={{0,1},{1,0},{2,3},{3,2},{4,5},{5,4},{6,7},{7,6},{8,9},{9,8},{10,11... | collective-permute-start | bytes 442376 | tf_op jit(solution)/shard_map/ppermute | solution.py:26
  33.3 6.7 %collective-permute-start.13 = (bf16[16,4608]{1,0:T(8,128)(2,1)S(1)}, bf16[16,4608]{1,0:T(8,128)(2,1)S(1)}, u32[]{:S(2)}, u32[]{:S(2)}) collective-permute-start(bf16[16,4608]{1,0:T(8,128)(2,1)S(1)} %collective-permute-done.12.refs_6_), channel_id=1, source_target_pairs={{0,2},{1,3},{2,0},{3,1},{4,6},{5,7},{6,4},{7,5},{8,10},{9,11},{10,... | collective-permute-start | bytes 442376 | tf_op jit(solution)/shard_map/ppermute | solution.py:26
  33.7 7.4 %collective-permute-start.14 = (bf16[16,4608]{1,0:T(8,128)(2,1)S(1)}, bf16[16,4608]{1,0:T(8,128)(2,1)S(1)}, u32[]{:S(2)}, u32[]{:S(2)}) collective-permute-start(bf16[16,4608]{1,0:T(8,128)(2,1)S(1)} %collective-permute-done.12.refs_6_), channel_id=1, source_target_pairs={{0,4},{1,5},{2,6},{3,7},{4,0},{5,1},{6,2},{7,3},{8,12},{9,13},{10,... | collective-permute-start | bytes 442376 | tf_op jit(solution)/shard_map/ppermute | solution.py:26
  34.7 13.7 %collective-permute-start.15 = (bf16[16,4608]{1,0:T(8,128)(2,1)S(1)}, bf16[16,4608]{1,0:T(8,128)(2,1)S(1)}, u32[]{:S(2)}, u32[]{:S(2)}) collective-permute-start(bf16[16,4608]{1,0:T(8,128)(2,1)S(1)} %collective-permute-done.12.refs_6_), channel_id=1, source_target_pairs={{0,6},{1,7},{2,4},{3,5},{4,2},{5,3},{6,0},{7,1},{8,14},{9,15},{10,... | collective-permute-start | bytes 442376 | tf_op jit(solution)/shard_map/ppermute | solution.py:26
  37.0 11.5 %collective-permute-start.16 = (bf16[16,4608]{1,0:T(8,128)(2,1)S(1)}, bf16[16,4608]{1,0:T(8,128)(2,1)S(1)}, u32[]{:S(2)}, u32[]{:S(2)}) collective-permute-start(bf16[16,4608]{1,0:T(8,128)(2,1)S(1)} %collective-permute-done.12.refs_6_), channel_id=1, source_target_pairs={{0,1},{1,0},{2,3},{3,2},{4,5},{5,4},{6,7},{7,6},{8,9},{9,8},{10,11... | collective-permute-start | bytes 442376 | tf_op jit(solution)/shard_map/ppermute | solution.py:26
  37.0 11.9 %collective-permute-start.21 = (bf16[16,4608]{1,0:T(8,128)(2,1)S(1)}, bf16[16,4608]{1,0:T(8,128)(2,1)S(1)}, u32[]{:S(2)}, u32[]{:S(2)}) collective-permute-start(bf16[16,4608]{1,0:T(8,128)(2,1)S(1)} %collective-permute-done.20.refs_6_), channel_id=1, source_target_pairs={{0,2},{1,3},{2,0},{3,1},{4,6},{5,7},{6,4},{7,5},{8,10},{9,11},{10,... | collective-permute-start | bytes 442376 | tf_op jit(solution)/shard_map/ppermute | solution.py:26
  40.1 9.0 %collective-permute-start.22 = (bf16[16,4608]{1,0:T(8,128)(2,1)S(1)}, bf16[16,4608]{1,0:T(8,128)(2,1)S(1)}, u32[]{:S(2)}, u32[]{:S(2)}) collective-permute-start(bf16[16,4608]{1,0:T(8,128)(2,1)S(1)} %collective-permute-done.20.refs_6_), channel_id=1, source_target_pairs={{0,4},{1,5},{2,6},{3,7},{4,0},{5,1},{6,2},{7,3},{8,12},{9,13},{10,... | collective-permute-start | bytes 442376 | tf_op jit(solution)/shard_map/ppermute | solution.py:26
  41.1 8.4 %collective-permute-start.23 = (bf16[16,4608]{1,0:T(8,128)(2,1)S(1)}, bf16[16,4608]{1,0:T(8,128)(2,1)S(1)}, u32[]{:S(2)}, u32[]{:S(2)}) collective-permute-start(bf16[16,4608]{1,0:T(8,128)(2,1)S(1)} %collective-permute-done.20.refs_6_), channel_id=1, source_target_pairs={{0,6},{1,7},{2,4},{3,5},{4,2},{5,3},{6,0},{7,1},{8,14},{9,15},{10,... | collective-permute-start | bytes 442376 | tf_op jit(solution)/shard_map/ppermute | solution.py:26
  45.2 4.6 %copy-start.1 = (bf16[16,36864]{1,0:T(8,128)(2,1)S(1)}, bf16[16,36864]{1,0:T(8,128)(2,1)}, u32[]{:S(2)}) copy-start(bf16[16,36864]{1,0:T(8,128)(2,1)} %refs_2_.1) | copy-start | bytes 3538948
  48.4 2.7 %collective-permute-start.9 = (bf16[16,4608]{1,0:T(8,128)(2,1)S(1)}, bf16[16,4608]{1,0:T(8,128)(2,1)S(1)}, u32[]{:S(2)}, u32[]{:S(2)}) collective-permute-start(bf16[16,4608]{1,0:T(8,128)(2,1)S(1)} %collective-permute-done.5.refs_7_), channel_id=1, source_target_pairs={{0,1},{1,0},{2,3},{3,2},{4,5},{5,4},{6,7},{7,6},{8,9},{9,8},{10,11... | collective-permute-start | bytes 442376 | tf_op jit(solution)/shard_map/ppermute | solution.py:26
  48.4 3.1 %collective-permute-start.10 = (bf16[16,4608]{1,0:T(8,128)(2,1)S(1)}, bf16[16,4608]{1,0:T(8,128)(2,1)S(1)}, u32[]{:S(2)}, u32[]{:S(2)}) collective-permute-start(bf16[16,4608]{1,0:T(8,128)(2,1)S(1)} %collective-permute-done.6.refs_8_), channel_id=1, source_target_pairs={{0,1},{1,0},{2,3},{3,2},{4,5},{5,4},{6,7},{7,6},{8,9},{9,8},{10,11... | collective-permute-start | bytes 442376 | tf_op jit(solution)/shard_map/ppermute | solution.py:26
  48.9 2.7 %collective-permute-start.11 = (bf16[16,4608]{1,0:T(8,128)(2,1)S(1)}, bf16[16,4608]{1,0:T(8,128)(2,1)S(1)}, u32[]{:S(2)}, u32[]{:S(2)}) collective-permute-start(bf16[16,4608]{1,0:T(8,128)(2,1)S(1)} %collective-permute-done.7.refs_9_), channel_id=1, source_target_pairs={{0,1},{1,0},{2,3},{3,2},{4,5},{5,4},{6,7},{7,6},{8,9},{9,8},{10,11... | collective-permute-start | bytes 442376 | tf_op jit(solution)/shard_map/ppermute | solution.py:26
  49.0 3.0 %collective-permute-start.17 = (bf16[16,4608]{1,0:T(8,128)(2,1)S(1)}, bf16[16,4608]{1,0:T(8,128)(2,1)S(1)}, u32[]{:S(2)}, u32[]{:S(2)}) collective-permute-start(bf16[16,4608]{1,0:T(8,128)(2,1)S(1)} %collective-permute-done.13.refs_7_), channel_id=1, source_target_pairs={{0,1},{1,0},{2,3},{3,2},{4,5},{5,4},{6,7},{7,6},{8,9},{9,8},{10,11... | collective-permute-start | bytes 442376 | tf_op jit(solution)/shard_map/ppermute | solution.py:26
  49.5 2.7 %collective-permute-start.18 = (bf16[16,4608]{1,0:T(8,128)(2,1)S(1)}, bf16[16,4608]{1,0:T(8,128)(2,1)S(1)}, u32[]{:S(2)}, u32[]{:S(2)}) collective-permute-start(bf16[16,4608]{1,0:T(8,128)(2,1)S(1)} %collective-permute-done.14.refs_8_), channel_id=1, source_target_pairs={{0,1},{1,0},{2,3},{3,2},{4,5},{5,4},{6,7},{7,6},{8,9},{9,8},{10,11... | collective-permute-start | bytes 442376 | tf_op jit(solution)/shard_map/ppermute | solution.py:26
  49.8 2.8 %copy-start.5 = (bf16[1,2,4,8,640]{4,3,2,1,0:T(8,128)(2,1)S(1)}, bf16[1,2,4,8,640]{4,3,2,1,0:T(8,128)(2,1)}, u32[]{:S(2)}) copy-start(bf16[1,2,4,8,640]{4,3,2,1,0:T(8,128)(2,1)} %get-tuple-element.49) | copy-start | bytes 245764
  49.8 2.8 %copy-start.8 = (bf16[2,4,8,640]{3,2,1,0:T(8,128)(2,1)S(1)}, bf16[2,4,8,640]{3,2,1,0:T(8,128)(2,1)}, u32[]{:S(2)}) copy-start(bf16[2,4,8,640]{3,2,1,0:T(8,128)(2,1)} %copy-done.7) | copy-start | bytes 245764
  49.8 2.8 %copy-start.10 = (bf16[2,4,8,640]{3,2,1,0:T(8,128)(2,1)S(1)}, bf16[2,4,8,640]{3,2,1,0:T(8,128)(2,1)}, u32[]{:S(2)}) copy-start(bf16[2,4,8,640]{3,2,1,0:T(8,128)(2,1)} %copy-done.9) | copy-start | bytes 245764
  51.0 5.2 %collective-permute-start.24 = (bf16[16,4608]{1,0:T(8,128)(2,1)S(1)}, bf16[16,4608]{1,0:T(8,128)(2,1)S(1)}, u32[]{:S(2)}, u32[]{:S(2)}) collective-permute-start(bf16[16,4608]{1,0:T(8,128)(2,1)S(1)} %collective-permute-done.20.refs_6_), channel_id=1, source_target_pairs={{0,1},{1,0},{2,3},{3,2},{4,5},{5,4},{6,7},{7,6},{8,9},{9,8},{10,11... | collective-permute-start | bytes 442376 | tf_op jit(solution)/shard_map/ppermute | solution.py:26
  51.5 3.4 %collective-permute-start.19 = (bf16[16,4608]{1,0:T(8,128)(2,1)S(1)}, bf16[16,4608]{1,0:T(8,128)(2,1)S(1)}, u32[]{:S(2)}, u32[]{:S(2)}) collective-permute-start(bf16[16,4608]{1,0:T(8,128)(2,1)S(1)} %collective-permute-done.15.refs_9_), channel_id=1, source_target_pairs={{0,1},{1,0},{2,3},{3,2},{4,5},{5,4},{6,7},{7,6},{8,9},{9,8},{10,11... | collective-permute-start | bytes 442376 | tf_op jit(solution)/shard_map/ppermute | solution.py:26
  51.6 4.6 %collective-permute-start.25 = (bf16[16,4608]{1,0:T(8,128)(2,1)S(1)}, bf16[16,4608]{1,0:T(8,128)(2,1)S(1)}, u32[]{:S(2)}, u32[]{:S(2)}) collective-permute-start(bf16[16,4608]{1,0:T(8,128)(2,1)S(1)} %collective-permute-done.21.refs_7_), channel_id=1, source_target_pairs={{0,1},{1,0},{2,3},{3,2},{4,5},{5,4},{6,7},{7,6},{8,9},{9,8},{10,11... | collective-permute-start | bytes 442376 | tf_op jit(solution)/shard_map/ppermute | solution.py:26
  52.0 4.2 %collective-permute-start.26 = (bf16[16,4608]{1,0:T(8,128)(2,1)S(1)}, bf16[16,4608]{1,0:T(8,128)(2,1)S(1)}, u32[]{:S(2)}, u32[]{:S(2)}) collective-permute-start(bf16[16,4608]{1,0:T(8,128)(2,1)S(1)} %collective-permute-done.22.refs_8_), channel_id=1, source_target_pairs={{0,1},{1,0},{2,3},{3,2},{4,5},{5,4},{6,7},{7,6},{8,9},{9,8},{10,11... | collective-permute-start | bytes 442376 | tf_op jit(solution)/shard_map/ppermute | solution.py:26
  52.1 4.1 %collective-permute-start.27 = (bf16[16,4608]{1,0:T(8,128)(2,1)S(1)}, bf16[16,4608]{1,0:T(8,128)(2,1)S(1)}, u32[]{:S(2)}, u32[]{:S(2)}) collective-permute-start(bf16[16,4608]{1,0:T(8,128)(2,1)S(1)} %collective-permute-done.23.refs_9_), channel_id=1, source_target_pairs={{0,1},{1,0},{2,3},{3,2},{4,5},{5,4},{6,7},{7,6},{8,9},{9,8},{10,11... | collective-permute-start | bytes 442376 | tf_op jit(solution)/shard_map/ppermute | solution.py:26
  56.3 1.4 %copy-start = (bf16[8,512,128]{2,1,0:T(8,128)(2,1)S(1)}, bf16[8,512,128]{2,1,0:T(8,128)(2,1)}, u32[]{:S(2)}) copy-start(bf16[8,512,128]{2,1,0:T(8,128)(2,1)} %value_ref.1) | copy-start | bytes 3145732
  64.5 0.7 copy-start.13
  64.5 0.8 copy-start.14
  64.5 6.1 %copy-start.12 = (bf16[5120]{0:T(1024)(128)(2,1)S(1)}, bf16[5120]{0:T(1024)(128)(2,1)}, u32[]{:S(2)}) copy-start(bf16[5120]{0:T(1024)(128)(2,1)} %param.24) | copy-start | bytes 30724
  64.5 9.3 %copy-start.11 = (bf16[4,5120]{1,0:T(4,128)(2,1)S(1)}, bf16[4,5120]{1,0:T(4,128)(2,1)}, u32[]{:S(2)}) copy-start(bf16[4,5120]{1,0:T(4,128)(2,1)} %param.15) | copy-start | bytes 122884
  64.8 1.5 %collective-permute-start.32 = (bf16[4,4,5120]{2,1,0:T(4,128)(2,1)S(1)}, bf16[4,4,5120]{2,1,0:T(4,128)(2,1)S(1)}, u32[]{:S(2)}, u32[]{:S(2)}) collective-permute-start(bf16[4,4,5120]{2,1,0:T(4,128)(2,1)S(1)} %fusion.12), channel_id=1, source_target_pairs={{0,1},{1,0},{2,3},{3,2},{4,5},{5,4},{6,7},{7,6},{8,9},{9,8},{10,11... | collective-permute-start | bytes 491528 | tf_op jit(solution)/shard_map/ppermute | solution.py:26
  66.4 5.0 %collective-permute-start.35 = (bf16[4,5120]{1,0:T(4,128)(2,1)S(1)}, bf16[4,5120]{1,0:T(4,128)(2,1)S(1)}, u32[]{:S(2)}, u32[]{:S(2)}) collective-permute-start(bf16[4,5120]{1,0:T(4,128)(2,1)S(1)} %get-tuple-element.77), channel_id=1, source_target_pairs={{0,6},{1,7},{2,4},{3,5},{4,2},{5,3},{6,0},{7,1},{8,14},{9,15},{10,... | collective-permute-start | bytes 122888 | tf_op jit(solution)/shard_map/ppermute | solution.py:26
  68.8 4.0 %collective-permute-start.34 = (bf16[4,5120]{1,0:T(4,128)(2,1)S(1)}, bf16[4,5120]{1,0:T(4,128)(2,1)S(1)}, u32[]{:S(2)}, u32[]{:S(2)}) collective-permute-start(bf16[4,5120]{1,0:T(4,128)(2,1)S(1)} %get-tuple-element.78), channel_id=1, source_target_pairs={{0,4},{1,5},{2,6},{3,7},{4,0},{5,1},{6,2},{7,3},{8,12},{9,13},{10,... | collective-permute-start | bytes 122888 | tf_op jit(solution)/shard_map/ppermute | solution.py:26
  69.8 4.0 %collective-permute-start.33 = (bf16[4,5120]{1,0:T(4,128)(2,1)S(1)}, bf16[4,5120]{1,0:T(4,128)(2,1)S(1)}, u32[]{:S(2)}, u32[]{:S(2)}) collective-permute-start(bf16[4,5120]{1,0:T(4,128)(2,1)S(1)} %get-tuple-element.76), channel_id=1, source_target_pairs={{0,2},{1,3},{2,0},{3,1},{4,6},{5,7},{6,4},{7,5},{8,10},{9,11},{10,... | collective-permute-start | bytes 122888 | tf_op jit(solution)/shard_map/ppermute | solution.py:26
  74.0 19.0 %copy-start.6 = (f32[4,5120]{1,0:T(4,128)}, f32[4,5120]{1,0:T(4,128)S(1)}, u32[]{:S(2)}) copy-start(f32[4,5120]{1,0:T(4,128)S(1)} %get-tuple-element.39) | copy-start | bytes 245764
  74.1 5.9 %collective-permute-start.38 = (bf16[4,5248]{1,0:T(4,128)(2,1)S(1)}, bf16[4,5248]{1,0:T(4,128)(2,1)S(1)}, u32[]{:S(2)}, u32[]{:S(2)}) collective-permute-start(bf16[4,5248]{1,0:T(4,128)(2,1)S(1)} %get-tuple-element.80), channel_id=1, source_target_pairs={{0,24},{8,16},{16,8},{24,0},{1,25},{9,17},{17,9},{25,1},{2,26},{10... | collective-permute-start | bytes 125960 | tf_op jit(solution)/shard_map/ppermute | solution.py:26
  77.8 4.9 %collective-permute-start.37 = (bf16[4,5248]{1,0:T(4,128)(2,1)S(1)}, bf16[4,5248]{1,0:T(4,128)(2,1)S(1)}, u32[]{:S(2)}, u32[]{:S(2)}) collective-permute-start(bf16[4,5248]{1,0:T(4,128)(2,1)S(1)} %get-tuple-element.80), channel_id=1, source_target_pairs={{0,16},{8,24},{16,0},{24,8},{1,17},{9,25},{17,1},{25,9},{2,18},{10... | collective-permute-start | bytes 125960 | tf_op jit(solution)/shard_map/ppermute | solution.py:26
  77.8 4.9 %collective-permute-start.36 = (bf16[4,5248]{1,0:T(4,128)(2,1)S(1)}, bf16[4,5248]{1,0:T(4,128)(2,1)S(1)}, u32[]{:S(2)}, u32[]{:S(2)}) collective-permute-start(bf16[4,5248]{1,0:T(4,128)(2,1)S(1)} %get-tuple-element.80), channel_id=1, source_target_pairs={{0,8},{8,0},{16,24},{24,16},{1,9},{9,1},{17,25},{25,17},{2,10},{10... | collective-permute-start | bytes 125960 | tf_op jit(solution)/shard_map/ppermute | solution.py:26
  82.9 7.3 %collective-permute-start.41 = (bf16[4,4,5248]{2,1,0:T(4,128)(2,1)S(1)}, bf16[4,4,5248]{2,1,0:T(4,128)(2,1)S(1)}, u32[]{:S(2)}, u32[]{:S(2)}) collective-permute-start(bf16[4,4,5248]{2,1,0:T(4,128)(2,1)S(1)} %pad_maximum_fusion.6), channel_id=1, source_target_pairs={{0,6},{1,7},{2,4},{3,5},{4,2},{5,3},{6,0},{7,1},{8,14},{9,15},{10,... | collective-permute-start | bytes 503816 | tf_op jit(solution)/shard_map/ppermute | solution.py:26
  85.1 6.5 %collective-permute-start.40 = (bf16[4,4,5248]{2,1,0:T(4,128)(2,1)S(1)}, bf16[4,4,5248]{2,1,0:T(4,128)(2,1)S(1)}, u32[]{:S(2)}, u32[]{:S(2)}) collective-permute-start(bf16[4,4,5248]{2,1,0:T(4,128)(2,1)S(1)} %pad_maximum_fusion.6), channel_id=1, source_target_pairs={{0,4},{1,5},{2,6},{3,7},{4,0},{5,1},{6,2},{7,3},{8,12},{9,13},{10,... | collective-permute-start | bytes 503816 | tf_op jit(solution)/shard_map/ppermute | solution.py:26
  85.1 6.5 %collective-permute-start.39 = (bf16[4,4,5248]{2,1,0:T(4,128)(2,1)S(1)}, bf16[4,4,5248]{2,1,0:T(4,128)(2,1)S(1)}, u32[]{:S(2)}, u32[]{:S(2)}) collective-permute-start(bf16[4,4,5248]{2,1,0:T(4,128)(2,1)S(1)} %pad_maximum_fusion.6), channel_id=1, source_target_pairs={{0,2},{1,3},{2,0},{3,1},{4,6},{5,7},{6,4},{7,5},{8,10},{9,11},{10,... | collective-permute-start | bytes 503816 | tf_op jit(solution)/shard_map/ppermute | solution.py:26
  92.2 2.2 %collective-permute-start.42 = (bf16[4,4,4,5248]{3,2,1,0:T(4,128)(2,1)S(1)}, bf16[4,4,4,5248]{3,2,1,0:T(4,128)(2,1)S(1)}, u32[]{:S(2)}, u32[]{:S(2)}) collective-permute-start(bf16[4,4,4,5248]{3,2,1,0:T(4,128)(2,1)S(1)} %pad_maximum_fusion.1), channel_id=1, source_target_pairs={{0,1},{1,0},{2,3},{3,2},{4,5},{5,4},{6,7},{7,6},{8,9},{9,8},{10,11... | collective-permute-start | bytes 2015240 | tf_op jit(solution)/shard_map/ppermute | solution.py:26
  107.3 2.4 %collective-permute-start.43 = (bf16[4,4,4,5120]{3,2,1,0:T(4,128)(2,1)}, bf16[4,4,4,5120]{3,2,1,0:T(4,128)(2,1)}, u32[]{:S(2)}, u32[]{:S(2)}) collective-permute-start(bf16[4,4,4,5120]{3,2,1,0:T(4,128)(2,1)} %squeeze.94), channel_id=1, source_target_pairs={{0,1},{1,0},{2,3},{3,2},{4,5},{5,4},{6,7},{7,6},{8,9},{9,8},{10,11... | collective-permute-start | bytes 1966088 | tf_op jit(solution)/shard_map/ppermute | solution.py:26
  111.5 8.1 %collective-permute-start.46 = (bf16[4,4,5120]{2,1,0:T(4,128)(2,1)S(1)}, bf16[4,4,5120]{2,1,0:T(4,128)(2,1)S(1)}, u32[]{:S(2)}, u32[]{:S(2)}) collective-permute-start(bf16[4,4,5120]{2,1,0:T(4,128)(2,1)S(1)} %get-tuple-element.45), channel_id=1, source_target_pairs={{0,6},{1,7},{2,4},{3,5},{4,2},{5,3},{6,0},{7,1},{8,14},{9,15},{10,... | collective-permute-start | bytes 491528 | tf_op jit(solution)/shard_map/ppermute | solution.py:26
  113.3 8.9 %collective-permute-start.45 = (bf16[4,4,5120]{2,1,0:T(4,128)(2,1)S(1)}, bf16[4,4,5120]{2,1,0:T(4,128)(2,1)S(1)}, u32[]{:S(2)}, u32[]{:S(2)}) collective-permute-start(bf16[4,4,5120]{2,1,0:T(4,128)(2,1)S(1)} %get-tuple-element.46), channel_id=1, source_target_pairs={{0,4},{1,5},{2,6},{3,7},{4,0},{5,1},{6,2},{7,3},{8,12},{9,13},{10,... | collective-permute-start | bytes 491528 | tf_op jit(solution)/shard_map/ppermute | solution.py:26
  114.3 7.9 %collective-permute-start.44 = (bf16[4,4,5120]{2,1,0:T(4,128)(2,1)S(1)}, bf16[4,4,5120]{2,1,0:T(4,128)(2,1)S(1)}, u32[]{:S(2)}, u32[]{:S(2)}) collective-permute-start(bf16[4,4,5120]{2,1,0:T(4,128)(2,1)S(1)} %get-tuple-element.44), channel_id=1, source_target_pairs={{0,2},{1,3},{2,0},{3,1},{4,6},{5,7},{6,4},{7,5},{8,10},{9,11},{10,... | collective-permute-start | bytes 491528 | tf_op jit(solution)/shard_map/ppermute | solution.py:26
  122.5 6.0 %collective-permute-start.49 = (bf16[4,5120]{1,0:T(4,128)(2,1)S(1)}, bf16[4,5120]{1,0:T(4,128)(2,1)S(1)}, u32[]{:S(2)}, u32[]{:S(2)}) collective-permute-start(bf16[4,5120]{1,0:T(4,128)(2,1)S(1)} %get-tuple-element.74), channel_id=1, source_target_pairs={{0,24},{8,16},{16,8},{24,0},{1,25},{9,17},{17,9},{25,1},{2,26},{10... | collective-permute-start | bytes 122888 | tf_op jit(solution)/shard_map/ppermute | solution.py:26
  123.8 5.8 %collective-permute-start.48 = (bf16[4,5120]{1,0:T(4,128)(2,1)S(1)}, bf16[4,5120]{1,0:T(4,128)(2,1)S(1)}, u32[]{:S(2)}, u32[]{:S(2)}) collective-permute-start(bf16[4,5120]{1,0:T(4,128)(2,1)S(1)} %get-tuple-element.75), channel_id=1, source_target_pairs={{0,16},{8,24},{16,0},{24,8},{1,17},{9,25},{17,1},{25,9},{2,18},{10... | collective-permute-start | bytes 122888 | tf_op jit(solution)/shard_map/ppermute | solution.py:26
  124.2 5.4 %collective-permute-start.47 = (bf16[4,5120]{1,0:T(4,128)(2,1)S(1)}, bf16[4,5120]{1,0:T(4,128)(2,1)S(1)}, u32[]{:S(2)}, u32[]{:S(2)}) collective-permute-start(bf16[4,5120]{1,0:T(4,128)(2,1)S(1)} %get-tuple-element.73), channel_id=1, source_target_pairs={{0,8},{8,0},{16,24},{24,16},{1,9},{9,1},{17,25},{25,17},{2,10},{10... | collective-permute-start | bytes 122888 | tf_op jit(solution)/shard_map/ppermute | solution.py:26
  (1 other events, 0.6 us)

commit v3 on v2

v3 whole, which is shorter than its diff:
```python
import functools

import jax
import jax.numpy as jnp
import numpy as np
from jax import lax
from jax.experimental import pallas as pl
from jax.experimental.pallas import tpu as pltpu
from jax.sharding import PartitionSpec as P

HEADS = 64
LAT = 512
TOPK = 6
BLOCK = 64
SUFFIX = 128
KDIM = 576


NEG_FILL = -1e30
SCORE_SCALE = 192.0 ** (-0.5)
NORM_EPS = 1e-06
LANES = 128
PAIR = 2 * KDIM
WIDE = KDIM + 64


def swap(value, axis, mask):
    size = lax.axis_size(axis)
    return lax.ppermute(value, axis, [(i, i ^ mask) for i in range(size)])


def dot(a, b, dims):
    return lax.dot_general(a, b, (dims, ((), ())), preferred_element_type=jnp.float32)


def vmem_call(kernel, out_shape, operands, flops, scalars=0, scratch=(), away=(), grant=16):
    specs = [pl.BlockSpec(memory_space=pltpu.SMEM)] * scalars
    specs += [pl.BlockSpec(memory_space=pltpu.VMEM)] * (len(operands) - scalars)
    specs += [pl.BlockSpec(memory_space=pl.ANY)] * len(away)
    size = sum(o.size * o.dtype.itemsize for o in operands)
    return pl.pallas_call(
        kernel,
        out_shape=out_shape,
        in_specs=specs,
        out_specs=jax.tree.map(lambda _: pl.BlockSpec(memory_space=pltpu.VMEM), out_shape),
        scratch_shapes=list(scratch),
        cost_estimate=pl.CostEstimate(flops=flops, bytes_accessed=size, transcendentals=0),
        compiler_params=pltpu.CompilerParams(vmem_limit_bytes=grant * 1024 * 1024),
    )(*operands, *away)


def suffix_kernel(pos, query_ref, keys_ref, count_hbm, mine_ref, other_ref, rows, count, sem):
    copy = pltpu.make_async_copy(count_hbm, count, sem)
    copy.start()
    place = pos[0]
    requests, heads, _ = query_ref.shape
    chips, group_rows, width = mine_ref.shape
    group = group_rows // requests
    members = heads // group
    all_scores = [
        dot(query_ref[r], keys_ref[r], ((1,), (1,))) * SCORE_SCALE for r in range(requests)
    ]
    copy.wait()
    for r in range(requests):
        scores = all_scores[r]
        live = lax.broadcasted_iota(jnp.int32, scores.shape, 1) < count[r]
        scores = jnp.where(live, scores, NEG_FILL)
        top = jnp.max(scores, axis=-1, keepdims=True).astype(jnp.bfloat16).astype(jnp.float32)
        weights = jnp.where(live, jnp.exp(scores - top), 0.0)
        total = jnp.sum(weights, axis=-1, keepdims=True)
        high = total.astype(jnp.bfloat16).astype(jnp.float32)
        numerator = dot(weights.astype(jnp.bfloat16), keys_ref[r, :, :LAT], ((1,), (0,)))
        lane = lax.broadcasted_iota(jnp.int32, (heads, LANES), 1)
        stats = jnp.where(lane == 0, top, jnp.where(lane == 1, high, total - high))
        full = jnp.concatenate([numerator, stats], axis=1)
        for g in range(members):
            rows[r, g] = full[g * group : (g + 1) * group]
    for j in range(members):
        taken = [rows[r, place ^ j] for r in range(requests)]
        out_ref = other_ref if j % 2 else mine_ref
        out_ref[j // 2] = jnp.concatenate(taken, axis=0).astype(jnp.bfloat16)


def join_kernel(mine_ref, other_ref, piece_ref, *outs):
    width = mine_ref.shape[2]
    blocks = piece_ref.shape[0]
    for k, out_ref in enumerate(outs):
        both = [mine_ref[k].astype(jnp.float32), other_ref[k].astype(jnp.float32)]
        out_ref[:, :width] = jnp.concatenate(both, axis=0).astype(jnp.bfloat16)
        for i in range(piece_ref.shape[1] // PAIR):
            out_ref[i * blocks : (i + 1) * blocks, width:] = piece_ref[:, i * PAIR : (i + 1) * PAIR]


def lane_pairs(refs, row):
    return [(ref, row, at) for ref in refs for at in range(0, ref.shape[1], PAIR)]


def stacked_pairs(refs, blocks):
    lane = refs[0].shape[1] - PAIR
    return [(ref, row, lane) for ref in refs for row in range(0, ref.shape[0], blocks)]


def pair_keys(pairs, blocks, spot):
    lane = lax.broadcasted_iota(jnp.int32, (blocks, LANES), 1)
    block = lax.broadcasted_iota(jnp.int32, (blocks, LANES), 0)
    first = (lane < 64).astype(jnp.float32).astype(jnp.bfloat16)
    last = (lane >= 64).astype(jnp.float32).astype(jnp.bfloat16)
    hot_even = (lane == 64 + spot + block).astype(jnp.float32).astype(jnp.bfloat16)
    hot_odd = (lane == spot + block).astype(jnp.float32).astype(jnp.bfloat16)
    even, odd = [], []
    for ref, row, at in pairs:
        keys = ref[row : row + blocks, at : at + PAIR]
        middle = keys[:, LAT : LAT + LANES]
        even.append(jnp.concatenate([keys[:, :LAT], middle * first + hot_even], axis=1))
        odd.append(jnp.concatenate([middle * last + hot_odd, keys[:, LAT + LANES :]], axis=1))
    return jnp.concatenate(even, axis=0), jnp.concatenate(odd, axis=0)


def advance(query_even, query_odd, even, odd, state):
    score_even = dot(query_even, even, ((1,), (1,))) * SCORE_SCALE
    score_odd = dot(query_odd, odd, ((1,), (1,))) * SCORE_SCALE
    top = jnp.maximum(
        jnp.max(score_even, axis=-1, keepdims=True), jnp.max(score_odd, axis=-1, keepdims=True)
    )
    if state is not None:
        top = jnp.maximum(top, state[0])
    weight_even = jnp.exp(score_even - top)
    weight_odd = jnp.exp(score_odd - top)
    total = jnp.sum(weight_even, axis=-1, keepdims=True)
    total = total + jnp.sum(weight_odd, axis=-1, keepdims=True)
    sum_even = dot(weight_even.astype(jnp.bfloat16), even[:, :LAT], ((1,), (0,)))
    sum_odd = dot(weight_odd.astype(jnp.bfloat16), odd, ((1,), (0,)))
    if state is not None:
        keep = jnp.exp(state[0] - top)
        total = total + state[1] * keep
        sum_even = sum_even + state[2] * keep
        sum_odd = sum_odd + state[3] * keep
    return top, total, sum_even, sum_odd


def put_state(state, refs):
    top_ref, total_ref, even_ref, odd_ref = refs
    top_ref[...] = jnp.broadcast_to(state[0], top_ref.shape)
    total_ref[...] = jnp.broadcast_to(state[1], total_ref.shape)
    even_ref[...] = state[2]
    odd_ref[...] = state[3]


def get_state(refs):
    return (refs[0][:, :1], refs[1][:, :1], refs[2][...], refs[3][...])


def state_shapes(rows):
    f32 = jnp.float32
    return [
        jax.ShapeDtypeStruct((rows, LANES), f32),
        jax.ShapeDtypeStruct((rows, LANES), f32),
        jax.ShapeDtypeStruct((rows, LAT), f32),
        jax.ShapeDtypeStruct((rows, WIDE), f32),
    ]


def first_kernel(variants, group, *refs):
    outs = refs[-4 - 2 * variants :]
    pool_ref, other_ref = refs[:2]
    mine = [ref[0] for ref in refs[2 : -4 - 2 * variants]]
    other = [other_ref[k] for k in range(other_ref.shape[0])]
    both = jnp.concatenate([p.astype(jnp.float32) for p in mine + other], axis=0)
    bias = both[:, group * KDIM :]
    rows = both.shape[0]
    lane = lax.broadcasted_iota(jnp.int32, (rows, LANES), 1)
    for v in range(variants):
        low = bias if v == 0 else pltpu.roll(bias, LANES - 64, 1)
        high = pltpu.roll(low, 64, 1)
        for h in range(group):
            at = h // 2 * PAIR
            if h % 2 == 0:
                wide = both[:, at : at + WIDE]
                last = jnp.where(lane < 64, wide[:, LAT:], high)
                even = jnp.concatenate([wide[:, :LAT], last], axis=1)
                odd = pltpu.roll(even, 64, 1)
            else:
                wide = both[:, at + LAT : at + PAIR]
                start = jnp.where(lane < 64, low, wide[:, :LANES])
                odd = jnp.concatenate([start, wide[:, LANES:]], axis=1)
                even = pltpu.roll(odd, WIDE - 64, 1)
            outs[2 * v][h * rows : (h + 1) * rows, :] = even.astype(jnp.bfloat16)
            outs[2 * v + 1][h * rows : (h + 1) * rows, :] = odd.astype(jnp.bfloat16)
    even, odd = pair_keys(lane_pairs([pool_ref], 0), pool_ref.shape[0], 0)
    put_state(advance(outs[0][...], outs[1][...], even, odd, None), outs[2 * variants :])


def walk(queries, sources, blocks, state):
    for q, pairs in sources:
        variant, spot = divmod(q * blocks, 64)
        even, odd = pair_keys(pairs, blocks, spot)
        query_even, query_odd = queries[2 * variant : 2 * variant + 2]
        state = advance(query_even[...], query_odd[...], even, odd, state)
    return state


def middle_kernel(variants, sources, blocks, *refs):
    queries, refs = refs[: 2 * variants], refs[2 * variants :]
    state, chunks, outs = refs[:4], refs[4:-4], refs[-4:]
    sources = [(q, lane_pairs(chunks, i * blocks)) for i, q in enumerate(sources)]
    put_state(walk(queries, sources, blocks, get_state(state)), outs)


def last_kernel(variants, chips, source, blocks, *refs):
    queries, refs = refs[: 2 * variants], refs[2 * variants :]
    state, refs = refs[:4], refs[4:]
    order_ref, value_ref, proj_ref = refs[:3]
    chunks, (keep_ref, away_ref) = refs[3:-2], refs[-2:]
    own = jnp.concatenate([ref[:, : LAT + LANES] for ref in chunks[:chips]], axis=0)
    own = dot(order_ref[...], own, ((1,), (0,)))
    sources = [(source, stacked_pairs(chunks, blocks))]
    top, total, even, odd = walk(queries, sources, blocks, get_state(state))
    stats = own[:, LAT:]
    own_top = stats[:, 0:1]
    new_top = jnp.maximum(top, own_top)
    keep = jnp.exp(top - new_top)
    own_keep = jnp.exp(own_top - new_top)
    total = total * keep + (stats[:, 1:2] + stats[:, 2:3]) * own_keep
    numerator = (even + odd[:, 64 : 64 + LAT]) * keep
    numerator = numerator + own[:, :LAT] * own_keep
    context = (numerator / total).astype(jnp.bfloat16)
    heads = value_ref.shape[0]
    rows = context.shape[0] // heads
    values = [
        dot(context[h * rows : (h + 1) * rows], value_ref[h], ((1,), (0,))).astype(jnp.bfloat16)
        for h in range(heads)
    ]
    values = jnp.concatenate(values, axis=1)
    step = 1024
    half = rows // 2
    for at in range(0, proj_ref.shape[1], step):
        part = dot(values, proj_ref[:, at : at + step], ((1,), (0,)))
        keep_ref[:, at : at + step] = part[:half]
        away_ref[:, at : at + step] = part[half:].astype(jnp.bfloat16)


def expert_kernel(pos, *refs):
    blocks, (gate_ref, up_ref, down_ref, keep_ref, away_ref) = refs[:-5], refs[-5:]
    width = down_ref.shape[2]
    rows = jnp.concatenate([b[:, :width] for b in blocks], axis=0)
    gates = jnp.concatenate([b[:, width:] for b in blocks], axis=0).astype(jnp.float32)
    lane = lax.broadcasted_iota(jnp.int32, gates.shape, 1)
    gate = jnp.sum(jnp.where(lane == pos[0], gates, 0.0), axis=1, keepdims=True)
    gate_part = dot(rows, gate_ref[0], ((1,), (0,)))
    up_part = dot(rows, up_ref[0], ((1,), (0,)))
    hidden = (gate_part / (1.0 + jnp.exp(-gate_part)) * up_part).astype(jnp.bfloat16)
    half = rows.shape[0] // 2
    step = 1024
    for at in range(0, width, step):
        part = dot(hidden, down_ref[0, :, at : at + step], ((1,), (0,))) * gate
        keep_ref[:, at : at + step] = part[:half].astype(keep_ref.dtype)
        away_ref[:, at : at + step] = part[half:].astype(jnp.bfloat16)


def halve_kernel(keep_ref, away_ref, *outs):
    rows = outs[0].shape[0]
    for k, out_ref in enumerate(outs):
        at = pl.ds(k * rows, rows)
        total = keep_ref[at, :].astype(jnp.float32) + away_ref[at, :].astype(jnp.float32)
        out_ref[...] = total.astype(out_ref.dtype)


def norm_kernel(hidden_ref, gain_ref, ids_ref, weight_ref, own_ref, *refs):
    arrived, (residual_ref, row_ref) = refs[:-2], refs[-2:]
    width = hidden_ref.shape[1]
    total = own_ref[...]
    for ref in arrived:
        total = total + ref[...].astype(jnp.float32)
    total = hidden_ref[...].astype(jnp.float32) + total
    residual_ref[...] = total
    scale = lax.rsqrt(jnp.mean(total * total, axis=-1, keepdims=True) + NORM_EPS)
    row_ref[:, :width] = (total * scale * gain_ref[...].astype(jnp.float32)).astype(jnp.bfloat16)
    lane = lax.broadcasted_iota(jnp.int32, (total.shape[0], LANES), 1)
    ids, weights = ids_ref[...], weight_ref[...].astype(jnp.float32)
    gates = jnp.zeros(lane.shape, jnp.float32)
    for j in range(TOPK):
        gates = gates + jnp.where(lane == ids[:, j : j + 1], weights[:, j : j + 1], 0.0)
    row_ref[:, width:] = gates.astype(jnp.bfloat16)


def stack_kernel(*refs):
    rows = jnp.concatenate([ref[...].astype(jnp.float32) for ref in refs[:-1]], axis=0)
    refs[-1][...] = rows.astype(jnp.bfloat16)


def halve(keep, away, blocks):
    rows, width = keep.shape[0] // blocks, keep.shape[1]
    shapes = [jax.ShapeDtypeStruct((rows, width), jnp.float32)]
    shapes += [jax.ShapeDtypeStruct((rows, width), jnp.bfloat16)] * (blocks - 1)
    return vmem_call(halve_kernel, shapes, [keep, swap(away, "expert", 1)], keep.size)


def spread(rows, members, holders):
    by_z = [rows] + [swap(rows, "dp", q) for q in range(1, holders)]
    shape = jax.ShapeDtypeStruct((holders * rows.shape[0], rows.shape[1]), rows.dtype)
    by_z = vmem_call(stack_kernel, shape, by_z, rows.size)
    blocks = [by_z] + [swap(by_z, "expert", 2 * k) for k in range(1, members // 2)]
    return blocks + [swap(block, "expert", 1) for block in blocks]


def gather_sums(keep, away, members, holders):
    chips = members // 2
    rows, width = keep.shape[0] // chips, keep.shape[1]
    total, *sent = halve(keep, away, chips)
    for k in range(1, chips):
        total = total + swap(sent[k - 1], "expert", 2 * k).astype(jnp.float32)
    total = total.reshape(holders, rows // holders, width)
    sent = total.astype(jnp.bfloat16)
    result = total[0]
    for q in range(1, holders):
        result = result + swap(sent[q], "dp", q).astype(jnp.float32)
    return result


def arrival_order(chips, requests, heads):
    source = np.arange(chips * 2 * requests * heads).reshape(chips, 2, requests, heads)
    source = source.transpose(3, 1, 0, 2).reshape(-1)
    order = np.zeros((source.size, source.size), np.float32)
    order[np.arange(source.size), source] = 1.0
    return jnp.asarray(order, jnp.bfloat16)


def per_device(
    hidden_in,
    query,
    prefix_pool,
    suffix_cache,
    block_list,
    prefix_count,
    suffix_count,
    value_up,
    out_proj,
    norm_gain,
    expert_ids,
    gate_weights,
    gate_proj,
    up_proj,
    down_proj,
):
    bf16 = jnp.bfloat16
    row_count, width = hidden_in.shape
    members = lax.axis_size("expert")
    holders = lax.axis_size("dp")
    chips = members // 2
    place = lax.axis_index("expert")
    shard = lax.axis_index("dp")
    shard_blocks = prefix_pool.shape[0]
    total_blocks = shard_blocks * holders

    piece_width = prefix_pool.shape[1] // members
    piece = lax.dynamic_slice_in_dim(prefix_pool, place * piece_width, piece_width, 1)
    arrived = [None] * holders
    for q in sorted(range(1, holders), key=lambda q: (bin(q).count("1"), q)):
        low = q & -q
        arrived[q] = swap(piece if q == low else arrived[q ^ low], "dp", low)

    group_heads = HEADS // members
    variants = -(-total_blocks // 64)
    in_prefix = jnp.arange(block_list.shape[1], dtype=jnp.int32)[None, :] < prefix_count[:, None]
    slots = jnp.arange(LANES, dtype=jnp.int32)
    ids = (shard ^ (slots // shard_blocks)) * shard_blocks + slots % shard_blocks
    member = jnp.any((block_list[:, :, None] == ids) & in_prefix[:, :, None], axis=1)
    bias = jnp.where(member, 0.0, NEG_FILL).astype(bf16)
    group_width = group_heads * KDIM
    asked = []
    for k in range(chips):
        pair = [
            lax.dynamic_slice_in_dim(query, (place ^ j) * group_width, group_width, 1)
            for j in (2 * k, 2 * k + 1)
        ]
        asked.append(jnp.stack([jnp.concatenate([part, bias], axis=1) for part in pair]))
    asked = [asked[0]] + [swap(asked[k], "expert", 2 * k) for k in range(1, chips)]

    early = jnp.concatenate(arrived[1:-1])
    chunks = [early] + [swap(early, "expert", 2 * k) for k in range(1, chips)]

    pos = jnp.stack([place, shard])
    partial = jax.ShapeDtypeStruct((chips, row_count * group_heads, LAT + LANES), bf16)
    mine, other = vmem_call(
        suffix_kernel,
        [partial, partial],
        [
            pos,
            query.reshape(row_count, HEADS, KDIM),
            suffix_cache.reshape(row_count, SUFFIX, KDIM),
        ],
        4 * row_count * HEADS * SUFFIX * KDIM,
        scalars=1,
        scratch=[
            pltpu.VMEM((row_count, members, group_heads, partial.shape[2]), jnp.float32),
            pltpu.SMEM(suffix_count.shape, jnp.int32),
            pltpu.SemaphoreType.DMA,
        ],
        away=[suffix_count],
    )
    other = swap(other, "expert", 1)
    joined = jax.ShapeDtypeStruct((2 * partial.shape[1], partial.shape[2] + PAIR), bf16)
    late = list(vmem_call(join_kernel, [joined] * chips, [mine, other, arrived[-1]], mine.size))
    late[-1], chunks[1] = lax.optimization_barrier((late[-1], chunks[1]))
    late = [late[0]] + [swap(late[k], "expert", 2 * k) for k in range(1, chips)]

    rows = members * row_count * group_heads
    wide = jax.ShapeDtypeStruct((rows, WIDE), bf16)
    *queries, top, total, even, odd = vmem_call(
        functools.partial(first_kernel, variants, group_heads),
        [wide] * (2 * variants) + state_shapes(rows),
        [prefix_pool, swap(jnp.stack([part[1] for part in asked]), "expert", 1)] + asked,
        40 * rows * prefix_pool.size,
    )
    chunks += [swap(block, "expert", 1) for block in chunks]
    state = vmem_call(
        functools.partial(middle_kernel, variants, list(range(1, holders - 1)), shard_blocks),
        state_shapes(rows),
        queries + [top, total, even, odd] + chunks,
        40 * rows * prefix_pool.size,
    )
    late += [swap(block, "expert", 1) for block in late]
    half = members * row_count // 2
    keep, away = vmem_call(
        functools.partial(last_kernel, variants, chips, holders - 1, shard_blocks),
        [
            jax.ShapeDtypeStruct((half, width), jnp.float32),
            jax.ShapeDtypeStruct((half, width), bf16),
        ],
        queries
        + list(state)
        + [arrival_order(chips, row_count, group_heads), value_up, out_proj]
        + late,
        4 * rows * prefix_pool.size + 4 * half * out_proj.size,
    )
    own, *sent = halve(keep, away, chips)
    sums = [swap(sent[k - 1], "expert", 2 * k) for k in range(1, chips)]
    residual_out, token_rows = vmem_call(
        norm_kernel,
        [
            jax.ShapeDtypeStruct((row_count, width), jnp.float32),
            jax.ShapeDtypeStruct((row_count, width + LANES), bf16),
        ],
        [hidden_in, norm_gain.reshape(1, width), expert_ids, gate_weights, own] + sums,
        10 * hidden_in.size,
    )

    blocks = spread(token_rows, members, holders)
    half = blocks[0].shape[0] * chips
    keep, away = vmem_call(
        expert_kernel,
        [
            jax.ShapeDtypeStruct((half, width), jnp.float32),
            jax.ShapeDtypeStruct((half, width), bf16),
        ],
        [pos] + blocks + [gate_proj, up_proj, down_proj],
        12 * half * gate_proj.size,
        scalars=1,
    )
    moe_sum = gather_sums(keep, away, members, holders)
    return (residual_out, moe_sum)


def solution(mesh):
    in_specs = (
        P(("dp", "expert"), None),
        P(("dp", "expert"), None),
        P("dp", None),
        P(("dp", "expert"), None),
        P(("dp", "expert"), None),
        P(("dp", "expert")),
        P(("dp", "expert")),
        P("expert", None, None),
        P("expert", None),
        P(),
        P(("dp", "expert"), None),
        P(("dp", "expert"), None),
        P("expert", None, "dp"),
        P("expert", None, "dp"),
        P("expert", "dp", None),
    )
    out_specs = (P(("dp", "expert"), None), P(("dp", "expert"), None))
    return jax.shard_map(
        per_device, mesh=mesh, in_specs=in_specs, out_specs=out_specs, check_vma=False
    )
```

time: 131 us -> 109 us (0.83)
  matrix products: 14.1 us -> 0 us
  starting transfers between devices: 52.1 us -> 39.8 us
  waiting for transfers between devices: 32.4 us -> 44.7 us
  other arithmetic: 10.7 us -> 2.84 us
  Pallas kernels: 7.75 us -> 13 us
  local copies, waits for them, and re-layouts: 11.9 us -> 6.9 us
    dot_general x3 -> x0, matrix products: 14.1 us -> none  [the longest x1 6.06 us: per_device(): partial = jnp.dot(value_rows, out_proj, preferred_element_type=jnp.float32)]
    ppermute x50 -> x43, waiting for transfers between devices: 32.4 us -> 44.7 us  [swap(): return lax.ppermute(value, axis, [(i, i ^ mask) for i in range(size)])]
    ppermute x50 -> x43, starting transfers between devices: 52.1 us -> 39.8 us  [swap(): return lax.ppermute(value, axis, [(i, i ^ mask) for i in range(size)])]
    pallas_call x6 -> x10, Pallas kernels: 7.75 us -> 13 us  [vmem_call(): pl.pallas_call(kernel, out_shape=out_shape, in_specs=specs, out_specs=jax...]
    another operation x13 -> x7, other arithmetic: 4.18 us -> 0.57 us  [the longest x5 0.36 us: per_device(): jnp.stack([jnp.concatenate([part, bias], axis=1) for part in pair])]
    squeeze x4 -> x0, local copies, waits for them, and re-layouts: 2.62 us -> none  [the longest x1 2.36 us: gather_sums(): partial[1]]
    convert_element_type x4 -> x0, other arithmetic: 1.77 us -> none  [the longest x1 1.56 us: gather_sums(): sent = held.astype(jnp.bfloat16)]
    reshape x7 -> x3, local copies, waits for them, and re-layouts: 3.75 us -> 3.05 us  [the longest x1 1.73 us: per_device(): suffix_cache.reshape(row_count, SUFFIX, KDIM)]
  transfers between devices with their start and end apart: 50 -> 43, of which waited for: 20 -> 23; matrix products, arithmetic and copies ran while one was open for 9% -> 6% of each run, Pallas kernels for 4% -> 5%
where the time goes in v3:
time: 109 us; the launch traced here: 108 us
  waiting for transfers between devices  44.7 us (41%)
  starting transfers between devices  39.8 us (37%)
  Pallas kernels  13 us (12%)
  local copies, waits for them, and re-layouts  6.9 us (6%)
  other arithmetic  2.84 us (3%)
    ppermute x43, waiting for transfers between devices, swap(): return lax.ppermute(value, axis, [(i, i ^ mask) for i in range(size)])  44.7 us
    ppermute x43, starting transfers between devices, swap(): return lax.ppermute(value, axis, [(i, i ^ mask) for i in range(size)])  39.8 us
    pallas_call x10, Pallas kernels, vmem_call(): pl.pallas_call(kernel, out_shape=out_shape, in_specs=specs, out_specs=jax...  13 us
  transfers between devices with their start and end apart: 43, of which 23 were waited for; matrix products, arithmetic and copies ran while one was open for 6% of the time, Pallas kernels for 5%

profile of v3, /device:TPU:0, one launch (start us, length us, event | category | flops | bytes accessed | tf_op | source)
XLA Modules:
  0.0 108.3 jit_solution(14706972671688811487)
XLA Ops:
  0.7 1.0 constant_dynamic-slice_fusion
  1.7 4.1 %collective-permute-start.5 = (bf16[16,4608]{1,0:T(8,128)(2,1)S(1)}, bf16[16,4608]{1,0:T(8,128)(2,1)S(1)}, u32[]{:S(2)}, u32[]{:S(2)}) collective-permute-start(bf16[16,4608]{1,0:T(8,128)(2,1)S(1)} %constant_dynamic-slice_fusion), channel_id=1, source_target_pairs={{0,16},{8,24},{16,0},{24,8},{1,17},{9,25},{17,1},{25,9},{2,18},{10... | collective-permute-start | bytes 442376 | tf_op jit(solution)/shard_map/ppermute | solution.py:29
  5.8 1.6 %collective-permute-start.4 = (bf16[16,4608]{1,0:T(8,128)(2,1)S(1)}, bf16[16,4608]{1,0:T(8,128)(2,1)S(1)}, u32[]{:S(2)}, u32[]{:S(2)}) collective-permute-start(bf16[16,4608]{1,0:T(8,128)(2,1)S(1)} %constant_dynamic-slice_fusion), channel_id=1, source_target_pairs={{0,8},{8,0},{16,24},{24,16},{1,9},{9,1},{17,25},{25,17},{2,10},{10... | collective-permute-start | bytes 442376 | tf_op jit(solution)/shard_map/ppermute | solution.py:29
  7.4 0.7 iota_compare_fusion
  8.1 0.8 and_reduce_fusion
  8.9 1.0 constant_dynamic-slice_fusion.1
  10.1 1.6 %collective-permute-start = (bf16[2,4,4736]{2,1,0:T(4,128)(2,1)S(1)}, bf16[2,4,4736]{2,1,0:T(4,128)(2,1)S(1)}, u32[]{:S(2)}, u32[]{:S(2)}) collective-permute-start(bf16[2,4,4736]{2,1,0:T(4,128)(2,1)S(1)} %pad_maximum_fusion.9), channel_id=1, source_target_pairs={{0,2},{1,3},{2,0},{3,1},{4,6},{5,7},{6,4},{7,5},{8,10},{9,11},{10,... | collective-permute-start | bytes 227336 | tf_op jit(solution)/shard_map/ppermute | solution.py:29
  11.8 1.6 %collective-permute-start.1 = (bf16[2,4,4736]{2,1,0:T(4,128)(2,1)S(1)}, bf16[2,4,4736]{2,1,0:T(4,128)(2,1)S(1)}, u32[]{:S(2)}, u32[]{:S(2)}) collective-permute-start(bf16[2,4,4736]{2,1,0:T(4,128)(2,1)S(1)} %pad_maximum_fusion.10), channel_id=1, source_target_pairs={{0,4},{1,5},{2,6},{3,7},{4,0},{5,1},{6,2},{7,3},{8,12},{9,13},{10,... | collective-permute-start | bytes 227336 | tf_op jit(solution)/shard_map/ppermute | solution.py:29
  13.4 0.5 collective-permute-start.2
  13.9 1.3 %reshape.69.query_ref = bf16[4,64,576]{2,1,0:T(8,128)(2,1)S(1)} reshape(bf16[4,36864]{1,0:T(4,128)(2,1)} %param.17) | data formatting | bytes 589824 | tf_op jit(solution)/shard_map/reshape | solution.py:389
  15.3 1.7 %reshape.70.keys_ref = bf16[4,128,576]{2,1,0:T(8,128)(2,1)S(1)} reshape(bf16[4,73728]{1,0:T(4,128)(2,1)} %param.19) | data formatting | bytes 1179648 | tf_op jit(solution)/shard_map/reshape | solution.py:390
  17.1 1.4 %shard_map.168 = (bf16[4,32,640]{2,1,0:T(8,128)(2,1)S(1)}, bf16[4,32,640]{2,1,0:T(8,128)(2,1)S(1)}) custom-call(s32[2]{0:T(128)S(1)} %pad_add_fusion.pos, bf16[4,64,576]{2,1,0:T(8,128)(2,1)S(1)} %reshape.69.query_ref, bf16[4,128,576]{2,1,0:T(8,128)(2,1)S(1)} %reshape.70.keys_ref, s32[4]{0:T(128)S(1)} %copy-done.9), custom_call_target="tpu_custom_call" | custom-call | flops 75497472 | bytes 884744 | tf_op jit(solution)/shard_map/pallas_call | solution.py:41
  18.8 1.5 %collective-permute-start.8 = (bf16[32,4608]{1,0:T(8,128)(2,1)S(1)}, bf16[32,4608]{1,0:T(8,128)(2,1)S(1)}, u32[]{:S(2)}, u32[]{:S(2)}) collective-permute-start(bf16[32,4608]{1,0:T(8,128)(2,1)S(1)} %constant_dynamic-update-slice_fusion.refs_6_), channel_id=1, source_target_pairs={{0,2},{1,3},{2,0},{3,1},{4,6},{5,7},{6,4},{7,5},{8,10},{9,11},{10,... | collective-permute-start | bytes 884744 | tf_op jit(solution)/shard_map/ppermute | solution.py:29
  20.3 0.4 collective-permute-start.7
  21.0 1.6 %collective-permute-start.9 = (bf16[32,4608]{1,0:T(8,128)(2,1)S(1)}, bf16[32,4608]{1,0:T(8,128)(2,1)S(1)}, u32[]{:S(2)}, u32[]{:S(2)}) collective-permute-start(bf16[32,4608]{1,0:T(8,128)(2,1)S(1)} %constant_dynamic-update-slice_fusion.refs_6_), channel_id=1, source_target_pairs={{0,4},{1,5},{2,6},{3,7},{4,0},{5,1},{6,2},{7,3},{8,12},{9,13},{10,... | collective-permute-start | bytes 884744 | tf_op jit(solution)/shard_map/ppermute | solution.py:29
  22.6 0.5 collective-permute-start.10
  23.1 3.2 %collective-permute-done.7.piece_ref = bf16[16,4608]{1,0:T(8,128)(2,1)S(1)} collective-permute-done((bf16[16,4608]{1,0:T(8,128)(2,1)S(1)}, bf16[16,4608]{1,0:T(8,128)(2,1)S(1)}, u32[]{:S(2)}, u32[]{:S(2)}) %collective-permute-start.7) | collective-permute-done | bytes 147488 | tf_op jit(solution)/shard_map/ppermute | solution.py:29
  26.4 2.3 %collective-permute-done.8.refs_7_ = bf16[32,4608]{1,0:T(8,128)(2,1)S(1)} collective-permute-done((bf16[32,4608]{1,0:T(8,128)(2,1)S(1)}, bf16[32,4608]{1,0:T(8,128)(2,1)S(1)}, u32[]{:S(2)}, u32[]{:S(2)}) %collective-permute-start.8) | collective-permute-done | bytes 294944 | tf_op jit(solution)/shard_map/ppermute | solution.py:29
  28.7 1.4 %collective-permute-start.15 = (bf16[64,1792]{1,0:T(8,128)(2,1)S(1)}, bf16[64,1792]{1,0:T(8,128)(2,1)S(1)}, u32[]{:S(2)}, u32[]{:S(2)}) collective-permute-start(bf16[64,1792]{1,0:T(8,128)(2,1)S(1)} %get-tuple-element.49), channel_id=1, source_target_pairs={{0,2},{1,3},{2,0},{3,1},{4,6},{5,7},{6,4},{7,5},{8,10},{9,11},{10,... | collective-permute-start | bytes 688136 | tf_op jit(solution)/shard_map/ppermute | solution.py:29
  30.2 1.6 %collective-permute-start.16 = (bf16[64,1792]{1,0:T(8,128)(2,1)S(1)}, bf16[64,1792]{1,0:T(8,128)(2,1)S(1)}, u32[]{:S(2)}, u32[]{:S(2)}) collective-permute-start(bf16[64,1792]{1,0:T(8,128)(2,1)S(1)} %get-tuple-element.50), channel_id=1, source_target_pairs={{0,4},{1,5},{2,6},{3,7},{4,0},{5,1},{6,2},{7,3},{8,12},{9,13},{10,... | collective-permute-start | bytes 688136 | tf_op jit(solution)/shard_map/ppermute | solution.py:29
  31.8 5.4 %collective-permute-done.9.refs_8_ = bf16[32,4608]{1,0:T(8,128)(2,1)S(1)} collective-permute-done((bf16[32,4608]{1,0:T(8,128)(2,1)S(1)}, bf16[32,4608]{1,0:T(8,128)(2,1)S(1)}, u32[]{:S(2)}, u32[]{:S(2)}) %collective-permute-start.9) | collective-permute-done | bytes 294944 | tf_op jit(solution)/shard_map/ppermute | solution.py:29
  37.2 1.5 %collective-permute-start.17 = (bf16[64,1792]{1,0:T(8,128)(2,1)S(1)}, bf16[64,1792]{1,0:T(8,128)(2,1)S(1)}, u32[]{:S(2)}, u32[]{:S(2)}) collective-permute-start(bf16[64,1792]{1,0:T(8,128)(2,1)S(1)} %get-tuple-element.51), channel_id=1, source_target_pairs={{0,6},{1,7},{2,4},{3,5},{4,2},{5,3},{6,0},{7,1},{8,14},{9,15},{10,... | collective-permute-start | bytes 688136 | tf_op jit(solution)/shard_map/ppermute | solution.py:29
  38.9 0.6 collective-permute-done.15.refs_10_
  39.5 1.3 %shard_map.167 = (bf16[256,640]{1,0:T(8,128)(2,1)S(1)}, bf16[256,640]{1,0:T(8,128)(2,1)S(1)}, f32[256,128]{1,0:T(8,128)S(1)}, f32[256,128]{1,0:T(8,128)S(1)}, f3...) custom-call(bf16[16,36864]{1,0:T(8,128)(2,1)S(1)} %copy-done.6, bf16[4,4,4736]{2,1,0:T(4,128)(2,1)S(1)} %collective-permute-done.3.refs_1_, ...), custom_call_target="tpu_custom_call" | custom-call | flops 6039797760 | bytes 1634304 | tf_op jit(solution)/shard_map/pallas_call | solution.py:41
  40.8 5.8 %collective-permute-done.16.refs_11_ = bf16[64,1792]{1,0:T(8,128)(2,1)S(1)} collective-permute-done((bf16[64,1792]{1,0:T(8,128)(2,1)S(1)}, bf16[64,1792]{1,0:T(8,128)(2,1)S(1)}, u32[]{:S(2)}, u32[]{:S(2)}) %collective-permute-start.16) | collective-permute-done | bytes 229408 | tf_op jit(solution)/shard_map/ppermute | solution.py:29
  46.6 0.5 collective-permute-start.19
  47.1 0.4 collective-permute-start.21
  47.6 2.6 %shard_map.170 = (f32[256,128]{1,0:T(8,128)S(1)}, f32[256,128]{1,0:T(8,128)S(1)}, f32[256,512]{1,0:T(8,128)S(1)}, f32[256,640]{1,0:T(8,128)S(1)}) custom-call(bf16[256,640]{1,0:T(8,128)(2,1)S(1)} %get-tuple-element.34.refs_0_, bf16[256,640]{1,0:T(8,128)(2,1)S(1)} %get-tuple-element.35.refs_1_, f32[256,128]{1,0:T(8,128)S(1)} %get-tuple-element.36.refs_2_, ...), custom_call_target="tpu_custom_call" | custom-call | flops 6039797760 | bytes 4456448 | tf_op jit(solution)/shard_map/pallas_call | solution.py:41
  50.2 0.8 slice-done.1
  51.1 0.6 slice-done.2
  51.9 3.7 %shard_map.171 = (f32[16,5120]{1,0:T(8,128)S(1)}, bf16[16,5120]{1,0:T(8,128)(2,1)S(1)}) custom-call(bf16[256,640]{1,0:T(8,128)(2,1)S(1)} %get-tuple-element.34.refs_0_, bf16[256,640]{1,0:T(8,128)(2,1)S(1)} %get-tuple-element.35.refs_1_, f32[256,128]{1,0:T(8,128)S(1)} %get-tuple-element.44.refs_2_, f32[256,128]{1,0:T(8,128)S(1)} %get-tuple-element.45.refs_3_, ...), custom_call_target="tpu_custom_call" | custom-call | flops 939524096 | bytes 15597568 | tf_op jit(solution)/shard_map/pallas_call | solution.py:41
  55.7 1.3 %collective-permute-done.22.away_ref = bf16[16,5120]{1,0:T(8,128)(2,1)S(1)} collective-permute-done((bf16[16,5120]{1,0:T(8,128)(2,1)S(1)}, bf16[16,5120]{1,0:T(8,128)(2,1)S(1)}, u32[]{:S(2)}, u32[]{:S(2)}) %collective-permute-start.22) | collective-permute-done | bytes 163872 | tf_op jit(solution)/shard_map/ppermute | solution.py:29
  57.1 0.7 collective-permute-start.23
  57.8 1.5 %collective-permute-start.24 = (bf16[4,5120]{1,0:T(4,128)(2,1)S(1)}, bf16[4,5120]{1,0:T(4,128)(2,1)S(1)}, u32[]{:S(2)}, u32[]{:S(2)}) collective-permute-start(bf16[4,5120]{1,0:T(4,128)(2,1)S(1)} %get-tuple-element.56), channel_id=1, source_target_pairs={{0,4},{1,5},{2,6},{3,7},{4,0},{5,1},{6,2},{7,3},{8,12},{9,13},{10,... | collective-permute-start | bytes 122888 | tf_op jit(solution)/shard_map/ppermute | solution.py:29
  59.2 1.4 %collective-permute-start.25 = (bf16[4,5120]{1,0:T(4,128)(2,1)S(1)}, bf16[4,5120]{1,0:T(4,128)(2,1)S(1)}, u32[]{:S(2)}, u32[]{:S(2)}) collective-permute-start(bf16[4,5120]{1,0:T(4,128)(2,1)S(1)} %get-tuple-element.57), channel_id=1, source_target_pairs={{0,6},{1,7},{2,4},{3,5},{4,2},{5,3},{6,0},{7,1},{8,14},{9,15},{10,... | collective-permute-start | bytes 122888 | tf_op jit(solution)/shard_map/ppermute | solution.py:29
  60.7 0.5 collective-permute-done.23.refs_0_
  61.2 0.6 collective-permute-done.24.refs_1_
  61.8 2.4 %collective-permute-done.25.refs_2_ = bf16[4,5120]{1,0:T(4,128)(2,1)S(1)} collective-permute-done((bf16[4,5120]{1,0:T(4,128)(2,1)S(1)}, bf16[4,5120]{1,0:T(4,128)(2,1)S(1)}, u32[]{:S(2)}, u32[]{:S(2)}) %collective-permute-start.25) | collective-permute-done | bytes 40992 | tf_op jit(solution)/shard_map/ppermute | solution.py:29
  64.1 0.7 shard_map.173
  64.8 1.6 %collective-permute-start.26 = (bf16[4,5248]{1,0:T(4,128)(2,1)S(1)}, bf16[4,5248]{1,0:T(4,128)(2,1)S(1)}, u32[]{:S(2)}, u32[]{:S(2)}) collective-permute-start(bf16[4,5248]{1,0:T(4,128)(2,1)S(1)} %get-tuple-element.59.refs_0_), channel_id=1, source_target_pairs={{0,8},{8,0},{16,24},{24,16},{1,9},{9,1},{17,25},{25,17},{2,10},{10... | collective-permute-start | bytes 125960 | tf_op jit(solution)/shard_map/ppermute | solution.py:29
  66.7 2.5 %collective-permute-start.28 = (bf16[4,5248]{1,0:T(4,128)(2,1)S(1)}, bf16[4,5248]{1,0:T(4,128)(2,1)S(1)}, u32[]{:S(2)}, u32[]{:S(2)}) collective-permute-start(bf16[4,5248]{1,0:T(4,128)(2,1)S(1)} %get-tuple-element.59.refs_0_), channel_id=1, source_target_pairs={{0,24},{8,16},{16,8},{24,0},{1,25},{9,17},{17,9},{25,1},{2,26},{10... | collective-permute-start | bytes 125960 | tf_op jit(solution)/shard_map/ppermute | solution.py:29
  69.2 0.4 collective-permute-done.26.refs_1_
  69.6 2.0 %collective-permute-done.27.refs_2_ = bf16[4,5248]{1,0:T(4,128)(2,1)S(1)} collective-permute-done((bf16[4,5248]{1,0:T(4,128)(2,1)S(1)}, bf16[4,5248]{1,0:T(4,128)(2,1)S(1)}, u32[]{:S(2)}, u32[]{:S(2)}) %collective-permute-start.27) | collective-permute-done | bytes 42016 | tf_op jit(solution)/shard_map/ppermute | solution.py:29
  71.6 0.9 collective-permute-done.28.refs_3_
  72.6 1.6 %collective-permute-start.29 = (bf16[16,5248]{1,0:T(8,128)(2,1)S(1)}, bf16[16,5248]{1,0:T(8,128)(2,1)S(1)}, u32[]{:S(2)}, u32[]{:S(2)}) collective-permute-start(bf16[16,5248]{1,0:T(8,128)(2,1)S(1)} %shard_map.174.refs_0_), channel_id=1, source_target_pairs={{0,2},{1,3},{2,0},{3,1},{4,6},{5,7},{6,4},{7,5},{8,10},{9,11},{10,... | collective-permute-start | bytes 503816 | tf_op jit(solution)/shard_map/ppermute | solution.py:29
  74.1 0.5 collective-permute-start.30
  74.7 1.5 %collective-permute-start.31 = (bf16[16,5248]{1,0:T(8,128)(2,1)S(1)}, bf16[16,5248]{1,0:T(8,128)(2,1)S(1)}, u32[]{:S(2)}, u32[]{:S(2)}) collective-permute-start(bf16[16,5248]{1,0:T(8,128)(2,1)S(1)} %shard_map.174.refs_0_), channel_id=1, source_target_pairs={{0,6},{1,7},{2,4},{3,5},{4,2},{5,3},{6,0},{7,1},{8,14},{9,15},{10,... | collective-permute-start | bytes 503816 | tf_op jit(solution)/shard_map/ppermute | solution.py:29
  76.1 1.9 %collective-permute-done.29.refs_1_ = bf16[16,5248]{1,0:T(8,128)(2,1)S(1)} collective-permute-done((bf16[16,5248]{1,0:T(8,128)(2,1)S(1)}, bf16[16,5248]{1,0:T(8,128)(2,1)S(1)}, u32[]{:S(2)}, u32[]{:S(2)}) %collective-permute-start.29) | collective-permute-done | bytes 167968 | tf_op jit(solution)/shard_map/ppermute | solution.py:29
  78.0 3.3 %collective-permute-done.30.refs_2_ = bf16[16,5248]{1,0:T(8,128)(2,1)S(1)} collective-permute-done((bf16[16,5248]{1,0:T(8,128)(2,1)S(1)}, bf16[16,5248]{1,0:T(8,128)(2,1)S(1)}, u32[]{:S(2)}, u32[]{:S(2)}) %collective-permute-start.30) | collective-permute-done | bytes 167968 | tf_op jit(solution)/shard_map/ppermute | solution.py:29
  81.3 0.5 collective-permute-start.35
  81.8 0.9 collective-permute-done.34.refs_6_
  83.0 3.1 %shard_map.175 = (f32[64,5120]{1,0:T(8,128)S(1)}, bf16[64,5120]{1,0:T(8,128)(2,1)S(1)}) custom-call(s32[2]{0:T(128)S(1)} %pad_add_fusion.pos, bf16[16,5248]{1,0:T(8,128)(2,1)S(1)} %shard_map.174.refs_0_, bf16[16,5248]{1,0:T(8,128)(2,1)S(1)} %collective-permute-done.29.refs_1_, bf16[16,5248]{1,0:T(8,128)(2,1)S(1)} %collective-permute-done.30.refs_2_, ...), custom_call_target="tpu_custom_call" | custom-call | flops 1509949440 | bytes 13139976 | tf_op jit(solution)/shard_map/pallas_call | solution.py:41
  86.4 1.8 %collective-permute-done.36.away_ref = bf16[64,5120]{1,0:T(8,128)(2,1)S(1)} collective-permute-done((bf16[64,5120]{1,0:T(8,128)(2,1)S(1)}, bf16[64,5120]{1,0:T(8,128)(2,1)S(1)}, u32[]{:S(2)}, u32[]{:S(2)}) %collective-permute-start.36) | collective-permute-done | bytes 655392 | tf_op jit(solution)/shard_map/ppermute | solution.py:29
  88.3 0.6 collective-permute-start.37
  88.9 0.9 collective-permute-start.38
  89.8 2.1 %collective-permute-start.39 = (bf16[16,5120]{1,0:T(8,128)(2,1)S(1)}, bf16[16,5120]{1,0:T(8,128)(2,1)S(1)}, u32[]{:S(2)}, u32[]{:S(2)}) collective-permute-start(bf16[16,5120]{1,0:T(8,128)(2,1)S(1)} %get-tuple-element.65), channel_id=1, source_target_pairs={{0,6},{1,7},{2,4},{3,5},{4,2},{5,3},{6,0},{7,1},{8,14},{9,15},{10,... | collective-permute-start | bytes 491528 | tf_op jit(solution)/shard_map/ppermute | solution.py:29
  91.9 3.5 %collective-permute-done.37 = bf16[16,5120]{1,0:T(8,128)(2,1)S(1)} collective-permute-done((bf16[16,5120]{1,0:T(8,128)(2,1)S(1)}, bf16[16,5120]{1,0:T(8,128)(2,1)S(1)}, u32[]{:S(2)}, u32[]{:S(2)}) %collective-permute-start.37) | collective-permute-done | bytes 163872 | tf_op jit(solution)/shard_map/ppermute | solution.py:29
  95.4 0.4 collective-permute-done.38
  95.9 2.7 %collective-permute-done.39 = bf16[16,5120]{1,0:T(8,128)(2,1)S(1)} collective-permute-done((bf16[16,5120]{1,0:T(8,128)(2,1)S(1)}, bf16[16,5120]{1,0:T(8,128)(2,1)S(1)}, u32[]{:S(2)}, u32[]{:S(2)}) %collective-permute-start.39) | collective-permute-done | bytes 163872 | tf_op jit(solution)/shard_map/ppermute | solution.py:29
  99.1 2.7 %collective-permute-start.41 = (bf16[4,5120]{1,0:T(4,128)(2,1)S(1)}, bf16[4,5120]{1,0:T(4,128)(2,1)S(1)}, u32[]{:S(2)}, u32[]{:S(2)}) collective-permute-start(bf16[4,5120]{1,0:T(4,128)(2,1)S(1)} %get-tuple-element.78), channel_id=1, source_target_pairs={{0,16},{8,24},{16,0},{24,8},{1,17},{9,25},{17,1},{25,9},{2,18},{10... | collective-permute-start | bytes 122888 | tf_op jit(solution)/shard_map/ppermute | solution.py:29
  101.8 1.3 %collective-permute-start.42 = (bf16[4,5120]{1,0:T(4,128)(2,1)S(1)}, bf16[4,5120]{1,0:T(4,128)(2,1)S(1)}, u32[]{:S(2)}, u32[]{:S(2)}) collective-permute-start(bf16[4,5120]{1,0:T(4,128)(2,1)S(1)} %get-tuple-element.77), channel_id=1, source_target_pairs={{0,24},{8,16},{16,8},{24,0},{1,25},{9,17},{17,9},{25,1},{2,26},{10... | collective-permute-start | bytes 122888 | tf_op jit(solution)/shard_map/ppermute | solution.py:29
  103.2 0.9 collective-permute-done.41
  104.1 3.6 %collective-permute-done.42 = bf16[4,5120]{1,0:T(4,128)(2,1)S(1)} collective-permute-done((bf16[4,5120]{1,0:T(4,128)(2,1)S(1)}, bf16[4,5120]{1,0:T(4,128)(2,1)S(1)}, u32[]{:S(2)}, u32[]{:S(2)}) %collective-permute-start.42) | collective-permute-done | bytes 40992 | tf_op jit(solution)/shard_map/ppermute | solution.py:29
  107.6 0.7 fusion.1
  (85 shorter events, 3.3 us)
Async XLA Ops:
  0.6 38.9 %copy-start.6 = (bf16[16,36864]{1,0:T(8,128)(2,1)S(1)}, bf16[16,36864]{1,0:T(8,128)(2,1)}, u32[]{:S(2)}) copy-start(bf16[16,36864]{1,0:T(8,128)(2,1)} %refs_0_.1) | copy-start | bytes 3538948
  0.6 16.4 %copy-start.9 = (s32[4]{0:T(128)S(1)}, s32[4]{0:T(128)}, u32[]{:S(2)}) copy-start(s32[4]{0:T(128)} %count_hbm.1) | copy-start | bytes 52
  1.7 17.1 %collective-permute-start.5 = (bf16[16,4608]{1,0:T(8,128)(2,1)S(1)}, bf16[16,4608]{1,0:T(8,128)(2,1)S(1)}, u32[]{:S(2)}, u32[]{:S(2)}) collective-permute-start(bf16[16,4608]{1,0:T(8,128)(2,1)S(1)} %constant_dynamic-slice_fusion), channel_id=1, source_target_pairs={{0,16},{8,24},{16,0},{24,8},{1,17},{9,25},{17,1},{25,9},{2,18},{10... | collective-permute-start | bytes 442376 | tf_op jit(solution)/shard_map/ppermute | solution.py:29
  5.8 13.0 %collective-permute-start.4 = (bf16[16,4608]{1,0:T(8,128)(2,1)S(1)}, bf16[16,4608]{1,0:T(8,128)(2,1)S(1)}, u32[]{:S(2)}, u32[]{:S(2)}) collective-permute-start(bf16[16,4608]{1,0:T(8,128)(2,1)S(1)} %constant_dynamic-slice_fusion), channel_id=1, source_target_pairs={{0,8},{8,0},{16,24},{24,16},{1,9},{9,1},{17,25},{25,17},{2,10},{10... | collective-permute-start | bytes 442376 | tf_op jit(solution)/shard_map/ppermute | solution.py:29
  10.1 8.4 %collective-permute-start = (bf16[2,4,4736]{2,1,0:T(4,128)(2,1)S(1)}, bf16[2,4,4736]{2,1,0:T(4,128)(2,1)S(1)}, u32[]{:S(2)}, u32[]{:S(2)}) collective-permute-start(bf16[2,4,4736]{2,1,0:T(4,128)(2,1)S(1)} %pad_maximum_fusion.9), channel_id=1, source_target_pairs={{0,2},{1,3},{2,0},{3,1},{4,6},{5,7},{6,4},{7,5},{8,10},{9,11},{10,... | collective-permute-start | bytes 227336 | tf_op jit(solution)/shard_map/ppermute | solution.py:29
  11.8 6.9 %collective-permute-start.1 = (bf16[2,4,4736]{2,1,0:T(4,128)(2,1)S(1)}, bf16[2,4,4736]{2,1,0:T(4,128)(2,1)S(1)}, u32[]{:S(2)}, u32[]{:S(2)}) collective-permute-start(bf16[2,4,4736]{2,1,0:T(4,128)(2,1)S(1)} %pad_maximum_fusion.10), channel_id=1, source_target_pairs={{0,4},{1,5},{2,6},{3,7},{4,0},{5,1},{6,2},{7,3},{8,12},{9,13},{10,... | collective-permute-start | bytes 227336 | tf_op jit(solution)/shard_map/ppermute | solution.py:29
  13.4 5.3 %collective-permute-start.2 = (bf16[2,4,4736]{2,1,0:T(4,128)(2,1)S(1)}, bf16[2,4,4736]{2,1,0:T(4,128)(2,1)S(1)}, u32[]{:S(2)}, u32[]{:S(2)}) collective-permute-start(bf16[2,4,4736]{2,1,0:T(4,128)(2,1)S(1)} %pad_maximum_fusion.11), channel_id=1, source_target_pairs={{0,6},{1,7},{2,4},{3,5},{4,2},{5,3},{6,0},{7,1},{8,14},{9,15},{10,... | collective-permute-start | bytes 227336 | tf_op jit(solution)/shard_map/ppermute | solution.py:29
  18.5 4.0 %collective-permute-start.6 = (bf16[4,32,640]{2,1,0:T(8,128)(2,1)S(1)}, bf16[4,32,640]{2,1,0:T(8,128)(2,1)S(1)}, u32[]{:S(2)}, u32[]{:S(2)}) collective-permute-start(bf16[4,32,640]{2,1,0:T(8,128)(2,1)S(1)} %get-tuple-element.41), channel_id=1, source_target_pairs={{0,1},{1,0},{2,3},{3,2},{4,5},{5,4},{6,7},{7,6},{8,9},{9,8},{10,11... | collective-permute-start | bytes 491528 | tf_op jit(solution)/shard_map/ppermute | solution.py:29
  18.8 9.9 %collective-permute-start.8 = (bf16[32,4608]{1,0:T(8,128)(2,1)S(1)}, bf16[32,4608]{1,0:T(8,128)(2,1)S(1)}, u32[]{:S(2)}, u32[]{:S(2)}) collective-permute-start(bf16[32,4608]{1,0:T(8,128)(2,1)S(1)} %constant_dynamic-update-slice_fusion.refs_6_), channel_id=1, source_target_pairs={{0,2},{1,3},{2,0},{3,1},{4,6},{5,7},{6,4},{7,5},{8,10},{9,11},{10,... | collective-permute-start | bytes 884744 | tf_op jit(solution)/shard_map/ppermute | solution.py:29
  20.3 6.0 %collective-permute-start.7 = (bf16[16,4608]{1,0:T(8,128)(2,1)S(1)}, bf16[16,4608]{1,0:T(8,128)(2,1)S(1)}, u32[]{:S(2)}, u32[]{:S(2)}) collective-permute-start(bf16[16,4608]{1,0:T(8,128)(2,1)S(1)} %collective-permute-done.5), channel_id=1, source_target_pairs={{0,8},{8,0},{16,24},{24,16},{1,9},{9,1},{17,25},{25,17},{2,10},{10... | collective-permute-start | bytes 442376 | tf_op jit(solution)/shard_map/ppermute | solution.py:29
  20.9 9.3 %collective-permute-start.3 = (bf16[4,4,4736]{2,1,0:T(4,128)(2,1)S(1)}, bf16[4,4,4736]{2,1,0:T(4,128)(2,1)S(1)}, u32[]{:S(2)}, u32[]{:S(2)}) collective-permute-start(bf16[4,4,4736]{2,1,0:T(4,128)(2,1)S(1)} %pad_maximum_fusion), channel_id=1, source_target_pairs={{0,1},{1,0},{2,3},{3,2},{4,5},{5,4},{6,7},{7,6},{8,9},{9,8},{10,11... | collective-permute-start | bytes 454664 | tf_op jit(solution)/shard_map/ppermute | solution.py:29
  21.0 16.2 %collective-permute-start.9 = (bf16[32,4608]{1,0:T(8,128)(2,1)S(1)}, bf16[32,4608]{1,0:T(8,128)(2,1)S(1)}, u32[]{:S(2)}, u32[]{:S(2)}) collective-permute-start(bf16[32,4608]{1,0:T(8,128)(2,1)S(1)} %constant_dynamic-update-slice_fusion.refs_6_), channel_id=1, source_target_pairs={{0,4},{1,5},{2,6},{3,7},{4,0},{5,1},{6,2},{7,3},{8,12},{9,13},{10,... | collective-permute-start | bytes 884744 | tf_op jit(solution)/shard_map/ppermute | solution.py:29
  22.6 14.6 %collective-permute-start.10 = (bf16[32,4608]{1,0:T(8,128)(2,1)S(1)}, bf16[32,4608]{1,0:T(8,128)(2,1)S(1)}, u32[]{:S(2)}, u32[]{:S(2)}) collective-permute-start(bf16[32,4608]{1,0:T(8,128)(2,1)S(1)} %constant_dynamic-update-slice_fusion.refs_6_), channel_id=1, source_target_pairs={{0,6},{1,7},{2,4},{3,5},{4,2},{5,3},{6,0},{7,1},{8,14},{9,15},{10,... | collective-permute-start | bytes 884744 | tf_op jit(solution)/shard_map/ppermute | solution.py:29
  26.3 12.4 %collective-permute-start.11 = (bf16[32,4608]{1,0:T(8,128)(2,1)S(1)}, bf16[32,4608]{1,0:T(8,128)(2,1)S(1)}, u32[]{:S(2)}, u32[]{:S(2)}) collective-permute-start(bf16[32,4608]{1,0:T(8,128)(2,1)S(1)} %constant_dynamic-update-slice_fusion.refs_6_), channel_id=1, source_target_pairs={{0,1},{1,0},{2,3},{3,2},{4,5},{5,4},{6,7},{7,6},{8,9},{9,8},{10,11... | collective-permute-start | bytes 884744 | tf_op jit(solution)/shard_map/ppermute | solution.py:29
  28.7 10.8 %collective-permute-start.15 = (bf16[64,1792]{1,0:T(8,128)(2,1)S(1)}, bf16[64,1792]{1,0:T(8,128)(2,1)S(1)}, u32[]{:S(2)}, u32[]{:S(2)}) collective-permute-start(bf16[64,1792]{1,0:T(8,128)(2,1)S(1)} %get-tuple-element.49), channel_id=1, source_target_pairs={{0,2},{1,3},{2,0},{3,1},{4,6},{5,7},{6,4},{7,5},{8,10},{9,11},{10,... | collective-permute-start | bytes 688136 | tf_op jit(solution)/shard_map/ppermute | solution.py:29
  30.2 16.4 %collective-permute-start.16 = (bf16[64,1792]{1,0:T(8,128)(2,1)S(1)}, bf16[64,1792]{1,0:T(8,128)(2,1)S(1)}, u32[]{:S(2)}, u32[]{:S(2)}) collective-permute-start(bf16[64,1792]{1,0:T(8,128)(2,1)S(1)} %get-tuple-element.50), channel_id=1, source_target_pairs={{0,4},{1,5},{2,6},{3,7},{4,0},{5,1},{6,2},{7,3},{8,12},{9,13},{10,... | collective-permute-start | bytes 688136 | tf_op jit(solution)/shard_map/ppermute | solution.py:29
  37.2 9.9 %collective-permute-start.12 = (bf16[32,4608]{1,0:T(8,128)(2,1)S(1)}, bf16[32,4608]{1,0:T(8,128)(2,1)S(1)}, u32[]{:S(2)}, u32[]{:S(2)}) collective-permute-start(bf16[32,4608]{1,0:T(8,128)(2,1)S(1)} %collective-permute-done.8.refs_7_), channel_id=1, source_target_pairs={{0,1},{1,0},{2,3},{3,2},{4,5},{5,4},{6,7},{7,6},{8,9},{9,8},{10,11... | collective-permute-start | bytes 884744 | tf_op jit(solution)/shard_map/ppermute | solution.py:29
  37.2 9.4 %collective-permute-start.17 = (bf16[64,1792]{1,0:T(8,128)(2,1)S(1)}, bf16[64,1792]{1,0:T(8,128)(2,1)S(1)}, u32[]{:S(2)}, u32[]{:S(2)}) collective-permute-start(bf16[64,1792]{1,0:T(8,128)(2,1)S(1)} %get-tuple-element.51), channel_id=1, source_target_pairs={{0,6},{1,7},{2,4},{3,5},{4,2},{5,3},{6,0},{7,1},{8,14},{9,15},{10,... | collective-permute-start | bytes 688136 | tf_op jit(solution)/shard_map/ppermute | solution.py:29
  38.7 8.5 %collective-permute-start.13 = (bf16[32,4608]{1,0:T(8,128)(2,1)S(1)}, bf16[32,4608]{1,0:T(8,128)(2,1)S(1)}, u32[]{:S(2)}, u32[]{:S(2)}) collective-permute-start(bf16[32,4608]{1,0:T(8,128)(2,1)S(1)} %collective-permute-done.9.refs_8_), channel_id=1, source_target_pairs={{0,1},{1,0},{2,3},{3,2},{4,5},{5,4},{6,7},{7,6},{8,9},{9,8},{10,11... | collective-permute-start | bytes 884744 | tf_op jit(solution)/shard_map/ppermute | solution.py:29
  39.5 8.1 %collective-permute-start.14 = (bf16[32,4608]{1,0:T(8,128)(2,1)S(1)}, bf16[32,4608]{1,0:T(8,128)(2,1)S(1)}, u32[]{:S(2)}, u32[]{:S(2)}) collective-permute-start(bf16[32,4608]{1,0:T(8,128)(2,1)S(1)} %collective-permute-done.10.refs_9_), channel_id=1, source_target_pairs={{0,1},{1,0},{2,3},{3,2},{4,5},{5,4},{6,7},{7,6},{8,9},{9,8},{10,11... | collective-permute-start | bytes 884744 | tf_op jit(solution)/shard_map/ppermute | solution.py:29
  46.6 3.6 %collective-permute-start.18 = (bf16[64,1792]{1,0:T(8,128)(2,1)S(1)}, bf16[64,1792]{1,0:T(8,128)(2,1)S(1)}, u32[]{:S(2)}, u32[]{:S(2)}) collective-permute-start(bf16[64,1792]{1,0:T(8,128)(2,1)S(1)} %get-tuple-element.48.refs_9_), channel_id=1, source_target_pairs={{0,1},{1,0},{2,3},{3,2},{4,5},{5,4},{6,7},{7,6},{8,9},{9,8},{10,11... | collective-permute-start | bytes 688136 | tf_op jit(solution)/shard_map/ppermute | solution.py:29
  46.6 3.6 %collective-permute-start.19 = (bf16[64,1792]{1,0:T(8,128)(2,1)S(1)}, bf16[64,1792]{1,0:T(8,128)(2,1)S(1)}, u32[]{:S(2)}, u32[]{:S(2)}) collective-permute-start(bf16[64,1792]{1,0:T(8,128)(2,1)S(1)} %collective-permute-done.15.refs_10_), channel_id=1, source_target_pairs={{0,1},{1,0},{2,3},{3,2},{4,5},{5,4},{6,7},{7,6},{8,9},{9,8},{10,11... | collective-permute-start | bytes 688136 | tf_op jit(solution)/shard_map/ppermute | solution.py:29
  47.1 3.1 %collective-permute-start.20 = (bf16[64,1792]{1,0:T(8,128)(2,1)S(1)}, bf16[64,1792]{1,0:T(8,128)(2,1)S(1)}, u32[]{:S(2)}, u32[]{:S(2)}) collective-permute-start(bf16[64,1792]{1,0:T(8,128)(2,1)S(1)} %collective-permute-done.16.refs_11_), channel_id=1, source_target_pairs={{0,1},{1,0},{2,3},{3,2},{4,5},{5,4},{6,7},{7,6},{8,9},{9,8},{10,11... | collective-permute-start | bytes 688136 | tf_op jit(solution)/shard_map/ppermute | solution.py:29
  47.1 3.1 %collective-permute-start.21 = (bf16[64,1792]{1,0:T(8,128)(2,1)S(1)}, bf16[64,1792]{1,0:T(8,128)(2,1)S(1)}, u32[]{:S(2)}, u32[]{:S(2)}) collective-permute-start(bf16[64,1792]{1,0:T(8,128)(2,1)S(1)} %collective-permute-done.17.refs_12_), channel_id=1, source_target_pairs={{0,1},{1,0},{2,3},{3,2},{4,5},{5,4},{6,7},{7,6},{8,9},{9,8},{10,11... | collective-permute-start | bytes 688136 | tf_op jit(solution)/shard_map/ppermute | solution.py:29
  47.6 2.6 %slice-start = ((s8[10485760]{0:T(1024)(128)(4,1)}), s8[4194304]{0:T(1024)(128)(4,1)S(1)}, s32[]{:S(2)}) async-start(s8[10485760]{0:T(1024)(128)(4,1)} %bitcast.18), calls=%async_computation | async-start | bytes 8388608
  47.6 3.5 %slice-start.1 = ((s8[10485760]{0:T(1024)(128)(4,1)}), s8[4194304]{0:T(1024)(128)(4,1)S(1)}, s32[]{:S(2)}) async-start(s8[10485760]{0:T(1024)(128)(4,1)} %bitcast.18), calls=%async_computation.1 | async-start | bytes 8388608
  47.6 4.1 %slice-start.2 = ((s8[10485760]{0:T(1024)(128)(4,1)}), s8[2097152]{0:T(1024)(128)(4,1)S(1)}, s32[]{:S(2)}) async-start(s8[10485760]{0:T(1024)(128)(4,1)} %bitcast.18), calls=%async_computation.2 | async-start | bytes 4194304
  47.6 4.3 %copy-start.3 = (bf16[8,512,128]{2,1,0:T(8,128)(2,1)S(1)}, bf16[8,512,128]{2,1,0:T(8,128)(2,1)}, u32[]{:S(2)}) copy-start(bf16[8,512,128]{2,1,0:T(8,128)(2,1)} %refs_7_.1) | copy-start | bytes 3145732
  47.6 4.3 %copy-start.4 = (bf16[256,256]{1,0:T(8,128)(2,1)S(1)}, bf16[256,256]{1,0:T(8,128)(2,1)}, u32[]{:S(2)}) copy-start(bf16[256,256]{1,0:T(8,128)(2,1)} %constant.65.clone.refs_6_) | copy-start | bytes 393220
  51.9 8.8 %copy-start.10 = (bf16[5120]{0:T(1024)(128)(2,1)S(1)}, bf16[5120]{0:T(1024)(128)(2,1)}, u32[]{:S(2)}) copy-start(bf16[5120]{0:T(1024)(128)(2,1)} %param.25) | copy-start | bytes 30724
  51.9 12.3 %copy-start.5 = (bf16[4,5120]{1,0:T(4,128)(2,1)S(1)}, bf16[4,5120]{1,0:T(4,128)(2,1)}, u32[]{:S(2)}) copy-start(bf16[4,5120]{1,0:T(4,128)(2,1)} %hidden_ref.1) | copy-start | bytes 122884
  51.9 12.3 %copy-start.7 = (s32[4,6]{1,0:T(4,128)S(1)}, s32[4,6]{1,0:T(4,128)}, u32[]{:S(2)}) copy-start(s32[4,6]{1,0:T(4,128)} %ids_ref.1) | copy-start | bytes 292
  51.9 12.2 %copy-start.8 = (bf16[4,6]{1,0:T(4,128)(2,1)S(1)}, bf16[4,6]{1,0:T(4,128)(2,1)}, u32[]{:S(2)}) copy-start(bf16[4,6]{1,0:T(4,128)(2,1)} %weight_ref.1) | copy-start | bytes 148
  51.9 31.0 %copy-start = (bf16[1,5120,384]{2,1,0:T(8,128)(2,1)S(1)}, bf16[1,5120,384]{2,1,0:T(8,128)(2,1)}, u32[]{:S(2)}) copy-start(bf16[1,5120,384]{2,1,0:T(8,128)(2,1)} %refs_8_.3) | copy-start | bytes 11796484
  51.9 31.0 %copy-start.1 = (bf16[1,5120,384]{2,1,0:T(8,128)(2,1)S(1)}, bf16[1,5120,384]{2,1,0:T(8,128)(2,1)}, u32[]{:S(2)}) copy-start(bf16[1,5120,384]{2,1,0:T(8,128)(2,1)} %refs_9_.1) | copy-start | bytes 11796484
  51.9 31.0 %copy-start.2 = (bf16[1,384,5120]{2,1,0:T(8,128)(2,1)S(1)}, bf16[1,384,5120]{2,1,0:T(8,128)(2,1)}, u32[]{:S(2)}) copy-start(bf16[1,384,5120]{2,1,0:T(8,128)(2,1)} %refs_10_.1) | copy-start | bytes 11796484
  55.6 1.4 %collective-permute-start.22 = (bf16[16,5120]{1,0:T(8,128)(2,1)S(1)}, bf16[16,5120]{1,0:T(8,128)(2,1)S(1)}, u32[]{:S(2)}, u32[]{:S(2)}) collective-permute-start(bf16[16,5120]{1,0:T(8,128)(2,1)S(1)} %get-tuple-element.53), channel_id=1, source_target_pairs={{0,1},{1,0},{2,3},{3,2},{4,5},{5,4},{6,7},{7,6},{8,9},{9,8},{10,11... | collective-permute-start | bytes 491528 | tf_op jit(solution)/shard_map/ppermute | solution.py:29
  57.1 4.1 %collective-permute-start.23 = (bf16[4,5120]{1,0:T(4,128)(2,1)S(1)}, bf16[4,5120]{1,0:T(4,128)(2,1)S(1)}, u32[]{:S(2)}, u32[]{:S(2)}) collective-permute-start(bf16[4,5120]{1,0:T(4,128)(2,1)S(1)} %get-tuple-element.55), channel_id=1, source_target_pairs={{0,2},{1,3},{2,0},{3,1},{4,6},{5,7},{6,4},{7,5},{8,10},{9,11},{10,... | collective-permute-start | bytes 122888 | tf_op jit(solution)/shard_map/ppermute | solution.py:29
  57.8 4.0 %collective-permute-start.24 = (bf16[4,5120]{1,0:T(4,128)(2,1)S(1)}, bf16[4,5120]{1,0:T(4,128)(2,1)S(1)}, u32[]{:S(2)}, u32[]{:S(2)}) collective-permute-start(bf16[4,5120]{1,0:T(4,128)(2,1)S(1)} %get-tuple-element.56), channel_id=1, source_target_pairs={{0,4},{1,5},{2,6},{3,7},{4,0},{5,1},{6,2},{7,3},{8,12},{9,13},{10,... | collective-permute-start | bytes 122888 | tf_op jit(solution)/shard_map/ppermute | solution.py:29
  59.2 4.9 %collective-permute-start.25 = (bf16[4,5120]{1,0:T(4,128)(2,1)S(1)}, bf16[4,5120]{1,0:T(4,128)(2,1)S(1)}, u32[]{:S(2)}, u32[]{:S(2)}) collective-permute-start(bf16[4,5120]{1,0:T(4,128)(2,1)S(1)} %get-tuple-element.57), channel_id=1, source_target_pairs={{0,6},{1,7},{2,4},{3,5},{4,2},{5,3},{6,0},{7,1},{8,14},{9,15},{10,... | collective-permute-start | bytes 122888 | tf_op jit(solution)/shard_map/ppermute | solution.py:29
  64.8 4.8 %collective-permute-start.26 = (bf16[4,5248]{1,0:T(4,128)(2,1)S(1)}, bf16[4,5248]{1,0:T(4,128)(2,1)S(1)}, u32[]{:S(2)}, u32[]{:S(2)}) collective-permute-start(bf16[4,5248]{1,0:T(4,128)(2,1)S(1)} %get-tuple-element.59.refs_0_), channel_id=1, source_target_pairs={{0,8},{8,0},{16,24},{24,16},{1,9},{9,1},{17,25},{25,17},{2,10},{10... | collective-permute-start | bytes 125960 | tf_op jit(solution)/shard_map/ppermute | solution.py:29
  66.4 5.2 %collective-permute-start.27 = (bf16[4,5248]{1,0:T(4,128)(2,1)S(1)}, bf16[4,5248]{1,0:T(4,128)(2,1)S(1)}, u32[]{:S(2)}, u32[]{:S(2)}) collective-permute-start(bf16[4,5248]{1,0:T(4,128)(2,1)S(1)} %get-tuple-element.59.refs_0_), channel_id=1, source_target_pairs={{0,16},{8,24},{16,0},{24,8},{1,17},{9,25},{17,1},{25,9},{2,18},{10... | collective-permute-start | bytes 125960 | tf_op jit(solution)/shard_map/ppermute | solution.py:29
  66.7 5.8 %collective-permute-start.28 = (bf16[4,5248]{1,0:T(4,128)(2,1)S(1)}, bf16[4,5248]{1,0:T(4,128)(2,1)S(1)}, u32[]{:S(2)}, u32[]{:S(2)}) collective-permute-start(bf16[4,5248]{1,0:T(4,128)(2,1)S(1)} %get-tuple-element.59.refs_0_), channel_id=1, source_target_pairs={{0,24},{8,16},{16,8},{24,0},{1,25},{9,17},{17,9},{25,1},{2,26},{10... | collective-permute-start | bytes 125960 | tf_op jit(solution)/shard_map/ppermute | solution.py:29
  72.6 5.4 %collective-permute-start.29 = (bf16[16,5248]{1,0:T(8,128)(2,1)S(1)}, bf16[16,5248]{1,0:T(8,128)(2,1)S(1)}, u32[]{:S(2)}, u32[]{:S(2)}) collective-permute-start(bf16[16,5248]{1,0:T(8,128)(2,1)S(1)} %shard_map.174.refs_0_), channel_id=1, source_target_pairs={{0,2},{1,3},{2,0},{3,1},{4,6},{5,7},{6,4},{7,5},{8,10},{9,11},{10,... | collective-permute-start | bytes 503816 | tf_op jit(solution)/shard_map/ppermute | solution.py:29
  74.1 7.2 %collective-permute-start.30 = (bf16[16,5248]{1,0:T(8,128)(2,1)S(1)}, bf16[16,5248]{1,0:T(8,128)(2,1)S(1)}, u32[]{:S(2)}, u32[]{:S(2)}) collective-permute-start(bf16[16,5248]{1,0:T(8,128)(2,1)S(1)} %shard_map.174.refs_0_), channel_id=1, source_target_pairs={{0,4},{1,5},{2,6},{3,7},{4,0},{5,1},{6,2},{7,3},{8,12},{9,13},{10,... | collective-permute-start | bytes 503816 | tf_op jit(solution)/shard_map/ppermute | solution.py:29
  74.7 6.7 %collective-permute-start.31 = (bf16[16,5248]{1,0:T(8,128)(2,1)S(1)}, bf16[16,5248]{1,0:T(8,128)(2,1)S(1)}, u32[]{:S(2)}, u32[]{:S(2)}) collective-permute-start(bf16[16,5248]{1,0:T(8,128)(2,1)S(1)} %shard_map.174.refs_0_), channel_id=1, source_target_pairs={{0,6},{1,7},{2,4},{3,5},{4,2},{5,3},{6,0},{7,1},{8,14},{9,15},{10,... | collective-permute-start | bytes 503816 | tf_op jit(solution)/shard_map/ppermute | solution.py:29
  76.1 5.7 %collective-permute-start.32 = (bf16[16,5248]{1,0:T(8,128)(2,1)S(1)}, bf16[16,5248]{1,0:T(8,128)(2,1)S(1)}, u32[]{:S(2)}, u32[]{:S(2)}) collective-permute-start(bf16[16,5248]{1,0:T(8,128)(2,1)S(1)} %shard_map.174.refs_0_), channel_id=1, source_target_pairs={{0,1},{1,0},{2,3},{3,2},{4,5},{5,4},{6,7},{7,6},{8,9},{9,8},{10,11... | collective-permute-start | bytes 503816 | tf_op jit(solution)/shard_map/ppermute | solution.py:29
  78.0 3.8 %collective-permute-start.33 = (bf16[16,5248]{1,0:T(8,128)(2,1)S(1)}, bf16[16,5248]{1,0:T(8,128)(2,1)S(1)}, u32[]{:S(2)}, u32[]{:S(2)}) collective-permute-start(bf16[16,5248]{1,0:T(8,128)(2,1)S(1)} %collective-permute-done.29.refs_1_), channel_id=1, source_target_pairs={{0,1},{1,0},{2,3},{3,2},{4,5},{5,4},{6,7},{7,6},{8,9},{9,8},{10,11... | collective-permute-start | bytes 503816 | tf_op jit(solution)/shard_map/ppermute | solution.py:29
  81.3 1.4 %collective-permute-start.34 = (bf16[16,5248]{1,0:T(8,128)(2,1)S(1)}, bf16[16,5248]{1,0:T(8,128)(2,1)S(1)}, u32[]{:S(2)}, u32[]{:S(2)}) collective-permute-start(bf16[16,5248]{1,0:T(8,128)(2,1)S(1)} %collective-permute-done.30.refs_2_), channel_id=1, source_target_pairs={{0,1},{1,0},{2,3},{3,2},{4,5},{5,4},{6,7},{7,6},{8,9},{9,8},{10,11... | collective-permute-start | bytes 503816 | tf_op jit(solution)/shard_map/ppermute | solution.py:29
  81.3 1.6 %collective-permute-start.35 = (bf16[16,5248]{1,0:T(8,128)(2,1)S(1)}, bf16[16,5248]{1,0:T(8,128)(2,1)S(1)}, u32[]{:S(2)}, u32[]{:S(2)}) collective-permute-start(bf16[16,5248]{1,0:T(8,128)(2,1)S(1)} %collective-permute-done.31.refs_3_), channel_id=1, source_target_pairs={{0,1},{1,0},{2,3},{3,2},{4,5},{5,4},{6,7},{7,6},{8,9},{9,8},{10,11... | collective-permute-start | bytes 503816 | tf_op jit(solution)/shard_map/ppermute | solution.py:29
  86.1 2.2 %collective-permute-start.36 = (bf16[64,5120]{1,0:T(8,128)(2,1)S(1)}, bf16[64,5120]{1,0:T(8,128)(2,1)S(1)}, u32[]{:S(2)}, u32[]{:S(2)}) collective-permute-start(bf16[64,5120]{1,0:T(8,128)(2,1)S(1)} %get-tuple-element.61), channel_id=1, source_target_pairs={{0,1},{1,0},{2,3},{3,2},{4,5},{5,4},{6,7},{7,6},{8,9},{9,8},{10,11... | collective-permute-start | bytes 1966088 | tf_op jit(solution)/shard_map/ppermute | solution.py:29
  88.3 7.1 %collective-permute-start.37 = (bf16[16,5120]{1,0:T(8,128)(2,1)S(1)}, bf16[16,5120]{1,0:T(8,128)(2,1)S(1)}, u32[]{:S(2)}, u32[]{:S(2)}) collective-permute-start(bf16[16,5120]{1,0:T(8,128)(2,1)S(1)} %get-tuple-element.63), channel_id=1, source_target_pairs={{0,2},{1,3},{2,0},{3,1},{4,6},{5,7},{6,4},{7,5},{8,10},{9,11},{10,... | collective-permute-start | bytes 491528 | tf_op jit(solution)/shard_map/ppermute | solution.py:29
  88.9 6.9 %collective-permute-start.38 = (bf16[16,5120]{1,0:T(8,128)(2,1)S(1)}, bf16[16,5120]{1,0:T(8,128)(2,1)S(1)}, u32[]{:S(2)}, u32[]{:S(2)}) collective-permute-start(bf16[16,5120]{1,0:T(8,128)(2,1)S(1)} %get-tuple-element.64), channel_id=1, source_target_pairs={{0,4},{1,5},{2,6},{3,7},{4,0},{5,1},{6,2},{7,3},{8,12},{9,13},{10,... | collective-permute-start | bytes 491528 | tf_op jit(solution)/shard_map/ppermute | solution.py:29
  89.8 8.7 %collective-permute-start.39 = (bf16[16,5120]{1,0:T(8,128)(2,1)S(1)}, bf16[16,5120]{1,0:T(8,128)(2,1)S(1)}, u32[]{:S(2)}, u32[]{:S(2)}) collective-permute-start(bf16[16,5120]{1,0:T(8,128)(2,1)S(1)} %get-tuple-element.65), channel_id=1, source_target_pairs={{0,6},{1,7},{2,4},{3,5},{4,2},{5,3},{6,0},{7,1},{8,14},{9,15},{10,... | collective-permute-start | bytes 491528 | tf_op jit(solution)/shard_map/ppermute | solution.py:29
  98.7 4.5 %collective-permute-start.40 = (bf16[4,5120]{1,0:T(4,128)(2,1)S(1)}, bf16[4,5120]{1,0:T(4,128)(2,1)S(1)}, u32[]{:S(2)}, u32[]{:S(2)}) collective-permute-start(bf16[4,5120]{1,0:T(4,128)(2,1)S(1)} %get-tuple-element.76), channel_id=1, source_target_pairs={{0,8},{8,0},{16,24},{24,16},{1,9},{9,1},{17,25},{25,17},{2,10},{10... | collective-permute-start | bytes 122888 | tf_op jit(solution)/shard_map/ppermute | solution.py:29
  99.1 5.0 %collective-permute-start.41 = (bf16[4,5120]{1,0:T(4,128)(2,1)S(1)}, bf16[4,5120]{1,0:T(4,128)(2,1)S(1)}, u32[]{:S(2)}, u32[]{:S(2)}) collective-permute-start(bf16[4,5120]{1,0:T(4,128)(2,1)S(1)} %get-tuple-element.78), channel_id=1, source_target_pairs={{0,16},{8,24},{16,0},{24,8},{1,17},{9,25},{17,1},{25,9},{2,18},{10... | collective-permute-start | bytes 122888 | tf_op jit(solution)/shard_map/ppermute | solution.py:29
  101.8 5.8 %collective-permute-start.42 = (bf16[4,5120]{1,0:T(4,128)(2,1)S(1)}, bf16[4,5120]{1,0:T(4,128)(2,1)S(1)}, u32[]{:S(2)}, u32[]{:S(2)}) collective-permute-start(bf16[4,5120]{1,0:T(4,128)(2,1)S(1)} %get-tuple-element.77), channel_id=1, source_target_pairs={{0,24},{8,16},{16,8},{24,0},{1,25},{9,17},{17,9},{25,1},{2,26},{10... | collective-permute-start | bytes 122888 | tf_op jit(solution)/shard_map/ppermute | solution.py:29

commit v4 on v3

--- a/solution.py
+++ b/solution.py
@@ -49,14 +49,14 @@
     )(*operands, *away)
 
 
-def suffix_kernel(pos, query_ref, keys_ref, count_hbm, mine_ref, other_ref, rows, count, sem):
+def suffix_kernel(pos, query_ref, keys_ref, count_hbm, *refs):
+    outs, (rows, count, sem) = refs[:-3], refs[-3:]
     copy = pltpu.make_async_copy(count_hbm, count, sem)
     copy.start()
     place = pos[0]
     requests, heads, _ = query_ref.shape
-    chips, group_rows, width = mine_ref.shape
-    group = group_rows // requests
-    members = heads // group
+    members = 2 * len(outs)
+    group = heads // members
     all_scores = [
         dot(query_ref[r], keys_ref[r], ((1,), (1,))) * SCORE_SCALE for r in range(requests)
     ]
@@ -75,18 +75,17 @@
         full = jnp.concatenate([numerator, stats], axis=1)
         for g in range(members):
             rows[r, g] = full[g * group : (g + 1) * group]
-    for j in range(members):
-        taken = [rows[r, place ^ j] for r in range(requests)]
-        out_ref = other_ref if j % 2 else mine_ref
-        out_ref[j // 2] = jnp.concatenate(taken, axis=0).astype(jnp.bfloat16)
-
-
-def join_kernel(mine_ref, other_ref, piece_ref, *outs):
-    width = mine_ref.shape[2]
+    for k, out_ref in enumerate(outs):
+        taken = [rows[r, place ^ (2 * k + s)] for s in range(2) for r in range(requests)]
+        out_ref[...] = jnp.concatenate(taken, axis=0).astype(jnp.bfloat16)
+
+
+def join_kernel(piece_ref, *refs):
+    half = len(refs) // 2
     blocks = piece_ref.shape[0]
-    for k, out_ref in enumerate(outs):
-        both = [mine_ref[k].astype(jnp.float32), other_ref[k].astype(jnp.float32)]
-        out_ref[:, :width] = jnp.concatenate(both, axis=0).astype(jnp.bfloat16)
+    for rows_ref, out_ref in zip(refs[:half], refs[half:]):
+        width = rows_ref.shape[1]
+        out_ref[:, :width] = rows_ref[...]
         for i in range(piece_ref.shape[1] // PAIR):
             out_ref[i * blocks : (i + 1) * blocks, width:] = piece_ref[:, i * PAIR : (i + 1) * PAIR]
 
@@ -202,7 +201,12 @@
 def middle_kernel(variants, sources, blocks, *refs):
     queries, refs = refs[: 2 * variants], refs[2 * variants :]
     state, chunks, outs = refs[:4], refs[4:-4], refs[-4:]
-    sources = [(q, lane_pairs(chunks, i * blocks)) for i, q in enumerate(sources)]
+    each = chunks[0].shape[0]
+    places = [(ref, row) for ref in chunks for row in range(0, ref.shape[0], each)]
+    sources = [
+        (q, [pair for ref, row in places for pair in lane_pairs([ref], row + i * blocks)])
+        for i, q in enumerate(sources)
+    ]
     put_state(walk(queries, sources, blocks, get_state(state)), outs)
 
 
@@ -211,8 +215,12 @@
     state, refs = refs[:4], refs[4:]
     order_ref, value_ref, proj_ref = refs[:3]
     chunks, (keep_ref, away_ref) = refs[3:-2], refs[-2:]
-    own = jnp.concatenate([ref[:, : LAT + LANES] for ref in chunks[:chips]], axis=0)
-    own = dot(order_ref[...], own, ((1,), (0,)))
+    half = chunks[0].shape[0] // 2
+    own = []
+    for k in range(chips):
+        own.append(chunks[k][:half, : LAT + LANES].astype(jnp.float32))
+        own.append(chunks[chips + k][half:, : LAT + LANES].astype(jnp.float32))
+    own = dot(order_ref[...], jnp.concatenate(own, axis=0).astype(jnp.bfloat16), ((1,), (0,)))
     sources = [(source, stacked_pairs(chunks, blocks))]
     top, total, even, odd = walk(queries, sources, blocks, get_state(state))
     stats = own[:, LAT:]
@@ -281,6 +289,12 @@
     for j in range(TOPK):
         gates = gates + jnp.where(lane == ids[:, j : j + 1], weights[:, j : j + 1], 0.0)
     row_ref[:, width:] = gates.astype(jnp.bfloat16)
+
+
+def pile_kernel(*refs):
+    rows = refs[0].shape[0]
+    for i, ref in enumerate(refs[:-1]):
+        refs[-1][i * rows : (i + 1) * rows, :] = ref[...]
 
 
 def stack_kernel(*refs):
@@ -377,13 +391,16 @@
     asked = [asked[0]] + [swap(asked[k], "expert", 2 * k) for k in range(1, chips)]
 
     early = jnp.concatenate(arrived[1:-1])
-    chunks = [early] + [swap(early, "expert", 2 * k) for k in range(1, chips)]
+    chunks = [early] + [swap(early, "expert", 2 * k) for k in range(1, chips - 1)]
+    *asked, early = lax.optimization_barrier((*asked, early))
+    chunks.append(swap(early, "expert", 2 * (chips - 1)))
 
     pos = jnp.stack([place, shard])
-    partial = jax.ShapeDtypeStruct((chips, row_count * group_heads, LAT + LANES), bf16)
-    mine, other = vmem_call(
+    query, suffix_cache, early = lax.optimization_barrier((query, suffix_cache, early))
+    partial = jax.ShapeDtypeStruct((2 * row_count * group_heads, LAT + LANES), bf16)
+    partials = vmem_call(
         suffix_kernel,
-        [partial, partial],
+        [partial] * chips,
         [
             pos,
             query.reshape(row_count, HEADS, KDIM),
@@ -392,16 +409,16 @@
         4 * row_count * HEADS * SUFFIX * KDIM,
         scalars=1,
         scratch=[
-            pltpu.VMEM((row_count, members, group_heads, partial.shape[2]), jnp.float32),
+            pltpu.VMEM((row_count, members, group_heads, partial.shape[1]), jnp.float32),
             pltpu.SMEM(suffix_count.shape, jnp.int32),
             pltpu.SemaphoreType.DMA,
         ],
         away=[suffix_count],
     )
-    other = swap(other, "expert", 1)
-    joined = jax.ShapeDtypeStruct((2 * partial.shape[1], partial.shape[2] + PAIR), bf16)
-    late = list(vmem_call(join_kernel, [joined] * chips, [mine, other, arrived[-1]], mine.size))
-    late[-1], chunks[1] = lax.optimization_barrier((late[-1], chunks[1]))
+    joined = jax.ShapeDtypeStruct((partial.shape[0], partial.shape[1] + PAIR), bf16)
+    late = list(
+        vmem_call(join_kernel, [joined] * chips, [arrived[-1]] + list(partials), piece.size)
+    )
     late = [late[0]] + [swap(late[k], "expert", 2 * k) for k in range(1, chips)]
 
     rows = members * row_count * group_heads
@@ -409,17 +426,27 @@
     *queries, top, total, even, odd = vmem_call(
         functools.partial(first_kernel, variants, group_heads),
         [wide] * (2 * variants) + state_shapes(rows),
-        [prefix_pool, swap(jnp.stack([part[1] for part in asked]), "expert", 1)] + asked,
+        [prefix_pool, swap(jnp.stack([part[1] for part in asked]), "expert", 1)]
+        + asked,
         40 * rows * prefix_pool.size,
     )
-    chunks += [swap(block, "expert", 1) for block in chunks]
+    *chunks, late[1], late[2] = lax.optimization_barrier((*chunks, late[1], late[2]))
+    held = vmem_call(
+        pile_kernel,
+        jax.ShapeDtypeStruct((chips * early.shape[0], early.shape[1]), bf16),
+        chunks,
+        chips * early.size,
+    )
+    chunks.append(swap(held, "expert", 1))
     state = vmem_call(
         functools.partial(middle_kernel, variants, list(range(1, holders - 1)), shard_blocks),
         state_shapes(rows),
         queries + [top, total, even, odd] + chunks,
         40 * rows * prefix_pool.size,
     )
-    late += [swap(block, "expert", 1) for block in late]
+    *held, top = lax.optimization_barrier((*late, state[0]))
+    state = [top, *state[1:]]
+    late = held + [swap(block, "expert", 1) for block in held]
     half = members * row_count // 2
     keep, away = vmem_call(
         functools.partial(last_kernel, variants, chips, holders - 1, shard_blocks),

time: 109 us -> 105 us (0.963)
  local copies, waits for them, and re-layouts: 6.9 us -> 4.16 us
  waiting for transfers between devices: 44.7 us -> 42.5 us
    ppermute x43 -> x39, waiting for transfers between devices: 44.7 us -> 42.5 us  [swap(): return lax.ppermute(value, axis, [(i, i ^ mask) for i in range(size)])]
    unnamed x29 -> x49, local copies, waits for them, and re-layouts: 1.7 us -> 0.15 us
    ppermute x43 -> x39, starting transfers between devices: 39.8 us -> 40.8 us  [swap(): return lax.ppermute(value, axis, [(i, i ^ mask) for i in range(size)])]
    pallas_call x10 -> x11, Pallas kernels: 13 us -> 13.1 us  [vmem_call(): pl.pallas_call(kernel, out_shape=out_shape, in_specs=specs, out_specs=jax...]
  transfers between devices with their start and end apart: 43 -> 39, of which waited for: 23 -> 25; matrix products, arithmetic and copies ran while one was open for 6% -> 5% of each run, Pallas kernels for 5% -> 5%
where the time goes in v4:
time: 105 us
  waiting for transfers between devices  42.5 us (40%)
  starting transfers between devices  40.8 us (39%)
  Pallas kernels  13.1 us (12%)
  local copies, waits for them, and re-layouts  4.16 us (4%)
  other arithmetic  2.84 us (3%)
  between operations  1.2 us (1%)
    ppermute x39, waiting for transfers between devices, swap(): return lax.ppermute(value, axis, [(i, i ^ mask) for i in range(size)])  42.5 us
    ppermute x39, starting transfers between devices, swap(): return lax.ppermute(value, axis, [(i, i ^ mask) for i in range(size)])  40.8 us
    pallas_call x11, Pallas kernels, vmem_call(): pl.pallas_call(kernel, out_shape=out_shape, in_specs=specs, out_specs=jax...  13.1 us
  transfers between devices with their start and end apart: 39, of which 25 were waited for; matrix products, arithmetic and copies ran while one was open for 5% of the time, Pallas kernels for 5%

profile of v4, /device:TPU:0, one launch (start us, length us, event | category | flops | bytes accessed | tf_op | source)
XLA Modules:
  0.0 104.5 jit_solution(8151654813727587474)
XLA Ops:
  0.6 0.9 constant_dynamic-slice_fusion
  1.6 4.1 %collective-permute-start.4 = (bf16[16,4608]{1,0:T(8,128)(2,1)S(1)}, bf16[16,4608]{1,0:T(8,128)(2,1)}, u32[]{:S(2)}, u32[]{:S(2)}) collective-permute-start(bf16[16,4608]{1,0:T(8,128)(2,1)S(1)} %constant_dynamic-slice_fusion), channel_id=1, source_target_pairs={{0,16},{8,24},{16,0},{24,8},{1,17},{9,25},{17,1},{25,9},{2,18},{10... | collective-permute-start | bytes 442376 | tf_op jit(solution)/shard_map/ppermute | solution.py:29
  5.7 1.6 %collective-permute-start.3 = (bf16[16,4608]{1,0:T(8,128)(2,1)S(1)}, bf16[16,4608]{1,0:T(8,128)(2,1)S(1)}, u32[]{:S(2)}, u32[]{:S(2)}) collective-permute-start(bf16[16,4608]{1,0:T(8,128)(2,1)S(1)} %constant_dynamic-slice_fusion), channel_id=1, source_target_pairs={{0,8},{8,0},{16,24},{24,16},{1,9},{9,1},{17,25},{25,17},{2,10},{10... | collective-permute-start | bytes 442376 | tf_op jit(solution)/shard_map/ppermute | solution.py:29
  7.3 0.7 iota_compare_fusion
  8.0 0.8 and_reduce_fusion
  8.8 1.0 constant_dynamic-slice_fusion.2
  10.1 2.5 %collective-permute-start.2 = (bf16[2,4,4736]{2,1,0:T(4,128)(2,1)S(1)}, bf16[2,4,4736]{2,1,0:T(4,128)(2,1)S(1)}, u32[]{:S(2)}, u32[]{:S(2)}) collective-permute-start(bf16[2,4,4736]{2,1,0:T(4,128)(2,1)S(1)} %pad_maximum_fusion.12), channel_id=1, source_target_pairs={{0,6},{1,7},{2,4},{3,5},{4,2},{5,3},{6,0},{7,1},{8,14},{9,15},{10,... | collective-permute-start | bytes 227336 | tf_op jit(solution)/shard_map/ppermute | solution.py:29
  12.6 0.6 collective-permute-start.1
  13.3 0.6 collective-permute-start
  14.0 0.6 collective-permute-start.6
  14.6 1.0 constant_dynamic-update-slice_fusion.refs_0_.refs_6_
  15.5 1.6 %collective-permute-start.7 = (bf16[32,4608]{1,0:T(8,128)(2,1)S(1)}, bf16[32,4608]{1,0:T(8,128)(2,1)S(1)}, u32[]{:S(2)}, u32[]{:S(2)}) collective-permute-start(bf16[32,4608]{1,0:T(8,128)(2,1)S(1)} %constant_dynamic-update-slice_fusion.refs_0_.refs_6_), channel_id=1, source_target_pairs={{0,2},{1,3},{2,0},{3,1},{4,6},{5,7},{6,4},{7,5},{8,10},{9,11},{10,... | collective-permute-start | bytes 884744 | tf_op jit(solution)/shard_map/ppermute | solution.py:29
  17.1 1.5 %collective-permute-start.8 = (bf16[32,4608]{1,0:T(8,128)(2,1)S(1)}, bf16[32,4608]{1,0:T(8,128)(2,1)S(1)}, u32[]{:S(2)}, u32[]{:S(2)}) collective-permute-start(bf16[32,4608]{1,0:T(8,128)(2,1)S(1)} %constant_dynamic-update-slice_fusion.refs_0_.refs_6_), channel_id=1, source_target_pairs={{0,4},{1,5},{2,6},{3,7},{4,0},{5,1},{6,2},{7,3},{8,12},{9,13},{10,... | collective-permute-start | bytes 884744 | tf_op jit(solution)/shard_map/ppermute | solution.py:29
  18.6 0.6 collective-permute-start.9
  19.3 0.7 reshape.70.keys_ref
  20.3 1.4 %shard_map.168 = (bf16[64,640]{1,0:T(8,128)(2,1)S(1)}, bf16[64,640]{1,0:T(8,128)(2,1)S(1)}, bf16[64,640]{1,0:T(8,128)(2,1)S(1)}, bf16[64,640]{1,0:T(8,128)(2,1)S(1)}) custom-call(s32[2]{0:T(128)S(1)} %pad_add_fusion.pos, bf16[4,64,576]{2,1,0:T(8,128)(2,1)S(1)} %reshape.69.query_ref, bf16[4,128,576]{2,1,0:T(8,128)(2,1)S(1)} %reshape.70.keys_ref, s32[4]{0:T(128)S(1)} %copy-done.17), custom_call_target="tpu_custom_call" | custom-call | flops 75497472 | bytes 884744 | tf_op jit(solution)/shard_map/pallas_call | solution.py:41
  21.9 2.4 %collective-permute-start.10 = (bf16[64,1792]{1,0:T(8,128)(2,1)S(1)}, bf16[64,1792]{1,0:T(8,128)(2,1)S(1)}, u32[]{:S(2)}, u32[]{:S(2)}) collective-permute-start(bf16[64,1792]{1,0:T(8,128)(2,1)S(1)} %get-tuple-element.66), channel_id=1, source_target_pairs={{0,2},{1,3},{2,0},{3,1},{4,6},{5,7},{6,4},{7,5},{8,10},{9,11},{10,... | collective-permute-start | bytes 688136 | tf_op jit(solution)/shard_map/ppermute | solution.py:29
  24.2 0.7 collective-permute-start.11
  25.0 7.8 %collective-permute-done.9.refs_3_.refs_9_ = bf16[32,4608]{1,0:T(8,128)(2,1)S(1)} collective-permute-done((bf16[32,4608]{1,0:T(8,128)(2,1)S(1)}, bf16[32,4608]{1,0:T(8,128)(2,1)S(1)}, u32[]{:S(2)}, u32[]{:S(2)}) %collective-permute-start.9) | collective-permute-done | bytes 294944 | tf_op jit(solution)/shard_map/ppermute | solution.py:29
  32.9 2.4 %collective-permute-done.10.refs_10_ = bf16[64,1792]{1,0:T(8,128)(2,1)S(1)} collective-permute-done((bf16[64,1792]{1,0:T(8,128)(2,1)S(1)}, bf16[64,1792]{1,0:T(8,128)(2,1)S(1)}, u32[]{:S(2)}, u32[]{:S(2)}) %collective-permute-start.10) | collective-permute-done | bytes 229408 | tf_op jit(solution)/shard_map/ppermute | solution.py:29
  35.3 0.4 collective-permute-done.11.refs_11_
  36.0 0.5 collective-permute-start.5
  36.5 1.5 %collective-permute-start.12 = (bf16[64,1792]{1,0:T(8,128)(2,1)S(1)}, bf16[64,1792]{1,0:T(8,128)(2,1)S(1)}, u32[]{:S(2)}, u32[]{:S(2)}) collective-permute-start(bf16[64,1792]{1,0:T(8,128)(2,1)S(1)} %get-tuple-element.70), channel_id=1, source_target_pairs={{0,6},{1,7},{2,4},{3,5},{4,2},{5,3},{6,0},{7,1},{8,14},{9,15},{10,... | collective-permute-start | bytes 688136 | tf_op jit(solution)/shard_map/ppermute | solution.py:29
  38.0 0.8 collective-permute-done.5.refs_1_
  38.9 1.3 %shard_map.167 = (bf16[256,640]{1,0:T(8,128)(2,1)S(1)}, bf16[256,640]{1,0:T(8,128)(2,1)S(1)}, f32[256,128]{1,0:T(8,128)S(1)}, f32[256,128]{1,0:T(8,128)S(1)}, f3...) custom-call(bf16[16,36864]{1,0:T(8,128)(2,1)S(1)} %copy-done.14, bf16[4,4,4736]{2,1,0:T(4,128)(2,1)S(1)} %collective-permute-done.5.refs_1_, ...), custom_call_target="tpu_custom_call" | custom-call | flops 6039797760 | bytes 1634304 | tf_op jit(solution)/shard_map/pallas_call | solution.py:41
  40.2 2.5 %shard_map.171 = (f32[256,128]{1,0:T(8,128)S(1)}, f32[256,128]{1,0:T(8,128)S(1)}, f32[256,512]{1,0:T(8,128)S(1)}, f32[256,640]{1,0:T(8,128)S(1)}) custom-call(bf16[256,640]{1,0:T(8,128)(2,1)S(1)} %get-tuple-element.56.refs_0_, bf16[256,640]{1,0:T(8,128)(2,1)S(1)} %get-tuple-element.57.refs_1_, f32[256,128]{1,0:T(8,128)S(1)} %get-tuple-element.71.refs_2_, ...), custom_call_target="tpu_custom_call" | custom-call | flops 6039797760 | bytes 4456448 | tf_op jit(solution)/shard_map/pallas_call | solution.py:41
  42.7 2.3 %collective-permute-done.12.refs_12_ = bf16[64,1792]{1,0:T(8,128)(2,1)S(1)} collective-permute-done((bf16[64,1792]{1,0:T(8,128)(2,1)S(1)}, bf16[64,1792]{1,0:T(8,128)(2,1)S(1)}, u32[]{:S(2)}, u32[]{:S(2)}) %collective-permute-start.12) | collective-permute-done | bytes 229408 | tf_op jit(solution)/shard_map/ppermute | solution.py:29
  45.0 0.5 collective-permute-start.15
  45.5 0.5 collective-permute-start.17
  46.0 0.5 collective-permute-done.14.refs_13_
  47.6 3.7 %shard_map.172 = (f32[16,5120]{1,0:T(8,128)S(1)}, bf16[16,5120]{1,0:T(8,128)(2,1)S(1)}) custom-call(bf16[256,640]{1,0:T(8,128)(2,1)S(1)} %get-tuple-element.56.refs_0_, bf16[256,640]{1,0:T(8,128)(2,1)S(1)} %get-tuple-element.57.refs_1_, f32[256,128]{1,0:T(8,128)S(1)} %get-tuple-element.80.refs_2_, f32[256,128]{1,0:T(8,128)S(1)} %get-tuple-element.81.refs_3_, ...), custom_call_target="tpu_custom_call" | custom-call | flops 939524096 | bytes 15597568 | tf_op jit(solution)/shard_map/pallas_call | solution.py:41
  51.5 1.2 %collective-permute-done.18.away_ref = bf16[16,5120]{1,0:T(8,128)(2,1)S(1)} collective-permute-done((bf16[16,5120]{1,0:T(8,128)(2,1)S(1)}, bf16[16,5120]{1,0:T(8,128)(2,1)S(1)}, u32[]{:S(2)}, u32[]{:S(2)}) %collective-permute-start.18) | collective-permute-done | bytes 163872 | tf_op jit(solution)/shard_map/ppermute | solution.py:29
  52.8 0.6 collective-permute-start.19
  53.4 1.5 %collective-permute-start.20 = (bf16[4,5120]{1,0:T(4,128)(2,1)S(1)}, bf16[4,5120]{1,0:T(4,128)(2,1)S(1)}, u32[]{:S(2)}, u32[]{:S(2)}) collective-permute-start(bf16[4,5120]{1,0:T(4,128)(2,1)S(1)} %get-tuple-element.92), channel_id=1, source_target_pairs={{0,4},{1,5},{2,6},{3,7},{4,0},{5,1},{6,2},{7,3},{8,12},{9,13},{10,... | collective-permute-start | bytes 122888 | tf_op jit(solution)/shard_map/ppermute | solution.py:29
  54.9 1.4 %collective-permute-start.21 = (bf16[4,5120]{1,0:T(4,128)(2,1)S(1)}, bf16[4,5120]{1,0:T(4,128)(2,1)S(1)}, u32[]{:S(2)}, u32[]{:S(2)}) collective-permute-start(bf16[4,5120]{1,0:T(4,128)(2,1)S(1)} %get-tuple-element.93), channel_id=1, source_target_pairs={{0,6},{1,7},{2,4},{3,5},{4,2},{5,3},{6,0},{7,1},{8,14},{9,15},{10,... | collective-permute-start | bytes 122888 | tf_op jit(solution)/shard_map/ppermute | solution.py:29
  56.3 0.5 collective-permute-done.19.refs_0_
  56.8 0.5 collective-permute-done.20.refs_1_
  57.4 2.4 %collective-permute-done.21.refs_2_ = bf16[4,5120]{1,0:T(4,128)(2,1)S(1)} collective-permute-done((bf16[4,5120]{1,0:T(4,128)(2,1)S(1)}, bf16[4,5120]{1,0:T(4,128)(2,1)S(1)}, u32[]{:S(2)}, u32[]{:S(2)}) %collective-permute-start.21) | collective-permute-done | bytes 40992 | tf_op jit(solution)/shard_map/ppermute | solution.py:29
  59.8 0.7 shard_map.174
  60.5 1.0 collective-permute-start.22
  61.4 2.7 %collective-permute-start.23 = (bf16[4,5248]{1,0:T(4,128)(2,1)S(1)}, bf16[4,5248]{1,0:T(4,128)(2,1)S(1)}, u32[]{:S(2)}, u32[]{:S(2)}) collective-permute-start(bf16[4,5248]{1,0:T(4,128)(2,1)S(1)} %get-tuple-element.95.refs_0_), channel_id=1, source_target_pairs={{0,16},{8,24},{16,0},{24,8},{1,17},{9,25},{17,1},{25,9},{2,18},{10... | collective-permute-start | bytes 125960 | tf_op jit(solution)/shard_map/ppermute | solution.py:29
  64.1 1.2 %collective-permute-start.24 = (bf16[4,5248]{1,0:T(4,128)(2,1)S(1)}, bf16[4,5248]{1,0:T(4,128)(2,1)S(1)}, u32[]{:S(2)}, u32[]{:S(2)}) collective-permute-start(bf16[4,5248]{1,0:T(4,128)(2,1)S(1)} %get-tuple-element.95.refs_0_), channel_id=1, source_target_pairs={{0,24},{8,16},{16,8},{24,0},{1,25},{9,17},{17,9},{25,1},{2,26},{10... | collective-permute-start | bytes 125960 | tf_op jit(solution)/shard_map/ppermute | solution.py:29
  65.3 1.8 %collective-permute-done.23.refs_2_ = bf16[4,5248]{1,0:T(4,128)(2,1)S(1)} collective-permute-done((bf16[4,5248]{1,0:T(4,128)(2,1)S(1)}, bf16[4,5248]{1,0:T(4,128)(2,1)S(1)}, u32[]{:S(2)}, u32[]{:S(2)}) %collective-permute-start.23) | collective-permute-done | bytes 42016 | tf_op jit(solution)/shard_map/ppermute | solution.py:29
  67.2 2.8 %collective-permute-done.24.refs_3_ = bf16[4,5248]{1,0:T(4,128)(2,1)S(1)} collective-permute-done((bf16[4,5248]{1,0:T(4,128)(2,1)S(1)}, bf16[4,5248]{1,0:T(4,128)(2,1)S(1)}, u32[]{:S(2)}, u32[]{:S(2)}) %collective-permute-start.24) | collective-permute-done | bytes 42016 | tf_op jit(solution)/shard_map/ppermute | solution.py:29
  70.0 1.6 %collective-permute-start.25 = (bf16[16,5248]{1,0:T(8,128)(2,1)S(1)}, bf16[16,5248]{1,0:T(8,128)(2,1)S(1)}, u32[]{:S(2)}, u32[]{:S(2)}) collective-permute-start(bf16[16,5248]{1,0:T(8,128)(2,1)S(1)} %shard_map.175.refs_0_), channel_id=1, source_target_pairs={{0,2},{1,3},{2,0},{3,1},{4,6},{5,7},{6,4},{7,5},{8,10},{9,11},{10,... | collective-permute-start | bytes 503816 | tf_op jit(solution)/shard_map/ppermute | solution.py:29
  71.6 0.5 collective-permute-start.26
  72.1 1.5 %collective-permute-start.27 = (bf16[16,5248]{1,0:T(8,128)(2,1)S(1)}, bf16[16,5248]{1,0:T(8,128)(2,1)S(1)}, u32[]{:S(2)}, u32[]{:S(2)}) collective-permute-start(bf16[16,5248]{1,0:T(8,128)(2,1)S(1)} %shard_map.175.refs_0_), channel_id=1, source_target_pairs={{0,6},{1,7},{2,4},{3,5},{4,2},{5,3},{6,0},{7,1},{8,14},{9,15},{10,... | collective-permute-start | bytes 503816 | tf_op jit(solution)/shard_map/ppermute | solution.py:29
  73.6 2.0 %collective-permute-done.25.refs_1_ = bf16[16,5248]{1,0:T(8,128)(2,1)S(1)} collective-permute-done((bf16[16,5248]{1,0:T(8,128)(2,1)S(1)}, bf16[16,5248]{1,0:T(8,128)(2,1)S(1)}, u32[]{:S(2)}, u32[]{:S(2)}) %collective-permute-start.25) | collective-permute-done | bytes 167968 | tf_op jit(solution)/shard_map/ppermute | solution.py:29
  75.5 3.2 %collective-permute-done.26.refs_2_ = bf16[16,5248]{1,0:T(8,128)(2,1)S(1)} collective-permute-done((bf16[16,5248]{1,0:T(8,128)(2,1)S(1)}, bf16[16,5248]{1,0:T(8,128)(2,1)S(1)}, u32[]{:S(2)}, u32[]{:S(2)}) %collective-permute-start.26) | collective-permute-done | bytes 167968 | tf_op jit(solution)/shard_map/ppermute | solution.py:29
  78.7 0.5 collective-permute-start.31
  79.2 0.9 collective-permute-done.30.refs_6_
  80.4 3.1 %shard_map.176 = (f32[64,5120]{1,0:T(8,128)S(1)}, bf16[64,5120]{1,0:T(8,128)(2,1)S(1)}) custom-call(s32[2]{0:T(128)S(1)} %pad_add_fusion.pos, bf16[16,5248]{1,0:T(8,128)(2,1)S(1)} %shard_map.175.refs_0_, bf16[16,5248]{1,0:T(8,128)(2,1)S(1)} %collective-permute-done.25.refs_1_, bf16[16,5248]{1,0:T(8,128)(2,1)S(1)} %collective-permute-done.26.refs_2_, ...), custom_call_target="tpu_custom_call" | custom-call | flops 1509949440 | bytes 13139976 | tf_op jit(solution)/shard_map/pallas_call | solution.py:41
  83.8 1.8 %collective-permute-done.32.away_ref = bf16[64,5120]{1,0:T(8,128)(2,1)S(1)} collective-permute-done((bf16[64,5120]{1,0:T(8,128)(2,1)S(1)}, bf16[64,5120]{1,0:T(8,128)(2,1)S(1)}, u32[]{:S(2)}, u32[]{:S(2)}) %collective-permute-start.32) | collective-permute-done | bytes 655392 | tf_op jit(solution)/shard_map/ppermute | solution.py:29
  85.8 0.6 collective-permute-start.33
  86.4 0.9 collective-permute-start.34
  87.3 2.1 %collective-permute-start.35 = (bf16[16,5120]{1,0:T(8,128)(2,1)S(1)}, bf16[16,5120]{1,0:T(8,128)(2,1)S(1)}, u32[]{:S(2)}, u32[]{:S(2)}) collective-permute-start(bf16[16,5120]{1,0:T(8,128)(2,1)S(1)} %get-tuple-element.101), channel_id=1, source_target_pairs={{0,6},{1,7},{2,4},{3,5},{4,2},{5,3},{6,0},{7,1},{8,14},{9,15},{10,... | collective-permute-start | bytes 491528 | tf_op jit(solution)/shard_map/ppermute | solution.py:29
  89.3 3.5 %collective-permute-done.33 = bf16[16,5120]{1,0:T(8,128)(2,1)S(1)} collective-permute-done((bf16[16,5120]{1,0:T(8,128)(2,1)S(1)}, bf16[16,5120]{1,0:T(8,128)(2,1)S(1)}, u32[]{:S(2)}, u32[]{:S(2)}) %collective-permute-start.33) | collective-permute-done | bytes 163872 | tf_op jit(solution)/shard_map/ppermute | solution.py:29
  92.9 0.4 collective-permute-done.34
  93.3 2.7 %collective-permute-done.35 = bf16[16,5120]{1,0:T(8,128)(2,1)S(1)} collective-permute-done((bf16[16,5120]{1,0:T(8,128)(2,1)S(1)}, bf16[16,5120]{1,0:T(8,128)(2,1)S(1)}, u32[]{:S(2)}, u32[]{:S(2)}) %collective-permute-start.35) | collective-permute-done | bytes 163872 | tf_op jit(solution)/shard_map/ppermute | solution.py:29
  96.2 1.8 %collective-permute-start.37 = (bf16[4,5120]{1,0:T(4,128)(2,1)S(1)}, bf16[4,5120]{1,0:T(4,128)(2,1)S(1)}, u32[]{:S(2)}, u32[]{:S(2)}) collective-permute-start(bf16[4,5120]{1,0:T(4,128)(2,1)S(1)} %get-tuple-element.114), channel_id=1, source_target_pairs={{0,16},{8,24},{16,0},{24,8},{1,17},{9,25},{17,1},{25,9},{2,18},{10... | collective-permute-start | bytes 122888 | tf_op jit(solution)/shard_map/ppermute | solution.py:29
  98.1 2.5 %collective-permute-start.38 = (bf16[4,5120]{1,0:T(4,128)(2,1)S(1)}, bf16[4,5120]{1,0:T(4,128)(2,1)S(1)}, u32[]{:S(2)}, u32[]{:S(2)}) collective-permute-start(bf16[4,5120]{1,0:T(4,128)(2,1)S(1)} %get-tuple-element.113), channel_id=1, source_target_pairs={{0,24},{8,16},{16,8},{24,0},{1,25},{9,17},{17,9},{25,1},{2,26},{10... | collective-permute-start | bytes 122888 | tf_op jit(solution)/shard_map/ppermute | solution.py:29
  100.6 0.6 collective-permute-done.37
  101.2 2.7 %collective-permute-done.38 = bf16[4,5120]{1,0:T(4,128)(2,1)S(1)} collective-permute-done((bf16[4,5120]{1,0:T(4,128)(2,1)S(1)}, bf16[4,5120]{1,0:T(4,128)(2,1)S(1)}, u32[]{:S(2)}, u32[]{:S(2)}) %collective-permute-start.38) | collective-permute-done | bytes 40992 | tf_op jit(solution)/shard_map/ppermute | solution.py:29
  103.9 0.7 fusion.1
  (103 shorter events, 3.6 us)
Async XLA Ops:
  1.6 17.7 %copy-start.19 = (bf16[4,73728]{1,0:T(4,128)(2,1)S(1)}, bf16[4,73728]{1,0:T(4,128)(2,1)}, u32[]{:S(2)}) copy-start(bf16[4,73728]{1,0:T(4,128)(2,1)} %param.19) | copy-start | bytes 1769476
  1.6 12.4 %collective-permute-start.4 = (bf16[16,4608]{1,0:T(8,128)(2,1)S(1)}, bf16[16,4608]{1,0:T(8,128)(2,1)}, u32[]{:S(2)}, u32[]{:S(2)}) collective-permute-start(bf16[16,4608]{1,0:T(8,128)(2,1)S(1)} %constant_dynamic-slice_fusion), channel_id=1, source_target_pairs={{0,16},{8,24},{16,0},{24,8},{1,17},{9,25},{17,1},{25,9},{2,18},{10... | collective-permute-start | bytes 442376 | tf_op jit(solution)/shard_map/ppermute | solution.py:29
  5.7 8.3 %collective-permute-start.3 = (bf16[16,4608]{1,0:T(8,128)(2,1)S(1)}, bf16[16,4608]{1,0:T(8,128)(2,1)S(1)}, u32[]{:S(2)}, u32[]{:S(2)}) collective-permute-start(bf16[16,4608]{1,0:T(8,128)(2,1)S(1)} %constant_dynamic-slice_fusion), channel_id=1, source_target_pairs={{0,8},{8,0},{16,24},{24,16},{1,9},{9,1},{17,25},{25,17},{2,10},{10... | collective-permute-start | bytes 442376 | tf_op jit(solution)/shard_map/ppermute | solution.py:29
  10.0 10.0 %copy-start.18 = (bf16[4,36864]{1,0:T(4,128)(2,1)S(1)}, bf16[4,36864]{1,0:T(4,128)(2,1)}, u32[]{:S(2)}) copy-start(bf16[4,36864]{1,0:T(4,128)(2,1)} %param.17) | copy-start | bytes 884740
  10.1 7.0 %collective-permute-start.2 = (bf16[2,4,4736]{2,1,0:T(4,128)(2,1)S(1)}, bf16[2,4,4736]{2,1,0:T(4,128)(2,1)S(1)}, u32[]{:S(2)}, u32[]{:S(2)}) collective-permute-start(bf16[2,4,4736]{2,1,0:T(4,128)(2,1)S(1)} %pad_maximum_fusion.12), channel_id=1, source_target_pairs={{0,6},{1,7},{2,4},{3,5},{4,2},{5,3},{6,0},{7,1},{8,14},{9,15},{10,... | collective-permute-start | bytes 227336 | tf_op jit(solution)/shard_map/ppermute | solution.py:29
  12.6 6.0 %collective-permute-start.1 = (bf16[2,4,4736]{2,1,0:T(4,128)(2,1)S(1)}, bf16[2,4,4736]{2,1,0:T(4,128)(2,1)S(1)}, u32[]{:S(2)}, u32[]{:S(2)}) collective-permute-start(bf16[2,4,4736]{2,1,0:T(4,128)(2,1)S(1)} %pad_maximum_fusion.11), channel_id=1, source_target_pairs={{0,4},{1,5},{2,6},{3,7},{4,0},{5,1},{6,2},{7,3},{8,12},{9,13},{10,... | collective-permute-start | bytes 227336 | tf_op jit(solution)/shard_map/ppermute | solution.py:29
  13.3 5.3 %collective-permute-start = (bf16[2,4,4736]{2,1,0:T(4,128)(2,1)S(1)}, bf16[2,4,4736]{2,1,0:T(4,128)(2,1)S(1)}, u32[]{:S(2)}, u32[]{:S(2)}) collective-permute-start(bf16[2,4,4736]{2,1,0:T(4,128)(2,1)S(1)} %pad_maximum_fusion.10), channel_id=1, source_target_pairs={{0,2},{1,3},{2,0},{3,1},{4,6},{5,7},{6,4},{7,5},{8,10},{9,11},{10,... | collective-permute-start | bytes 227336 | tf_op jit(solution)/shard_map/ppermute | solution.py:29
  13.9 11.0 %copy-start.4 = (bf16[2,4,4736]{2,1,0:T(4,128)(2,1)}, bf16[2,4,4736]{2,1,0:T(4,128)(2,1)S(1)}, u32[]{:S(2)}) copy-start(bf16[2,4,4736]{2,1,0:T(4,128)(2,1)S(1)} %pad_maximum_fusion.9.refs_2_) | copy-start | bytes 227332
  14.0 7.8 %collective-permute-start.6 = (bf16[16,4608]{1,0:T(8,128)(2,1)}, bf16[16,4608]{1,0:T(8,128)(2,1)S(1)}, u32[]{:S(2)}, u32[]{:S(2)}) collective-permute-start(bf16[16,4608]{1,0:T(8,128)(2,1)} %collective-permute-done.4), channel_id=1, source_target_pairs={{0,8},{8,0},{16,24},{24,16},{1,9},{9,1},{17,25},{25,17},{2,10},{10... | collective-permute-start | bytes 442376 | tf_op jit(solution)/shard_map/ppermute | solution.py:29
  15.5 17.3 %collective-permute-start.7 = (bf16[32,4608]{1,0:T(8,128)(2,1)S(1)}, bf16[32,4608]{1,0:T(8,128)(2,1)S(1)}, u32[]{:S(2)}, u32[]{:S(2)}) collective-permute-start(bf16[32,4608]{1,0:T(8,128)(2,1)S(1)} %constant_dynamic-update-slice_fusion.refs_0_.refs_6_), channel_id=1, source_target_pairs={{0,2},{1,3},{2,0},{3,1},{4,6},{5,7},{6,4},{7,5},{8,10},{9,11},{10,... | collective-permute-start | bytes 884744 | tf_op jit(solution)/shard_map/ppermute | solution.py:29
  17.1 7.9 %copy-start.8 = (bf16[2,4,4736]{2,1,0:T(4,128)(2,1)}, bf16[2,4,4736]{2,1,0:T(4,128)(2,1)S(1)}, u32[]{:S(2)}) copy-start(bf16[2,4,4736]{2,1,0:T(4,128)(2,1)S(1)} %collective-permute-done.2.refs_5_) | copy-start | bytes 227332
  17.1 15.8 %collective-permute-start.8 = (bf16[32,4608]{1,0:T(8,128)(2,1)S(1)}, bf16[32,4608]{1,0:T(8,128)(2,1)S(1)}, u32[]{:S(2)}, u32[]{:S(2)}) collective-permute-start(bf16[32,4608]{1,0:T(8,128)(2,1)S(1)} %constant_dynamic-update-slice_fusion.refs_0_.refs_6_), channel_id=1, source_target_pairs={{0,4},{1,5},{2,6},{3,7},{4,0},{5,1},{6,2},{7,3},{8,12},{9,13},{10,... | collective-permute-start | bytes 884744 | tf_op jit(solution)/shard_map/ppermute | solution.py:29
  18.6 14.2 %collective-permute-start.9 = (bf16[32,4608]{1,0:T(8,128)(2,1)S(1)}, bf16[32,4608]{1,0:T(8,128)(2,1)S(1)}, u32[]{:S(2)}, u32[]{:S(2)}) collective-permute-start(bf16[32,4608]{1,0:T(8,128)(2,1)S(1)} %constant_dynamic-update-slice_fusion.refs_0_.refs_6_), channel_id=1, source_target_pairs={{0,6},{1,7},{2,4},{3,5},{4,2},{5,3},{6,0},{7,1},{8,14},{9,15},{10,... | collective-permute-start | bytes 884744 | tf_op jit(solution)/shard_map/ppermute | solution.py:29
  21.9 13.4 %collective-permute-start.10 = (bf16[64,1792]{1,0:T(8,128)(2,1)S(1)}, bf16[64,1792]{1,0:T(8,128)(2,1)S(1)}, u32[]{:S(2)}, u32[]{:S(2)}) collective-permute-start(bf16[64,1792]{1,0:T(8,128)(2,1)S(1)} %get-tuple-element.66), channel_id=1, source_target_pairs={{0,2},{1,3},{2,0},{3,1},{4,6},{5,7},{6,4},{7,5},{8,10},{9,11},{10,... | collective-permute-start | bytes 688136 | tf_op jit(solution)/shard_map/ppermute | solution.py:29
  24.2 11.4 %collective-permute-start.11 = (bf16[64,1792]{1,0:T(8,128)(2,1)S(1)}, bf16[64,1792]{1,0:T(8,128)(2,1)S(1)}, u32[]{:S(2)}, u32[]{:S(2)}) collective-permute-start(bf16[64,1792]{1,0:T(8,128)(2,1)S(1)} %get-tuple-element.67), channel_id=1, source_target_pairs={{0,4},{1,5},{2,6},{3,7},{4,0},{5,1},{6,2},{7,3},{8,12},{9,13},{10,... | collective-permute-start | bytes 688136 | tf_op jit(solution)/shard_map/ppermute | solution.py:29
  24.9 10.9 %slice-start.3 = ((bf16[2,4,4736]{2,1,0:T(4,128)(2,1)}), bf16[1,4,4736]{2,1,0:T(4,128)(2,1)S(1)}, s32[]{:S(2)}) async-start(bf16[2,4,4736]{2,1,0:T(4,128)(2,1)} %copy-done.4), calls=%async_computation.3 | async-start | bytes 75776 | tf_op jit(solution)/shard_map/slice | solution.py:429
  24.9 10.9 %slice-start.6 = ((bf16[2,4,4736]{2,1,0:T(4,128)(2,1)}), bf16[1,4,4736]{2,1,0:T(4,128)(2,1)S(1)}, s32[]{:S(2)}) async-start(bf16[2,4,4736]{2,1,0:T(4,128)(2,1)} %copy-done.12), calls=%async_computation.6 | async-start | bytes 75776 | tf_op jit(solution)/shard_map/slice | solution.py:429
  24.9 10.9 %slice-start.5 = ((bf16[2,4,4736]{2,1,0:T(4,128)(2,1)}), bf16[1,4,4736]{2,1,0:T(4,128)(2,1)S(1)}, s32[]{:S(2)}) async-start(bf16[2,4,4736]{2,1,0:T(4,128)(2,1)} %copy-done.10), calls=%async_computation.5 | async-start | bytes 75776 | tf_op jit(solution)/shard_map/slice | solution.py:429
  25.0 10.9 %slice-start.4 = ((bf16[2,4,4736]{2,1,0:T(4,128)(2,1)}), bf16[1,4,4736]{2,1,0:T(4,128)(2,1)S(1)}, s32[]{:S(2)}) async-start(bf16[2,4,4736]{2,1,0:T(4,128)(2,1)} %copy-done.8), calls=%async_computation.4 | async-start | bytes 75776 | tf_op jit(solution)/shard_map/slice | solution.py:429
  25.0 13.9 %copy-start.5 = (bf16[2,4,4736]{2,1,0:T(4,128)(2,1)S(1)}, bf16[2,4,4736]{2,1,0:T(4,128)(2,1)}, u32[]{:S(2)}) copy-start(bf16[2,4,4736]{2,1,0:T(4,128)(2,1)} %copy-done.4) | copy-start | bytes 227332
  25.0 13.9 %copy-start.9 = (bf16[2,4,4736]{2,1,0:T(4,128)(2,1)S(1)}, bf16[2,4,4736]{2,1,0:T(4,128)(2,1)}, u32[]{:S(2)}) copy-start(bf16[2,4,4736]{2,1,0:T(4,128)(2,1)} %copy-done.8) | copy-start | bytes 227332
  25.0 13.9 %copy-start.11 = (bf16[2,4,4736]{2,1,0:T(4,128)(2,1)S(1)}, bf16[2,4,4736]{2,1,0:T(4,128)(2,1)}, u32[]{:S(2)}) copy-start(bf16[2,4,4736]{2,1,0:T(4,128)(2,1)} %copy-done.10) | copy-start | bytes 227332
  25.0 13.8 %copy-start.13 = (bf16[2,4,4736]{2,1,0:T(4,128)(2,1)S(1)}, bf16[2,4,4736]{2,1,0:T(4,128)(2,1)}, u32[]{:S(2)}) copy-start(bf16[2,4,4736]{2,1,0:T(4,128)(2,1)} %copy-done.12) | copy-start | bytes 227332
  25.0 13.8 %copy-start.14 = (bf16[16,36864]{1,0:T(8,128)(2,1)S(1)}, bf16[16,36864]{1,0:T(8,128)(2,1)}, u32[]{:S(2)}) copy-start(bf16[16,36864]{1,0:T(8,128)(2,1)} %refs_0_.1) | copy-start | bytes 3538948
  35.7 4.4 %collective-permute-start.13 = (bf16[128,4608]{1,0:T(8,128)(2,1)S(1)}, bf16[128,4608]{1,0:T(8,128)(2,1)S(1)}, u32[]{:S(2)}, u32[]{:S(2)}) collective-permute-start(bf16[128,4608]{1,0:T(8,128)(2,1)S(1)} %shard_map.170), channel_id=1, source_target_pairs={{0,1},{1,0},{2,3},{3,2},{4,5},{5,4},{6,7},{7,6},{8,9},{9,8},{10,11... | collective-permute-start | bytes 3538952 | tf_op jit(solution)/shard_map/ppermute | solution.py:29
  36.0 2.9 %collective-permute-start.5 = (bf16[4,4,4736]{2,1,0:T(4,128)(2,1)S(1)}, bf16[4,4,4736]{2,1,0:T(4,128)(2,1)S(1)}, u32[]{:S(2)}, u32[]{:S(2)}) collective-permute-start(bf16[4,4,4736]{2,1,0:T(4,128)(2,1)S(1)} %pad_maximum_fusion), channel_id=1, source_target_pairs={{0,1},{1,0},{2,3},{3,2},{4,5},{5,4},{6,7},{7,6},{8,9},{9,8},{10,11... | collective-permute-start | bytes 454664 | tf_op jit(solution)/shard_map/ppermute | solution.py:29
  36.5 8.5 %collective-permute-start.12 = (bf16[64,1792]{1,0:T(8,128)(2,1)S(1)}, bf16[64,1792]{1,0:T(8,128)(2,1)S(1)}, u32[]{:S(2)}, u32[]{:S(2)}) collective-permute-start(bf16[64,1792]{1,0:T(8,128)(2,1)S(1)} %get-tuple-element.70), channel_id=1, source_target_pairs={{0,6},{1,7},{2,4},{3,5},{4,2},{5,3},{6,0},{7,1},{8,14},{9,15},{10,... | collective-permute-start | bytes 688136 | tf_op jit(solution)/shard_map/ppermute | solution.py:29
  40.1 7.3 %slice-start = ((s8[10485760]{0:T(1024)(128)(4,1)}), s8[4194304]{0:T(1024)(128)(4,1)S(1)}, s32[]{:S(2)}) async-start(s8[10485760]{0:T(1024)(128)(4,1)} %bitcast.18), calls=%async_computation | async-start | bytes 8388608
  40.2 7.3 %slice-start.1 = ((s8[10485760]{0:T(1024)(128)(4,1)}), s8[4194304]{0:T(1024)(128)(4,1)S(1)}, s32[]{:S(2)}) async-start(s8[10485760]{0:T(1024)(128)(4,1)} %bitcast.18), calls=%async_computation.1 | async-start | bytes 8388608
  40.2 7.3 %slice-start.2 = ((s8[10485760]{0:T(1024)(128)(4,1)}), s8[2097152]{0:T(1024)(128)(4,1)S(1)}, s32[]{:S(2)}) async-start(s8[10485760]{0:T(1024)(128)(4,1)} %bitcast.18), calls=%async_computation.2 | async-start | bytes 4194304
  40.2 7.3 %copy-start.3 = (bf16[8,512,128]{2,1,0:T(8,128)(2,1)S(1)}, bf16[8,512,128]{2,1,0:T(8,128)(2,1)}, u32[]{:S(2)}) copy-start(bf16[8,512,128]{2,1,0:T(8,128)(2,1)} %refs_7_.1) | copy-start | bytes 3145732
  40.2 7.3 %copy-start.6 = (bf16[256,256]{1,0:T(8,128)(2,1)S(1)}, bf16[256,256]{1,0:T(8,128)(2,1)}, u32[]{:S(2)}) copy-start(bf16[256,256]{1,0:T(8,128)(2,1)} %constant.65.clone.refs_6_) | copy-start | bytes 393220
  45.0 1.5 %collective-permute-start.14 = (bf16[64,1792]{1,0:T(8,128)(2,1)S(1)}, bf16[64,1792]{1,0:T(8,128)(2,1)S(1)}, u32[]{:S(2)}, u32[]{:S(2)}) collective-permute-start(bf16[64,1792]{1,0:T(8,128)(2,1)S(1)} %get-tuple-element.84.refs_9_), channel_id=1, source_target_pairs={{0,1},{1,0},{2,3},{3,2},{4,5},{5,4},{6,7},{7,6},{8,9},{9,8},{10,11... | collective-permute-start | bytes 688136 | tf_op jit(solution)/shard_map/ppermute | solution.py:29
  45.0 1.8 %collective-permute-start.15 = (bf16[64,1792]{1,0:T(8,128)(2,1)S(1)}, bf16[64,1792]{1,0:T(8,128)(2,1)S(1)}, u32[]{:S(2)}, u32[]{:S(2)}) collective-permute-start(bf16[64,1792]{1,0:T(8,128)(2,1)S(1)} %collective-permute-done.10.refs_10_), channel_id=1, source_target_pairs={{0,1},{1,0},{2,3},{3,2},{4,5},{5,4},{6,7},{7,6},{8,9},{9,8},{10,11... | collective-permute-start | bytes 688136 | tf_op jit(solution)/shard_map/ppermute | solution.py:29
  45.5 1.6 %collective-permute-start.16 = (bf16[64,1792]{1,0:T(8,128)(2,1)S(1)}, bf16[64,1792]{1,0:T(8,128)(2,1)S(1)}, u32[]{:S(2)}, u32[]{:S(2)}) collective-permute-start(bf16[64,1792]{1,0:T(8,128)(2,1)S(1)} %collective-permute-done.11.refs_11_), channel_id=1, source_target_pairs={{0,1},{1,0},{2,3},{3,2},{4,5},{5,4},{6,7},{7,6},{8,9},{9,8},{10,11... | collective-permute-start | bytes 688136 | tf_op jit(solution)/shard_map/ppermute | solution.py:29
  45.5 2.0 %collective-permute-start.17 = (bf16[64,1792]{1,0:T(8,128)(2,1)S(1)}, bf16[64,1792]{1,0:T(8,128)(2,1)S(1)}, u32[]{:S(2)}, u32[]{:S(2)}) collective-permute-start(bf16[64,1792]{1,0:T(8,128)(2,1)S(1)} %collective-permute-done.12.refs_12_), channel_id=1, source_target_pairs={{0,1},{1,0},{2,3},{3,2},{4,5},{5,4},{6,7},{7,6},{8,9},{9,8},{10,11... | collective-permute-start | bytes 688136 | tf_op jit(solution)/shard_map/ppermute | solution.py:29
  47.5 8.8 %copy-start.20 = (bf16[5120]{0:T(1024)(128)(2,1)S(1)}, bf16[5120]{0:T(1024)(128)(2,1)}, u32[]{:S(2)}) copy-start(bf16[5120]{0:T(1024)(128)(2,1)} %param.25) | copy-start | bytes 30724
  47.5 12.3 %copy-start.7 = (bf16[4,5120]{1,0:T(4,128)(2,1)S(1)}, bf16[4,5120]{1,0:T(4,128)(2,1)}, u32[]{:S(2)}) copy-start(bf16[4,5120]{1,0:T(4,128)(2,1)} %hidden_ref.1) | copy-start | bytes 122884
  47.5 12.3 %copy-start.15 = (s32[4,6]{1,0:T(4,128)S(1)}, s32[4,6]{1,0:T(4,128)}, u32[]{:S(2)}) copy-start(s32[4,6]{1,0:T(4,128)} %ids_ref.1) | copy-start | bytes 292
  47.5 12.3 %copy-start.16 = (bf16[4,6]{1,0:T(4,128)(2,1)S(1)}, bf16[4,6]{1,0:T(4,128)(2,1)}, u32[]{:S(2)}) copy-start(bf16[4,6]{1,0:T(4,128)(2,1)} %weight_ref.1) | copy-start | bytes 148
  47.6 32.8 %copy-start = (bf16[1,5120,384]{2,1,0:T(8,128)(2,1)S(1)}, bf16[1,5120,384]{2,1,0:T(8,128)(2,1)}, u32[]{:S(2)}) copy-start(bf16[1,5120,384]{2,1,0:T(8,128)(2,1)} %refs_8_.3) | copy-start | bytes 11796484
  47.6 32.8 %copy-start.1 = (bf16[1,5120,384]{2,1,0:T(8,128)(2,1)S(1)}, bf16[1,5120,384]{2,1,0:T(8,128)(2,1)}, u32[]{:S(2)}) copy-start(bf16[1,5120,384]{2,1,0:T(8,128)(2,1)} %refs_9_.1) | copy-start | bytes 11796484
  47.6 32.8 %copy-start.2 = (bf16[1,384,5120]{2,1,0:T(8,128)(2,1)S(1)}, bf16[1,384,5120]{2,1,0:T(8,128)(2,1)}, u32[]{:S(2)}) copy-start(bf16[1,384,5120]{2,1,0:T(8,128)(2,1)} %refs_10_.1) | copy-start | bytes 11796484
  51.3 1.4 %collective-permute-start.18 = (bf16[16,5120]{1,0:T(8,128)(2,1)S(1)}, bf16[16,5120]{1,0:T(8,128)(2,1)S(1)}, u32[]{:S(2)}, u32[]{:S(2)}) collective-permute-start(bf16[16,5120]{1,0:T(8,128)(2,1)S(1)} %get-tuple-element.89), channel_id=1, source_target_pairs={{0,1},{1,0},{2,3},{3,2},{4,5},{5,4},{6,7},{7,6},{8,9},{9,8},{10,11... | collective-permute-start | bytes 491528 | tf_op jit(solution)/shard_map/ppermute | solution.py:29
  52.8 4.1 %collective-permute-start.19 = (bf16[4,5120]{1,0:T(4,128)(2,1)S(1)}, bf16[4,5120]{1,0:T(4,128)(2,1)S(1)}, u32[]{:S(2)}, u32[]{:S(2)}) collective-permute-start(bf16[4,5120]{1,0:T(4,128)(2,1)S(1)} %get-tuple-element.91), channel_id=1, source_target_pairs={{0,2},{1,3},{2,0},{3,1},{4,6},{5,7},{6,4},{7,5},{8,10},{9,11},{10,... | collective-permute-start | bytes 122888 | tf_op jit(solution)/shard_map/ppermute | solution.py:29
  53.4 4.0 %collective-permute-start.20 = (bf16[4,5120]{1,0:T(4,128)(2,1)S(1)}, bf16[4,5120]{1,0:T(4,128)(2,1)S(1)}, u32[]{:S(2)}, u32[]{:S(2)}) collective-permute-start(bf16[4,5120]{1,0:T(4,128)(2,1)S(1)} %get-tuple-element.92), channel_id=1, source_target_pairs={{0,4},{1,5},{2,6},{3,7},{4,0},{5,1},{6,2},{7,3},{8,12},{9,13},{10,... | collective-permute-start | bytes 122888 | tf_op jit(solution)/shard_map/ppermute | solution.py:29
  54.9 4.9 %collective-permute-start.21 = (bf16[4,5120]{1,0:T(4,128)(2,1)S(1)}, bf16[4,5120]{1,0:T(4,128)(2,1)S(1)}, u32[]{:S(2)}, u32[]{:S(2)}) collective-permute-start(bf16[4,5120]{1,0:T(4,128)(2,1)S(1)} %get-tuple-element.93), channel_id=1, source_target_pairs={{0,6},{1,7},{2,4},{3,5},{4,2},{5,3},{6,0},{7,1},{8,14},{9,15},{10,... | collective-permute-start | bytes 122888 | tf_op jit(solution)/shard_map/ppermute | solution.py:29
  60.5 4.9 %collective-permute-start.22 = (bf16[4,5248]{1,0:T(4,128)(2,1)S(1)}, bf16[4,5248]{1,0:T(4,128)(2,1)S(1)}, u32[]{:S(2)}, u32[]{:S(2)}) collective-permute-start(bf16[4,5248]{1,0:T(4,128)(2,1)S(1)} %get-tuple-element.95.refs_0_), channel_id=1, source_target_pairs={{0,8},{8,0},{16,24},{24,16},{1,9},{9,1},{17,25},{25,17},{2,10},{10... | collective-permute-start | bytes 125960 | tf_op jit(solution)/shard_map/ppermute | solution.py:29
  61.4 5.7 %collective-permute-start.23 = (bf16[4,5248]{1,0:T(4,128)(2,1)S(1)}, bf16[4,5248]{1,0:T(4,128)(2,1)S(1)}, u32[]{:S(2)}, u32[]{:S(2)}) collective-permute-start(bf16[4,5248]{1,0:T(4,128)(2,1)S(1)} %get-tuple-element.95.refs_0_), channel_id=1, source_target_pairs={{0,16},{8,24},{16,0},{24,8},{1,17},{9,25},{17,1},{25,9},{2,18},{10... | collective-permute-start | bytes 125960 | tf_op jit(solution)/shard_map/ppermute | solution.py:29
  64.1 5.8 %collective-permute-start.24 = (bf16[4,5248]{1,0:T(4,128)(2,1)S(1)}, bf16[4,5248]{1,0:T(4,128)(2,1)S(1)}, u32[]{:S(2)}, u32[]{:S(2)}) collective-permute-start(bf16[4,5248]{1,0:T(4,128)(2,1)S(1)} %get-tuple-element.95.refs_0_), channel_id=1, source_target_pairs={{0,24},{8,16},{16,8},{24,0},{1,25},{9,17},{17,9},{25,1},{2,26},{10... | collective-permute-start | bytes 125960 | tf_op jit(solution)/shard_map/ppermute | solution.py:29
  70.0 5.5 %collective-permute-start.25 = (bf16[16,5248]{1,0:T(8,128)(2,1)S(1)}, bf16[16,5248]{1,0:T(8,128)(2,1)S(1)}, u32[]{:S(2)}, u32[]{:S(2)}) collective-permute-start(bf16[16,5248]{1,0:T(8,128)(2,1)S(1)} %shard_map.175.refs_0_), channel_id=1, source_target_pairs={{0,2},{1,3},{2,0},{3,1},{4,6},{5,7},{6,4},{7,5},{8,10},{9,11},{10,... | collective-permute-start | bytes 503816 | tf_op jit(solution)/shard_map/ppermute | solution.py:29
  71.6 7.2 %collective-permute-start.26 = (bf16[16,5248]{1,0:T(8,128)(2,1)S(1)}, bf16[16,5248]{1,0:T(8,128)(2,1)S(1)}, u32[]{:S(2)}, u32[]{:S(2)}) collective-permute-start(bf16[16,5248]{1,0:T(8,128)(2,1)S(1)} %shard_map.175.refs_0_), channel_id=1, source_target_pairs={{0,4},{1,5},{2,6},{3,7},{4,0},{5,1},{6,2},{7,3},{8,12},{9,13},{10,... | collective-permute-start | bytes 503816 | tf_op jit(solution)/shard_map/ppermute | solution.py:29
  72.1 6.7 %collective-permute-start.27 = (bf16[16,5248]{1,0:T(8,128)(2,1)S(1)}, bf16[16,5248]{1,0:T(8,128)(2,1)S(1)}, u32[]{:S(2)}, u32[]{:S(2)}) collective-permute-start(bf16[16,5248]{1,0:T(8,128)(2,1)S(1)} %shard_map.175.refs_0_), channel_id=1, source_target_pairs={{0,6},{1,7},{2,4},{3,5},{4,2},{5,3},{6,0},{7,1},{8,14},{9,15},{10,... | collective-permute-start | bytes 503816 | tf_op jit(solution)/shard_map/ppermute | solution.py:29
  73.6 5.7 %collective-permute-start.28 = (bf16[16,5248]{1,0:T(8,128)(2,1)S(1)}, bf16[16,5248]{1,0:T(8,128)(2,1)S(1)}, u32[]{:S(2)}, u32[]{:S(2)}) collective-permute-start(bf16[16,5248]{1,0:T(8,128)(2,1)S(1)} %shard_map.175.refs_0_), channel_id=1, source_target_pairs={{0,1},{1,0},{2,3},{3,2},{4,5},{5,4},{6,7},{7,6},{8,9},{9,8},{10,11... | collective-permute-start | bytes 503816 | tf_op jit(solution)/shard_map/ppermute | solution.py:29
  75.5 3.7 %collective-permute-start.29 = (bf16[16,5248]{1,0:T(8,128)(2,1)S(1)}, bf16[16,5248]{1,0:T(8,128)(2,1)S(1)}, u32[]{:S(2)}, u32[]{:S(2)}) collective-permute-start(bf16[16,5248]{1,0:T(8,128)(2,1)S(1)} %collective-permute-done.25.refs_1_), channel_id=1, source_target_pairs={{0,1},{1,0},{2,3},{3,2},{4,5},{5,4},{6,7},{7,6},{8,9},{9,8},{10,11... | collective-permute-start | bytes 503816 | tf_op jit(solution)/shard_map/ppermute | solution.py:29
  78.7 1.4 %collective-permute-start.30 = (bf16[16,5248]{1,0:T(8,128)(2,1)S(1)}, bf16[16,5248]{1,0:T(8,128)(2,1)S(1)}, u32[]{:S(2)}, u32[]{:S(2)}) collective-permute-start(bf16[16,5248]{1,0:T(8,128)(2,1)S(1)} %collective-permute-done.26.refs_2_), channel_id=1, source_target_pairs={{0,1},{1,0},{2,3},{3,2},{4,5},{5,4},{6,7},{7,6},{8,9},{9,8},{10,11... | collective-permute-start | bytes 503816 | tf_op jit(solution)/shard_map/ppermute | solution.py:29
  78.7 1.6 %collective-permute-start.31 = (bf16[16,5248]{1,0:T(8,128)(2,1)S(1)}, bf16[16,5248]{1,0:T(8,128)(2,1)S(1)}, u32[]{:S(2)}, u32[]{:S(2)}) collective-permute-start(bf16[16,5248]{1,0:T(8,128)(2,1)S(1)} %collective-permute-done.27.refs_3_), channel_id=1, source_target_pairs={{0,1},{1,0},{2,3},{3,2},{4,5},{5,4},{6,7},{7,6},{8,9},{9,8},{10,11... | collective-permute-start | bytes 503816 | tf_op jit(solution)/shard_map/ppermute | solution.py:29
  83.5 2.2 %collective-permute-start.32 = (bf16[64,5120]{1,0:T(8,128)(2,1)S(1)}, bf16[64,5120]{1,0:T(8,128)(2,1)S(1)}, u32[]{:S(2)}, u32[]{:S(2)}) collective-permute-start(bf16[64,5120]{1,0:T(8,128)(2,1)S(1)} %get-tuple-element.97), channel_id=1, source_target_pairs={{0,1},{1,0},{2,3},{3,2},{4,5},{5,4},{6,7},{7,6},{8,9},{9,8},{10,11... | collective-permute-start | bytes 1966088 | tf_op jit(solution)/shard_map/ppermute | solution.py:29
  85.8 7.1 %collective-permute-start.33 = (bf16[16,5120]{1,0:T(8,128)(2,1)S(1)}, bf16[16,5120]{1,0:T(8,128)(2,1)S(1)}, u32[]{:S(2)}, u32[]{:S(2)}) collective-permute-start(bf16[16,5120]{1,0:T(8,128)(2,1)S(1)} %get-tuple-element.99), channel_id=1, source_target_pairs={{0,2},{1,3},{2,0},{3,1},{4,6},{5,7},{6,4},{7,5},{8,10},{9,11},{10,... | collective-permute-start | bytes 491528 | tf_op jit(solution)/shard_map/ppermute | solution.py:29
  86.4 6.9 %collective-permute-start.34 = (bf16[16,5120]{1,0:T(8,128)(2,1)S(1)}, bf16[16,5120]{1,0:T(8,128)(2,1)S(1)}, u32[]{:S(2)}, u32[]{:S(2)}) collective-permute-start(bf16[16,5120]{1,0:T(8,128)(2,1)S(1)} %get-tuple-element.100), channel_id=1, source_target_pairs={{0,4},{1,5},{2,6},{3,7},{4,0},{5,1},{6,2},{7,3},{8,12},{9,13},{10,... | collective-permute-start | bytes 491528 | tf_op jit(solution)/shard_map/ppermute | solution.py:29
  87.3 8.7 %collective-permute-start.35 = (bf16[16,5120]{1,0:T(8,128)(2,1)S(1)}, bf16[16,5120]{1,0:T(8,128)(2,1)S(1)}, u32[]{:S(2)}, u32[]{:S(2)}) collective-permute-start(bf16[16,5120]{1,0:T(8,128)(2,1)S(1)} %get-tuple-element.101), channel_id=1, source_target_pairs={{0,6},{1,7},{2,4},{3,5},{4,2},{5,3},{6,0},{7,1},{8,14},{9,15},{10,... | collective-permute-start | bytes 491528 | tf_op jit(solution)/shard_map/ppermute | solution.py:29
  96.1 4.5 %collective-permute-start.36 = (bf16[4,5120]{1,0:T(4,128)(2,1)S(1)}, bf16[4,5120]{1,0:T(4,128)(2,1)S(1)}, u32[]{:S(2)}, u32[]{:S(2)}) collective-permute-start(bf16[4,5120]{1,0:T(4,128)(2,1)S(1)} %get-tuple-element.112), channel_id=1, source_target_pairs={{0,8},{8,0},{16,24},{24,16},{1,9},{9,1},{17,25},{25,17},{2,10},{10... | collective-permute-start | bytes 122888 | tf_op jit(solution)/shard_map/ppermute | solution.py:29
  96.2 5.0 %collective-permute-start.37 = (bf16[4,5120]{1,0:T(4,128)(2,1)S(1)}, bf16[4,5120]{1,0:T(4,128)(2,1)S(1)}, u32[]{:S(2)}, u32[]{:S(2)}) collective-permute-start(bf16[4,5120]{1,0:T(4,128)(2,1)S(1)} %get-tuple-element.114), channel_id=1, source_target_pairs={{0,16},{8,24},{16,0},{24,8},{1,17},{9,25},{17,1},{25,9},{2,18},{10... | collective-permute-start | bytes 122888 | tf_op jit(solution)/shard_map/ppermute | solution.py:29
  98.1 5.8 %collective-permute-start.38 = (bf16[4,5120]{1,0:T(4,128)(2,1)S(1)}, bf16[4,5120]{1,0:T(4,128)(2,1)S(1)}, u32[]{:S(2)}, u32[]{:S(2)}) collective-permute-start(bf16[4,5120]{1,0:T(4,128)(2,1)S(1)} %get-tuple-element.113), channel_id=1, source_target_pairs={{0,24},{8,16},{16,8},{24,0},{1,25},{9,17},{17,9},{25,1},{2,26},{10... | collective-permute-start | bytes 122888 | tf_op jit(solution)/shard_map/ppermute | solution.py:29
  (3 other events, 19.7 us)

commit v5 on v4

--- a/solution.py
+++ b/solution.py
@@ -310,10 +310,12 @@
 
 
 def spread(rows, members, holders):
-    by_z = [rows] + [swap(rows, "dp", q) for q in range(1, holders)]
+    by_z = [swap(rows, "dp", q) for q in reversed(range(1, holders))]
+    by_z = [rows] + by_z[::-1]
     shape = jax.ShapeDtypeStruct((holders * rows.shape[0], rows.shape[1]), rows.dtype)
     by_z = vmem_call(stack_kernel, shape, by_z, rows.size)
-    blocks = [by_z] + [swap(by_z, "expert", 2 * k) for k in range(1, members // 2)]
+    blocks = [swap(by_z, "expert", 2 * k) for k in reversed(range(1, members // 2))]
+    blocks = [by_z] + blocks[::-1]
     return blocks + [swap(block, "expert", 1) for block in blocks]
 
 
@@ -321,12 +323,12 @@
     chips = members // 2
     rows, width = keep.shape[0] // chips, keep.shape[1]
     total, *sent = halve(keep, away, chips)
-    for k in range(1, chips):
+    for k in reversed(range(1, chips)):
         total = total + swap(sent[k - 1], "expert", 2 * k).astype(jnp.float32)
     total = total.reshape(holders, rows // holders, width)
     sent = total.astype(jnp.bfloat16)
     result = total[0]
-    for q in range(1, holders):
+    for q in reversed(range(1, holders)):
         result = result + swap(sent[q], "dp", q).astype(jnp.float32)
     return result
 
@@ -461,7 +463,7 @@
         4 * rows * prefix_pool.size + 4 * half * out_proj.size,
     )
     own, *sent = halve(keep, away, chips)
-    sums = [swap(sent[k - 1], "expert", 2 * k) for k in range(1, chips)]
+    sums = [swap(sent[k - 1], "expert", 2 * k) for k in reversed(range(1, chips))]
     residual_out, token_rows = vmem_call(
         norm_kernel,
         [

time: 105 us -> 104 us (level)
  transfers between devices with their start and end apart: 39 -> 39, of which waited for: 25 -> 24; matrix products, arithmetic and copies ran while one was open for 5% -> 5% of each run, Pallas kernels for 5% -> 5%
where the time goes in v5:
time: 104 us
  waiting for transfers between devices  42.5 us (41%)
  starting transfers between devices  40.1 us (39%)
  Pallas kernels  13.1 us (13%)
  local copies, waits for them, and re-layouts  4.16 us (4%)
  other arithmetic  2.84 us (3%)
  between operations  1.22 us (1%)
    ppermute x39, waiting for transfers between devices, swap(): return lax.ppermute(value, axis, [(i, i ^ mask) for i in range(size)])  42.5 us
    ppermute x39, starting transfers between devices, swap(): return lax.ppermute(value, axis, [(i, i ^ mask) for i in range(size)])  40.1 us
    pallas_call x11, Pallas kernels, vmem_call(): pl.pallas_call(kernel, out_shape=out_shape, in_specs=specs, out_specs=jax...  13.1 us
  transfers between devices with their start and end apart: 39, of which 24 were waited for; matrix products, arithmetic and copies ran while one was open for 5% of the time, Pallas kernels for 5%

profile of v5, /device:TPU:0, one launch (start us, length us, event | category | flops | bytes accessed | tf_op | source)
XLA Modules:
  0.0 103.9 jit_solution(8796160173768015953)
XLA Ops:
  0.6 0.9 constant_dynamic-slice_fusion
  1.6 4.1 %collective-permute-start.4 = (bf16[16,4608]{1,0:T(8,128)(2,1)S(1)}, bf16[16,4608]{1,0:T(8,128)(2,1)}, u32[]{:S(2)}, u32[]{:S(2)}) collective-permute-start(bf16[16,4608]{1,0:T(8,128)(2,1)S(1)} %constant_dynamic-slice_fusion), channel_id=1, source_target_pairs={{0,16},{8,24},{16,0},{24,8},{1,17},{9,25},{17,1},{25,9},{2,18},{10... | collective-permute-start | bytes 442376 | tf_op jit(solution)/shard_map/ppermute | solution.py:29
  5.7 1.6 %collective-permute-start.3 = (bf16[16,4608]{1,0:T(8,128)(2,1)S(1)}, bf16[16,4608]{1,0:T(8,128)(2,1)S(1)}, u32[]{:S(2)}, u32[]{:S(2)}) collective-permute-start(bf16[16,4608]{1,0:T(8,128)(2,1)S(1)} %constant_dynamic-slice_fusion), channel_id=1, source_target_pairs={{0,8},{8,0},{16,24},{24,16},{1,9},{9,1},{17,25},{25,17},{2,10},{10... | collective-permute-start | bytes 442376 | tf_op jit(solution)/shard_map/ppermute | solution.py:29
  7.3 0.7 iota_compare_fusion
  8.0 0.8 and_reduce_fusion
  8.8 1.0 constant_dynamic-slice_fusion.2
  10.1 2.5 %collective-permute-start.2 = (bf16[2,4,4736]{2,1,0:T(4,128)(2,1)S(1)}, bf16[2,4,4736]{2,1,0:T(4,128)(2,1)S(1)}, u32[]{:S(2)}, u32[]{:S(2)}) collective-permute-start(bf16[2,4,4736]{2,1,0:T(4,128)(2,1)S(1)} %pad_maximum_fusion.12), channel_id=1, source_target_pairs={{0,6},{1,7},{2,4},{3,5},{4,2},{5,3},{6,0},{7,1},{8,14},{9,15},{10,... | collective-permute-start | bytes 227336 | tf_op jit(solution)/shard_map/ppermute | solution.py:29
  12.6 0.6 collective-permute-start.1
  13.3 0.6 collective-permute-start
  14.0 0.6 collective-permute-start.6
  14.6 1.0 constant_dynamic-update-slice_fusion.refs_0_.refs_6_
  15.5 1.6 %collective-permute-start.7 = (bf16[32,4608]{1,0:T(8,128)(2,1)S(1)}, bf16[32,4608]{1,0:T(8,128)(2,1)S(1)}, u32[]{:S(2)}, u32[]{:S(2)}) collective-permute-start(bf16[32,4608]{1,0:T(8,128)(2,1)S(1)} %constant_dynamic-update-slice_fusion.refs_0_.refs_6_), channel_id=1, source_target_pairs={{0,2},{1,3},{2,0},{3,1},{4,6},{5,7},{6,4},{7,5},{8,10},{9,11},{10,... | collective-permute-start | bytes 884744 | tf_op jit(solution)/shard_map/ppermute | solution.py:29
  17.1 1.5 %collective-permute-start.8 = (bf16[32,4608]{1,0:T(8,128)(2,1)S(1)}, bf16[32,4608]{1,0:T(8,128)(2,1)S(1)}, u32[]{:S(2)}, u32[]{:S(2)}) collective-permute-start(bf16[32,4608]{1,0:T(8,128)(2,1)S(1)} %constant_dynamic-update-slice_fusion.refs_0_.refs_6_), channel_id=1, source_target_pairs={{0,4},{1,5},{2,6},{3,7},{4,0},{5,1},{6,2},{7,3},{8,12},{9,13},{10,... | collective-permute-start | bytes 884744 | tf_op jit(solution)/shard_map/ppermute | solution.py:29
  18.6 0.6 collective-permute-start.9
  19.3 0.7 reshape.70.keys_ref
  20.0 0.4 reshape.69.query_ref
  20.3 1.4 %shard_map.168 = (bf16[64,640]{1,0:T(8,128)(2,1)S(1)}, bf16[64,640]{1,0:T(8,128)(2,1)S(1)}, bf16[64,640]{1,0:T(8,128)(2,1)S(1)}, bf16[64,640]{1,0:T(8,128)(2,1)S(1)}) custom-call(s32[2]{0:T(128)S(1)} %pad_add_fusion.pos, bf16[4,64,576]{2,1,0:T(8,128)(2,1)S(1)} %reshape.69.query_ref, bf16[4,128,576]{2,1,0:T(8,128)(2,1)S(1)} %reshape.70.keys_ref, s32[4]{0:T(128)S(1)} %copy-done.17), custom_call_target="tpu_custom_call" | custom-call | flops 75497472 | bytes 884744 | tf_op jit(solution)/shard_map/pallas_call | solution.py:41
  21.9 2.4 %collective-permute-start.10 = (bf16[64,1792]{1,0:T(8,128)(2,1)S(1)}, bf16[64,1792]{1,0:T(8,128)(2,1)S(1)}, u32[]{:S(2)}, u32[]{:S(2)}) collective-permute-start(bf16[64,1792]{1,0:T(8,128)(2,1)S(1)} %get-tuple-element.66), channel_id=1, source_target_pairs={{0,2},{1,3},{2,0},{3,1},{4,6},{5,7},{6,4},{7,5},{8,10},{9,11},{10,... | collective-permute-start | bytes 688136 | tf_op jit(solution)/shard_map/ppermute | solution.py:29
  24.2 0.7 collective-permute-start.11
  25.0 7.8 %collective-permute-done.9.refs_3_.refs_9_ = bf16[32,4608]{1,0:T(8,128)(2,1)S(1)} collective-permute-done((bf16[32,4608]{1,0:T(8,128)(2,1)S(1)}, bf16[32,4608]{1,0:T(8,128)(2,1)S(1)}, u32[]{:S(2)}, u32[]{:S(2)}) %collective-permute-start.9) | collective-permute-done | bytes 294944 | tf_op jit(solution)/shard_map/ppermute | solution.py:29
  32.9 2.4 %collective-permute-done.10.refs_10_ = bf16[64,1792]{1,0:T(8,128)(2,1)S(1)} collective-permute-done((bf16[64,1792]{1,0:T(8,128)(2,1)S(1)}, bf16[64,1792]{1,0:T(8,128)(2,1)S(1)}, u32[]{:S(2)}, u32[]{:S(2)}) %collective-permute-start.10) | collective-permute-done | bytes 229408 | tf_op jit(solution)/shard_map/ppermute | solution.py:29
  35.3 0.4 collective-permute-done.11.refs_11_
  36.0 0.5 collective-permute-start.5
  36.5 1.5 %collective-permute-start.12 = (bf16[64,1792]{1,0:T(8,128)(2,1)S(1)}, bf16[64,1792]{1,0:T(8,128)(2,1)S(1)}, u32[]{:S(2)}, u32[]{:S(2)}) collective-permute-start(bf16[64,1792]{1,0:T(8,128)(2,1)S(1)} %get-tuple-element.70), channel_id=1, source_target_pairs={{0,6},{1,7},{2,4},{3,5},{4,2},{5,3},{6,0},{7,1},{8,14},{9,15},{10,... | collective-permute-start | bytes 688136 | tf_op jit(solution)/shard_map/ppermute | solution.py:29
  38.0 0.8 collective-permute-done.5.refs_1_
  38.9 1.3 %shard_map.167 = (bf16[256,640]{1,0:T(8,128)(2,1)S(1)}, bf16[256,640]{1,0:T(8,128)(2,1)S(1)}, f32[256,128]{1,0:T(8,128)S(1)}, f32[256,128]{1,0:T(8,128)S(1)}, f3...) custom-call(bf16[16,36864]{1,0:T(8,128)(2,1)S(1)} %copy-done.14, bf16[4,4,4736]{2,1,0:T(4,128)(2,1)S(1)} %collective-permute-done.5.refs_1_, ...), custom_call_target="tpu_custom_call" | custom-call | flops 6039797760 | bytes 1634304 | tf_op jit(solution)/shard_map/pallas_call | solution.py:41
  40.2 2.5 %shard_map.171 = (f32[256,128]{1,0:T(8,128)S(1)}, f32[256,128]{1,0:T(8,128)S(1)}, f32[256,512]{1,0:T(8,128)S(1)}, f32[256,640]{1,0:T(8,128)S(1)}) custom-call(bf16[256,640]{1,0:T(8,128)(2,1)S(1)} %get-tuple-element.56.refs_0_, bf16[256,640]{1,0:T(8,128)(2,1)S(1)} %get-tuple-element.57.refs_1_, f32[256,128]{1,0:T(8,128)S(1)} %get-tuple-element.71.refs_2_, ...), custom_call_target="tpu_custom_call" | custom-call | flops 6039797760 | bytes 4456448 | tf_op jit(solution)/shard_map/pallas_call | solution.py:41
  42.7 2.3 %collective-permute-done.12.refs_12_ = bf16[64,1792]{1,0:T(8,128)(2,1)S(1)} collective-permute-done((bf16[64,1792]{1,0:T(8,128)(2,1)S(1)}, bf16[64,1792]{1,0:T(8,128)(2,1)S(1)}, u32[]{:S(2)}, u32[]{:S(2)}) %collective-permute-start.12) | collective-permute-done | bytes 229408 | tf_op jit(solution)/shard_map/ppermute | solution.py:29
  45.0 0.5 collective-permute-start.15
  45.5 0.5 collective-permute-start.17
  46.0 0.5 collective-permute-done.14.refs_13_
  47.6 3.7 %shard_map.172 = (f32[16,5120]{1,0:T(8,128)S(1)}, bf16[16,5120]{1,0:T(8,128)(2,1)S(1)}) custom-call(bf16[256,640]{1,0:T(8,128)(2,1)S(1)} %get-tuple-element.56.refs_0_, bf16[256,640]{1,0:T(8,128)(2,1)S(1)} %get-tuple-element.57.refs_1_, f32[256,128]{1,0:T(8,128)S(1)} %get-tuple-element.80.refs_2_, f32[256,128]{1,0:T(8,128)S(1)} %get-tuple-element.81.refs_3_, ...), custom_call_target="tpu_custom_call" | custom-call | flops 939524096 | bytes 15597568 | tf_op jit(solution)/shard_map/pallas_call | solution.py:41
  51.5 1.2 %collective-permute-done.18.away_ref = bf16[16,5120]{1,0:T(8,128)(2,1)S(1)} collective-permute-done((bf16[16,5120]{1,0:T(8,128)(2,1)S(1)}, bf16[16,5120]{1,0:T(8,128)(2,1)S(1)}, u32[]{:S(2)}, u32[]{:S(2)}) %collective-permute-start.18) | collective-permute-done | bytes 163872 | tf_op jit(solution)/shard_map/ppermute | solution.py:29
  52.8 1.6 %collective-permute-start.19 = (bf16[4,5120]{1,0:T(4,128)(2,1)S(1)}, bf16[4,5120]{1,0:T(4,128)(2,1)S(1)}, u32[]{:S(2)}, u32[]{:S(2)}) collective-permute-start(bf16[4,5120]{1,0:T(4,128)(2,1)S(1)} %get-tuple-element.91), channel_id=1, source_target_pairs={{0,6},{1,7},{2,4},{3,5},{4,2},{5,3},{6,0},{7,1},{8,14},{9,15},{10,... | collective-permute-start | bytes 122888 | tf_op jit(solution)/shard_map/ppermute | solution.py:29
  54.3 0.5 collective-permute-start.20
  54.8 1.5 %collective-permute-start.21 = (bf16[4,5120]{1,0:T(4,128)(2,1)S(1)}, bf16[4,5120]{1,0:T(4,128)(2,1)S(1)}, u32[]{:S(2)}, u32[]{:S(2)}) collective-permute-start(bf16[4,5120]{1,0:T(4,128)(2,1)S(1)} %get-tuple-element.93), channel_id=1, source_target_pairs={{0,2},{1,3},{2,0},{3,1},{4,6},{5,7},{6,4},{7,5},{8,10},{9,11},{10,... | collective-permute-start | bytes 122888 | tf_op jit(solution)/shard_map/ppermute | solution.py:29
  56.3 1.4 %collective-permute-done.19.refs_0_ = bf16[4,5120]{1,0:T(4,128)(2,1)S(1)} collective-permute-done((bf16[4,5120]{1,0:T(4,128)(2,1)S(1)}, bf16[4,5120]{1,0:T(4,128)(2,1)S(1)}, u32[]{:S(2)}, u32[]{:S(2)}) %collective-permute-start.19) | collective-permute-done | bytes 40992 | tf_op jit(solution)/shard_map/ppermute | solution.py:29
  57.8 0.5 collective-permute-done.20.refs_1_
  58.3 0.5 collective-permute-done.21.refs_2_
  58.8 0.7 shard_map.174
  59.5 1.0 collective-permute-start.22
  60.5 2.7 %collective-permute-start.23 = (bf16[4,5248]{1,0:T(4,128)(2,1)S(1)}, bf16[4,5248]{1,0:T(4,128)(2,1)S(1)}, u32[]{:S(2)}, u32[]{:S(2)}) collective-permute-start(bf16[4,5248]{1,0:T(4,128)(2,1)S(1)} %get-tuple-element.95.refs_0_), channel_id=1, source_target_pairs={{0,16},{8,24},{16,0},{24,8},{1,17},{9,25},{17,1},{25,9},{2,18},{10... | collective-permute-start | bytes 125960 | tf_op jit(solution)/shard_map/ppermute | solution.py:29
  63.2 1.2 %collective-permute-start.24 = (bf16[4,5248]{1,0:T(4,128)(2,1)S(1)}, bf16[4,5248]{1,0:T(4,128)(2,1)S(1)}, u32[]{:S(2)}, u32[]{:S(2)}) collective-permute-start(bf16[4,5248]{1,0:T(4,128)(2,1)S(1)} %get-tuple-element.95.refs_0_), channel_id=1, source_target_pairs={{0,24},{8,16},{16,8},{24,0},{1,25},{9,17},{17,9},{25,1},{2,26},{10... | collective-permute-start | bytes 125960 | tf_op jit(solution)/shard_map/ppermute | solution.py:29
  64.4 1.0 collective-permute-done.23.refs_2_
  65.4 3.6 %collective-permute-done.24.refs_3_ = bf16[4,5248]{1,0:T(4,128)(2,1)S(1)} collective-permute-done((bf16[4,5248]{1,0:T(4,128)(2,1)S(1)}, bf16[4,5248]{1,0:T(4,128)(2,1)S(1)}, u32[]{:S(2)}, u32[]{:S(2)}) %collective-permute-start.24) | collective-permute-done | bytes 42016 | tf_op jit(solution)/shard_map/ppermute | solution.py:29
  69.0 1.6 %collective-permute-start.25 = (bf16[16,5248]{1,0:T(8,128)(2,1)S(1)}, bf16[16,5248]{1,0:T(8,128)(2,1)S(1)}, u32[]{:S(2)}, u32[]{:S(2)}) collective-permute-start(bf16[16,5248]{1,0:T(8,128)(2,1)S(1)} %shard_map.175.refs_0_), channel_id=1, source_target_pairs={{0,2},{1,3},{2,0},{3,1},{4,6},{5,7},{6,4},{7,5},{8,10},{9,11},{10,... | collective-permute-start | bytes 503816 | tf_op jit(solution)/shard_map/ppermute | solution.py:29
  70.6 1.5 %collective-permute-start.26 = (bf16[16,5248]{1,0:T(8,128)(2,1)S(1)}, bf16[16,5248]{1,0:T(8,128)(2,1)S(1)}, u32[]{:S(2)}, u32[]{:S(2)}) collective-permute-start(bf16[16,5248]{1,0:T(8,128)(2,1)S(1)} %shard_map.175.refs_0_), channel_id=1, source_target_pairs={{0,4},{1,5},{2,6},{3,7},{4,0},{5,1},{6,2},{7,3},{8,12},{9,13},{10,... | collective-permute-start | bytes 503816 | tf_op jit(solution)/shard_map/ppermute | solution.py:29
  72.1 0.5 collective-permute-start.27
  72.6 2.3 %collective-permute-done.25.refs_1_ = bf16[16,5248]{1,0:T(8,128)(2,1)S(1)} collective-permute-done((bf16[16,5248]{1,0:T(8,128)(2,1)S(1)}, bf16[16,5248]{1,0:T(8,128)(2,1)S(1)}, u32[]{:S(2)}, u32[]{:S(2)}) %collective-permute-start.25) | collective-permute-done | bytes 167968 | tf_op jit(solution)/shard_map/ppermute | solution.py:29
  74.9 1.9 %collective-permute-done.26.refs_2_ = bf16[16,5248]{1,0:T(8,128)(2,1)S(1)} collective-permute-done((bf16[16,5248]{1,0:T(8,128)(2,1)S(1)}, bf16[16,5248]{1,0:T(8,128)(2,1)S(1)}, u32[]{:S(2)}, u32[]{:S(2)}) %collective-permute-start.26) | collective-permute-done | bytes 167968 | tf_op jit(solution)/shard_map/ppermute | solution.py:29
  76.8 1.5 %collective-permute-done.27.refs_3_ = bf16[16,5248]{1,0:T(8,128)(2,1)S(1)} collective-permute-done((bf16[16,5248]{1,0:T(8,128)(2,1)S(1)}, bf16[16,5248]{1,0:T(8,128)(2,1)S(1)}, u32[]{:S(2)}, u32[]{:S(2)}) %collective-permute-start.27) | collective-permute-done | bytes 167968 | tf_op jit(solution)/shard_map/ppermute | solution.py:29
  78.4 1.4 %collective-permute-done.31.refs_7_ = bf16[16,5248]{1,0:T(8,128)(2,1)S(1)} collective-permute-done((bf16[16,5248]{1,0:T(8,128)(2,1)S(1)}, bf16[16,5248]{1,0:T(8,128)(2,1)S(1)}, u32[]{:S(2)}, u32[]{:S(2)}) %collective-permute-start.31) | collective-permute-done | bytes 167968 | tf_op jit(solution)/shard_map/ppermute | solution.py:29
  79.8 3.1 %shard_map.176 = (f32[64,5120]{1,0:T(8,128)S(1)}, bf16[64,5120]{1,0:T(8,128)(2,1)S(1)}) custom-call(s32[2]{0:T(128)S(1)} %pad_add_fusion.pos, bf16[16,5248]{1,0:T(8,128)(2,1)S(1)} %shard_map.175.refs_0_, bf16[16,5248]{1,0:T(8,128)(2,1)S(1)} %collective-permute-done.25.refs_1_, bf16[16,5248]{1,0:T(8,128)(2,1)S(1)} %collective-permute-done.26.refs_2_, ...), custom_call_target="tpu_custom_call" | custom-call | flops 1509949440 | bytes 13139976 | tf_op jit(solution)/shard_map/pallas_call | solution.py:41
  83.1 2.0 %collective-permute-done.32.away_ref = bf16[64,5120]{1,0:T(8,128)(2,1)S(1)} collective-permute-done((bf16[64,5120]{1,0:T(8,128)(2,1)S(1)}, bf16[64,5120]{1,0:T(8,128)(2,1)S(1)}, u32[]{:S(2)}, u32[]{:S(2)}) %collective-permute-start.32) | collective-permute-done | bytes 655392 | tf_op jit(solution)/shard_map/ppermute | solution.py:29
  85.2 1.2 %collective-permute-start.33 = (bf16[16,5120]{1,0:T(8,128)(2,1)S(1)}, bf16[16,5120]{1,0:T(8,128)(2,1)S(1)}, u32[]{:S(2)}, u32[]{:S(2)}) collective-permute-start(bf16[16,5120]{1,0:T(8,128)(2,1)S(1)} %get-tuple-element.99), channel_id=1, source_target_pairs={{0,6},{1,7},{2,4},{3,5},{4,2},{5,3},{6,0},{7,1},{8,14},{9,15},{10,... | collective-permute-start | bytes 491528 | tf_op jit(solution)/shard_map/ppermute | solution.py:29
  86.4 0.9 collective-permute-start.34
  87.3 1.5 %collective-permute-start.35 = (bf16[16,5120]{1,0:T(8,128)(2,1)S(1)}, bf16[16,5120]{1,0:T(8,128)(2,1)S(1)}, u32[]{:S(2)}, u32[]{:S(2)}) collective-permute-start(bf16[16,5120]{1,0:T(8,128)(2,1)S(1)} %get-tuple-element.101), channel_id=1, source_target_pairs={{0,2},{1,3},{2,0},{3,1},{4,6},{5,7},{6,4},{7,5},{8,10},{9,11},{10,... | collective-permute-start | bytes 491528 | tf_op jit(solution)/shard_map/ppermute | solution.py:29
  88.7 4.5 %collective-permute-done.33 = bf16[16,5120]{1,0:T(8,128)(2,1)S(1)} collective-permute-done((bf16[16,5120]{1,0:T(8,128)(2,1)S(1)}, bf16[16,5120]{1,0:T(8,128)(2,1)S(1)}, u32[]{:S(2)}, u32[]{:S(2)}) %collective-permute-start.33) | collective-permute-done | bytes 163872 | tf_op jit(solution)/shard_map/ppermute | solution.py:29
  93.2 2.7 %collective-permute-done.34 = bf16[16,5120]{1,0:T(8,128)(2,1)S(1)} collective-permute-done((bf16[16,5120]{1,0:T(8,128)(2,1)S(1)}, bf16[16,5120]{1,0:T(8,128)(2,1)S(1)}, u32[]{:S(2)}, u32[]{:S(2)}) %collective-permute-start.34) | collective-permute-done | bytes 163872 | tf_op jit(solution)/shard_map/ppermute | solution.py:29
  96.1 1.4 %collective-permute-start.36 = (bf16[4,5120]{1,0:T(4,128)(2,1)S(1)}, bf16[4,5120]{1,0:T(4,128)(2,1)S(1)}, u32[]{:S(2)}, u32[]{:S(2)}) collective-permute-start(bf16[4,5120]{1,0:T(4,128)(2,1)S(1)} %get-tuple-element.112), channel_id=1, source_target_pairs={{0,24},{8,16},{16,8},{24,0},{1,25},{9,17},{17,9},{25,1},{2,26},{10... | collective-permute-start | bytes 122888 | tf_op jit(solution)/shard_map/ppermute | solution.py:29
  97.6 2.9 %collective-permute-start.38 = (bf16[4,5120]{1,0:T(4,128)(2,1)S(1)}, bf16[4,5120]{1,0:T(4,128)(2,1)S(1)}, u32[]{:S(2)}, u32[]{:S(2)}) collective-permute-start(bf16[4,5120]{1,0:T(4,128)(2,1)S(1)} %get-tuple-element.113), channel_id=1, source_target_pairs={{0,8},{8,0},{16,24},{24,16},{1,9},{9,1},{17,25},{25,17},{2,10},{10... | collective-permute-start | bytes 122888 | tf_op jit(solution)/shard_map/ppermute | solution.py:29
  100.5 1.5 %collective-permute-done.36 = bf16[4,5120]{1,0:T(4,128)(2,1)S(1)} collective-permute-done((bf16[4,5120]{1,0:T(4,128)(2,1)S(1)}, bf16[4,5120]{1,0:T(4,128)(2,1)S(1)}, u32[]{:S(2)}, u32[]{:S(2)}) %collective-permute-start.36) | collective-permute-done | bytes 40992 | tf_op jit(solution)/shard_map/ppermute | solution.py:29
  102.0 1.2 %collective-permute-done.37 = bf16[4,5120]{1,0:T(4,128)(2,1)S(1)} collective-permute-done((bf16[4,5120]{1,0:T(4,128)(2,1)S(1)}, bf16[4,5120]{1,0:T(4,128)(2,1)S(1)}, u32[]{:S(2)}, u32[]{:S(2)}) %collective-permute-start.37) | collective-permute-done | bytes 40992 | tf_op jit(solution)/shard_map/ppermute | solution.py:29
  103.2 0.7 fusion.1
  (103 shorter events, 3.0 us)
Async XLA Ops:
  1.6 17.7 %copy-start.19 = (bf16[4,73728]{1,0:T(4,128)(2,1)S(1)}, bf16[4,73728]{1,0:T(4,128)(2,1)}, u32[]{:S(2)}) copy-start(bf16[4,73728]{1,0:T(4,128)(2,1)} %param.19) | copy-start | bytes 1769476
  1.6 12.4 %collective-permute-start.4 = (bf16[16,4608]{1,0:T(8,128)(2,1)S(1)}, bf16[16,4608]{1,0:T(8,128)(2,1)}, u32[]{:S(2)}, u32[]{:S(2)}) collective-permute-start(bf16[16,4608]{1,0:T(8,128)(2,1)S(1)} %constant_dynamic-slice_fusion), channel_id=1, source_target_pairs={{0,16},{8,24},{16,0},{24,8},{1,17},{9,25},{17,1},{25,9},{2,18},{10... | collective-permute-start | bytes 442376 | tf_op jit(solution)/shard_map/ppermute | solution.py:29
  5.7 8.3 %collective-permute-start.3 = (bf16[16,4608]{1,0:T(8,128)(2,1)S(1)}, bf16[16,4608]{1,0:T(8,128)(2,1)S(1)}, u32[]{:S(2)}, u32[]{:S(2)}) collective-permute-start(bf16[16,4608]{1,0:T(8,128)(2,1)S(1)} %constant_dynamic-slice_fusion), channel_id=1, source_target_pairs={{0,8},{8,0},{16,24},{24,16},{1,9},{9,1},{17,25},{25,17},{2,10},{10... | collective-permute-start | bytes 442376 | tf_op jit(solution)/shard_map/ppermute | solution.py:29
  10.0 10.0 %copy-start.18 = (bf16[4,36864]{1,0:T(4,128)(2,1)S(1)}, bf16[4,36864]{1,0:T(4,128)(2,1)}, u32[]{:S(2)}) copy-start(bf16[4,36864]{1,0:T(4,128)(2,1)} %param.17) | copy-start | bytes 884740
  10.1 7.0 %collective-permute-start.2 = (bf16[2,4,4736]{2,1,0:T(4,128)(2,1)S(1)}, bf16[2,4,4736]{2,1,0:T(4,128)(2,1)S(1)}, u32[]{:S(2)}, u32[]{:S(2)}) collective-permute-start(bf16[2,4,4736]{2,1,0:T(4,128)(2,1)S(1)} %pad_maximum_fusion.12), channel_id=1, source_target_pairs={{0,6},{1,7},{2,4},{3,5},{4,2},{5,3},{6,0},{7,1},{8,14},{9,15},{10,... | collective-permute-start | bytes 227336 | tf_op jit(solution)/shard_map/ppermute | solution.py:29
  12.6 6.0 %collective-permute-start.1 = (bf16[2,4,4736]{2,1,0:T(4,128)(2,1)S(1)}, bf16[2,4,4736]{2,1,0:T(4,128)(2,1)S(1)}, u32[]{:S(2)}, u32[]{:S(2)}) collective-permute-start(bf16[2,4,4736]{2,1,0:T(4,128)(2,1)S(1)} %pad_maximum_fusion.11), channel_id=1, source_target_pairs={{0,4},{1,5},{2,6},{3,7},{4,0},{5,1},{6,2},{7,3},{8,12},{9,13},{10,... | collective-permute-start | bytes 227336 | tf_op jit(solution)/shard_map/ppermute | solution.py:29
  13.3 5.3 %collective-permute-start = (bf16[2,4,4736]{2,1,0:T(4,128)(2,1)S(1)}, bf16[2,4,4736]{2,1,0:T(4,128)(2,1)S(1)}, u32[]{:S(2)}, u32[]{:S(2)}) collective-permute-start(bf16[2,4,4736]{2,1,0:T(4,128)(2,1)S(1)} %pad_maximum_fusion.10), channel_id=1, source_target_pairs={{0,2},{1,3},{2,0},{3,1},{4,6},{5,7},{6,4},{7,5},{8,10},{9,11},{10,... | collective-permute-start | bytes 227336 | tf_op jit(solution)/shard_map/ppermute | solution.py:29
  13.9 11.0 %copy-start.4 = (bf16[2,4,4736]{2,1,0:T(4,128)(2,1)}, bf16[2,4,4736]{2,1,0:T(4,128)(2,1)S(1)}, u32[]{:S(2)}) copy-start(bf16[2,4,4736]{2,1,0:T(4,128)(2,1)S(1)} %pad_maximum_fusion.9.refs_2_) | copy-start | bytes 227332
  14.0 7.8 %collective-permute-start.6 = (bf16[16,4608]{1,0:T(8,128)(2,1)}, bf16[16,4608]{1,0:T(8,128)(2,1)S(1)}, u32[]{:S(2)}, u32[]{:S(2)}) collective-permute-start(bf16[16,4608]{1,0:T(8,128)(2,1)} %collective-permute-done.4), channel_id=1, source_target_pairs={{0,8},{8,0},{16,24},{24,16},{1,9},{9,1},{17,25},{25,17},{2,10},{10... | collective-permute-start | bytes 442376 | tf_op jit(solution)/shard_map/ppermute | solution.py:29
  15.5 17.3 %collective-permute-start.7 = (bf16[32,4608]{1,0:T(8,128)(2,1)S(1)}, bf16[32,4608]{1,0:T(8,128)(2,1)S(1)}, u32[]{:S(2)}, u32[]{:S(2)}) collective-permute-start(bf16[32,4608]{1,0:T(8,128)(2,1)S(1)} %constant_dynamic-update-slice_fusion.refs_0_.refs_6_), channel_id=1, source_target_pairs={{0,2},{1,3},{2,0},{3,1},{4,6},{5,7},{6,4},{7,5},{8,10},{9,11},{10,... | collective-permute-start | bytes 884744 | tf_op jit(solution)/shard_map/ppermute | solution.py:29
  17.1 7.9 %copy-start.8 = (bf16[2,4,4736]{2,1,0:T(4,128)(2,1)}, bf16[2,4,4736]{2,1,0:T(4,128)(2,1)S(1)}, u32[]{:S(2)}) copy-start(bf16[2,4,4736]{2,1,0:T(4,128)(2,1)S(1)} %collective-permute-done.2.refs_5_) | copy-start | bytes 227332
  17.1 15.8 %collective-permute-start.8 = (bf16[32,4608]{1,0:T(8,128)(2,1)S(1)}, bf16[32,4608]{1,0:T(8,128)(2,1)S(1)}, u32[]{:S(2)}, u32[]{:S(2)}) collective-permute-start(bf16[32,4608]{1,0:T(8,128)(2,1)S(1)} %constant_dynamic-update-slice_fusion.refs_0_.refs_6_), channel_id=1, source_target_pairs={{0,4},{1,5},{2,6},{3,7},{4,0},{5,1},{6,2},{7,3},{8,12},{9,13},{10,... | collective-permute-start | bytes 884744 | tf_op jit(solution)/shard_map/ppermute | solution.py:29
  18.6 14.2 %collective-permute-start.9 = (bf16[32,4608]{1,0:T(8,128)(2,1)S(1)}, bf16[32,4608]{1,0:T(8,128)(2,1)S(1)}, u32[]{:S(2)}, u32[]{:S(2)}) collective-permute-start(bf16[32,4608]{1,0:T(8,128)(2,1)S(1)} %constant_dynamic-update-slice_fusion.refs_0_.refs_6_), channel_id=1, source_target_pairs={{0,6},{1,7},{2,4},{3,5},{4,2},{5,3},{6,0},{7,1},{8,14},{9,15},{10,... | collective-permute-start | bytes 884744 | tf_op jit(solution)/shard_map/ppermute | solution.py:29
  21.9 13.4 %collective-permute-start.10 = (bf16[64,1792]{1,0:T(8,128)(2,1)S(1)}, bf16[64,1792]{1,0:T(8,128)(2,1)S(1)}, u32[]{:S(2)}, u32[]{:S(2)}) collective-permute-start(bf16[64,1792]{1,0:T(8,128)(2,1)S(1)} %get-tuple-element.66), channel_id=1, source_target_pairs={{0,2},{1,3},{2,0},{3,1},{4,6},{5,7},{6,4},{7,5},{8,10},{9,11},{10,... | collective-permute-start | bytes 688136 | tf_op jit(solution)/shard_map/ppermute | solution.py:29
  24.2 11.4 %collective-permute-start.11 = (bf16[64,1792]{1,0:T(8,128)(2,1)S(1)}, bf16[64,1792]{1,0:T(8,128)(2,1)S(1)}, u32[]{:S(2)}, u32[]{:S(2)}) collective-permute-start(bf16[64,1792]{1,0:T(8,128)(2,1)S(1)} %get-tuple-element.67), channel_id=1, source_target_pairs={{0,4},{1,5},{2,6},{3,7},{4,0},{5,1},{6,2},{7,3},{8,12},{9,13},{10,... | collective-permute-start | bytes 688136 | tf_op jit(solution)/shard_map/ppermute | solution.py:29
  24.9 10.9 %slice-start.3 = ((bf16[2,4,4736]{2,1,0:T(4,128)(2,1)}), bf16[1,4,4736]{2,1,0:T(4,128)(2,1)S(1)}, s32[]{:S(2)}) async-start(bf16[2,4,4736]{2,1,0:T(4,128)(2,1)} %copy-done.4), calls=%async_computation.3 | async-start | bytes 75776 | tf_op jit(solution)/shard_map/slice | solution.py:431
  24.9 10.9 %slice-start.6 = ((bf16[2,4,4736]{2,1,0:T(4,128)(2,1)}), bf16[1,4,4736]{2,1,0:T(4,128)(2,1)S(1)}, s32[]{:S(2)}) async-start(bf16[2,4,4736]{2,1,0:T(4,128)(2,1)} %copy-done.12), calls=%async_computation.6 | async-start | bytes 75776 | tf_op jit(solution)/shard_map/slice | solution.py:431
  24.9 10.9 %slice-start.5 = ((bf16[2,4,4736]{2,1,0:T(4,128)(2,1)}), bf16[1,4,4736]{2,1,0:T(4,128)(2,1)S(1)}, s32[]{:S(2)}) async-start(bf16[2,4,4736]{2,1,0:T(4,128)(2,1)} %copy-done.10), calls=%async_computation.5 | async-start | bytes 75776 | tf_op jit(solution)/shard_map/slice | solution.py:431
  25.0 10.9 %slice-start.4 = ((bf16[2,4,4736]{2,1,0:T(4,128)(2,1)}), bf16[1,4,4736]{2,1,0:T(4,128)(2,1)S(1)}, s32[]{:S(2)}) async-start(bf16[2,4,4736]{2,1,0:T(4,128)(2,1)} %copy-done.8), calls=%async_computation.4 | async-start | bytes 75776 | tf_op jit(solution)/shard_map/slice | solution.py:431
  25.0 13.9 %copy-start.5 = (bf16[2,4,4736]{2,1,0:T(4,128)(2,1)S(1)}, bf16[2,4,4736]{2,1,0:T(4,128)(2,1)}, u32[]{:S(2)}) copy-start(bf16[2,4,4736]{2,1,0:T(4,128)(2,1)} %copy-done.4) | copy-start | bytes 227332
  25.0 13.9 %copy-start.9 = (bf16[2,4,4736]{2,1,0:T(4,128)(2,1)S(1)}, bf16[2,4,4736]{2,1,0:T(4,128)(2,1)}, u32[]{:S(2)}) copy-start(bf16[2,4,4736]{2,1,0:T(4,128)(2,1)} %copy-done.8) | copy-start | bytes 227332
  25.0 13.9 %copy-start.11 = (bf16[2,4,4736]{2,1,0:T(4,128)(2,1)S(1)}, bf16[2,4,4736]{2,1,0:T(4,128)(2,1)}, u32[]{:S(2)}) copy-start(bf16[2,4,4736]{2,1,0:T(4,128)(2,1)} %copy-done.10) | copy-start | bytes 227332
  25.0 13.8 %copy-start.13 = (bf16[2,4,4736]{2,1,0:T(4,128)(2,1)S(1)}, bf16[2,4,4736]{2,1,0:T(4,128)(2,1)}, u32[]{:S(2)}) copy-start(bf16[2,4,4736]{2,1,0:T(4,128)(2,1)} %copy-done.12) | copy-start | bytes 227332
  25.0 13.8 %copy-start.14 = (bf16[16,36864]{1,0:T(8,128)(2,1)S(1)}, bf16[16,36864]{1,0:T(8,128)(2,1)}, u32[]{:S(2)}) copy-start(bf16[16,36864]{1,0:T(8,128)(2,1)} %refs_0_.1) | copy-start | bytes 3538948
  35.7 4.4 %collective-permute-start.13 = (bf16[128,4608]{1,0:T(8,128)(2,1)S(1)}, bf16[128,4608]{1,0:T(8,128)(2,1)S(1)}, u32[]{:S(2)}, u32[]{:S(2)}) collective-permute-start(bf16[128,4608]{1,0:T(8,128)(2,1)S(1)} %shard_map.170), channel_id=1, source_target_pairs={{0,1},{1,0},{2,3},{3,2},{4,5},{5,4},{6,7},{7,6},{8,9},{9,8},{10,11... | collective-permute-start | bytes 3538952 | tf_op jit(solution)/shard_map/ppermute | solution.py:29
  36.0 2.9 %collective-permute-start.5 = (bf16[4,4,4736]{2,1,0:T(4,128)(2,1)S(1)}, bf16[4,4,4736]{2,1,0:T(4,128)(2,1)S(1)}, u32[]{:S(2)}, u32[]{:S(2)}) collective-permute-start(bf16[4,4,4736]{2,1,0:T(4,128)(2,1)S(1)} %pad_maximum_fusion), channel_id=1, source_target_pairs={{0,1},{1,0},{2,3},{3,2},{4,5},{5,4},{6,7},{7,6},{8,9},{9,8},{10,11... | collective-permute-start | bytes 454664 | tf_op jit(solution)/shard_map/ppermute | solution.py:29
  36.5 8.5 %collective-permute-start.12 = (bf16[64,1792]{1,0:T(8,128)(2,1)S(1)}, bf16[64,1792]{1,0:T(8,128)(2,1)S(1)}, u32[]{:S(2)}, u32[]{:S(2)}) collective-permute-start(bf16[64,1792]{1,0:T(8,128)(2,1)S(1)} %get-tuple-element.70), channel_id=1, source_target_pairs={{0,6},{1,7},{2,4},{3,5},{4,2},{5,3},{6,0},{7,1},{8,14},{9,15},{10,... | collective-permute-start | bytes 688136 | tf_op jit(solution)/shard_map/ppermute | solution.py:29
  40.1 7.3 %slice-start = ((s8[10485760]{0:T(1024)(128)(4,1)}), s8[4194304]{0:T(1024)(128)(4,1)S(1)}, s32[]{:S(2)}) async-start(s8[10485760]{0:T(1024)(128)(4,1)} %bitcast.18), calls=%async_computation | async-start | bytes 8388608
  40.2 7.3 %slice-start.1 = ((s8[10485760]{0:T(1024)(128)(4,1)}), s8[4194304]{0:T(1024)(128)(4,1)S(1)}, s32[]{:S(2)}) async-start(s8[10485760]{0:T(1024)(128)(4,1)} %bitcast.18), calls=%async_computation.1 | async-start | bytes 8388608
  40.2 7.3 %slice-start.2 = ((s8[10485760]{0:T(1024)(128)(4,1)}), s8[2097152]{0:T(1024)(128)(4,1)S(1)}, s32[]{:S(2)}) async-start(s8[10485760]{0:T(1024)(128)(4,1)} %bitcast.18), calls=%async_computation.2 | async-start | bytes 4194304
  40.2 7.3 %copy-start.3 = (bf16[8,512,128]{2,1,0:T(8,128)(2,1)S(1)}, bf16[8,512,128]{2,1,0:T(8,128)(2,1)}, u32[]{:S(2)}) copy-start(bf16[8,512,128]{2,1,0:T(8,128)(2,1)} %refs_7_.1) | copy-start | bytes 3145732
  40.2 7.3 %copy-start.6 = (bf16[256,256]{1,0:T(8,128)(2,1)S(1)}, bf16[256,256]{1,0:T(8,128)(2,1)}, u32[]{:S(2)}) copy-start(bf16[256,256]{1,0:T(8,128)(2,1)} %constant.65.clone.refs_6_) | copy-start | bytes 393220
  45.0 1.5 %collective-permute-start.14 = (bf16[64,1792]{1,0:T(8,128)(2,1)S(1)}, bf16[64,1792]{1,0:T(8,128)(2,1)S(1)}, u32[]{:S(2)}, u32[]{:S(2)}) collective-permute-start(bf16[64,1792]{1,0:T(8,128)(2,1)S(1)} %get-tuple-element.84.refs_9_), channel_id=1, source_target_pairs={{0,1},{1,0},{2,3},{3,2},{4,5},{5,4},{6,7},{7,6},{8,9},{9,8},{10,11... | collective-permute-start | bytes 688136 | tf_op jit(solution)/shard_map/ppermute | solution.py:29
  45.0 1.8 %collective-permute-start.15 = (bf16[64,1792]{1,0:T(8,128)(2,1)S(1)}, bf16[64,1792]{1,0:T(8,128)(2,1)S(1)}, u32[]{:S(2)}, u32[]{:S(2)}) collective-permute-start(bf16[64,1792]{1,0:T(8,128)(2,1)S(1)} %collective-permute-done.10.refs_10_), channel_id=1, source_target_pairs={{0,1},{1,0},{2,3},{3,2},{4,5},{5,4},{6,7},{7,6},{8,9},{9,8},{10,11... | collective-permute-start | bytes 688136 | tf_op jit(solution)/shard_map/ppermute | solution.py:29
  45.5 1.6 %collective-permute-start.16 = (bf16[64,1792]{1,0:T(8,128)(2,1)S(1)}, bf16[64,1792]{1,0:T(8,128)(2,1)S(1)}, u32[]{:S(2)}, u32[]{:S(2)}) collective-permute-start(bf16[64,1792]{1,0:T(8,128)(2,1)S(1)} %collective-permute-done.11.refs_11_), channel_id=1, source_target_pairs={{0,1},{1,0},{2,3},{3,2},{4,5},{5,4},{6,7},{7,6},{8,9},{9,8},{10,11... | collective-permute-start | bytes 688136 | tf_op jit(solution)/shard_map/ppermute | solution.py:29
  45.5 2.0 %collective-permute-start.17 = (bf16[64,1792]{1,0:T(8,128)(2,1)S(1)}, bf16[64,1792]{1,0:T(8,128)(2,1)S(1)}, u32[]{:S(2)}, u32[]{:S(2)}) collective-permute-start(bf16[64,1792]{1,0:T(8,128)(2,1)S(1)} %collective-permute-done.12.refs_12_), channel_id=1, source_target_pairs={{0,1},{1,0},{2,3},{3,2},{4,5},{5,4},{6,7},{7,6},{8,9},{9,8},{10,11... | collective-permute-start | bytes 688136 | tf_op jit(solution)/shard_map/ppermute | solution.py:29
  47.5 8.8 %copy-start.20 = (bf16[5120]{0:T(1024)(128)(2,1)S(1)}, bf16[5120]{0:T(1024)(128)(2,1)}, u32[]{:S(2)}) copy-start(bf16[5120]{0:T(1024)(128)(2,1)} %param.25) | copy-start | bytes 30724
  47.5 11.3 %copy-start.7 = (bf16[4,5120]{1,0:T(4,128)(2,1)S(1)}, bf16[4,5120]{1,0:T(4,128)(2,1)}, u32[]{:S(2)}) copy-start(bf16[4,5120]{1,0:T(4,128)(2,1)} %hidden_ref.1) | copy-start | bytes 122884
  47.5 11.3 %copy-start.15 = (s32[4,6]{1,0:T(4,128)S(1)}, s32[4,6]{1,0:T(4,128)}, u32[]{:S(2)}) copy-start(s32[4,6]{1,0:T(4,128)} %ids_ref.1) | copy-start | bytes 292
  47.5 11.3 %copy-start.16 = (bf16[4,6]{1,0:T(4,128)(2,1)S(1)}, bf16[4,6]{1,0:T(4,128)(2,1)}, u32[]{:S(2)}) copy-start(bf16[4,6]{1,0:T(4,128)(2,1)} %weight_ref.1) | copy-start | bytes 148
  47.6 32.2 %copy-start = (bf16[1,5120,384]{2,1,0:T(8,128)(2,1)S(1)}, bf16[1,5120,384]{2,1,0:T(8,128)(2,1)}, u32[]{:S(2)}) copy-start(bf16[1,5120,384]{2,1,0:T(8,128)(2,1)} %refs_8_.3) | copy-start | bytes 11796484
  47.6 32.2 %copy-start.1 = (bf16[1,5120,384]{2,1,0:T(8,128)(2,1)S(1)}, bf16[1,5120,384]{2,1,0:T(8,128)(2,1)}, u32[]{:S(2)}) copy-start(bf16[1,5120,384]{2,1,0:T(8,128)(2,1)} %refs_9_.1) | copy-start | bytes 11796484
  47.6 32.2 %copy-start.2 = (bf16[1,384,5120]{2,1,0:T(8,128)(2,1)S(1)}, bf16[1,384,5120]{2,1,0:T(8,128)(2,1)}, u32[]{:S(2)}) copy-start(bf16[1,384,5120]{2,1,0:T(8,128)(2,1)} %refs_10_.1) | copy-start | bytes 11796484
  51.3 1.4 %collective-permute-start.18 = (bf16[16,5120]{1,0:T(8,128)(2,1)S(1)}, bf16[16,5120]{1,0:T(8,128)(2,1)S(1)}, u32[]{:S(2)}, u32[]{:S(2)}) collective-permute-start(bf16[16,5120]{1,0:T(8,128)(2,1)S(1)} %get-tuple-element.89), channel_id=1, source_target_pairs={{0,1},{1,0},{2,3},{3,2},{4,5},{5,4},{6,7},{7,6},{8,9},{9,8},{10,11... | collective-permute-start | bytes 491528 | tf_op jit(solution)/shard_map/ppermute | solution.py:29
  52.8 5.0 %collective-permute-start.19 = (bf16[4,5120]{1,0:T(4,128)(2,1)S(1)}, bf16[4,5120]{1,0:T(4,128)(2,1)S(1)}, u32[]{:S(2)}, u32[]{:S(2)}) collective-permute-start(bf16[4,5120]{1,0:T(4,128)(2,1)S(1)} %get-tuple-element.91), channel_id=1, source_target_pairs={{0,6},{1,7},{2,4},{3,5},{4,2},{5,3},{6,0},{7,1},{8,14},{9,15},{10,... | collective-permute-start | bytes 122888 | tf_op jit(solution)/shard_map/ppermute | solution.py:29
  54.3 4.0 %collective-permute-start.20 = (bf16[4,5120]{1,0:T(4,128)(2,1)S(1)}, bf16[4,5120]{1,0:T(4,128)(2,1)S(1)}, u32[]{:S(2)}, u32[]{:S(2)}) collective-permute-start(bf16[4,5120]{1,0:T(4,128)(2,1)S(1)} %get-tuple-element.92), channel_id=1, source_target_pairs={{0,4},{1,5},{2,6},{3,7},{4,0},{5,1},{6,2},{7,3},{8,12},{9,13},{10,... | collective-permute-start | bytes 122888 | tf_op jit(solution)/shard_map/ppermute | solution.py:29
  54.8 4.0 %collective-permute-start.21 = (bf16[4,5120]{1,0:T(4,128)(2,1)S(1)}, bf16[4,5120]{1,0:T(4,128)(2,1)S(1)}, u32[]{:S(2)}, u32[]{:S(2)}) collective-permute-start(bf16[4,5120]{1,0:T(4,128)(2,1)S(1)} %get-tuple-element.93), channel_id=1, source_target_pairs={{0,2},{1,3},{2,0},{3,1},{4,6},{5,7},{6,4},{7,5},{8,10},{9,11},{10,... | collective-permute-start | bytes 122888 | tf_op jit(solution)/shard_map/ppermute | solution.py:29
  59.5 4.9 %collective-permute-start.22 = (bf16[4,5248]{1,0:T(4,128)(2,1)S(1)}, bf16[4,5248]{1,0:T(4,128)(2,1)S(1)}, u32[]{:S(2)}, u32[]{:S(2)}) collective-permute-start(bf16[4,5248]{1,0:T(4,128)(2,1)S(1)} %get-tuple-element.95.refs_0_), channel_id=1, source_target_pairs={{0,8},{8,0},{16,24},{24,16},{1,9},{9,1},{17,25},{25,17},{2,10},{10... | collective-permute-start | bytes 125960 | tf_op jit(solution)/shard_map/ppermute | solution.py:29
  60.5 4.9 %collective-permute-start.23 = (bf16[4,5248]{1,0:T(4,128)(2,1)S(1)}, bf16[4,5248]{1,0:T(4,128)(2,1)S(1)}, u32[]{:S(2)}, u32[]{:S(2)}) collective-permute-start(bf16[4,5248]{1,0:T(4,128)(2,1)S(1)} %get-tuple-element.95.refs_0_), channel_id=1, source_target_pairs={{0,16},{8,24},{16,0},{24,8},{1,17},{9,25},{17,1},{25,9},{2,18},{10... | collective-permute-start | bytes 125960 | tf_op jit(solution)/shard_map/ppermute | solution.py:29
  63.2 5.8 %collective-permute-start.24 = (bf16[4,5248]{1,0:T(4,128)(2,1)S(1)}, bf16[4,5248]{1,0:T(4,128)(2,1)S(1)}, u32[]{:S(2)}, u32[]{:S(2)}) collective-permute-start(bf16[4,5248]{1,0:T(4,128)(2,1)S(1)} %get-tuple-element.95.refs_0_), channel_id=1, source_target_pairs={{0,24},{8,16},{16,8},{24,0},{1,25},{9,17},{17,9},{25,1},{2,26},{10... | collective-permute-start | bytes 125960 | tf_op jit(solution)/shard_map/ppermute | solution.py:29
  69.0 5.9 %collective-permute-start.25 = (bf16[16,5248]{1,0:T(8,128)(2,1)S(1)}, bf16[16,5248]{1,0:T(8,128)(2,1)S(1)}, u32[]{:S(2)}, u32[]{:S(2)}) collective-permute-start(bf16[16,5248]{1,0:T(8,128)(2,1)S(1)} %shard_map.175.refs_0_), channel_id=1, source_target_pairs={{0,2},{1,3},{2,0},{3,1},{4,6},{5,7},{6,4},{7,5},{8,10},{9,11},{10,... | collective-permute-start | bytes 503816 | tf_op jit(solution)/shard_map/ppermute | solution.py:29
  70.6 6.2 %collective-permute-start.26 = (bf16[16,5248]{1,0:T(8,128)(2,1)S(1)}, bf16[16,5248]{1,0:T(8,128)(2,1)S(1)}, u32[]{:S(2)}, u32[]{:S(2)}) collective-permute-start(bf16[16,5248]{1,0:T(8,128)(2,1)S(1)} %shard_map.175.refs_0_), channel_id=1, source_target_pairs={{0,4},{1,5},{2,6},{3,7},{4,0},{5,1},{6,2},{7,3},{8,12},{9,13},{10,... | collective-permute-start | bytes 503816 | tf_op jit(solution)/shard_map/ppermute | solution.py:29
  72.1 6.3 %collective-permute-start.27 = (bf16[16,5248]{1,0:T(8,128)(2,1)S(1)}, bf16[16,5248]{1,0:T(8,128)(2,1)S(1)}, u32[]{:S(2)}, u32[]{:S(2)}) collective-permute-start(bf16[16,5248]{1,0:T(8,128)(2,1)S(1)} %shard_map.175.refs_0_), channel_id=1, source_target_pairs={{0,6},{1,7},{2,4},{3,5},{4,2},{5,3},{6,0},{7,1},{8,14},{9,15},{10,... | collective-permute-start | bytes 503816 | tf_op jit(solution)/shard_map/ppermute | solution.py:29
  72.6 5.8 %collective-permute-start.28 = (bf16[16,5248]{1,0:T(8,128)(2,1)S(1)}, bf16[16,5248]{1,0:T(8,128)(2,1)S(1)}, u32[]{:S(2)}, u32[]{:S(2)}) collective-permute-start(bf16[16,5248]{1,0:T(8,128)(2,1)S(1)} %shard_map.175.refs_0_), channel_id=1, source_target_pairs={{0,1},{1,0},{2,3},{3,2},{4,5},{5,4},{6,7},{7,6},{8,9},{9,8},{10,11... | collective-permute-start | bytes 503816 | tf_op jit(solution)/shard_map/ppermute | solution.py:29
  74.9 3.5 %collective-permute-start.29 = (bf16[16,5248]{1,0:T(8,128)(2,1)S(1)}, bf16[16,5248]{1,0:T(8,128)(2,1)S(1)}, u32[]{:S(2)}, u32[]{:S(2)}) collective-permute-start(bf16[16,5248]{1,0:T(8,128)(2,1)S(1)} %collective-permute-done.25.refs_1_), channel_id=1, source_target_pairs={{0,1},{1,0},{2,3},{3,2},{4,5},{5,4},{6,7},{7,6},{8,9},{9,8},{10,11... | collective-permute-start | bytes 503816 | tf_op jit(solution)/shard_map/ppermute | solution.py:29
  76.8 1.6 %collective-permute-start.30 = (bf16[16,5248]{1,0:T(8,128)(2,1)S(1)}, bf16[16,5248]{1,0:T(8,128)(2,1)S(1)}, u32[]{:S(2)}, u32[]{:S(2)}) collective-permute-start(bf16[16,5248]{1,0:T(8,128)(2,1)S(1)} %collective-permute-done.26.refs_2_), channel_id=1, source_target_pairs={{0,1},{1,0},{2,3},{3,2},{4,5},{5,4},{6,7},{7,6},{8,9},{9,8},{10,11... | collective-permute-start | bytes 503816 | tf_op jit(solution)/shard_map/ppermute | solution.py:29
  78.4 1.4 %collective-permute-start.31 = (bf16[16,5248]{1,0:T(8,128)(2,1)S(1)}, bf16[16,5248]{1,0:T(8,128)(2,1)S(1)}, u32[]{:S(2)}, u32[]{:S(2)}) collective-permute-start(bf16[16,5248]{1,0:T(8,128)(2,1)S(1)} %collective-permute-done.27.refs_3_), channel_id=1, source_target_pairs={{0,1},{1,0},{2,3},{3,2},{4,5},{5,4},{6,7},{7,6},{8,9},{9,8},{10,11... | collective-permute-start | bytes 503816 | tf_op jit(solution)/shard_map/ppermute | solution.py:29
  82.9 2.2 %collective-permute-start.32 = (bf16[64,5120]{1,0:T(8,128)(2,1)S(1)}, bf16[64,5120]{1,0:T(8,128)(2,1)S(1)}, u32[]{:S(2)}, u32[]{:S(2)}) collective-permute-start(bf16[64,5120]{1,0:T(8,128)(2,1)S(1)} %get-tuple-element.97), channel_id=1, source_target_pairs={{0,1},{1,0},{2,3},{3,2},{4,5},{5,4},{6,7},{7,6},{8,9},{9,8},{10,11... | collective-permute-start | bytes 1966088 | tf_op jit(solution)/shard_map/ppermute | solution.py:29
  85.2 8.1 %collective-permute-start.33 = (bf16[16,5120]{1,0:T(8,128)(2,1)S(1)}, bf16[16,5120]{1,0:T(8,128)(2,1)S(1)}, u32[]{:S(2)}, u32[]{:S(2)}) collective-permute-start(bf16[16,5120]{1,0:T(8,128)(2,1)S(1)} %get-tuple-element.99), channel_id=1, source_target_pairs={{0,6},{1,7},{2,4},{3,5},{4,2},{5,3},{6,0},{7,1},{8,14},{9,15},{10,... | collective-permute-start | bytes 491528 | tf_op jit(solution)/shard_map/ppermute | solution.py:29
  86.4 9.5 %collective-permute-start.34 = (bf16[16,5120]{1,0:T(8,128)(2,1)S(1)}, bf16[16,5120]{1,0:T(8,128)(2,1)S(1)}, u32[]{:S(2)}, u32[]{:S(2)}) collective-permute-start(bf16[16,5120]{1,0:T(8,128)(2,1)S(1)} %get-tuple-element.100), channel_id=1, source_target_pairs={{0,4},{1,5},{2,6},{3,7},{4,0},{5,1},{6,2},{7,3},{8,12},{9,13},{10,... | collective-permute-start | bytes 491528 | tf_op jit(solution)/shard_map/ppermute | solution.py:29
  87.3 8.7 %collective-permute-start.35 = (bf16[16,5120]{1,0:T(8,128)(2,1)S(1)}, bf16[16,5120]{1,0:T(8,128)(2,1)S(1)}, u32[]{:S(2)}, u32[]{:S(2)}) collective-permute-start(bf16[16,5120]{1,0:T(8,128)(2,1)S(1)} %get-tuple-element.101), channel_id=1, source_target_pairs={{0,2},{1,3},{2,0},{3,1},{4,6},{5,7},{6,4},{7,5},{8,10},{9,11},{10,... | collective-permute-start | bytes 491528 | tf_op jit(solution)/shard_map/ppermute | solution.py:29
  96.1 6.0 %collective-permute-start.36 = (bf16[4,5120]{1,0:T(4,128)(2,1)S(1)}, bf16[4,5120]{1,0:T(4,128)(2,1)S(1)}, u32[]{:S(2)}, u32[]{:S(2)}) collective-permute-start(bf16[4,5120]{1,0:T(4,128)(2,1)S(1)} %get-tuple-element.112), channel_id=1, source_target_pairs={{0,24},{8,16},{16,8},{24,0},{1,25},{9,17},{17,9},{25,1},{2,26},{10... | collective-permute-start | bytes 122888 | tf_op jit(solution)/shard_map/ppermute | solution.py:29
  97.4 5.8 %collective-permute-start.37 = (bf16[4,5120]{1,0:T(4,128)(2,1)S(1)}, bf16[4,5120]{1,0:T(4,128)(2,1)S(1)}, u32[]{:S(2)}, u32[]{:S(2)}) collective-permute-start(bf16[4,5120]{1,0:T(4,128)(2,1)S(1)} %get-tuple-element.114), channel_id=1, source_target_pairs={{0,16},{8,24},{16,0},{24,8},{1,17},{9,25},{17,1},{25,9},{2,18},{10... | collective-permute-start | bytes 122888 | tf_op jit(solution)/shard_map/ppermute | solution.py:29
  97.6 5.6 %collective-permute-start.38 = (bf16[4,5120]{1,0:T(4,128)(2,1)S(1)}, bf16[4,5120]{1,0:T(4,128)(2,1)S(1)}, u32[]{:S(2)}, u32[]{:S(2)}) collective-permute-start(bf16[4,5120]{1,0:T(4,128)(2,1)S(1)} %get-tuple-element.113), channel_id=1, source_target_pairs={{0,8},{8,0},{16,24},{24,16},{1,9},{9,1},{17,25},{25,17},{2,10},{10... | collective-permute-start | bytes 122888 | tf_op jit(solution)/shard_map/ppermute | solution.py:29
  (3 other events, 19.7 us)

commit v6 on v5

--- a/solution.py
+++ b/solution.py
@@ -446,9 +446,9 @@
         queries + [top, total, even, odd] + chunks,
         40 * rows * prefix_pool.size,
     )
-    *held, top = lax.optimization_barrier((*late, state[0]))
+    late[-1], top = lax.optimization_barrier((late[-1], state[0]))
     state = [top, *state[1:]]
-    late = held + [swap(block, "expert", 1) for block in held]
+    late += [swap(block, "expert", 1) for block in late]
     half = members * row_count // 2
     keep, away = vmem_call(
         functools.partial(last_kernel, variants, chips, holders - 1, shard_blocks),

time: 104 us -> 103 us (level)
  transfers between devices with their start and end apart: 39 -> 39, of which waited for: 24 -> 21; matrix products, arithmetic and copies ran while one was open for 5% -> 5% of each run, Pallas kernels for 5% -> 5%
where the time goes in v6:
time: 103 us
  waiting for transfers between devices  42 us (41%)
  starting transfers between devices  39.6 us (38%)
  Pallas kernels  13.1 us (13%)
  local copies, waits for them, and re-layouts  4.15 us (4%)
  other arithmetic  2.84 us (3%)
  between operations  1.2 us (1%)
    ppermute x39, waiting for transfers between devices, swap(): return lax.ppermute(value, axis, [(i, i ^ mask) for i in range(size)])  42 us
    ppermute x39, starting transfers between devices, swap(): return lax.ppermute(value, axis, [(i, i ^ mask) for i in range(size)])  39.6 us
    pallas_call x11, Pallas kernels, vmem_call(): pl.pallas_call(kernel, out_shape=out_shape, in_specs=specs, out_specs=jax...  13.1 us
  transfers between devices with their start and end apart: 39, of which 21 were waited for; matrix products, arithmetic and copies ran while one was open for 5% of the time, Pallas kernels for 5%

profile of v6, /device:TPU:0, one launch (start us, length us, event | category | flops | bytes accessed | tf_op | source)
XLA Modules:
  0.0 102.9 jit_solution(5809142977721029307)
XLA Ops:
  0.6 0.9 constant_dynamic-slice_fusion
  1.6 4.1 %collective-permute-start.4 = (bf16[16,4608]{1,0:T(8,128)(2,1)S(1)}, bf16[16,4608]{1,0:T(8,128)(2,1)}, u32[]{:S(2)}, u32[]{:S(2)}) collective-permute-start(bf16[16,4608]{1,0:T(8,128)(2,1)S(1)} %constant_dynamic-slice_fusion), channel_id=1, source_target_pairs={{0,16},{8,24},{16,0},{24,8},{1,17},{9,25},{17,1},{25,9},{2,18},{10... | collective-permute-start | bytes 442376 | tf_op jit(solution)/shard_map/ppermute | solution.py:29
  5.7 1.6 %collective-permute-start.3 = (bf16[16,4608]{1,0:T(8,128)(2,1)S(1)}, bf16[16,4608]{1,0:T(8,128)(2,1)S(1)}, u32[]{:S(2)}, u32[]{:S(2)}) collective-permute-start(bf16[16,4608]{1,0:T(8,128)(2,1)S(1)} %constant_dynamic-slice_fusion), channel_id=1, source_target_pairs={{0,8},{8,0},{16,24},{24,16},{1,9},{9,1},{17,25},{25,17},{2,10},{10... | collective-permute-start | bytes 442376 | tf_op jit(solution)/shard_map/ppermute | solution.py:29
  7.3 0.7 iota_compare_fusion
  8.0 0.8 and_reduce_fusion
  8.8 1.0 constant_dynamic-slice_fusion.2
  10.1 2.5 %collective-permute-start.2 = (bf16[2,4,4736]{2,1,0:T(4,128)(2,1)S(1)}, bf16[2,4,4736]{2,1,0:T(4,128)(2,1)S(1)}, u32[]{:S(2)}, u32[]{:S(2)}) collective-permute-start(bf16[2,4,4736]{2,1,0:T(4,128)(2,1)S(1)} %pad_maximum_fusion.12), channel_id=1, source_target_pairs={{0,6},{1,7},{2,4},{3,5},{4,2},{5,3},{6,0},{7,1},{8,14},{9,15},{10,... | collective-permute-start | bytes 227336 | tf_op jit(solution)/shard_map/ppermute | solution.py:29
  12.6 0.6 collective-permute-start.1
  13.3 0.6 collective-permute-start
  14.0 0.6 collective-permute-start.6
  14.6 1.0 constant_dynamic-update-slice_fusion.refs_0_.refs_6_
  15.5 1.6 %collective-permute-start.8 = (bf16[32,4608]{1,0:T(8,128)(2,1)S(1)}, bf16[32,4608]{1,0:T(8,128)(2,1)S(1)}, u32[]{:S(2)}, u32[]{:S(2)}) collective-permute-start(bf16[32,4608]{1,0:T(8,128)(2,1)S(1)} %constant_dynamic-update-slice_fusion.refs_0_.refs_6_), channel_id=1, source_target_pairs={{0,2},{1,3},{2,0},{3,1},{4,6},{5,7},{6,4},{7,5},{8,10},{9,11},{10,... | collective-permute-start | bytes 884744 | tf_op jit(solution)/shard_map/ppermute | solution.py:29
  17.1 1.5 %collective-permute-start.9 = (bf16[32,4608]{1,0:T(8,128)(2,1)S(1)}, bf16[32,4608]{1,0:T(8,128)(2,1)S(1)}, u32[]{:S(2)}, u32[]{:S(2)}) collective-permute-start(bf16[32,4608]{1,0:T(8,128)(2,1)S(1)} %constant_dynamic-update-slice_fusion.refs_0_.refs_6_), channel_id=1, source_target_pairs={{0,4},{1,5},{2,6},{3,7},{4,0},{5,1},{6,2},{7,3},{8,12},{9,13},{10,... | collective-permute-start | bytes 884744 | tf_op jit(solution)/shard_map/ppermute | solution.py:29
  18.6 0.6 collective-permute-start.10
  19.3 0.7 reshape.70.keys_ref
  20.0 0.4 reshape.69.query_ref
  20.3 1.4 %shard_map.168 = (bf16[64,640]{1,0:T(8,128)(2,1)S(1)}, bf16[64,640]{1,0:T(8,128)(2,1)S(1)}, bf16[64,640]{1,0:T(8,128)(2,1)S(1)}, bf16[64,640]{1,0:T(8,128)(2,1)S(1)}) custom-call(s32[2]{0:T(128)S(1)} %pad_add_fusion.pos, bf16[4,64,576]{2,1,0:T(8,128)(2,1)S(1)} %reshape.69.query_ref, bf16[4,128,576]{2,1,0:T(8,128)(2,1)S(1)} %reshape.70.keys_ref, s32[4]{0:T(128)S(1)} %copy-done.17), custom_call_target="tpu_custom_call" | custom-call | flops 75497472 | bytes 884744 | tf_op jit(solution)/shard_map/pallas_call | solution.py:41
  21.9 2.4 %collective-permute-start.11 = (bf16[64,1792]{1,0:T(8,128)(2,1)S(1)}, bf16[64,1792]{1,0:T(8,128)(2,1)S(1)}, u32[]{:S(2)}, u32[]{:S(2)}) collective-permute-start(bf16[64,1792]{1,0:T(8,128)(2,1)S(1)} %get-tuple-element.67), channel_id=1, source_target_pairs={{0,2},{1,3},{2,0},{3,1},{4,6},{5,7},{6,4},{7,5},{8,10},{9,11},{10,... | collective-permute-start | bytes 688136 | tf_op jit(solution)/shard_map/ppermute | solution.py:29
  24.2 0.7 collective-permute-start.12
  25.0 7.8 %collective-permute-done.10.refs_3_.refs_9_ = bf16[32,4608]{1,0:T(8,128)(2,1)S(1)} collective-permute-done((bf16[32,4608]{1,0:T(8,128)(2,1)S(1)}, bf16[32,4608]{1,0:T(8,128)(2,1)S(1)}, u32[]{:S(2)}, u32[]{:S(2)}) %collective-permute-start.10) | collective-permute-done | bytes 294944 | tf_op jit(solution)/shard_map/ppermute | solution.py:29
  32.9 2.4 %collective-permute-done.11.refs_10_ = bf16[64,1792]{1,0:T(8,128)(2,1)S(1)} collective-permute-done((bf16[64,1792]{1,0:T(8,128)(2,1)S(1)}, bf16[64,1792]{1,0:T(8,128)(2,1)S(1)}, u32[]{:S(2)}, u32[]{:S(2)}) %collective-permute-start.11) | collective-permute-done | bytes 229408 | tf_op jit(solution)/shard_map/ppermute | solution.py:29
  35.3 0.4 collective-permute-done.12.refs_11_
  36.0 0.5 collective-permute-start.5
  36.5 1.5 %collective-permute-start.7 = (bf16[64,1792]{1,0:T(8,128)(2,1)S(1)}, bf16[64,1792]{1,0:T(8,128)(2,1)S(1)}, u32[]{:S(2)}, u32[]{:S(2)}) collective-permute-start(bf16[64,1792]{1,0:T(8,128)(2,1)S(1)} %get-tuple-element.62), channel_id=1, source_target_pairs={{0,6},{1,7},{2,4},{3,5},{4,2},{5,3},{6,0},{7,1},{8,14},{9,15},{10,... | collective-permute-start | bytes 688136 | tf_op jit(solution)/shard_map/ppermute | solution.py:29
  38.0 0.8 collective-permute-done.5.refs_1_
  38.9 1.3 %shard_map.167 = (bf16[256,640]{1,0:T(8,128)(2,1)S(1)}, bf16[256,640]{1,0:T(8,128)(2,1)S(1)}, f32[256,128]{1,0:T(8,128)S(1)}, f32[256,128]{1,0:T(8,128)S(1)}, f3...) custom-call(bf16[16,36864]{1,0:T(8,128)(2,1)S(1)} %copy-done.14, bf16[4,4,4736]{2,1,0:T(4,128)(2,1)S(1)} %collective-permute-done.5.refs_1_, ...), custom_call_target="tpu_custom_call" | custom-call | flops 6039797760 | bytes 1634304 | tf_op jit(solution)/shard_map/pallas_call | solution.py:41
  40.3 0.4 collective-permute-start.16
  40.8 2.5 %shard_map.171 = (f32[256,128]{1,0:T(8,128)S(1)}, f32[256,128]{1,0:T(8,128)S(1)}, f32[256,512]{1,0:T(8,128)S(1)}, f32[256,640]{1,0:T(8,128)S(1)}) custom-call(bf16[256,640]{1,0:T(8,128)(2,1)S(1)} %get-tuple-element.53.refs_0_, bf16[256,640]{1,0:T(8,128)(2,1)S(1)} %get-tuple-element.54.refs_1_, f32[256,128]{1,0:T(8,128)S(1)} %get-tuple-element.63.refs_2_, ...), custom_call_target="tpu_custom_call" | custom-call | flops 6039797760 | bytes 4456448 | tf_op jit(solution)/shard_map/pallas_call | solution.py:41
  43.3 1.7 %collective-permute-done.7.refs_12_ = bf16[64,1792]{1,0:T(8,128)(2,1)S(1)} collective-permute-done((bf16[64,1792]{1,0:T(8,128)(2,1)S(1)}, bf16[64,1792]{1,0:T(8,128)(2,1)S(1)}, u32[]{:S(2)}, u32[]{:S(2)}) %collective-permute-start.7) | collective-permute-done | bytes 229408 | tf_op jit(solution)/shard_map/ppermute | solution.py:29
  45.0 1.5 %collective-permute-done.17.refs_16_ = bf16[64,1792]{1,0:T(8,128)(2,1)S(1)} collective-permute-done((bf16[64,1792]{1,0:T(8,128)(2,1)S(1)}, bf16[64,1792]{1,0:T(8,128)(2,1)S(1)}, u32[]{:S(2)}, u32[]{:S(2)}) %collective-permute-start.17) | collective-permute-done | bytes 229408 | tf_op jit(solution)/shard_map/ppermute | solution.py:29
  46.6 3.7 %shard_map.172 = (f32[16,5120]{1,0:T(8,128)S(1)}, bf16[16,5120]{1,0:T(8,128)(2,1)S(1)}) custom-call(bf16[256,640]{1,0:T(8,128)(2,1)S(1)} %get-tuple-element.53.refs_0_, bf16[256,640]{1,0:T(8,128)(2,1)S(1)} %get-tuple-element.54.refs_1_, f32[256,128]{1,0:T(8,128)S(1)} %get-tuple-element.74.refs_2_, f32[256,128]{1,0:T(8,128)S(1)} %get-tuple-element.75.refs_3_, ...), custom_call_target="tpu_custom_call" | custom-call | flops 939524096 | bytes 15597568 | tf_op jit(solution)/shard_map/pallas_call | solution.py:41
  50.4 1.3 %collective-permute-done.18.away_ref = bf16[16,5120]{1,0:T(8,128)(2,1)S(1)} collective-permute-done((bf16[16,5120]{1,0:T(8,128)(2,1)S(1)}, bf16[16,5120]{1,0:T(8,128)(2,1)S(1)}, u32[]{:S(2)}, u32[]{:S(2)}) %collective-permute-start.18) | collective-permute-done | bytes 163872 | tf_op jit(solution)/shard_map/ppermute | solution.py:29
  51.8 1.6 %collective-permute-start.19 = (bf16[4,5120]{1,0:T(4,128)(2,1)S(1)}, bf16[4,5120]{1,0:T(4,128)(2,1)S(1)}, u32[]{:S(2)}, u32[]{:S(2)}) collective-permute-start(bf16[4,5120]{1,0:T(4,128)(2,1)S(1)} %get-tuple-element.85), channel_id=1, source_target_pairs={{0,6},{1,7},{2,4},{3,5},{4,2},{5,3},{6,0},{7,1},{8,14},{9,15},{10,... | collective-permute-start | bytes 122888 | tf_op jit(solution)/shard_map/ppermute | solution.py:29
  53.3 0.5 collective-permute-start.20
  53.8 1.5 %collective-permute-start.21 = (bf16[4,5120]{1,0:T(4,128)(2,1)S(1)}, bf16[4,5120]{1,0:T(4,128)(2,1)S(1)}, u32[]{:S(2)}, u32[]{:S(2)}) collective-permute-start(bf16[4,5120]{1,0:T(4,128)(2,1)S(1)} %get-tuple-element.87), channel_id=1, source_target_pairs={{0,2},{1,3},{2,0},{3,1},{4,6},{5,7},{6,4},{7,5},{8,10},{9,11},{10,... | collective-permute-start | bytes 122888 | tf_op jit(solution)/shard_map/ppermute | solution.py:29
  55.4 1.4 %collective-permute-done.19.refs_0_ = bf16[4,5120]{1,0:T(4,128)(2,1)S(1)} collective-permute-done((bf16[4,5120]{1,0:T(4,128)(2,1)S(1)}, bf16[4,5120]{1,0:T(4,128)(2,1)S(1)}, u32[]{:S(2)}, u32[]{:S(2)}) %collective-permute-start.19) | collective-permute-done | bytes 40992 | tf_op jit(solution)/shard_map/ppermute | solution.py:29
  56.8 0.5 collective-permute-done.20.refs_1_
  57.3 0.5 collective-permute-done.21.refs_2_
  57.9 0.7 shard_map.174
  58.5 1.0 collective-permute-start.22
  59.5 2.7 %collective-permute-start.23 = (bf16[4,5248]{1,0:T(4,128)(2,1)S(1)}, bf16[4,5248]{1,0:T(4,128)(2,1)S(1)}, u32[]{:S(2)}, u32[]{:S(2)}) collective-permute-start(bf16[4,5248]{1,0:T(4,128)(2,1)S(1)} %get-tuple-element.89.refs_0_), channel_id=1, source_target_pairs={{0,16},{8,24},{16,0},{24,8},{1,17},{9,25},{17,1},{25,9},{2,18},{10... | collective-permute-start | bytes 125960 | tf_op jit(solution)/shard_map/ppermute | solution.py:29
  62.2 1.2 %collective-permute-start.24 = (bf16[4,5248]{1,0:T(4,128)(2,1)S(1)}, bf16[4,5248]{1,0:T(4,128)(2,1)S(1)}, u32[]{:S(2)}, u32[]{:S(2)}) collective-permute-start(bf16[4,5248]{1,0:T(4,128)(2,1)S(1)} %get-tuple-element.89.refs_0_), channel_id=1, source_target_pairs={{0,24},{8,16},{16,8},{24,0},{1,25},{9,17},{17,9},{25,1},{2,26},{10... | collective-permute-start | bytes 125960 | tf_op jit(solution)/shard_map/ppermute | solution.py:29
  63.4 1.0 %collective-permute-done.23.refs_2_ = bf16[4,5248]{1,0:T(4,128)(2,1)S(1)} collective-permute-done((bf16[4,5248]{1,0:T(4,128)(2,1)S(1)}, bf16[4,5248]{1,0:T(4,128)(2,1)S(1)}, u32[]{:S(2)}, u32[]{:S(2)}) %collective-permute-start.23) | collective-permute-done | bytes 42016 | tf_op jit(solution)/shard_map/ppermute | solution.py:29
  64.4 3.6 %collective-permute-done.24.refs_3_ = bf16[4,5248]{1,0:T(4,128)(2,1)S(1)} collective-permute-done((bf16[4,5248]{1,0:T(4,128)(2,1)S(1)}, bf16[4,5248]{1,0:T(4,128)(2,1)S(1)}, u32[]{:S(2)}, u32[]{:S(2)}) %collective-permute-start.24) | collective-permute-done | bytes 42016 | tf_op jit(solution)/shard_map/ppermute | solution.py:29
  68.1 1.6 %collective-permute-start.25 = (bf16[16,5248]{1,0:T(8,128)(2,1)S(1)}, bf16[16,5248]{1,0:T(8,128)(2,1)S(1)}, u32[]{:S(2)}, u32[]{:S(2)}) collective-permute-start(bf16[16,5248]{1,0:T(8,128)(2,1)S(1)} %shard_map.175.refs_0_), channel_id=1, source_target_pairs={{0,2},{1,3},{2,0},{3,1},{4,6},{5,7},{6,4},{7,5},{8,10},{9,11},{10,... | collective-permute-start | bytes 503816 | tf_op jit(solution)/shard_map/ppermute | solution.py:29
  69.6 1.5 %collective-permute-start.26 = (bf16[16,5248]{1,0:T(8,128)(2,1)S(1)}, bf16[16,5248]{1,0:T(8,128)(2,1)S(1)}, u32[]{:S(2)}, u32[]{:S(2)}) collective-permute-start(bf16[16,5248]{1,0:T(8,128)(2,1)S(1)} %shard_map.175.refs_0_), channel_id=1, source_target_pairs={{0,4},{1,5},{2,6},{3,7},{4,0},{5,1},{6,2},{7,3},{8,12},{9,13},{10,... | collective-permute-start | bytes 503816 | tf_op jit(solution)/shard_map/ppermute | solution.py:29
  71.1 0.5 collective-permute-start.27
  71.6 2.3 %collective-permute-done.25.refs_1_ = bf16[16,5248]{1,0:T(8,128)(2,1)S(1)} collective-permute-done((bf16[16,5248]{1,0:T(8,128)(2,1)S(1)}, bf16[16,5248]{1,0:T(8,128)(2,1)S(1)}, u32[]{:S(2)}, u32[]{:S(2)}) %collective-permute-start.25) | collective-permute-done | bytes 167968 | tf_op jit(solution)/shard_map/ppermute | solution.py:29
  73.9 1.9 %collective-permute-done.26.refs_2_ = bf16[16,5248]{1,0:T(8,128)(2,1)S(1)} collective-permute-done((bf16[16,5248]{1,0:T(8,128)(2,1)S(1)}, bf16[16,5248]{1,0:T(8,128)(2,1)S(1)}, u32[]{:S(2)}, u32[]{:S(2)}) %collective-permute-start.26) | collective-permute-done | bytes 167968 | tf_op jit(solution)/shard_map/ppermute | solution.py:29
  75.9 1.5 %collective-permute-done.27.refs_3_ = bf16[16,5248]{1,0:T(8,128)(2,1)S(1)} collective-permute-done((bf16[16,5248]{1,0:T(8,128)(2,1)S(1)}, bf16[16,5248]{1,0:T(8,128)(2,1)S(1)}, u32[]{:S(2)}, u32[]{:S(2)}) %collective-permute-start.27) | collective-permute-done | bytes 167968 | tf_op jit(solution)/shard_map/ppermute | solution.py:29
  77.4 1.4 %collective-permute-done.31.refs_7_ = bf16[16,5248]{1,0:T(8,128)(2,1)S(1)} collective-permute-done((bf16[16,5248]{1,0:T(8,128)(2,1)S(1)}, bf16[16,5248]{1,0:T(8,128)(2,1)S(1)}, u32[]{:S(2)}, u32[]{:S(2)}) %collective-permute-start.31) | collective-permute-done | bytes 167968 | tf_op jit(solution)/shard_map/ppermute | solution.py:29
  78.8 3.1 %shard_map.176 = (f32[64,5120]{1,0:T(8,128)S(1)}, bf16[64,5120]{1,0:T(8,128)(2,1)S(1)}) custom-call(s32[2]{0:T(128)S(1)} %pad_add_fusion.pos, bf16[16,5248]{1,0:T(8,128)(2,1)S(1)} %shard_map.175.refs_0_, bf16[16,5248]{1,0:T(8,128)(2,1)S(1)} %collective-permute-done.25.refs_1_, bf16[16,5248]{1,0:T(8,128)(2,1)S(1)} %collective-permute-done.26.refs_2_, ...), custom_call_target="tpu_custom_call" | custom-call | flops 1509949440 | bytes 13139976 | tf_op jit(solution)/shard_map/pallas_call | solution.py:41
  81.9 0.2 collective-permute-start.32
  82.1 2.0 %collective-permute-done.32.away_ref = bf16[64,5120]{1,0:T(8,128)(2,1)S(1)} collective-permute-done((bf16[64,5120]{1,0:T(8,128)(2,1)S(1)}, bf16[64,5120]{1,0:T(8,128)(2,1)S(1)}, u32[]{:S(2)}, u32[]{:S(2)}) %collective-permute-start.32) | collective-permute-done | bytes 655392 | tf_op jit(solution)/shard_map/ppermute | solution.py:29
  84.2 1.2 %collective-permute-start.33 = (bf16[16,5120]{1,0:T(8,128)(2,1)S(1)}, bf16[16,5120]{1,0:T(8,128)(2,1)S(1)}, u32[]{:S(2)}, u32[]{:S(2)}) collective-permute-start(bf16[16,5120]{1,0:T(8,128)(2,1)S(1)} %get-tuple-element.93), channel_id=1, source_target_pairs={{0,6},{1,7},{2,4},{3,5},{4,2},{5,3},{6,0},{7,1},{8,14},{9,15},{10,... | collective-permute-start | bytes 491528 | tf_op jit(solution)/shard_map/ppermute | solution.py:29
  85.4 0.9 collective-permute-start.34
  86.3 1.5 %collective-permute-start.35 = (bf16[16,5120]{1,0:T(8,128)(2,1)S(1)}, bf16[16,5120]{1,0:T(8,128)(2,1)S(1)}, u32[]{:S(2)}, u32[]{:S(2)}) collective-permute-start(bf16[16,5120]{1,0:T(8,128)(2,1)S(1)} %get-tuple-element.95), channel_id=1, source_target_pairs={{0,2},{1,3},{2,0},{3,1},{4,6},{5,7},{6,4},{7,5},{8,10},{9,11},{10,... | collective-permute-start | bytes 491528 | tf_op jit(solution)/shard_map/ppermute | solution.py:29
  87.8 4.5 %collective-permute-done.33 = bf16[16,5120]{1,0:T(8,128)(2,1)S(1)} collective-permute-done((bf16[16,5120]{1,0:T(8,128)(2,1)S(1)}, bf16[16,5120]{1,0:T(8,128)(2,1)S(1)}, u32[]{:S(2)}, u32[]{:S(2)}) %collective-permute-start.33) | collective-permute-done | bytes 163872 | tf_op jit(solution)/shard_map/ppermute | solution.py:29
  92.3 2.7 %collective-permute-done.34 = bf16[16,5120]{1,0:T(8,128)(2,1)S(1)} collective-permute-done((bf16[16,5120]{1,0:T(8,128)(2,1)S(1)}, bf16[16,5120]{1,0:T(8,128)(2,1)S(1)}, u32[]{:S(2)}, u32[]{:S(2)}) %collective-permute-start.34) | collective-permute-done | bytes 163872 | tf_op jit(solution)/shard_map/ppermute | solution.py:29
  95.1 1.4 %collective-permute-start.36 = (bf16[4,5120]{1,0:T(4,128)(2,1)S(1)}, bf16[4,5120]{1,0:T(4,128)(2,1)S(1)}, u32[]{:S(2)}, u32[]{:S(2)}) collective-permute-start(bf16[4,5120]{1,0:T(4,128)(2,1)S(1)} %get-tuple-element.106), channel_id=1, source_target_pairs={{0,24},{8,16},{16,8},{24,0},{1,25},{9,17},{17,9},{25,1},{2,26},{10... | collective-permute-start | bytes 122888 | tf_op jit(solution)/shard_map/ppermute | solution.py:29
  96.6 2.9 %collective-permute-start.38 = (bf16[4,5120]{1,0:T(4,128)(2,1)S(1)}, bf16[4,5120]{1,0:T(4,128)(2,1)S(1)}, u32[]{:S(2)}, u32[]{:S(2)}) collective-permute-start(bf16[4,5120]{1,0:T(4,128)(2,1)S(1)} %get-tuple-element.107), channel_id=1, source_target_pairs={{0,8},{8,0},{16,24},{24,16},{1,9},{9,1},{17,25},{25,17},{2,10},{10... | collective-permute-start | bytes 122888 | tf_op jit(solution)/shard_map/ppermute | solution.py:29
  99.5 1.5 %collective-permute-done.36 = bf16[4,5120]{1,0:T(4,128)(2,1)S(1)} collective-permute-done((bf16[4,5120]{1,0:T(4,128)(2,1)S(1)}, bf16[4,5120]{1,0:T(4,128)(2,1)S(1)}, u32[]{:S(2)}, u32[]{:S(2)}) %collective-permute-start.36) | collective-permute-done | bytes 40992 | tf_op jit(solution)/shard_map/ppermute | solution.py:29
  101.0 1.2 %collective-permute-done.37 = bf16[4,5120]{1,0:T(4,128)(2,1)S(1)} collective-permute-done((bf16[4,5120]{1,0:T(4,128)(2,1)S(1)}, bf16[4,5120]{1,0:T(4,128)(2,1)S(1)}, u32[]{:S(2)}, u32[]{:S(2)}) %collective-permute-start.37) | collective-permute-done | bytes 40992 | tf_op jit(solution)/shard_map/ppermute | solution.py:29
  102.2 0.7 fusion.1
  (103 shorter events, 1.9 us)
Async XLA Ops:
  1.6 17.7 %copy-start.19 = (bf16[4,73728]{1,0:T(4,128)(2,1)S(1)}, bf16[4,73728]{1,0:T(4,128)(2,1)}, u32[]{:S(2)}) copy-start(bf16[4,73728]{1,0:T(4,128)(2,1)} %param.19) | copy-start | bytes 1769476
  1.6 12.4 %collective-permute-start.4 = (bf16[16,4608]{1,0:T(8,128)(2,1)S(1)}, bf16[16,4608]{1,0:T(8,128)(2,1)}, u32[]{:S(2)}, u32[]{:S(2)}) collective-permute-start(bf16[16,4608]{1,0:T(8,128)(2,1)S(1)} %constant_dynamic-slice_fusion), channel_id=1, source_target_pairs={{0,16},{8,24},{16,0},{24,8},{1,17},{9,25},{17,1},{25,9},{2,18},{10... | collective-permute-start | bytes 442376 | tf_op jit(solution)/shard_map/ppermute | solution.py:29
  5.7 8.3 %collective-permute-start.3 = (bf16[16,4608]{1,0:T(8,128)(2,1)S(1)}, bf16[16,4608]{1,0:T(8,128)(2,1)S(1)}, u32[]{:S(2)}, u32[]{:S(2)}) collective-permute-start(bf16[16,4608]{1,0:T(8,128)(2,1)S(1)} %constant_dynamic-slice_fusion), channel_id=1, source_target_pairs={{0,8},{8,0},{16,24},{24,16},{1,9},{9,1},{17,25},{25,17},{2,10},{10... | collective-permute-start | bytes 442376 | tf_op jit(solution)/shard_map/ppermute | solution.py:29
  10.0 10.0 %copy-start.18 = (bf16[4,36864]{1,0:T(4,128)(2,1)S(1)}, bf16[4,36864]{1,0:T(4,128)(2,1)}, u32[]{:S(2)}) copy-start(bf16[4,36864]{1,0:T(4,128)(2,1)} %param.17) | copy-start | bytes 884740
  10.1 7.0 %collective-permute-start.2 = (bf16[2,4,4736]{2,1,0:T(4,128)(2,1)S(1)}, bf16[2,4,4736]{2,1,0:T(4,128)(2,1)S(1)}, u32[]{:S(2)}, u32[]{:S(2)}) collective-permute-start(bf16[2,4,4736]{2,1,0:T(4,128)(2,1)S(1)} %pad_maximum_fusion.12), channel_id=1, source_target_pairs={{0,6},{1,7},{2,4},{3,5},{4,2},{5,3},{6,0},{7,1},{8,14},{9,15},{10,... | collective-permute-start | bytes 227336 | tf_op jit(solution)/shard_map/ppermute | solution.py:29
  12.6 6.0 %collective-permute-start.1 = (bf16[2,4,4736]{2,1,0:T(4,128)(2,1)S(1)}, bf16[2,4,4736]{2,1,0:T(4,128)(2,1)S(1)}, u32[]{:S(2)}, u32[]{:S(2)}) collective-permute-start(bf16[2,4,4736]{2,1,0:T(4,128)(2,1)S(1)} %pad_maximum_fusion.11), channel_id=1, source_target_pairs={{0,4},{1,5},{2,6},{3,7},{4,0},{5,1},{6,2},{7,3},{8,12},{9,13},{10,... | collective-permute-start | bytes 227336 | tf_op jit(solution)/shard_map/ppermute | solution.py:29
  13.3 7.1 %copy-start.17 = (s32[4]{0:T(128)S(1)}, s32[4]{0:T(128)}, u32[]{:S(2)}) copy-start(s32[4]{0:T(128)} %count_hbm.1) | copy-start | bytes 52
  13.3 5.3 %collective-permute-start = (bf16[2,4,4736]{2,1,0:T(4,128)(2,1)S(1)}, bf16[2,4,4736]{2,1,0:T(4,128)(2,1)S(1)}, u32[]{:S(2)}, u32[]{:S(2)}) collective-permute-start(bf16[2,4,4736]{2,1,0:T(4,128)(2,1)S(1)} %pad_maximum_fusion.10), channel_id=1, source_target_pairs={{0,2},{1,3},{2,0},{3,1},{4,6},{5,7},{6,4},{7,5},{8,10},{9,11},{10,... | collective-permute-start | bytes 227336 | tf_op jit(solution)/shard_map/ppermute | solution.py:29
  13.9 11.0 %copy-start.4 = (bf16[2,4,4736]{2,1,0:T(4,128)(2,1)}, bf16[2,4,4736]{2,1,0:T(4,128)(2,1)S(1)}, u32[]{:S(2)}) copy-start(bf16[2,4,4736]{2,1,0:T(4,128)(2,1)S(1)} %pad_maximum_fusion.9.refs_2_) | copy-start | bytes 227332
  14.0 7.8 %collective-permute-start.6 = (bf16[16,4608]{1,0:T(8,128)(2,1)}, bf16[16,4608]{1,0:T(8,128)(2,1)S(1)}, u32[]{:S(2)}, u32[]{:S(2)}) collective-permute-start(bf16[16,4608]{1,0:T(8,128)(2,1)} %collective-permute-done.4), channel_id=1, source_target_pairs={{0,8},{8,0},{16,24},{24,16},{1,9},{9,1},{17,25},{25,17},{2,10},{10... | collective-permute-start | bytes 442376 | tf_op jit(solution)/shard_map/ppermute | solution.py:29
  15.5 17.3 %collective-permute-start.8 = (bf16[32,4608]{1,0:T(8,128)(2,1)S(1)}, bf16[32,4608]{1,0:T(8,128)(2,1)S(1)}, u32[]{:S(2)}, u32[]{:S(2)}) collective-permute-start(bf16[32,4608]{1,0:T(8,128)(2,1)S(1)} %constant_dynamic-update-slice_fusion.refs_0_.refs_6_), channel_id=1, source_target_pairs={{0,2},{1,3},{2,0},{3,1},{4,6},{5,7},{6,4},{7,5},{8,10},{9,11},{10,... | collective-permute-start | bytes 884744 | tf_op jit(solution)/shard_map/ppermute | solution.py:29
  17.1 7.9 %copy-start.8 = (bf16[2,4,4736]{2,1,0:T(4,128)(2,1)}, bf16[2,4,4736]{2,1,0:T(4,128)(2,1)S(1)}, u32[]{:S(2)}) copy-start(bf16[2,4,4736]{2,1,0:T(4,128)(2,1)S(1)} %collective-permute-done.2.refs_5_) | copy-start | bytes 227332
  17.1 15.8 %collective-permute-start.9 = (bf16[32,4608]{1,0:T(8,128)(2,1)S(1)}, bf16[32,4608]{1,0:T(8,128)(2,1)S(1)}, u32[]{:S(2)}, u32[]{:S(2)}) collective-permute-start(bf16[32,4608]{1,0:T(8,128)(2,1)S(1)} %constant_dynamic-update-slice_fusion.refs_0_.refs_6_), channel_id=1, source_target_pairs={{0,4},{1,5},{2,6},{3,7},{4,0},{5,1},{6,2},{7,3},{8,12},{9,13},{10,... | collective-permute-start | bytes 884744 | tf_op jit(solution)/shard_map/ppermute | solution.py:29
  18.6 6.3 %copy-start.10 = (bf16[2,4,4736]{2,1,0:T(4,128)(2,1)}, bf16[2,4,4736]{2,1,0:T(4,128)(2,1)S(1)}, u32[]{:S(2)}) copy-start(bf16[2,4,4736]{2,1,0:T(4,128)(2,1)S(1)} %collective-permute-done.1.refs_4_) | copy-start | bytes 227332
  18.6 6.3 %copy-start.12 = (bf16[2,4,4736]{2,1,0:T(4,128)(2,1)}, bf16[2,4,4736]{2,1,0:T(4,128)(2,1)S(1)}, u32[]{:S(2)}) copy-start(bf16[2,4,4736]{2,1,0:T(4,128)(2,1)S(1)} %collective-permute-done.refs_3_) | copy-start | bytes 227332
  18.6 14.2 %collective-permute-start.10 = (bf16[32,4608]{1,0:T(8,128)(2,1)S(1)}, bf16[32,4608]{1,0:T(8,128)(2,1)S(1)}, u32[]{:S(2)}, u32[]{:S(2)}) collective-permute-start(bf16[32,4608]{1,0:T(8,128)(2,1)S(1)} %constant_dynamic-update-slice_fusion.refs_0_.refs_6_), channel_id=1, source_target_pairs={{0,6},{1,7},{2,4},{3,5},{4,2},{5,3},{6,0},{7,1},{8,14},{9,15},{10,... | collective-permute-start | bytes 884744 | tf_op jit(solution)/shard_map/ppermute | solution.py:29
  21.9 13.4 %collective-permute-start.11 = (bf16[64,1792]{1,0:T(8,128)(2,1)S(1)}, bf16[64,1792]{1,0:T(8,128)(2,1)S(1)}, u32[]{:S(2)}, u32[]{:S(2)}) collective-permute-start(bf16[64,1792]{1,0:T(8,128)(2,1)S(1)} %get-tuple-element.67), channel_id=1, source_target_pairs={{0,2},{1,3},{2,0},{3,1},{4,6},{5,7},{6,4},{7,5},{8,10},{9,11},{10,... | collective-permute-start | bytes 688136 | tf_op jit(solution)/shard_map/ppermute | solution.py:29
  24.2 11.4 %collective-permute-start.12 = (bf16[64,1792]{1,0:T(8,128)(2,1)S(1)}, bf16[64,1792]{1,0:T(8,128)(2,1)S(1)}, u32[]{:S(2)}, u32[]{:S(2)}) collective-permute-start(bf16[64,1792]{1,0:T(8,128)(2,1)S(1)} %get-tuple-element.68), channel_id=1, source_target_pairs={{0,4},{1,5},{2,6},{3,7},{4,0},{5,1},{6,2},{7,3},{8,12},{9,13},{10,... | collective-permute-start | bytes 688136 | tf_op jit(solution)/shard_map/ppermute | solution.py:29
  24.9 10.9 %slice-start.3 = ((bf16[2,4,4736]{2,1,0:T(4,128)(2,1)}), bf16[1,4,4736]{2,1,0:T(4,128)(2,1)S(1)}, s32[]{:S(2)}) async-start(bf16[2,4,4736]{2,1,0:T(4,128)(2,1)} %copy-done.4), calls=%async_computation.3 | async-start | bytes 75776 | tf_op jit(solution)/shard_map/slice | solution.py:431
  24.9 10.9 %slice-start.6 = ((bf16[2,4,4736]{2,1,0:T(4,128)(2,1)}), bf16[1,4,4736]{2,1,0:T(4,128)(2,1)S(1)}, s32[]{:S(2)}) async-start(bf16[2,4,4736]{2,1,0:T(4,128)(2,1)} %copy-done.12), calls=%async_computation.6 | async-start | bytes 75776 | tf_op jit(solution)/shard_map/slice | solution.py:431
  24.9 10.9 %slice-start.5 = ((bf16[2,4,4736]{2,1,0:T(4,128)(2,1)}), bf16[1,4,4736]{2,1,0:T(4,128)(2,1)S(1)}, s32[]{:S(2)}) async-start(bf16[2,4,4736]{2,1,0:T(4,128)(2,1)} %copy-done.10), calls=%async_computation.5 | async-start | bytes 75776 | tf_op jit(solution)/shard_map/slice | solution.py:431
  25.0 10.9 %slice-start.4 = ((bf16[2,4,4736]{2,1,0:T(4,128)(2,1)}), bf16[1,4,4736]{2,1,0:T(4,128)(2,1)S(1)}, s32[]{:S(2)}) async-start(bf16[2,4,4736]{2,1,0:T(4,128)(2,1)} %copy-done.8), calls=%async_computation.4 | async-start | bytes 75776 | tf_op jit(solution)/shard_map/slice | solution.py:431
  25.0 13.9 %copy-start.5 = (bf16[2,4,4736]{2,1,0:T(4,128)(2,1)S(1)}, bf16[2,4,4736]{2,1,0:T(4,128)(2,1)}, u32[]{:S(2)}) copy-start(bf16[2,4,4736]{2,1,0:T(4,128)(2,1)} %copy-done.4) | copy-start | bytes 227332
  25.0 13.9 %copy-start.9 = (bf16[2,4,4736]{2,1,0:T(4,128)(2,1)S(1)}, bf16[2,4,4736]{2,1,0:T(4,128)(2,1)}, u32[]{:S(2)}) copy-start(bf16[2,4,4736]{2,1,0:T(4,128)(2,1)} %copy-done.8) | copy-start | bytes 227332
  25.0 13.9 %copy-start.11 = (bf16[2,4,4736]{2,1,0:T(4,128)(2,1)S(1)}, bf16[2,4,4736]{2,1,0:T(4,128)(2,1)}, u32[]{:S(2)}) copy-start(bf16[2,4,4736]{2,1,0:T(4,128)(2,1)} %copy-done.10) | copy-start | bytes 227332
  25.0 13.8 %copy-start.13 = (bf16[2,4,4736]{2,1,0:T(4,128)(2,1)S(1)}, bf16[2,4,4736]{2,1,0:T(4,128)(2,1)}, u32[]{:S(2)}) copy-start(bf16[2,4,4736]{2,1,0:T(4,128)(2,1)} %copy-done.12) | copy-start | bytes 227332
  25.0 13.8 %copy-start.14 = (bf16[16,36864]{1,0:T(8,128)(2,1)S(1)}, bf16[16,36864]{1,0:T(8,128)(2,1)}, u32[]{:S(2)}) copy-start(bf16[16,36864]{1,0:T(8,128)(2,1)} %refs_0_.1) | copy-start | bytes 3538948
  35.7 5.0 %collective-permute-start.13 = (bf16[128,4608]{1,0:T(8,128)(2,1)S(1)}, bf16[128,4608]{1,0:T(8,128)(2,1)S(1)}, u32[]{:S(2)}, u32[]{:S(2)}) collective-permute-start(bf16[128,4608]{1,0:T(8,128)(2,1)S(1)} %shard_map.170), channel_id=1, source_target_pairs={{0,1},{1,0},{2,3},{3,2},{4,5},{5,4},{6,7},{7,6},{8,9},{9,8},{10,11... | collective-permute-start | bytes 3538952 | tf_op jit(solution)/shard_map/ppermute | solution.py:29
  36.0 2.9 %collective-permute-start.5 = (bf16[4,4,4736]{2,1,0:T(4,128)(2,1)S(1)}, bf16[4,4,4736]{2,1,0:T(4,128)(2,1)S(1)}, u32[]{:S(2)}, u32[]{:S(2)}) collective-permute-start(bf16[4,4,4736]{2,1,0:T(4,128)(2,1)S(1)} %pad_maximum_fusion), channel_id=1, source_target_pairs={{0,1},{1,0},{2,3},{3,2},{4,5},{5,4},{6,7},{7,6},{8,9},{9,8},{10,11... | collective-permute-start | bytes 454664 | tf_op jit(solution)/shard_map/ppermute | solution.py:29
  36.5 8.5 %collective-permute-start.7 = (bf16[64,1792]{1,0:T(8,128)(2,1)S(1)}, bf16[64,1792]{1,0:T(8,128)(2,1)S(1)}, u32[]{:S(2)}, u32[]{:S(2)}) collective-permute-start(bf16[64,1792]{1,0:T(8,128)(2,1)S(1)} %get-tuple-element.62), channel_id=1, source_target_pairs={{0,6},{1,7},{2,4},{3,5},{4,2},{5,3},{6,0},{7,1},{8,14},{9,15},{10,... | collective-permute-start | bytes 688136 | tf_op jit(solution)/shard_map/ppermute | solution.py:29
  38.0 7.0 %collective-permute-start.14 = (bf16[64,1792]{1,0:T(8,128)(2,1)S(1)}, bf16[64,1792]{1,0:T(8,128)(2,1)S(1)}, u32[]{:S(2)}, u32[]{:S(2)}) collective-permute-start(bf16[64,1792]{1,0:T(8,128)(2,1)S(1)} %get-tuple-element.78.refs_9_), channel_id=1, source_target_pairs={{0,1},{1,0},{2,3},{3,2},{4,5},{5,4},{6,7},{7,6},{8,9},{9,8},{10,11... | collective-permute-start | bytes 688136 | tf_op jit(solution)/shard_map/ppermute | solution.py:29
  40.1 4.9 %collective-permute-start.15 = (bf16[64,1792]{1,0:T(8,128)(2,1)S(1)}, bf16[64,1792]{1,0:T(8,128)(2,1)S(1)}, u32[]{:S(2)}, u32[]{:S(2)}) collective-permute-start(bf16[64,1792]{1,0:T(8,128)(2,1)S(1)} %collective-permute-done.11.refs_10_), channel_id=1, source_target_pairs={{0,1},{1,0},{2,3},{3,2},{4,5},{5,4},{6,7},{7,6},{8,9},{9,8},{10,11... | collective-permute-start | bytes 688136 | tf_op jit(solution)/shard_map/ppermute | solution.py:29
  40.3 4.7 %collective-permute-start.16 = (bf16[64,1792]{1,0:T(8,128)(2,1)S(1)}, bf16[64,1792]{1,0:T(8,128)(2,1)S(1)}, u32[]{:S(2)}, u32[]{:S(2)}) collective-permute-start(bf16[64,1792]{1,0:T(8,128)(2,1)S(1)} %collective-permute-done.12.refs_11_), channel_id=1, source_target_pairs={{0,1},{1,0},{2,3},{3,2},{4,5},{5,4},{6,7},{7,6},{8,9},{9,8},{10,11... | collective-permute-start | bytes 688136 | tf_op jit(solution)/shard_map/ppermute | solution.py:29
  40.7 5.8 %slice-start.1 = ((s8[10485760]{0:T(1024)(128)(4,1)}), s8[4194304]{0:T(1024)(128)(4,1)S(1)}, s32[]{:S(2)}) async-start(s8[10485760]{0:T(1024)(128)(4,1)} %bitcast.18), calls=%async_computation.1 | async-start | bytes 8388608
  40.7 5.8 %slice-start.2 = ((s8[10485760]{0:T(1024)(128)(4,1)}), s8[2097152]{0:T(1024)(128)(4,1)S(1)}, s32[]{:S(2)}) async-start(s8[10485760]{0:T(1024)(128)(4,1)} %bitcast.18), calls=%async_computation.2 | async-start | bytes 4194304
  45.0 1.5 %collective-permute-start.17 = (bf16[64,1792]{1,0:T(8,128)(2,1)S(1)}, bf16[64,1792]{1,0:T(8,128)(2,1)S(1)}, u32[]{:S(2)}, u32[]{:S(2)}) collective-permute-start(bf16[64,1792]{1,0:T(8,128)(2,1)S(1)} %collective-permute-done.7.refs_12_), channel_id=1, source_target_pairs={{0,1},{1,0},{2,3},{3,2},{4,5},{5,4},{6,7},{7,6},{8,9},{9,8},{10,11... | collective-permute-start | bytes 688136 | tf_op jit(solution)/shard_map/ppermute | solution.py:29
  46.5 8.8 %copy-start.20 = (bf16[5120]{0:T(1024)(128)(2,1)S(1)}, bf16[5120]{0:T(1024)(128)(2,1)}, u32[]{:S(2)}) copy-start(bf16[5120]{0:T(1024)(128)(2,1)} %param.25) | copy-start | bytes 30724
  46.5 11.3 %copy-start.7 = (bf16[4,5120]{1,0:T(4,128)(2,1)S(1)}, bf16[4,5120]{1,0:T(4,128)(2,1)}, u32[]{:S(2)}) copy-start(bf16[4,5120]{1,0:T(4,128)(2,1)} %hidden_ref.1) | copy-start | bytes 122884
  46.5 11.3 %copy-start.15 = (s32[4,6]{1,0:T(4,128)S(1)}, s32[4,6]{1,0:T(4,128)}, u32[]{:S(2)}) copy-start(s32[4,6]{1,0:T(4,128)} %ids_ref.1) | copy-start | bytes 292
  46.6 11.3 %copy-start.16 = (bf16[4,6]{1,0:T(4,128)(2,1)S(1)}, bf16[4,6]{1,0:T(4,128)(2,1)}, u32[]{:S(2)}) copy-start(bf16[4,6]{1,0:T(4,128)(2,1)} %weight_ref.1) | copy-start | bytes 148
  46.6 32.2 %copy-start = (bf16[1,5120,384]{2,1,0:T(8,128)(2,1)S(1)}, bf16[1,5120,384]{2,1,0:T(8,128)(2,1)}, u32[]{:S(2)}) copy-start(bf16[1,5120,384]{2,1,0:T(8,128)(2,1)} %refs_8_.3) | copy-start | bytes 11796484
  46.6 32.2 %copy-start.1 = (bf16[1,5120,384]{2,1,0:T(8,128)(2,1)S(1)}, bf16[1,5120,384]{2,1,0:T(8,128)(2,1)}, u32[]{:S(2)}) copy-start(bf16[1,5120,384]{2,1,0:T(8,128)(2,1)} %refs_9_.1) | copy-start | bytes 11796484
  46.6 32.2 %copy-start.2 = (bf16[1,384,5120]{2,1,0:T(8,128)(2,1)S(1)}, bf16[1,384,5120]{2,1,0:T(8,128)(2,1)}, u32[]{:S(2)}) copy-start(bf16[1,384,5120]{2,1,0:T(8,128)(2,1)} %refs_10_.1) | copy-start | bytes 11796484
  50.3 1.4 %collective-permute-start.18 = (bf16[16,5120]{1,0:T(8,128)(2,1)S(1)}, bf16[16,5120]{1,0:T(8,128)(2,1)S(1)}, u32[]{:S(2)}, u32[]{:S(2)}) collective-permute-start(bf16[16,5120]{1,0:T(8,128)(2,1)S(1)} %get-tuple-element.83), channel_id=1, source_target_pairs={{0,1},{1,0},{2,3},{3,2},{4,5},{5,4},{6,7},{7,6},{8,9},{9,8},{10,11... | collective-permute-start | bytes 491528 | tf_op jit(solution)/shard_map/ppermute | solution.py:29
  51.8 5.0 %collective-permute-start.19 = (bf16[4,5120]{1,0:T(4,128)(2,1)S(1)}, bf16[4,5120]{1,0:T(4,128)(2,1)S(1)}, u32[]{:S(2)}, u32[]{:S(2)}) collective-permute-start(bf16[4,5120]{1,0:T(4,128)(2,1)S(1)} %get-tuple-element.85), channel_id=1, source_target_pairs={{0,6},{1,7},{2,4},{3,5},{4,2},{5,3},{6,0},{7,1},{8,14},{9,15},{10,... | collective-permute-start | bytes 122888 | tf_op jit(solution)/shard_map/ppermute | solution.py:29
  53.3 4.0 %collective-permute-start.20 = (bf16[4,5120]{1,0:T(4,128)(2,1)S(1)}, bf16[4,5120]{1,0:T(4,128)(2,1)S(1)}, u32[]{:S(2)}, u32[]{:S(2)}) collective-permute-start(bf16[4,5120]{1,0:T(4,128)(2,1)S(1)} %get-tuple-element.86), channel_id=1, source_target_pairs={{0,4},{1,5},{2,6},{3,7},{4,0},{5,1},{6,2},{7,3},{8,12},{9,13},{10,... | collective-permute-start | bytes 122888 | tf_op jit(solution)/shard_map/ppermute | solution.py:29
  53.8 4.0 %collective-permute-start.21 = (bf16[4,5120]{1,0:T(4,128)(2,1)S(1)}, bf16[4,5120]{1,0:T(4,128)(2,1)S(1)}, u32[]{:S(2)}, u32[]{:S(2)}) collective-permute-start(bf16[4,5120]{1,0:T(4,128)(2,1)S(1)} %get-tuple-element.87), channel_id=1, source_target_pairs={{0,2},{1,3},{2,0},{3,1},{4,6},{5,7},{6,4},{7,5},{8,10},{9,11},{10,... | collective-permute-start | bytes 122888 | tf_op jit(solution)/shard_map/ppermute | solution.py:29
  58.5 4.9 %collective-permute-start.22 = (bf16[4,5248]{1,0:T(4,128)(2,1)S(1)}, bf16[4,5248]{1,0:T(4,128)(2,1)S(1)}, u32[]{:S(2)}, u32[]{:S(2)}) collective-permute-start(bf16[4,5248]{1,0:T(4,128)(2,1)S(1)} %get-tuple-element.89.refs_0_), channel_id=1, source_target_pairs={{0,8},{8,0},{16,24},{24,16},{1,9},{9,1},{17,25},{25,17},{2,10},{10... | collective-permute-start | bytes 125960 | tf_op jit(solution)/shard_map/ppermute | solution.py:29
  59.5 4.9 %collective-permute-start.23 = (bf16[4,5248]{1,0:T(4,128)(2,1)S(1)}, bf16[4,5248]{1,0:T(4,128)(2,1)S(1)}, u32[]{:S(2)}, u32[]{:S(2)}) collective-permute-start(bf16[4,5248]{1,0:T(4,128)(2,1)S(1)} %get-tuple-element.89.refs_0_), channel_id=1, source_target_pairs={{0,16},{8,24},{16,0},{24,8},{1,17},{9,25},{17,1},{25,9},{2,18},{10... | collective-permute-start | bytes 125960 | tf_op jit(solution)/shard_map/ppermute | solution.py:29
  62.2 5.8 %collective-permute-start.24 = (bf16[4,5248]{1,0:T(4,128)(2,1)S(1)}, bf16[4,5248]{1,0:T(4,128)(2,1)S(1)}, u32[]{:S(2)}, u32[]{:S(2)}) collective-permute-start(bf16[4,5248]{1,0:T(4,128)(2,1)S(1)} %get-tuple-element.89.refs_0_), channel_id=1, source_target_pairs={{0,24},{8,16},{16,8},{24,0},{1,25},{9,17},{17,9},{25,1},{2,26},{10... | collective-permute-start | bytes 125960 | tf_op jit(solution)/shard_map/ppermute | solution.py:29
  68.1 5.9 %collective-permute-start.25 = (bf16[16,5248]{1,0:T(8,128)(2,1)S(1)}, bf16[16,5248]{1,0:T(8,128)(2,1)S(1)}, u32[]{:S(2)}, u32[]{:S(2)}) collective-permute-start(bf16[16,5248]{1,0:T(8,128)(2,1)S(1)} %shard_map.175.refs_0_), channel_id=1, source_target_pairs={{0,2},{1,3},{2,0},{3,1},{4,6},{5,7},{6,4},{7,5},{8,10},{9,11},{10,... | collective-permute-start | bytes 503816 | tf_op jit(solution)/shard_map/ppermute | solution.py:29
  69.6 6.2 %collective-permute-start.26 = (bf16[16,5248]{1,0:T(8,128)(2,1)S(1)}, bf16[16,5248]{1,0:T(8,128)(2,1)S(1)}, u32[]{:S(2)}, u32[]{:S(2)}) collective-permute-start(bf16[16,5248]{1,0:T(8,128)(2,1)S(1)} %shard_map.175.refs_0_), channel_id=1, source_target_pairs={{0,4},{1,5},{2,6},{3,7},{4,0},{5,1},{6,2},{7,3},{8,12},{9,13},{10,... | collective-permute-start | bytes 503816 | tf_op jit(solution)/shard_map/ppermute | solution.py:29
  71.1 6.3 %collective-permute-start.27 = (bf16[16,5248]{1,0:T(8,128)(2,1)S(1)}, bf16[16,5248]{1,0:T(8,128)(2,1)S(1)}, u32[]{:S(2)}, u32[]{:S(2)}) collective-permute-start(bf16[16,5248]{1,0:T(8,128)(2,1)S(1)} %shard_map.175.refs_0_), channel_id=1, source_target_pairs={{0,6},{1,7},{2,4},{3,5},{4,2},{5,3},{6,0},{7,1},{8,14},{9,15},{10,... | collective-permute-start | bytes 503816 | tf_op jit(solution)/shard_map/ppermute | solution.py:29
  71.6 5.8 %collective-permute-start.28 = (bf16[16,5248]{1,0:T(8,128)(2,1)S(1)}, bf16[16,5248]{1,0:T(8,128)(2,1)S(1)}, u32[]{:S(2)}, u32[]{:S(2)}) collective-permute-start(bf16[16,5248]{1,0:T(8,128)(2,1)S(1)} %shard_map.175.refs_0_), channel_id=1, source_target_pairs={{0,1},{1,0},{2,3},{3,2},{4,5},{5,4},{6,7},{7,6},{8,9},{9,8},{10,11... | collective-permute-start | bytes 503816 | tf_op jit(solution)/shard_map/ppermute | solution.py:29
  73.9 3.5 %collective-permute-start.29 = (bf16[16,5248]{1,0:T(8,128)(2,1)S(1)}, bf16[16,5248]{1,0:T(8,128)(2,1)S(1)}, u32[]{:S(2)}, u32[]{:S(2)}) collective-permute-start(bf16[16,5248]{1,0:T(8,128)(2,1)S(1)} %collective-permute-done.25.refs_1_), channel_id=1, source_target_pairs={{0,1},{1,0},{2,3},{3,2},{4,5},{5,4},{6,7},{7,6},{8,9},{9,8},{10,11... | collective-permute-start | bytes 503816 | tf_op jit(solution)/shard_map/ppermute | solution.py:29
  75.9 1.6 %collective-permute-start.30 = (bf16[16,5248]{1,0:T(8,128)(2,1)S(1)}, bf16[16,5248]{1,0:T(8,128)(2,1)S(1)}, u32[]{:S(2)}, u32[]{:S(2)}) collective-permute-start(bf16[16,5248]{1,0:T(8,128)(2,1)S(1)} %collective-permute-done.26.refs_2_), channel_id=1, source_target_pairs={{0,1},{1,0},{2,3},{3,2},{4,5},{5,4},{6,7},{7,6},{8,9},{9,8},{10,11... | collective-permute-start | bytes 503816 | tf_op jit(solution)/shard_map/ppermute | solution.py:29
  77.4 1.4 %collective-permute-start.31 = (bf16[16,5248]{1,0:T(8,128)(2,1)S(1)}, bf16[16,5248]{1,0:T(8,128)(2,1)S(1)}, u32[]{:S(2)}, u32[]{:S(2)}) collective-permute-start(bf16[16,5248]{1,0:T(8,128)(2,1)S(1)} %collective-permute-done.27.refs_3_), channel_id=1, source_target_pairs={{0,1},{1,0},{2,3},{3,2},{4,5},{5,4},{6,7},{7,6},{8,9},{9,8},{10,11... | collective-permute-start | bytes 503816 | tf_op jit(solution)/shard_map/ppermute | solution.py:29
  81.9 2.2 %collective-permute-start.32 = (bf16[64,5120]{1,0:T(8,128)(2,1)S(1)}, bf16[64,5120]{1,0:T(8,128)(2,1)S(1)}, u32[]{:S(2)}, u32[]{:S(2)}) collective-permute-start(bf16[64,5120]{1,0:T(8,128)(2,1)S(1)} %get-tuple-element.91), channel_id=1, source_target_pairs={{0,1},{1,0},{2,3},{3,2},{4,5},{5,4},{6,7},{7,6},{8,9},{9,8},{10,11... | collective-permute-start | bytes 1966088 | tf_op jit(solution)/shard_map/ppermute | solution.py:29
  84.2 8.1 %collective-permute-start.33 = (bf16[16,5120]{1,0:T(8,128)(2,1)S(1)}, bf16[16,5120]{1,0:T(8,128)(2,1)S(1)}, u32[]{:S(2)}, u32[]{:S(2)}) collective-permute-start(bf16[16,5120]{1,0:T(8,128)(2,1)S(1)} %get-tuple-element.93), channel_id=1, source_target_pairs={{0,6},{1,7},{2,4},{3,5},{4,2},{5,3},{6,0},{7,1},{8,14},{9,15},{10,... | collective-permute-start | bytes 491528 | tf_op jit(solution)/shard_map/ppermute | solution.py:29
  85.4 9.5 %collective-permute-start.34 = (bf16[16,5120]{1,0:T(8,128)(2,1)S(1)}, bf16[16,5120]{1,0:T(8,128)(2,1)S(1)}, u32[]{:S(2)}, u32[]{:S(2)}) collective-permute-start(bf16[16,5120]{1,0:T(8,128)(2,1)S(1)} %get-tuple-element.94), channel_id=1, source_target_pairs={{0,4},{1,5},{2,6},{3,7},{4,0},{5,1},{6,2},{7,3},{8,12},{9,13},{10,... | collective-permute-start | bytes 491528 | tf_op jit(solution)/shard_map/ppermute | solution.py:29
  86.3 8.7 %collective-permute-start.35 = (bf16[16,5120]{1,0:T(8,128)(2,1)S(1)}, bf16[16,5120]{1,0:T(8,128)(2,1)S(1)}, u32[]{:S(2)}, u32[]{:S(2)}) collective-permute-start(bf16[16,5120]{1,0:T(8,128)(2,1)S(1)} %get-tuple-element.95), channel_id=1, source_target_pairs={{0,2},{1,3},{2,0},{3,1},{4,6},{5,7},{6,4},{7,5},{8,10},{9,11},{10,... | collective-permute-start | bytes 491528 | tf_op jit(solution)/shard_map/ppermute | solution.py:29
  95.1 6.0 %collective-permute-start.36 = (bf16[4,5120]{1,0:T(4,128)(2,1)S(1)}, bf16[4,5120]{1,0:T(4,128)(2,1)S(1)}, u32[]{:S(2)}, u32[]{:S(2)}) collective-permute-start(bf16[4,5120]{1,0:T(4,128)(2,1)S(1)} %get-tuple-element.106), channel_id=1, source_target_pairs={{0,24},{8,16},{16,8},{24,0},{1,25},{9,17},{17,9},{25,1},{2,26},{10... | collective-permute-start | bytes 122888 | tf_op jit(solution)/shard_map/ppermute | solution.py:29
  96.4 5.8 %collective-permute-start.37 = (bf16[4,5120]{1,0:T(4,128)(2,1)S(1)}, bf16[4,5120]{1,0:T(4,128)(2,1)S(1)}, u32[]{:S(2)}, u32[]{:S(2)}) collective-permute-start(bf16[4,5120]{1,0:T(4,128)(2,1)S(1)} %get-tuple-element.108), channel_id=1, source_target_pairs={{0,16},{8,24},{16,0},{24,8},{1,17},{9,25},{17,1},{25,9},{2,18},{10... | collective-permute-start | bytes 122888 | tf_op jit(solution)/shard_map/ppermute | solution.py:29
  96.6 5.6 %collective-permute-start.38 = (bf16[4,5120]{1,0:T(4,128)(2,1)S(1)}, bf16[4,5120]{1,0:T(4,128)(2,1)S(1)}, u32[]{:S(2)}, u32[]{:S(2)}) collective-permute-start(bf16[4,5120]{1,0:T(4,128)(2,1)S(1)} %get-tuple-element.107), channel_id=1, source_target_pairs={{0,8},{8,0},{16,24},{24,16},{1,9},{9,1},{17,25},{25,17},{2,10},{10... | collective-permute-start | bytes 122888 | tf_op jit(solution)/shard_map/ppermute | solution.py:29
  (3 other events, 17.3 us)
